TPU v7x, 32 devices: a whole 2x2x4 slice. The times are simulated.
32 devices in a mesh: dp: 4 (over y, core), fsdp: 8 (over z, x).
Axes of the slice: x: 2, y: 2, z: 4, core: 2. Of those that a mesh axis runs over, the one named last changes fastest.
Arguments:
- doc_inputs: float32 [32, 512, 768], P(('dp', 'fsdp')), may hold values from -6 to 6
- query_inputs: float32 [384, 32, 768], P(('dp', 'fsdp')), may hold values from -6 to 6
- doc_mask: int32 [32, 512], P(('dp', 'fsdp')), may hold values from 0 to 1, as said below
- query_lengths: int32 [384], P(('dp', 'fsdp')), may hold values from 8 to 32, as said below
- doc_cotangent: float32 [32, 512, 768], P(('dp', 'fsdp')), may hold values from -6 to 6
- query_cotangent: float32 [384, 32, 768], P(('dp', 'fsdp')), may hold values from -6 to 6
- qkv_weight: float32 [768, 2304], P(('dp', 'fsdp')), may hold values from -0.078125 to 0.078125
- out_weight: float32 [768, 768], P(('dp', 'fsdp')), may hold values from -1.75 to 1.75
- in_weight: float32 [768, 4096], P(('dp', 'fsdp')), may hold values from -0.21875 to 0.21875
- ff_weight: float32 [2048, 768], P(('dp', 'fsdp')), may hold values from -0.25 to 0.25
- attn_gain: float32 [768], replicated, may hold values from 0.1 to 1.9
- ffn_gain: float32 [768], replicated, may hold values from 0.1 to 1.9
- bias_table: float32 [32, 12], replicated, may hold values from -4 to 4
Outputs:
- doc_outputs: float32 [32, 512, 768], P(('dp', 'fsdp'))
- query_outputs: float32 [384, 32, 768], P(('dp', 'fsdp'))
- doc_input_grad: float32 [32, 512, 768], P(('dp', 'fsdp'))
- query_input_grad: float32 [384, 32, 768], P(('dp', 'fsdp'))
- qkv_weight_grad: float32 [768, 2304], P(('dp', 'fsdp'))
- out_weight_grad: float32 [768, 768], P(('dp', 'fsdp'))
- in_weight_grad: float32 [768, 4096], P(('dp', 'fsdp'))
- ff_weight_grad: float32 [2048, 768], P(('dp', 'fsdp'))
- attn_gain_grad: float32 [768], replicated
- ffn_gain_grad: float32 [768], replicated
- bias_table_grad: float32 [32, 12], replicated
Inputs may be any that keep to these rules, and one draw needn't show every extreme that they name: `doc_mask`: each document's row is ones on a prefix of 256 or more positions and zeros after it; some document has no padding. `query_lengths`: some query group is full and some has exactly 8 real tokens.
All inputs are finite; a program needn't handle non-finite values.
Results may differ from a plain program's by a relative error of at most 0.014.
The roundings to bfloat16 on the way count: a program that leaves them out, or rounds other values in their place, can miss the bound.
Values may be sent and summed in bfloat16 or wider, within the bound.
No kernel may reach another device: no remote copies, remote signals or barrier semaphores. Data moves between devices by JAX's collectives and lax.ppermute only.
A program may use at most 192 MiB of HBM per device.

v0:
```python
import jax
import jax.numpy as jnp
from jax import lax
from jax.sharding import PartitionSpec as P

epsilon = 1e-06
highest = lax.Precision.HIGHEST


def rms_norm(values, gain_vector):
    inverse = lax.rsqrt(jnp.mean(values * values, axis=-1, keepdims=True) + epsilon)
    return values * inverse * gain_vector


def buckets_of(length):
    places = jnp.arange(length, dtype=jnp.int32)
    relative = places[None, :] - places[:, None]
    distance = jnp.abs(relative)
    larger = jnp.zeros_like(distance)
    for threshold in (12, 16, 23, 32, 46, 64, 91):
        larger = larger + (distance >= threshold).astype(jnp.int32)
    bucket = jnp.where(distance < 8, distance, 8 + larger)
    return bucket + 16 * (relative > 0).astype(jnp.int32)


def bucket_tables(length, bias_table):
    labels = jnp.arange(bias_table.shape[0], dtype=jnp.int32)
    onehot = (buckets_of(length)[:, :, None] == labels).astype(jnp.float32)
    position_bias = jnp.einsum("qkn,nh->hqk", onehot, bias_table, precision=highest)
    return (position_bias, onehot.astype(jnp.bfloat16))


def gated_unit(gate_up):
    hidden_size = gate_up.shape[-1] // 2
    return jax.nn.gelu(gate_up[:, :hidden_size], approximate=True) * gate_up[:, hidden_size:]


def score_block(packed, key_mask, position_bias):
    queries = packed[:, :, 0]
    key_rows = packed[:, :, 1]
    masking = jnp.where(key_mask > 0, 0.0, -1000000000.0).astype(jnp.float32)
    scores = jnp.einsum("bqhc,bkhc->bhqk", queries, key_rows, preferred_element_type=jnp.float32)
    return scores + position_bias[None] + masking[:, None, None, :]


def attend_forward(packed, key_mask, position_bias):
    scores = score_block(packed, key_mask, position_bias)
    row_peak = jnp.max(scores, axis=-1, keepdims=True)
    raised = jnp.exp(scores - row_peak)
    row_total = jnp.sum(raised, axis=-1, keepdims=True)
    probs_low = (raised / row_total).astype(jnp.bfloat16)
    mixed_rows = jnp.einsum(
        "bhqk,bkhc->bqhc", probs_low, packed[:, :, 2], preferred_element_type=jnp.float32
    )
    return (mixed_rows.astype(jnp.bfloat16), row_peak[..., 0] + jnp.log(row_total[..., 0]))


def attend_backward(packed, key_mask, position_bias, onehot, log_total, grad_mixed):
    queries = packed[:, :, 0]
    key_rows = packed[:, :, 1]
    value_rows = packed[:, :, 2]
    scores = score_block(packed, key_mask, position_bias)
    probs = jnp.exp(scores - log_total[..., None])
    probs_low = probs.astype(jnp.bfloat16)
    grad_values = jnp.einsum(
        "bhqk,bqhc->bkhc", probs_low, grad_mixed, preferred_element_type=jnp.float32
    )
    grad_probs = jnp.einsum(
        "bqhc,bkhc->bhqk", grad_mixed, value_rows, preferred_element_type=jnp.float32
    )
    weighted = jnp.sum(probs * grad_probs, axis=-1, keepdims=True)
    grad_scores = (probs * (grad_probs - weighted)).astype(jnp.bfloat16)
    grad_queries = jnp.einsum(
        "bhqk,bkhc->bqhc", grad_scores, key_rows, preferred_element_type=jnp.float32
    )
    grad_keys = jnp.einsum(
        "bhqk,bqhc->bkhc", grad_scores, queries, preferred_element_type=jnp.float32
    )
    grad_table = jnp.einsum("bhqk,qkn->nh", grad_scores, onehot, preferred_element_type=jnp.float32)
    stacked = jnp.stack([grad_queries, grad_keys, grad_values], axis=2)
    return (stacked.astype(jnp.bfloat16), grad_table)


def body(
    doc_inputs,
    query_inputs,
    doc_mask,
    query_lengths,
    doc_cotangent,
    query_cotangent,
    qkv_weight,
    out_weight,
    in_weight,
    ff_weight,
    attn_gain,
    ffn_gain,
    bias_table,
):
    doc_count, doc_length, model_width = doc_inputs.shape
    group_count, group_length = (query_inputs.shape[0], query_inputs.shape[1])
    head_count = bias_table.shape[1]
    head_size = model_width // head_count
    doc_rows = doc_count * doc_length
    shards = (
        qkv_weight.astype(jnp.bfloat16),
        out_weight.astype(jnp.bfloat16),
        in_weight.astype(jnp.bfloat16),
        ff_weight.astype(jnp.bfloat16),
    )
    full_qkv, full_out, full_in, full_ff = (
        lax.all_gather(shards[0], ("dp", "fsdp"), axis=0, tiled=True),
        lax.all_gather(shards[1], ("dp", "fsdp"), axis=0, tiled=True),
        lax.all_gather(shards[2], ("dp", "fsdp"), axis=0, tiled=True),
        lax.all_gather(shards[3], ("dp", "fsdp"), axis=0, tiled=True),
    )
    places = jnp.arange(group_length, dtype=jnp.int32)
    query_mask = (places[None, :] < query_lengths[:, None]).astype(jnp.int32)
    doc_bias, doc_onehot = bucket_tables(doc_length, bias_table)
    query_bias, query_onehot = bucket_tables(group_length, bias_table)
    rows = jnp.concatenate(
        [doc_inputs.reshape(doc_rows, model_width), query_inputs.reshape(-1, model_width)], axis=0
    )
    normed, norm_pull = jax.vjp(rms_norm, rows, attn_gain)
    normed_low = normed.astype(jnp.bfloat16)
    projected = jnp.dot(normed_low, full_qkv, preferred_element_type=jnp.float32).astype(
        jnp.bfloat16
    )
    doc_packed = projected[:doc_rows].reshape(doc_count, doc_length, 3, head_count, head_size)
    query_packed = projected[doc_rows:].reshape(group_count, group_length, 3, head_count, head_size)

    def doc_forward(pieces):
        packed, key_mask = pieces
        mixed_rows, log_total = attend_forward(packed[None], key_mask[None], doc_bias)
        return (mixed_rows[0], log_total[0])

    doc_mixed, doc_log_total = lax.map(doc_forward, (doc_packed, doc_mask))
    query_mixed, query_log_total = attend_forward(query_packed, query_mask, query_bias)
    mixed_all = jnp.concatenate(
        [doc_mixed.reshape(doc_rows, model_width), query_mixed.reshape(-1, model_width)], axis=0
    )
    middle = rows + jnp.dot(mixed_all, full_out, preferred_element_type=jnp.float32)
    normed_two, norm_pull_two = jax.vjp(rms_norm, middle, ffn_gain)
    normed_two_low = normed_two.astype(jnp.bfloat16)
    gate_up = jnp.dot(normed_two_low, full_in, preferred_element_type=jnp.float32)
    activated, gated_pull = jax.vjp(gated_unit, gate_up)
    activated_low = activated.astype(jnp.bfloat16)
    outputs = middle + jnp.dot(activated_low, full_ff, preferred_element_type=jnp.float32)
    full_qkv, full_out, full_in, full_ff = (
        lax.all_gather(shards[0], ("dp", "fsdp"), axis=0, tiled=True),
        lax.all_gather(shards[1], ("dp", "fsdp"), axis=0, tiled=True),
        lax.all_gather(shards[2], ("dp", "fsdp"), axis=0, tiled=True),
        lax.all_gather(shards[3], ("dp", "fsdp"), axis=0, tiled=True),
    )
    cotangent = jnp.concatenate(
        [doc_cotangent.reshape(doc_rows, model_width), query_cotangent.reshape(-1, model_width)],
        axis=0,
    )
    cotangent_low = cotangent.astype(jnp.bfloat16)
    grad_ff = jnp.einsum(
        "rf,rd->fd", activated_low, cotangent_low, preferred_element_type=jnp.float32
    )
    grad_activated = jnp.einsum(
        "rd,fd->rf", cotangent_low, full_ff, preferred_element_type=jnp.float32
    )
    (grad_gate_up,) = gated_pull(grad_activated)
    grad_gate_low = grad_gate_up.astype(jnp.bfloat16)
    grad_in = jnp.einsum(
        "rd,re->de", normed_two_low, grad_gate_low, preferred_element_type=jnp.float32
    )
    grad_normed_two = jnp.einsum(
        "re,de->rd", grad_gate_low, full_in, preferred_element_type=jnp.float32
    )
    grad_middle, grad_ffn_gain = norm_pull_two(grad_normed_two)
    grad_middle = grad_middle + cotangent
    in_grad_shard, ff_grad_shard = (
        lax.psum_scatter(grad_in, ("dp", "fsdp"), scatter_dimension=0, tiled=True),
        lax.psum_scatter(grad_ff, ("dp", "fsdp"), scatter_dimension=0, tiled=True),
    )
    grad_middle_low = grad_middle.astype(jnp.bfloat16)
    grad_out = jnp.einsum(
        "rd,re->de", mixed_all, grad_middle_low, preferred_element_type=jnp.float32
    )
    grad_mixed = jnp.einsum(
        "re,de->rd", grad_middle_low, full_out, preferred_element_type=jnp.float32
    ).astype(jnp.bfloat16)
    doc_grad_mixed = grad_mixed[:doc_rows].reshape(doc_count, doc_length, head_count, head_size)
    query_grad_mixed = grad_mixed[doc_rows:].reshape(
        group_count, group_length, head_count, head_size
    )

    def doc_backward(running, pieces):
        packed, key_mask, log_total, grad_rows = pieces
        grad_packed, grad_table = attend_backward(
            packed[None], key_mask[None], doc_bias, doc_onehot, log_total[None], grad_rows[None]
        )
        return (running + grad_table, grad_packed[0])

    doc_table, doc_grad_packed = lax.scan(
        doc_backward,
        jnp.zeros_like(bias_table),
        (doc_packed, doc_mask, doc_log_total, doc_grad_mixed),
    )
    query_grad_packed, query_table = attend_backward(
        query_packed, query_mask, query_bias, query_onehot, query_log_total, query_grad_mixed
    )
    grad_projected = jnp.concatenate(
        [
            doc_grad_packed.reshape(doc_rows, 3 * model_width),
            query_grad_packed.reshape(-1, 3 * model_width),
        ],
        axis=0,
    )
    grad_qkv = jnp.einsum(
        "rd,re->de", normed_low, grad_projected, preferred_element_type=jnp.float32
    )
    grad_normed = jnp.einsum(
        "re,de->rd", grad_projected, full_qkv, preferred_element_type=jnp.float32
    )
    grad_rows, grad_attn_gain = norm_pull(grad_normed)
    grad_inputs = grad_middle + grad_rows
    qkv_grad_shard, out_grad_shard = (
        lax.psum_scatter(grad_qkv, ("dp", "fsdp"), scatter_dimension=0, tiled=True),
        lax.psum_scatter(grad_out, ("dp", "fsdp"), scatter_dimension=0, tiled=True),
    )
    attn_gain_grad, ffn_gain_grad, bias_table_grad = lax.psum(
        (grad_attn_gain, grad_ffn_gain, doc_table + query_table), ("dp", "fsdp")
    )
    return (
        outputs[:doc_rows].reshape(doc_inputs.shape),
        outputs[doc_rows:].reshape(query_inputs.shape),
        grad_inputs[:doc_rows].reshape(doc_inputs.shape),
        grad_inputs[doc_rows:].reshape(query_inputs.shape),
        qkv_grad_shard,
        out_grad_shard,
        in_grad_shard,
        ff_grad_shard,
        attn_gain_grad,
        ffn_gain_grad,
        bias_table_grad,
    )


def solution(mesh):
    placed = (
        P(("dp", "fsdp"), None, None),
        P(("dp", "fsdp"), None, None),
        P(("dp", "fsdp"), None),
        P(("dp", "fsdp")),
        P(("dp", "fsdp"), None, None),
        P(("dp", "fsdp"), None, None),
        P(("dp", "fsdp"), None),
        P(("dp", "fsdp"), None),
        P(("dp", "fsdp"), None),
        P(("dp", "fsdp"), None),
        P(),
        P(),
        P(),
    )
    return jax.shard_map(
        body,
        mesh=mesh,
        in_specs=placed,
        out_specs=(
            P(("dp", "fsdp"), None, None),
            P(("dp", "fsdp"), None, None),
            P(("dp", "fsdp"), None, None),
            P(("dp", "fsdp"), None, None),
            P(("dp", "fsdp"), None),
            P(("dp", "fsdp"), None),
            P(("dp", "fsdp"), None),
            P(("dp", "fsdp"), None),
            P(),
            P(),
            P(),
        ),
        check_vma=False,
    )
```

profile of v0, /device:TPU:0, one launch (start us, length us, event | category | flops | bytes accessed | tf_op | source)
XLA Modules:
  0.0 818.5 jit_solution(10282185169242262554)
XLA Ops:
  7.3 1.7 convert_element_type.242
  9.0 1.5 convert_element_type.266
  10.6 1.7 convert_element_type.268
  12.4 1.6 convert_element_type.270
  14.6 1.9 multiply_reduce_fusion.6
  17.1 1.1 convolution_bitcast_fusion
  18.4 13.8 %fusion = f32[512,512,12]{0,2,1:T(8,128)} fusion(s32[512,512]{0,1:T(8,128)S(1)} %fusion.48, f32[32,12]{0,1:T(8,128)S(1)} %copy-done), kind=kOutput, calls=%fused_computation.2 | convolution fusion | flops 1216348160 | bytes 13633024 | tf_op jit(solution)/shard_map/qkn,nh->hqk/dot_general | solution.py:29
  32.2 42.3 %all-gather.5.cloned.1.call-done = bf16[768,2304]{1,0:T(8,128)(2,1)} async-done(((bf16[24,2304]{1,0:T(8,128)(2,1)}), bf16[768,2304]{1,0:T(8,128)(2,1)}) %all-gather.5.cloned.1.call-update) | async-done | bytes 3538960 | tf_op jit(solution)/shard_map/all_gather | solution.py:111
  74.5 5.8 convolution_convert_fusion
  80.3 1.3 slice.84
  81.8 2.5 copy.65
  84.3 6.4 reshape.331
  90.7 3.3 fusion.95
  94.1 0.9 fusion.96
  96.2 0.8 fusion.26
  97.1 1.7 copy.74
  98.7 2.4 reshape.332
  101.1 1.1 copy.75
  102.1 15.2 %fusion.97 = (f32[12,512]{1,0:T(8,128)S(1)}, f32[12,512,512]{1,2,0:T(8,128)S(1)}) fusion(f32[512]{0:T(512)S(1)} %bitcast.153, f32[512,512,12]{0,2,1:T(8,128)} %fusion, bf16[1,512,3,12,64]{1,4,3,2,0:T(8,128)(2,1)} %bitcast.124), kind=kOutput, calls=%fused_computation.158 | convolution fusion | flops 412084224 | bytes 30959616 | tf_op jit(solution)/shard_map/while/body/eval_jaxpr/bqhc,bkhc->bhqk/dot_general | solution.py:42
  117.3 1.9 fusion.5
  119.2 2.8 copy-done.2
  122.7 4.7 fusion.33
  127.4 3.7 all-gather.7.cloned.1.call-done
  131.1 5.1 multiply_reduce_fusion.5
  136.2 66.9 %all-gather.9.cloned.1.call-done = bf16[768,4096]{1,0:T(8,128)(2,1)} async-done(((bf16[24,4096]{1,0:T(8,128)(2,1)}), bf16[768,4096]{1,0:T(8,128)(2,1)}) %all-gather.9.cloned.1.call-update) | async-done | bytes 6291472 | tf_op jit(solution)/shard_map/all_gather | solution.py:113
  203.1 11.9 %fusion.94 = f32[896,4096]{1,0:T(8,128)} fusion(bf16[768,4096]{1,0:T(8,128)(2,1)} %all-gather.9.cloned.1.call-done, f32[896,768]{1,0:T(8,128)} %get-tuple-element.76, f32[768]{0:T(1024)S(1)} %copy-done.40, f32[896]{0:T(1024)S(1)} %fusion.85), kind=kOutput, calls=%fused_computation.155 | convolution fusion | flops 5639208960 | bytes 23730688 | tf_op jit(solution)/shard_map/dot_general | solution.py:144
  215.0 49.1 %all-gather.11.cloned.1.call-done = bf16[2048,768]{1,0:T(8,128)(2,1)} async-done(((bf16[64,768]{1,0:T(8,128)(2,1)}), bf16[2048,768]{1,0:T(8,128)(2,1)}) %all-gather.11.cloned.1.call-update) | async-done | bytes 3145744 | tf_op jit(solution)/shard_map/all_gather | solution.py:114
  264.1 16.6 %fusion.22 = (f32[896,2048]{1,0:T(8,128)}, f32[896,2048]{1,0:T(8,128)}, bf16[896,2048]{1,0:T(8,128)(2,1)}) fusion(f32[896,4096]{1,0:T(8,128)} %fusion.94, bf16[2048,768]{1,0:T(8,128)(2,1)} %all-gather.11.cloned.1.call-done, f32[384,768]{1,0:T(8,128)S(1)} %bitcast.148, f32[512,768]{1,0:T(8,128)} %bitcast.145), kind=kOutput, calls=%fused_computation.50 | convolution fusion | flops 2865364992 | bytes 38928384 | tf_op jit(solution)/shard_map/rd,fd->rf/dot_general | solution.py:162
  280.8 15.9 %multiply_reduce_fusion.1 = (f32[768]{0:T(1024)}, f32[896]{0:T(1024)}, f32[896,768]{1,0:T(8,128)}) fusion(f32[896,768]{1,0:T(8,128)} %get-tuple-element.76, f32[896]{0:T(1024)S(1)} %fusion.85, f32[768]{0:T(1024)S(1)} %copy-done.40, bf16[768,4096]{1,0:T(8,128)(2,1)} %all-gather.9.cloned.1.call-done, f32[896,2048]{1,0:T(8,128)} %get-tuple-element.66, ...), kind=kOutput, calls=%fused_computation.40 | convolution fusion | flops 5648611328 | bytes 26489856 | tf_op jit(solution)/shard_map/re,de->rd/dot_general | solution.py:170
  297.4 3.8 fusion.18
  301.2 1.6 copy-done.5
  302.8 2.8 fusion.58
  305.7 8.7 %fusion.67 = f32[2048,768]{1,0:T(8,128)} fusion(bf16[896,2048]{1,0:T(8,128)(2,1)} %get-tuple-element.67, f32[384,768]{1,0:T(8,128)S(1)} %bitcast.150, f32[512,768]{1,0:T(8,128)} %bitcast.147), kind=kOutput, calls=%fused_computation.119 | convolution fusion | flops 2821324800 | bytes 12713984 | tf_op jit(solution)/shard_map/rf,rd->fd/dot_general | solution.py:159
  315.4 3.6 convolution_convert_fusion.1
  319.0 0.9 slice.93
  319.9 2.1 copy.79
  322.1 3.2 reshape.338
  325.3 2.9 multiply_reduce_fusion.7
  328.1 0.8 convert_reduce_fusion
  331.8 0.9 pad_maximum_fusion.1
  332.7 3.7 copy.83
  336.3 6.6 convert_element_type.280
  342.9 4.0 copy.84
  347.0 11.6 %multiply_reduce_fusion = (f32[12,512]{1,0:T(8,128)S(1)}, f32[12,512,512]{1,2,0:T(8,128)}) fusion(f32[12,512,512]{1,2,0:T(8,128)} %copy-done.2, f32[12,512]{1,0:T(8,128)S(1)} %log_add_fusion.1, bf16[512,12,64]{0,2,1:T(8,128)(2,1)S(1)} %bitcast.129, bf16[1,512,3,12,64]{1,4,3,2,0:T(8,128)(2,1)S(1)} %bitcast.126), kind=kOutput, calls=%fused_computation.10 | convolution fusion | flops 412084224 | bytes 26796032 | tf_op jit(solution)/shard_map/while/body/eval_jaxpr/bqhc,bkhc->bhqk/dot_general | solution.py:68
  358.6 1.3 slice-done.2
  359.9 7.0 multiply_convert_fusion
  366.9 2.0 fusion.35
  369.6 1.1 fusion.34
  370.7 2.0 fusion.36
  373.1 1.4 copy-done.22
  374.6 0.8 copy-done.19
  376.0 6.8 fusion.20
  383.5 15.6 %fusion.46 = f32[768,4096]{1,0:T(8,128)} fusion(f32[896,2048]{1,0:T(8,128)} %get-tuple-element.66, f32[896,2048]{1,0:T(8,128)} %get-tuple-element.65, f32[896,768]{1,0:T(8,128)} %get-tuple-element.76, f32[768]{0:T(1024)S(1)} %copy-done.41, f32[896]{0:T(1024)S(1)} %fusion.85), kind=kOutput, calls=%fused_computation.92 | convolution fusion | flops 5646548992 | bytes 30022144 | tf_op jit(solution)/shard_map/rd,re->de/dot_general | solution.py:167
  399.1 7.0 convolution_add_fusion.1
  406.1 1.5 copy-done.21
  407.6 1.1 slice.91
  408.8 4.0 multiply_reduce_fusion.2
  413.4 1.1 slice.95
  414.5 5.3 fusion.42
  420.2 38.3 %all-reduce.2 = (f32[768]{0:T(1024)}, f32[768]{0:T(1024)}, f32[32,12]{0,1:T(8,128)}) all-reduce(f32[768]{0:T(1024)S(1)} %get-tuple-element.49, f32[768]{0:T(1024)S(1)} %copy-done.44, f32[32,12]{0,1:T(8,128)S(1)} %fusion.45), channel_id=1, replica_groups=mesh['dp'=4,'fsdp'=8] {'dp','fsdp'}, use_global_device_ids=true, to_apply=%region_15.16 | all-reduce | flops 1920 | bytes 15360 | tf_op jit(solution)/shard_map/psum | solution.py:225
  458.5 3.8 slice_bitcast_fusion
  462.3 61.9 %reduce-scatter.11.cloned.1.call-done = f32[64,768]{1,0:T(8,128)} async-done(((f32[2048,768]{1,0:T(8,128)}), f32[64,768]{1,0:T(8,128)}) %reduce-scatter.11.cloned.1.call-update) | async-done | bytes 196624 | tf_op jit(solution)/shard_map/reduce_scatter | solution.py:177
  524.2 124.6 %reduce-scatter.5.cloned.1.call-done = f32[24,2304]{1,0:T(8,128)} async-done(((f32[768,2304]{1,0:T(8,128)}), f32[24,2304]{1,0:T(8,128)}) %reduce-scatter.5.cloned.1.call-update) | async-done | bytes 221200 | tf_op jit(solution)/shard_map/reduce_scatter | solution.py:222
  648.8 162.6 %reduce-scatter.9.cloned.1.call-done = f32[24,4096]{1,0:T(8,128)} async-done(((f32[768,4096]{1,0:T(8,128)}), f32[24,4096]{1,0:T(8,128)}) %reduce-scatter.9.cloned.1.call-update) | async-done | bytes 393232 | tf_op jit(solution)/shard_map/reduce_scatter | solution.py:176
  (142 shorter events, 11.6 us)
Async XLA Ops:
  7.2 9.9 %copy-start = (f32[32,12]{0,1:T(8,128)S(1)}, f32[32,12]{0,1:T(8,128)}, u32[]{:S(2)}) copy-start(f32[32,12]{0,1:T(8,128)} %param.25) | copy-start | bytes 4612
  7.2 7.3 copy-start.45
  7.2 7.4 copy-start.12
  7.2 9.3 %copy-start.46 = (s32[12]{0:T(128)S(1)}, s32[12]{0:T(128)}, u32[]{:S(2)}) copy-start(s32[12]{0:T(128)} %param.16) | copy-start | bytes 148
  7.2 67.3 %all-gather.5.cloned.1.call-start = ((), (), s32[]{:S(2)}) async-start(), calls=%async_computation.4 | async-start | bytes 3649536 | tf_op jit(solution)/shard_map/all_gather | solution.py:111
  9.0 122.1 %all-gather.7.cloned.1.call-start = ((), (), s32[]{:S(2)}) async-start(), calls=%async_computation.5 | async-start | bytes 1216512 | tf_op jit(solution)/shard_map/all_gather | solution.py:112
  10.6 192.5 %all-gather.9.cloned.1.call-start = ((), (), s32[]{:S(2)}) async-start(), calls=%async_computation.6 | async-start | bytes 6488064 | tf_op jit(solution)/shard_map/all_gather | solution.py:113
  12.4 251.8 %all-gather.11.cloned.1.call-start = ((), (), s32[]{:S(2)}) async-start(), calls=%async_computation.7 | async-start | bytes 3244032 | tf_op jit(solution)/shard_map/all_gather | solution.py:114
  14.0 448.3 %reduce-scatter.7.cloned.1.call-start = ((), (), s32[]{:S(2)}) async-start(), calls=%async_computation.9 | async-start | bytes 2433024 | tf_op jit(solution)/shard_map/reduce_scatter | solution.py:223
  14.1 2.7 copy-start.36
  14.5 17.7 %copy-start.15 = (s32[512,512]{0,1:T(8,128)}, s32[512,512]{0,1:T(8,128)S(1)}, u32[]{:S(2)}) copy-start(s32[512,512]{0,1:T(8,128)S(1)} %fusion.48) | copy-start | bytes 3145732
  16.5 0.6 copy-start.38
  18.4 56.2 %copy-start.42 = (f32[768]{0:T(1024)S(1)}, f32[768]{0:T(1024)}, u32[]{:S(2)}) copy-start(f32[768]{0:T(1024)} %param.23) | copy-start | bytes 9220
  94.0 1.7 copy-start.7
  94.1 1.7 copy-start.9
  94.1 2.2 copy-start.17
  94.9 2.1 copy-start.27
  95.8 1.3 copy-start.30
  117.3 4.7 copy-start.2
  117.3 4.7 copy-start.32
  122.1 0.6 copy-start.34
  122.7 8.4 %copy-start.18 = (f32[12,32,768]{2,1,0:T(8,128)S(1)}, f32[12,32,768]{2,1,0:T(8,128)}, u32[]{:S(2)}) copy-start(f32[12,32,768]{2,1,0:T(8,128)} %param.14) | copy-start | bytes 3538948
  131.1 72.0 %copy-start.40 = (f32[768]{0:T(1024)S(1)}, f32[768]{0:T(1024)}, u32[]{:S(2)}) copy-start(f32[768]{0:T(1024)} %param.24) | copy-start | bytes 9220
  203.1 61.0 %copy-start.26 = (f32[12,32,768]{2,1,0:T(8,128)S(1)}, f32[12,32,768]{2,1,0:T(8,128)}, u32[]{:S(2)}) copy-start(f32[12,32,768]{2,1,0:T(8,128)} %param.18) | copy-start | bytes 3538948
  297.4 5.4 copy-start.29
  297.4 5.4 copy-start.48
  301.2 1.6 copy-start.5
  305.6 218.6 %reduce-scatter.11.cloned.1.call-start = ((), (), s32[]{:S(2)}) async-start(), calls=%async_computation.11 | async-start | bytes 6488064 | tf_op jit(solution)/shard_map/reduce_scatter | solution.py:177
  314.4 0.8 copy-start.33
  314.4 0.8 copy-start.35
  314.4 0.9 copy-start.28
  314.4 1.0 copy-start.31
  314.5 334.4 %reduce-scatter.5.cloned.1.call-start = ((), (), s32[]{:S(2)}) async-start(), calls=%async_computation.8 | async-start | bytes 7299072 | tf_op jit(solution)/shard_map/reduce_scatter | solution.py:222
  328.1 1.4 copy-start.10
  328.9 1.5 copy-start.8
  329.6 1.5 copy-start.11
  342.9 4.0 copy-start.4
  347.0 11.6 %slice-start = ((s8[12582912]{0:T(1024)(128)(4,1)}), s8[4194304]{0:T(1024)(128)(4,1)S(1)}, s32[]{:S(2)}) async-start(s8[12582912]{0:T(1024)(128)(4,1)} %bitcast.120), calls=%async_computation.12 | async-start | bytes 8388608
  347.0 11.6 %slice-start.1 = ((s8[12582912]{0:T(1024)(128)(4,1)}), s8[4194304]{0:T(1024)(128)(4,1)S(1)}, s32[]{:S(2)}) async-start(s8[12582912]{0:T(1024)(128)(4,1)} %bitcast.120), calls=%async_computation.13 | async-start | bytes 8388608
  347.0 12.9 %slice-start.2 = ((s8[12582912]{0:T(1024)(128)(4,1)}), s8[4194304]{0:T(1024)(128)(4,1)S(1)}, s32[]{:S(2)}) async-start(s8[12582912]{0:T(1024)(128)(4,1)} %bitcast.120), calls=%async_computation.14 | async-start | bytes 8388608
  366.9 2.7 copy-start.3
  372.8 1.8 copy-start.13
  372.8 2.6 copy-start.19
  372.8 3.2 copy-start.24
  372.8 3.1 copy-start.43
  373.1 1.4 copy-start.22
  382.8 0.7 copy-start.41
  382.8 428.6 %reduce-scatter.9.cloned.1.call-start = ((), (), s32[]{:S(2)}) async-start(), calls=%async_computation.10 | async-start | bytes 12976128 | tf_op jit(solution)/shard_map/reduce_scatter | solution.py:176
  399.1 9.6 %copy-start.23 = (bf16[1,512,3,12,64]{1,4,3,2,0:T(8,128)(2,1)S(1)}, bf16[1,512,3,12,64]{1,4,3,2,0:T(8,128)(2,1)}, u32[]{:S(2)}) copy-start(bf16[1,512,3,12,64]{1,4,3,2,0:T(8,128)(2,1)} %copy-done.22) | copy-start | bytes 7077892
  399.1 9.6 %copy-start.25 = (bf16[384,2304]{0,1:T(8,128)(2,1)S(1)}, bf16[384,2304]{0,1:T(8,128)(2,1)}, u32[]{:S(2)}) copy-start(bf16[384,2304]{0,1:T(8,128)(2,1)} %copy.84) | copy-start | bytes 5308420
  399.1 9.6 %copy-start.47 = (bf16[768,2304]{1,0:T(8,128)(2,1)S(1)}, bf16[768,2304]{1,0:T(8,128)(2,1)}, u32[]{:S(2)}) copy-start(bf16[768,2304]{1,0:T(8,128)(2,1)} %all-gather.5.cloned.1.call-done) | copy-start | bytes 10616836
  406.1 1.5 copy-start.21
  407.6 6.9 slice-start.3
  408.7 4.0 copy-start.39
  408.7 4.0 copy-start.6
  408.7 4.0 copy-start.14
  408.7 4.0 copy-start.20
  408.7 5.8 slice-start.4
  412.8 1.7 copy-start.16
  414.5 5.3 copy-start.37
  414.5 5.6 copy-start.44
  420.2 391.3 %copy-start.1 = (f32[32,12]{0,1:T(8,128)S(1)}, f32[32,12]{0,1:T(8,128)}, u32[]{:S(2)}) copy-start(f32[32,12]{0,1:T(8,128)} %param.25) | copy-start | bytes 4612
Sparse Core Ops, SparseCore 0:
  11.6 62.8 all-gather.4
  78.1 52.9 all-gather.6
  134.6 68.4 all-gather.8
  206.5 57.5 all-gather.10
  305.7 97.8 reduce-scatter.6
  410.6 113.5 reduce-scatter.10
  530.5 118.3 reduce-scatter.4
  656.5 154.9 reduce-scatter.8
where the time goes:
time: 822 us; the launch traced here: 819 us
  waiting for transfers between devices  511 us (62%)
  matrix products  167 us (20%)
  local copies, waits for them, and re-layouts  60.4 us (7%)
  blocking collectives  38.3 us (5%)
  other arithmetic  25.9 us (3%)
  between operations  15 us (2%)
    reduce_scatter x1, waiting for transfers between devices, body(): lax.psum_scatter(grad_in, ('dp', 'fsdp'), scatter_dimension=0, tiled=True)  163 us
    reduce_scatter x1, waiting for transfers between devices, body(): lax.psum_scatter(grad_qkv, ('dp', 'fsdp'), scatter_dimension=0, tiled=True)  125 us
    all_gather x1, waiting for transfers between devices, body(): lax.all_gather(shards[2], ('dp', 'fsdp'), axis=0, tiled=True)  66.9 us
    reduce_scatter x1, waiting for transfers between devices, body(): lax.psum_scatter(grad_ff, ('dp', 'fsdp'), scatter_dimension=0, tiled=True)  61.9 us
    all_gather x1, waiting for transfers between devices, body(): lax.all_gather(shards[3], ('dp', 'fsdp'), axis=0, tiled=True)  49.1 us
    all_gather x1, waiting for transfers between devices, body(): lax.all_gather(shards[0], ('dp', 'fsdp'), axis=0, tiled=True)  42.3 us
    psum x1, blocking collectives, body(): lax.psum((grad_attn_gain, grad_ffn_gain, doc_table + query_table), ('dp',...  38.3 us
    dot_general x1, matrix products, body(): jnp.einsum('rd,fd->rf', cotangent_low, full_ff, preferred_element_type=jn...  16.6 us
  transfers between devices with their start and end apart: 8, of which 7 were waited for; matrix products, arithmetic and copies ran while one was open for 24% of the time, Pallas kernels for 0%

commit v1 on v0

--- a/solution.py
+++ b/solution.py
@@ -1,7 +1,12 @@
 import jax
 import jax.numpy as jnp
 from jax import lax
+import numpy as np
+from jax.experimental import pallas as pl
+from jax.experimental.pallas import tpu as pltpu
 from jax.sharding import PartitionSpec as P
+
+both = ("dp", "fsdp")
 
 epsilon = 1e-06
 highest = lax.Precision.HIGHEST
@@ -79,6 +84,125 @@
     grad_table = jnp.einsum("bhqk,qkn->nh", grad_scores, onehot, preferred_element_type=jnp.float32)
     stacked = jnp.stack([grad_queries, grad_keys, grad_values], axis=2)
     return (stacked.astype(jnp.bfloat16), grad_table)
+
+
+def place_index(y, c, z, x):
+    return ((y * 2 + c) * 4 + z) * 2 + x
+
+
+def flip_pairs(dy=0, dc=0, dz=0, dx=0):
+    pairs = []
+    for y in range(2):
+        for c in range(2):
+            for z in range(4):
+                for x in range(2):
+                    pairs.append(
+                        (place_index(y, c, z, x), place_index(y ^ dy, c ^ dc, z ^ dz, x ^ dx))
+                    )
+    return pairs
+
+
+def swap(values, **flips):
+    return lax.ppermute(values, both, flip_pairs(**flips))
+
+
+def own_place():
+    outer = lax.axis_index("dp")
+    inner = lax.axis_index("fsdp")
+    return outer // 2, outer % 2, inner // 2, inner % 2
+
+
+def unpack_kernel(place_ref, *refs):
+    pieces, full_ref, sems = refs[:8], refs[8], refs[9]
+    y, c, z, x = place_ref[0], place_ref[1], place_ref[2], place_ref[3]
+    copies = []
+    for number, piece in enumerate(pieces):
+        flip_c, kind = number // 4, number % 4
+        for first in range(2):
+            for second in range(2):
+                if kind < 2:
+                    dx, dy, dz = first, kind, second
+                else:
+                    dy, dx, dz = first, kind - 2, second + 2
+                target = place_index(y ^ dy, c ^ flip_c, z ^ dz, x ^ dx)
+                copies.append(
+                    pltpu.make_async_copy(
+                        piece.at[first, second], full_ref.at[target], sems.at[len(copies)]
+                    )
+                )
+    for copy in copies:
+        copy.start()
+    for copy in copies:
+        copy.wait()
+
+
+def unpack(place, pieces):
+    rows, columns = pieces[0].shape[2:]
+    return pl.pallas_call(
+        unpack_kernel,
+        out_shape=jax.ShapeDtypeStruct((32, rows, columns), pieces[0].dtype),
+        in_specs=[pl.BlockSpec(memory_space=pltpu.SMEM)]
+        + [pl.BlockSpec(memory_space=pl.ANY)] * 8,
+        out_specs=pl.BlockSpec(memory_space=pltpu.VMEM),
+        scratch_shapes=[pltpu.SemaphoreType.DMA((32,))],
+        compiler_params=pltpu.CompilerParams(vmem_limit_bytes=24 * 2**20),
+        name="unpack",
+    )(place, *pieces).reshape(32 * rows, columns)
+
+
+def hand_routed():
+    return (lax.axis_size("dp"), lax.axis_size("fsdp")) == (4, 8)
+
+
+def gather_rows(shard, place):
+    if not hand_routed():
+        return lax.all_gather(shard, both, axis=0, tiled=True)
+    near = swap(shard, dz=1)
+    first = jnp.stack([shard, near])
+    second = jnp.stack([swap(shard, dz=2), swap(shard, dz=3)])
+    first = jnp.stack([first, swap(first, dx=1)])
+    second = jnp.stack([second, swap(second, dy=1)])
+    first_far = swap(first, dy=1)
+    second_far = swap(second, dx=1)
+    here = [first, first_far, second, second_far]
+    return unpack(place, here + [swap(piece, dc=1) for piece in here])
+
+
+def added(kept, arrived):
+    return (kept.astype(jnp.float32) + arrived.astype(jnp.float32)).astype(jnp.bfloat16)
+
+
+def pick(values, index, axis):
+    return lax.dynamic_index_in_dim(values, index, axis, keepdims=False)
+
+
+def scatter_rows(partial, place):
+    if not hand_routed():
+        return lax.psum_scatter(
+            partial.astype(jnp.float32), both, scatter_dimension=0, tiled=True
+        )
+    y, c, z, x = place
+    rows = partial.shape[0] // 32
+    parts = partial.reshape(2, 2, 4, 2, rows, partial.shape[1])
+    parts = added(pick(parts, c, 1), swap(pick(parts, 1 - c, 1), dc=1))
+    first, second = parts[:, :2], parts[:, 2:]
+    first = added(pick(first, x, 2), swap(pick(first, 1 - x, 2), dx=1))
+    second = added(pick(second, y, 0), swap(pick(second, 1 - y, 0), dy=1))
+    first = added(pick(first, y, 0), swap(pick(first, 1 - y, 0), dy=1))
+    second = added(pick(second, x, 1), swap(pick(second, 1 - x, 1), dx=1))
+    column = jnp.concatenate([first, second], axis=0)
+    total = pick(column, z, 0).astype(jnp.float32)
+    for flip in (1, 2, 3):
+        total = total + swap(pick(column, z ^ flip, 0), dz=flip).astype(jnp.float32)
+    return total
+
+
+def add_everywhere(values):
+    if not hand_routed():
+        return lax.psum(values, both)
+    for flips in ({"dc": 1}, {"dx": 1}, {"dy": 1}, {"dz": 1}, {"dz": 2}):
+        values = values + swap(values, **flips)
+    return values
 
 
 def body(
@@ -107,12 +231,13 @@
         in_weight.astype(jnp.bfloat16),
         ff_weight.astype(jnp.bfloat16),
     )
-    full_qkv, full_out, full_in, full_ff = (
-        lax.all_gather(shards[0], ("dp", "fsdp"), axis=0, tiled=True),
-        lax.all_gather(shards[1], ("dp", "fsdp"), axis=0, tiled=True),
-        lax.all_gather(shards[2], ("dp", "fsdp"), axis=0, tiled=True),
-        lax.all_gather(shards[3], ("dp", "fsdp"), axis=0, tiled=True),
-    )
+    place = own_place()
+    place_vector = jnp.stack(place).astype(jnp.int32)
+    full_attention = gather_rows(jnp.concatenate([shards[0], shards[1]], axis=1), place_vector)
+    full_qkv = full_attention[:, : 3 * model_width]
+    full_out = full_attention[:, 3 * model_width :]
+    full_in = gather_rows(shards[2], place_vector)
+    full_ff = gather_rows(shards[3], place_vector)
     places = jnp.arange(group_length, dtype=jnp.int32)
     query_mask = (places[None, :] < query_lengths[:, None]).astype(jnp.int32)
     doc_bias, doc_onehot = bucket_tables(doc_length, bias_table)
@@ -145,12 +270,6 @@
     activated, gated_pull = jax.vjp(gated_unit, gate_up)
     activated_low = activated.astype(jnp.bfloat16)
     outputs = middle + jnp.dot(activated_low, full_ff, preferred_element_type=jnp.float32)
-    full_qkv, full_out, full_in, full_ff = (
-        lax.all_gather(shards[0], ("dp", "fsdp"), axis=0, tiled=True),
-        lax.all_gather(shards[1], ("dp", "fsdp"), axis=0, tiled=True),
-        lax.all_gather(shards[2], ("dp", "fsdp"), axis=0, tiled=True),
-        lax.all_gather(shards[3], ("dp", "fsdp"), axis=0, tiled=True),
-    )
     cotangent = jnp.concatenate(
         [doc_cotangent.reshape(doc_rows, model_width), query_cotangent.reshape(-1, model_width)],
         axis=0,
@@ -172,10 +291,8 @@
     )
     grad_middle, grad_ffn_gain = norm_pull_two(grad_normed_two)
     grad_middle = grad_middle + cotangent
-    in_grad_shard, ff_grad_shard = (
-        lax.psum_scatter(grad_in, ("dp", "fsdp"), scatter_dimension=0, tiled=True),
-        lax.psum_scatter(grad_ff, ("dp", "fsdp"), scatter_dimension=0, tiled=True),
-    )
+    in_grad_shard = scatter_rows(grad_in.astype(jnp.bfloat16), place)
+    ff_grad_shard = scatter_rows(grad_ff.astype(jnp.bfloat16), place)
     grad_middle_low = grad_middle.astype(jnp.bfloat16)
     grad_out = jnp.einsum(
         "rd,re->de", mixed_all, grad_middle_low, preferred_element_type=jnp.float32
@@ -218,13 +335,18 @@
     )
     grad_rows, grad_attn_gain = norm_pull(grad_normed)
     grad_inputs = grad_middle + grad_rows
-    qkv_grad_shard, out_grad_shard = (
-        lax.psum_scatter(grad_qkv, ("dp", "fsdp"), scatter_dimension=0, tiled=True),
-        lax.psum_scatter(grad_out, ("dp", "fsdp"), scatter_dimension=0, tiled=True),
-    )
-    attn_gain_grad, ffn_gain_grad, bias_table_grad = lax.psum(
-        (grad_attn_gain, grad_ffn_gain, doc_table + query_table), ("dp", "fsdp")
-    )
+    attention_shard = scatter_rows(
+        jnp.concatenate([grad_qkv, grad_out], axis=1).astype(jnp.bfloat16), place
+    )
+    qkv_grad_shard = attention_shard[:, : 3 * model_width]
+    out_grad_shard = attention_shard[:, 3 * model_width :]
+    small = jnp.concatenate(
+        [grad_attn_gain, grad_ffn_gain, (doc_table + query_table).reshape(-1)]
+    )
+    small = add_everywhere(small)
+    attn_gain_grad = small[:model_width]
+    ffn_gain_grad = small[model_width : 2 * model_width]
+    bias_table_grad = small[2 * model_width :].reshape(bias_table.shape)
     return (
         outputs[:doc_rows].reshape(doc_inputs.shape),
         outputs[doc_rows:].reshape(query_inputs.shape),

time: 822 us -> 448 us (0.55)
  waiting for transfers between devices: 511 us -> 83.2 us
  starting transfers between devices: 0.33 us -> 72.9 us
  blocking collectives: 38.3 us -> 0 us
  Pallas kernels: 0 us -> 20.9 us
  other arithmetic: 25.9 us -> 41.4 us
  between operations: 15 us -> 2.58 us
  matrix products: 167 us -> 158 us
    reduce_scatter x4 -> x0, waiting for transfers between devices: 349 us -> none  [the longest x1 163 us: body(): lax.psum_scatter(grad_in, ('dp', 'fsdp'), scatter_dimension=0, tiled=True)]
    all_gather x4 -> x0, waiting for transfers between devices: 162 us -> none  [the longest x1 66.9 us: body(): lax.all_gather(shards[2], ('dp', 'fsdp'), axis=0, tiled=True)]
    ppermute x0 -> x62, waiting for transfers between devices: none -> 83.2 us  [swap(): return lax.ppermute(values, both, flip_pairs(**flips))]
    ppermute x0 -> x62, starting transfers between devices: none -> 72.9 us  [swap(): return lax.ppermute(values, both, flip_pairs(**flips))]
    psum x1 -> x0, blocking collectives: 38.3 us -> none  [body(): lax.psum((grad_attn_gain, grad_ffn_gain, doc_table + query_table), ('dp',...]
    pallas_call x0 -> x3, Pallas kernels: none -> 20.9 us  [unpack(): pl.pallas_call(unpack_kernel, out_shape=jax.ShapeDtypeStruct((32, rows, c...]
    unnamed x108 -> x136, local copies, waits for them, and re-layouts: 15 us -> 6.48 us
  transfers between devices with their start and end apart: 8 -> 62, of which waited for: 7 -> 23; matrix products, arithmetic and copies ran while one was open for 24% -> 25% of each run, Pallas kernels for 0% -> 3%
where the time goes in v1:
time: 448 us; the launch traced here: 441 us
  matrix products  158 us (35%)
  waiting for transfers between devices  83.2 us (19%)
  starting transfers between devices  72.9 us (16%)
  local copies, waits for them, and re-layouts  62.8 us (14%)
  other arithmetic  41.4 us (9%)
  Pallas kernels  20.9 us (5%)
    ppermute x62, waiting for transfers between devices, swap(): return lax.ppermute(values, both, flip_pairs(**flips))  83.2 us
    ppermute x62, starting transfers between devices, swap(): return lax.ppermute(values, both, flip_pairs(**flips))  72.9 us
    pallas_call x3, Pallas kernels, unpack(): pl.pallas_call(unpack_kernel, out_shape=jax.ShapeDtypeStruct((32, rows, c...  20.9 us
    dot_general x1, matrix products, body(): jnp.einsum('rd,fd->rf', cotangent_low, full_ff, preferred_element_type=jn...  16.4 us
    dot_general x2, matrix products, score_block(): jnp.einsum('bqhc,bkhc->bhqk', queries, key_rows, preferred_element_type=j...  16 us
    dot_general x1, matrix products, body(): jnp.einsum('re,de->rd', grad_gate_low, full_in, preferred_element_type=jn...  15.3 us
    dot_general x2, matrix products, bucket_tables(): jnp.einsum('qkn,nh->hqk', onehot, bias_table, precision=highest)  15.2 us
    dot_general x1, matrix products, body(): jnp.einsum('rd,re->de', normed_two_low, grad_gate_low, preferred_element_...  15 us
  transfers between devices with their start and end apart: 62, of which 23 were waited for; matrix products, arithmetic and copies ran while one was open for 25% of the time, Pallas kernels for 3%

profile of v1, /device:TPU:0, one launch (start us, length us, event | category | flops | bytes accessed | tf_op | source)
XLA Modules:
  0.0 441.3 jit_solution(15583959185615169885)
XLA Ops:
  2.4 4.0 collective-permute-start.25
  12.5 2.5 collective-permute-start
  24.8 3.0 collective-permute-start.11
  28.9 2.3 collective-permute-done.4
  36.8 7.6 %collective-permute-done.14 = bf16[24,4096]{1,0:T(8,128)(2,1)S(1)} collective-permute-done((bf16[24,4096]{1,0:T(8,128)(2,1)}, bf16[24,4096]{1,0:T(8,128)(2,1)S(1)}, u32[]{:S(2)}, u32[]{:S(2)}) %collective-permute-start.14) | collective-permute-done | bytes 196640 | tf_op jit(solution)/shard_map/ppermute | solution.py:106
  48.9 2.2 collective-permute-done.5
  51.2 4.8 %collective-permute-done.12 = bf16[2,24,4096]{2,1,0:T(8,128)(2,1)S(1)} collective-permute-done((bf16[2,24,4096]{2,1,0:T(8,128)(2,1)S(1)}, bf16[2,24,4096]{2,1,0:T(8,128)(2,1)S(1)}, u32[]{:S(2)}, u32[]{:S(2)}) %collective-permute-start.12) | collective-permute-done | bytes 393248 | tf_op jit(solution)/shard_map/ppermute | solution.py:106
  56.2 2.3 collective-permute-start.6
  58.6 5.8 %collective-permute-done.28.refs_3_ = bf16[2,2,64,768]{3,2,1,0:T(8,128)(2,1)S(1)} collective-permute-done((bf16[2,2,64,768]{3,2,1,0:T(8,128)(2,1)S(1)}, bf16[2,2,64,768]{3,2,1,0:T(8,128)(2,1)S(1)}, u32[]{:S(2)}, u32[]{:S(2)}) %collective-permute-start.28) | collective-permute-done | bytes 393248 | tf_op jit(solution)/shard_map/ppermute | solution.py:106
  65.1 4.5 %collective-permute-start.17 = (bf16[2,2,24,4096]{3,2,1,0:T(8,128)(2,1)S(1)}, bf16[2,2,24,4096]{3,2,1,0:T(8,128)(2,1)S(1)}, u32[]{:S(2)}, u32[]{:S(2)}) collective-permute-start(bf16[2,2,24,4096]{3,2,1,0:T(8,128)(2,1)S(1)} %pad_maximum_fusion.11.refs_2_), channel_id=1, source_target_pairs={{0,1},{1,0},{2,3},{3,2},{4,5},{5,4},{6,7},{7,6},{8,9},{9,8},{10,11... | collective-permute-start | bytes 2359304 | tf_op jit(solution)/shard_map/ppermute | solution.py:106
  69.6 7.4 %collective-permute-done.6.refs_3_ = bf16[2,2,24,3072]{3,2,1,0:T(8,128)(2,1)S(1)} collective-permute-done((bf16[2,2,24,3072]{3,2,1,0:T(8,128)(2,1)S(1)}, bf16[2,2,24,3072]{3,2,1,0:T(8,128)(2,1)S(1)}, u32[]{:S(2)}, u32[]{:S(2)}) %collective-permute-start.6) | collective-permute-done | bytes 589856 | tf_op jit(solution)/shard_map/ppermute | solution.py:106
  77.8 14.1 %fusion = f32[512,512,12]{0,2,1:T(8,128)} fusion(s32[512,512]{0,1:T(8,128)S(1)} %fusion.57, f32[32,12]{0,1:T(8,128)S(1)} %copy-done), kind=kOutput, calls=%fused_computation.2 | convolution fusion | flops 1216348160 | bytes 13633024 | tf_op jit(solution)/shard_map/qkn,nh->hqk/dot_general | solution.py:34
  91.9 5.6 %unpack.5 = bf16[32,64,768]{2,1,0:T(8,128)(2,1)S(1)} custom-call(s32[4]{0:T(128)S(1)} %pad_add_fusion.place_ref, bf16[2,2,64,768]{3,2,1,0:T(8,128)(2,1)S(1)} %pad_maximum_fusion.16.refs_0_, bf16[2,2,64,768]{3,2,1,0:T(8,128)(2,1)S(1)} %collective-permute-done.24.refs_1_, bf16[2,2,64,768]{3,2,1,0:T(8,128)(2,1)S(1)} %pad_maximum_fusion.17.refs_2_, ...), custom_call_target="tpu_custom_call" | custom-call | tf_op jit(solution)/shard_map/unpack/pallas_call | solution.py:141
  98.7 8.0 %unpack.3 = bf16[32,24,3072]{2,1,0:T(8,128)(2,1)S(1)} custom-call(s32[4]{0:T(128)S(1)} %pad_add_fusion.place_ref, bf16[2,2,24,3072]{3,2,1,0:T(8,128)(2,1)S(1)} %pad_maximum_fusion.12.refs_0_, bf16[2,2,24,3072]{3,2,1,0:T(8,128)(2,1)S(1)} %collective-permute-done.2.refs_1_, bf16[2,2,24,3072]{3,2,1,0:T(8,128)(2,1)S(1)} %pad_maximum_fusion.13.refs_2_, ...), custom_call_target="tpu_custom_call" | custom-call | tf_op jit(solution)/shard_map/unpack/pallas_call | solution.py:141
  106.7 4.2 convolution_convert_fusion.1
  113.8 4.3 copy.79
  118.1 6.4 %reshape.400 = bf16[12,32,3,12,64]{4,3,2,1,0:T(8,128)(2,1)} reshape(bf16[384,2304]{1,0:T(8,128)(2,1)} %slice.148) | data formatting | bytes 3538944 | tf_op jit(solution)/shard_map/reshape | solution.py:254
  124.5 3.3 fusion.149
  132.5 3.0 reshape.401
  137.6 15.2 %fusion.155 = (f32[12,512]{1,0:T(8,128)S(1)}, f32[12,512,512]{1,2,0:T(8,128)S(1)}) fusion(f32[512]{0:T(512)S(1)} %bitcast.334, f32[512,512,12]{0,2,1:T(8,128)} %fusion, bf16[1,512,3,12,64]{1,4,3,2,0:T(8,128)(2,1)} %bitcast.287), kind=kOutput, calls=%fused_computation.303 | convolution fusion | flops 412084224 | bytes 30959616 | tf_op jit(solution)/shard_map/while/body/eval_jaxpr/bqhc,bkhc->bhqk/dot_general | solution.py:47
  154.7 2.7 copy-done.6
  157.4 3.9 fusion.41
  161.4 3.0 multiply_reduce_fusion.5
  164.5 7.3 %unpack.4 = bf16[32,24,4096]{2,1,0:T(8,128)(2,1)S(1)} custom-call(s32[4]{0:T(128)S(1)} %pad_add_fusion.place_ref, bf16[2,2,24,4096]{3,2,1,0:T(8,128)(2,1)S(1)} %pad_maximum_fusion.10.refs_0_, bf16[2,2,24,4096]{3,2,1,0:T(8,128)(2,1)S(1)} %collective-permute-done.13.refs_1_, bf16[2,2,24,4096]{3,2,1,0:T(8,128)(2,1)S(1)} %pad_maximum_fusion.11.refs_2_, ...), custom_call_target="tpu_custom_call" | custom-call | tf_op jit(solution)/shard_map/unpack/pallas_call | solution.py:141
  171.8 9.1 %fusion.148 = f32[896,4096]{1,0:T(8,128)} fusion(bf16[768,4096]{1,0:T(8,128)(2,1)S(1)} %bitcast.277, f32[896,768]{1,0:T(8,128)S(1)} %get-tuple-element.132, f32[768]{0:T(1024)S(1)} %copy-done.55, f32[896]{0:T(1024)S(1)} %fusion.132), kind=kOutput, calls=%fused_computation.296 | convolution fusion | flops 5639208960 | bytes 23730688 | tf_op jit(solution)/shard_map/dot_general | solution.py:269
  181.0 16.4 %fusion.26 = (f32[896,2048]{1,0:T(8,128)}, f32[896,2048]{1,0:T(8,128)}, bf16[896,2048]{1,0:T(8,128)(2,1)}) fusion(f32[896,4096]{1,0:T(8,128)} %fusion.148, bf16[2048,768]{1,0:T(8,128)(2,1)S(1)} %bitcast.283, f32[384,768]{1,0:T(8,128)S(1)} %bitcast.317, f32[512,768]{1,0:T(8,128)S(1)} %bitcast.314), kind=kOutput, calls=%fused_computation.66 | convolution fusion | flops 2865364992 | bytes 38928384 | tf_op jit(solution)/shard_map/rd,fd->rf/dot_general | solution.py:281
  197.4 15.3 %multiply_reduce_fusion.1 = (f32[768]{0:T(1024)S(1)}, f32[896]{0:T(1024)S(1)}, f32[896,768]{1,0:T(8,128)}) fusion(f32[896,768]{1,0:T(8,128)} %copy-done.36, f32[896]{0:T(1024)S(1)} %fusion.132, f32[768]{0:T(1024)S(1)} %copy-done.55, bf16[768,4096]{1,0:T(8,128)(2,1)} %bitcast.278, f32[896,2048]{1,0:T(8,128)} %get-tuple-element.85, ...), kind=kOutput, calls=%fused_computation.58 | convolution fusion | flops 5648611328 | bytes 26489856 | tf_op jit(solution)/shard_map/re,de->rd/dot_general | solution.py:289
  212.7 15.0 %convolution_convert_fusion = bf16[768,4096]{1,0:T(8,128)(2,1)} fusion(f32[896,2048]{1,0:T(8,128)} %get-tuple-element.85, f32[896,2048]{1,0:T(8,128)} %get-tuple-element.84, f32[896,768]{1,0:T(8,128)} %copy-done.36, f32[768]{0:T(1024)S(1)} %copy-done.55, f32[896]{0:T(1024)S(1)} %fusion.132), kind=kOutput, calls=%fused_computation.27 | convolution fusion | flops 5649694720 | bytes 23730688 | tf_op jit(solution)/shard_map/rd,re->de/dot_general | solution.py:286
  227.7 6.8 %convolution_add_fusion.1 = f32[896,768]{1,0:T(8,128)} fusion(f32[896,768]{1,0:T(8,128)S(1)} %copy-done.37, bf16[896,2048]{1,0:T(8,128)(2,1)} %get-tuple-element.86, bf16[2048,768]{1,0:T(8,128)(2,1)S(1)} %bitcast.284), kind=kOutput, calls=%fused_computation.83 | convolution fusion | flops 2819260416 | bytes 12320768 | tf_op jit(solution)/shard_map/dot_general | solution.py:272
  234.5 5.0 %convolution_convert_fusion.3 = bf16[2048,768]{1,0:T(8,128)(2,1)} fusion(bf16[896,2048]{1,0:T(8,128)(2,1)S(1)} %copy-done.61, f32[384,768]{1,0:T(8,128)S(1)} %bitcast.318, f32[512,768]{1,0:T(8,128)S(1)} %bitcast.315), kind=kOutput, calls=%fused_computation.45 | convolution fusion | flops 2822897664 | bytes 9568256 | tf_op jit(solution)/shard_map/rf,rd->fd/dot_general | solution.py:278
  240.2 3.6 convolution_convert_fusion.4
  244.7 2.3 copy.93
  247.0 2.9 reshape.409
  250.0 3.0 multiply_reduce_fusion.7
  258.1 2.9 fusion.44
  261.0 5.9 %multiply_reduce_fusion = (f32[12,512]{1,0:T(8,128)S(1)}, f32[12,512,512]{1,2,0:T(8,128)}) fusion(f32[12,512,512]{1,2,0:T(8,128)S(1)} %bitcast.286, f32[12,512]{1,0:T(8,128)S(1)} %log_add_fusion.1, bf16[512,12,64]{0,2,1:T(8,128)(2,1)S(1)} %bitcast.293, bf16[1,512,3,12,64]{1,4,3,2,0:T(8,128)(2,1)S(1)} %bitcast.289), kind=kOutput, calls=%fused_computation.10 | convolution fusion | flops 412084224 | bytes 26796032 | tf_op jit(solution)/shard_map/while/body/eval_jaxpr/bqhc,bkhc->bhqk/dot_general | solution.py:73
  267.0 6.9 %multiply_convert_fusion = bf16[12,512,512]{1,2,0:T(8,128)(2,1)S(1)} fusion(f32[12,512,512]{1,2,0:T(8,128)} %get-tuple-element.137, f32[12,512,512]{1,2,0:T(8,128)S(1)} %bitcast.286, f32[12,512]{1,0:T(8,128)S(1)} %get-tuple-element.136, f32[12,512]{1,0:T(8,128)S(1)} %log_add_fusion.1), kind=kLoop, calls=%fused_computation.9 | loop fusion | flops 12582912 | bytes 31506432 | tf_op jit(solution)/shard_map/while/body/eval_jaxpr/convert_element_type | solution.py:77
  273.9 5.1 %fusion.52 = f32[32,12]{0,1:T(8,128)S(1)} fusion(bf16[12,512,512]{1,2,0:T(8,128)(2,1)S(1)} %multiply_convert_fusion, s32[512,512]{0,1:T(8,128)S(1)} %copy-done.25), kind=kOutput, calls=%fused_computation.120 | convolution fusion | flops 226492416 | bytes 7341568 | tf_op jit(solution)/shard_map/while/body/eval_jaxpr/bhqk,qkn->nh/dot_general | solution.py:84
  279.0 2.9 fusion.43
  285.0 3.7 copy.97
  288.7 5.5 %convert_element_type.513 = bf16[384,2304]{1,0:T(8,128)(2,1)S(1)} reshape(bf16[12,32,3,12,64]{4,3,2,1,0:T(8,128)(2,1)} %copy.97) | data formatting | bytes 3538944 | tf_op jit(solution)/shard_map/convert_element_type | solution.py:86
  294.3 2.2 copy.98
  298.6 8.3 %multiply_reduce_fusion.2 = (f32[768]{0:T(1024)S(1)}, f32[896]{0:T(1024)S(1)}, f32[896,768]{1,0:T(8,128)}) fusion(f32[896]{0:T(1024)S(1)} %copy-done.53, f32[384,768]{1,0:T(8,128)} %bitcast.303, f32[512,768]{1,0:T(8,128)S(1)} %bitcast.300, f32[768]{0:T(1024)S(1)} %copy-done.57, bf16[768,3072]{1,0:T(8,128)(2,1)} %bitcast.282, bf16[384,2304]{0,1:T(8,128)(2,1)} %copy.98, ...), kind=kOutput, calls=%fused_computation.59 | convolution fusion | flops 3183966720 | bytes 13186048 | tf_op jit(solution)/shard_map/re,de->rd/dot_general | solution.py:333
  306.9 6.3 %convolution_convert_fusion.2 = bf16[768,2304]{1,0:T(8,128)(2,1)} fusion(bf16[384,2304]{0,1:T(8,128)(2,1)S(1)} %copy-done.40, bf16[512,2304]{0,1:T(8,128)(2,1)S(1)} %bitcast.313, f32[768]{0:T(1024)S(1)} %copy-done.57, f32[896]{0:T(1024)S(1)} %copy-done.53, f32[384,768]{1,0:T(8,128)S(1)} %bitcast.307, f32[512,768]{1,0:T(8,128)S(1)} %bitcast.301), kind=kOutput, calls=%fused_computation.36 | convolution fusion | flops 3183673344 | bytes 10426880 | tf_op jit(solution)/shard_map/rd,re->de/dot_general | solution.py:330
  314.7 2.3 constant_dynamic-slice_fusion.3
  319.4 3.7 convolution_convert_fusion.7
  323.1 3.3 collective-permute-start.58
  329.1 2.6 collective-permute-done.59
  331.7 4.8 %collective-permute-start.60 = (f32[1920]{0:T(1024)S(1)}, f32[1920]{0:T(1024)S(1)}, u32[]{:S(2)}, u32[]{:S(2)}) collective-permute-start(f32[1920]{0:T(1024)S(1)} %add.519), channel_id=1, source_target_pairs={{0,2},{1,3},{2,0},{3,1},{4,6},{5,7},{6,4},{7,5},{8,10},{9,11},{10,... | collective-permute-start | bytes 23048 | tf_op jit(solution)/shard_map/ppermute | solution.py:106
  353.4 5.1 %collective-permute-done.51 = bf16[2,64,768]{2,1,0:T(8,128)(2,1)S(1)} collective-permute-done((bf16[2,64,768]{2,1,0:T(8,128)(2,1)S(1)}, bf16[2,64,768]{2,1,0:T(8,128)(2,1)S(1)}, u32[]{:S(2)}, u32[]{:S(2)}) %collective-permute-start.51) | collective-permute-done | bytes 196640 | tf_op jit(solution)/shard_map/ppermute | solution.py:106
  369.1 2.3 collective-permute-done.55
  374.2 5.4 %collective-permute-done.34 = bf16[2,2,24,3072]{3,2,1,0:T(8,128)(2,1)} collective-permute-done((bf16[2,2,24,3072]{3,2,1,0:T(8,128)(2,1)S(1)}, bf16[2,2,24,3072]{3,2,1,0:T(8,128)(2,1)}, u32[]{:S(2)}, u32[]{:S(2)}) %collective-permute-start.34) | collective-permute-done | bytes 589856 | tf_op jit(solution)/shard_map/ppermute | solution.py:106
  382.5 7.0 %collective-permute-done.36 = bf16[2,2,24,3072]{3,2,0,1:T(8,128)(2,1)S(1)} collective-permute-done((bf16[2,2,24,3072]{3,2,0,1:T(8,128)(2,1)S(1)}, bf16[2,2,24,3072]{3,2,0,1:T(8,128)(2,1)S(1)}, u32[]{:S(2)}, u32[]{:S(2)}) %collective-permute-start.36) | collective-permute-done | bytes 589856 | tf_op jit(solution)/shard_map/ppermute | solution.py:106
  390.8 2.8 fusion.16
  396.1 3.5 collective-permute-done.37
  399.9 2.2 collective-permute-start.38
  402.1 2.4 collective-permute-start.40
  404.5 7.5 %collective-permute-done.42 = bf16[2,2,24,4096]{3,2,1,0:T(8,128)(2,1)S(1)} collective-permute-done((bf16[2,2,24,4096]{3,2,1,0:T(8,128)(2,1)S(1)}, bf16[2,2,24,4096]{3,2,1,0:T(8,128)(2,1)S(1)}, u32[]{:S(2)}, u32[]{:S(2)}) %collective-permute-start.42) | collective-permute-done | bytes 786464 | tf_op jit(solution)/shard_map/ppermute | solution.py:106
  412.3 2.5 collective-permute-start.43
  415.7 5.5 %collective-permute-done.43 = bf16[2,24,4096]{2,1,0:T(8,128)(2,1)S(1)} collective-permute-done((bf16[2,24,4096]{2,1,0:T(8,128)(2,1)S(1)}, bf16[2,24,4096]{2,1,0:T(8,128)(2,1)S(1)}, u32[]{:S(2)}, u32[]{:S(2)}) %collective-permute-start.43) | collective-permute-done | bytes 393248 | tf_op jit(solution)/shard_map/ppermute | solution.py:106
  423.3 3.1 collective-permute-start.46
  426.3 2.4 collective-permute-start.48
  430.3 3.8 collective-permute-done.46
  434.1 5.9 %collective-permute-done.47 = bf16[24,4096]{1,0:T(8,128)(2,1)S(1)} collective-permute-done((bf16[24,4096]{1,0:T(8,128)(2,1)S(1)}, bf16[24,4096]{1,0:T(8,128)(2,1)S(1)}, u32[]{:S(2)}, u32[]{:S(2)}) %collective-permute-start.47) | collective-permute-done | bytes 196640 | tf_op jit(solution)/shard_map/ppermute | solution.py:106
  (342 shorter events, 104.1 us)
Async XLA Ops:
  2.4 19.9 %collective-permute-start.25 = (bf16[64,768]{1,0:T(8,128)(2,1)}, bf16[64,768]{1,0:T(8,128)(2,1)}, u32[]{:S(2)}, u32[]{:S(2)}) collective-permute-start(bf16[64,768]{1,0:T(8,128)(2,1)} %convert_element_type.503), channel_id=1, source_target_pairs={{0,4},{1,5},{2,6},{3,7},{4,0},{5,1},{6,2},{7,3},{8,12},{9,13},{10,... | collective-permute-start | bytes 294920 | tf_op jit(solution)/shard_map/ppermute | solution.py:106
  6.5 18.3 %collective-permute-start.22 = (bf16[64,768]{1,0:T(8,128)(2,1)}, bf16[64,768]{1,0:T(8,128)(2,1)}, u32[]{:S(2)}, u32[]{:S(2)}) collective-permute-start(bf16[64,768]{1,0:T(8,128)(2,1)} %convert_element_type.503), channel_id=1, source_target_pairs={{0,2},{1,3},{2,0},{3,1},{4,6},{5,7},{6,4},{7,5},{8,10},{9,11},{10,... | collective-permute-start | bytes 294920 | tf_op jit(solution)/shard_map/ppermute | solution.py:106
  8.0 14.3 %collective-permute-start.26 = (bf16[64,768]{1,0:T(8,128)(2,1)}, bf16[64,768]{1,0:T(8,128)(2,1)}, u32[]{:S(2)}, u32[]{:S(2)}) collective-permute-start(bf16[64,768]{1,0:T(8,128)(2,1)} %convert_element_type.503), channel_id=1, source_target_pairs={{0,6},{1,7},{2,4},{3,5},{4,2},{5,3},{6,0},{7,1},{8,14},{9,15},{10,... | collective-permute-start | bytes 294920 | tf_op jit(solution)/shard_map/ppermute | solution.py:106
  10.6 18.2 %collective-permute-start.3 = (bf16[24,3072]{1,0:T(8,128)(2,1)}, bf16[24,3072]{1,0:T(8,128)(2,1)}, u32[]{:S(2)}, u32[]{:S(2)}) collective-permute-start(bf16[24,3072]{1,0:T(8,128)(2,1)} %get-tuple-element.124), channel_id=1, source_target_pairs={{0,4},{1,5},{2,6},{3,7},{4,0},{5,1},{6,2},{7,3},{8,12},{9,13},{10,... | collective-permute-start | bytes 442376 | tf_op jit(solution)/shard_map/ppermute | solution.py:106
  12.5 21.1 %collective-permute-start = (bf16[24,3072]{1,0:T(8,128)(2,1)}, bf16[24,3072]{1,0:T(8,128)(2,1)S(1)}, u32[]{:S(2)}, u32[]{:S(2)}) collective-permute-start(bf16[24,3072]{1,0:T(8,128)(2,1)} %get-tuple-element.124), channel_id=1, source_target_pairs={{0,2},{1,3},{2,0},{3,1},{4,6},{5,7},{6,4},{7,5},{8,10},{9,11},{10,... | collective-permute-start | bytes 442376 | tf_op jit(solution)/shard_map/ppermute | solution.py:106
  19.6 87.1 %copy-start.52 = (f32[896]{0:T(1024)}, f32[896]{0:T(1024)S(1)}, u32[]{:S(2)}) copy-start(f32[896]{0:T(1024)S(1)} %fusion.131) | copy-start | bytes 10756
  22.3 55.5 %copy-start.24 = (s32[512,512]{0,1:T(8,128)}, s32[512,512]{0,1:T(8,128)S(1)}, u32[]{:S(2)}) copy-start(s32[512,512]{0,1:T(8,128)S(1)} %fusion.57) | copy-start | bytes 3145732
  22.3 8.9 %collective-permute-start.4 = (bf16[24,3072]{1,0:T(8,128)(2,1)}, bf16[24,3072]{1,0:T(8,128)(2,1)S(1)}, u32[]{:S(2)}, u32[]{:S(2)}) collective-permute-start(bf16[24,3072]{1,0:T(8,128)(2,1)} %get-tuple-element.124), channel_id=1, source_target_pairs={{0,6},{1,7},{2,4},{3,5},{4,2},{5,3},{6,0},{7,1},{8,14},{9,15},{10,... | collective-permute-start | bytes 442376 | tf_op jit(solution)/shard_map/ppermute | solution.py:106
  22.4 22.0 %collective-permute-start.14 = (bf16[24,4096]{1,0:T(8,128)(2,1)}, bf16[24,4096]{1,0:T(8,128)(2,1)S(1)}, u32[]{:S(2)}, u32[]{:S(2)}) collective-permute-start(bf16[24,4096]{1,0:T(8,128)(2,1)} %convert_element_type.501), channel_id=1, source_target_pairs={{0,4},{1,5},{2,6},{3,7},{4,0},{5,1},{6,2},{7,3},{8,12},{9,13},{10,... | collective-permute-start | bytes 589832 | tf_op jit(solution)/shard_map/ppermute | solution.py:106
  24.8 10.4 %collective-permute-start.11 = (bf16[24,4096]{1,0:T(8,128)(2,1)}, bf16[24,4096]{1,0:T(8,128)(2,1)S(1)}, u32[]{:S(2)}, u32[]{:S(2)}) collective-permute-start(bf16[24,4096]{1,0:T(8,128)(2,1)} %convert_element_type.501), channel_id=1, source_target_pairs={{0,2},{1,3},{2,0},{3,1},{4,6},{5,7},{6,4},{7,5},{8,10},{9,11},{10,... | collective-permute-start | bytes 589832 | tf_op jit(solution)/shard_map/ppermute | solution.py:106
  28.8 17.2 %collective-permute-start.15 = (bf16[24,4096]{1,0:T(8,128)(2,1)S(1)}, bf16[24,4096]{1,0:T(8,128)(2,1)S(1)}, u32[]{:S(2)}, u32[]{:S(2)}) collective-permute-start(bf16[24,4096]{1,0:T(8,128)(2,1)S(1)} %copy-done.46), channel_id=1, source_target_pairs={{0,6},{1,7},{2,4},{3,5},{4,2},{5,3},{6,0},{7,1},{8,14},{9,15},{10,... | collective-permute-start | bytes 589832 | tf_op jit(solution)/shard_map/ppermute | solution.py:106
  31.2 16.9 %collective-permute-start.23 = (bf16[2,64,768]{2,1,0:T(8,128)(2,1)S(1)}, bf16[2,64,768]{2,1,0:T(8,128)(2,1)S(1)}, u32[]{:S(2)}, u32[]{:S(2)}) collective-permute-start(bf16[2,64,768]{2,1,0:T(8,128)(2,1)S(1)} %get-tuple-element.122), channel_id=1, source_target_pairs={{0,1},{1,0},{2,3},{3,2},{4,5},{5,4},{6,7},{7,6},{8,9},{9,8},{10,11... | collective-permute-start | bytes 589832 | tf_op jit(solution)/shard_map/ppermute | solution.py:106
  33.6 13.8 %collective-permute-start.27 = (bf16[2,64,768]{2,1,0:T(8,128)(2,1)S(1)}, bf16[2,64,768]{2,1,0:T(8,128)(2,1)S(1)}, u32[]{:S(2)}, u32[]{:S(2)}) collective-permute-start(bf16[2,64,768]{2,1,0:T(8,128)(2,1)S(1)} %get-tuple-element.120), channel_id=1, source_target_pairs={{0,16},{1,17},{2,18},{3,19},{4,20},{5,21},{6,22},{7,23},{8,24},{9,... | collective-permute-start | bytes 589832 | tf_op jit(solution)/shard_map/ppermute | solution.py:106
  35.3 13.0 %collective-permute-start.1 = (bf16[2,24,3072]{2,1,0:T(8,128)(2,1)S(1)}, bf16[2,24,3072]{2,1,0:T(8,128)(2,1)S(1)}, u32[]{:S(2)}, u32[]{:S(2)}) collective-permute-start(bf16[2,24,3072]{2,1,0:T(8,128)(2,1)S(1)} %get-tuple-element.118), channel_id=1, source_target_pairs={{0,1},{1,0},{2,3},{3,2},{4,5},{5,4},{6,7},{7,6},{8,9},{9,8},{10,11... | collective-permute-start | bytes 884744 | tf_op jit(solution)/shard_map/ppermute | solution.py:106
  44.4 6.7 %collective-permute-start.5 = (bf16[2,24,3072]{2,1,0:T(8,128)(2,1)S(1)}, bf16[2,24,3072]{2,1,0:T(8,128)(2,1)S(1)}, u32[]{:S(2)}, u32[]{:S(2)}) collective-permute-start(bf16[2,24,3072]{2,1,0:T(8,128)(2,1)S(1)} %get-tuple-element.116), channel_id=1, source_target_pairs={{0,16},{1,17},{2,18},{3,19},{4,20},{5,21},{6,22},{7,23},{8,24},{9,... | collective-permute-start | bytes 884744 | tf_op jit(solution)/shard_map/ppermute | solution.py:106
  45.9 10.1 %collective-permute-start.12 = (bf16[2,24,4096]{2,1,0:T(8,128)(2,1)S(1)}, bf16[2,24,4096]{2,1,0:T(8,128)(2,1)S(1)}, u32[]{:S(2)}, u32[]{:S(2)}) collective-permute-start(bf16[2,24,4096]{2,1,0:T(8,128)(2,1)S(1)} %get-tuple-element.114), channel_id=1, source_target_pairs={{0,1},{1,0},{2,3},{3,2},{4,5},{5,4},{6,7},{7,6},{8,9},{9,8},{10,11... | collective-permute-start | bytes 1179656 | tf_op jit(solution)/shard_map/ppermute | solution.py:106
  47.5 8.8 %collective-permute-start.16 = (bf16[2,24,4096]{2,1,0:T(8,128)(2,1)S(1)}, bf16[2,24,4096]{2,1,0:T(8,128)(2,1)S(1)}, u32[]{:S(2)}, u32[]{:S(2)}) collective-permute-start(bf16[2,24,4096]{2,1,0:T(8,128)(2,1)S(1)} %get-tuple-element.112), channel_id=1, source_target_pairs={{0,16},{1,17},{2,18},{3,19},{4,20},{5,21},{6,22},{7,23},{8,24},{9,... | collective-permute-start | bytes 1179656 | tf_op jit(solution)/shard_map/ppermute | solution.py:106
  48.1 8.1 %collective-permute-start.31 = (bf16[2,2,64,768]{3,2,1,0:T(8,128)(2,1)S(1)}, bf16[2,2,64,768]{3,2,1,0:T(8,128)(2,1)S(1)}, u32[]{:S(2)}, u32[]{:S(2)}) collective-permute-start(bf16[2,2,64,768]{3,2,1,0:T(8,128)(2,1)S(1)} %pad_maximum_fusion.17.refs_2_), channel_id=1, source_target_pairs={{0,8},{1,9},{2,10},{3,11},{4,12},{5,13},{6,14},{7,15},{8,0},{9,1},... | collective-permute-start | bytes 1179656 | tf_op jit(solution)/shard_map/ppermute | solution.py:106
  48.2 16.1 %collective-permute-start.28 = (bf16[2,2,64,768]{3,2,1,0:T(8,128)(2,1)S(1)}, bf16[2,2,64,768]{3,2,1,0:T(8,128)(2,1)S(1)}, u32[]{:S(2)}, u32[]{:S(2)}) collective-permute-start(bf16[2,2,64,768]{3,2,1,0:T(8,128)(2,1)S(1)} %pad_maximum_fusion.17.refs_2_), channel_id=1, source_target_pairs={{0,1},{1,0},{2,3},{3,2},{4,5},{5,4},{6,7},{7,6},{8,9},{9,8},{10,11... | collective-permute-start | bytes 1179656 | tf_op jit(solution)/shard_map/ppermute | solution.py:106
  51.1 13.3 %collective-permute-start.29 = (bf16[2,2,64,768]{3,2,1,0:T(8,128)(2,1)S(1)}, bf16[2,2,64,768]{3,2,1,0:T(8,128)(2,1)S(1)}, u32[]{:S(2)}, u32[]{:S(2)}) collective-permute-start(bf16[2,2,64,768]{3,2,1,0:T(8,128)(2,1)S(1)} %pad_maximum_fusion.16.refs_0_), channel_id=1, source_target_pairs={{0,8},{1,9},{2,10},{3,11},{4,12},{5,13},{6,14},{7,15},{8,0},{9,1},... | collective-permute-start | bytes 1179656 | tf_op jit(solution)/shard_map/ppermute | solution.py:106
  56.0 8.9 %collective-permute-start.24 = (bf16[2,2,64,768]{3,2,1,0:T(8,128)(2,1)S(1)}, bf16[2,2,64,768]{3,2,1,0:T(8,128)(2,1)S(1)}, u32[]{:S(2)}, u32[]{:S(2)}) collective-permute-start(bf16[2,2,64,768]{3,2,1,0:T(8,128)(2,1)S(1)} %pad_maximum_fusion.16.refs_0_), channel_id=1, source_target_pairs={{0,16},{1,17},{2,18},{3,19},{4,20},{5,21},{6,22},{7,23},{8,24},{9,... | collective-permute-start | bytes 1179656 | tf_op jit(solution)/shard_map/ppermute | solution.py:106
  56.2 8.9 %collective-permute-start.9 = (bf16[2,2,24,3072]{3,2,1,0:T(8,128)(2,1)S(1)}, bf16[2,2,24,3072]{3,2,1,0:T(8,128)(2,1)S(1)}, u32[]{:S(2)}, u32[]{:S(2)}) collective-permute-start(bf16[2,2,24,3072]{3,2,1,0:T(8,128)(2,1)S(1)} %pad_maximum_fusion.13.refs_2_), channel_id=1, source_target_pairs={{0,8},{1,9},{2,10},{3,11},{4,12},{5,13},{6,14},{7,15},{8,0},{9,1},... | collective-permute-start | bytes 1769480 | tf_op jit(solution)/shard_map/ppermute | solution.py:106
  56.2 20.8 %collective-permute-start.6 = (bf16[2,2,24,3072]{3,2,1,0:T(8,128)(2,1)S(1)}, bf16[2,2,24,3072]{3,2,1,0:T(8,128)(2,1)S(1)}, u32[]{:S(2)}, u32[]{:S(2)}) collective-permute-start(bf16[2,2,24,3072]{3,2,1,0:T(8,128)(2,1)S(1)} %pad_maximum_fusion.13.refs_2_), channel_id=1, source_target_pairs={{0,1},{1,0},{2,3},{3,2},{4,5},{5,4},{6,7},{7,6},{8,9},{9,8},{10,11... | collective-permute-start | bytes 1769480 | tf_op jit(solution)/shard_map/ppermute | solution.py:106
  64.4 12.8 %collective-permute-start.2 = (bf16[2,2,24,3072]{3,2,1,0:T(8,128)(2,1)S(1)}, bf16[2,2,24,3072]{3,2,1,0:T(8,128)(2,1)S(1)}, u32[]{:S(2)}, u32[]{:S(2)}) collective-permute-start(bf16[2,2,24,3072]{3,2,1,0:T(8,128)(2,1)S(1)} %pad_maximum_fusion.12.refs_0_), channel_id=1, source_target_pairs={{0,16},{1,17},{2,18},{3,19},{4,20},{5,21},{6,22},{7,23},{8,24},{9,... | collective-permute-start | bytes 1769480 | tf_op jit(solution)/shard_map/ppermute | solution.py:106
  64.5 12.8 %collective-permute-start.32 = (bf16[2,2,64,768]{3,2,1,0:T(8,128)(2,1)S(1)}, bf16[2,2,64,768]{3,2,1,0:T(8,128)(2,1)S(1)}, u32[]{:S(2)}, u32[]{:S(2)}) collective-permute-start(bf16[2,2,64,768]{3,2,1,0:T(8,128)(2,1)S(1)} %collective-permute-done.28.refs_3_), channel_id=1, source_target_pairs={{0,8},{1,9},{2,10},{3,11},{4,12},{5,13},{6,14},{7,15},{8,0},{9,1},... | collective-permute-start | bytes 1179656 | tf_op jit(solution)/shard_map/ppermute | solution.py:106
  64.9 12.9 %collective-permute-start.30 = (bf16[2,2,64,768]{3,2,1,0:T(8,128)(2,1)S(1)}, bf16[2,2,64,768]{3,2,1,0:T(8,128)(2,1)S(1)}, u32[]{:S(2)}, u32[]{:S(2)}) collective-permute-start(bf16[2,2,64,768]{3,2,1,0:T(8,128)(2,1)S(1)} %collective-permute-done.24.refs_1_), channel_id=1, source_target_pairs={{0,8},{1,9},{2,10},{3,11},{4,12},{5,13},{6,14},{7,15},{8,0},{9,1},... | collective-permute-start | bytes 1179656 | tf_op jit(solution)/shard_map/ppermute | solution.py:106
  65.1 33.0 %collective-permute-start.17 = (bf16[2,2,24,4096]{3,2,1,0:T(8,128)(2,1)S(1)}, bf16[2,2,24,4096]{3,2,1,0:T(8,128)(2,1)S(1)}, u32[]{:S(2)}, u32[]{:S(2)}) collective-permute-start(bf16[2,2,24,4096]{3,2,1,0:T(8,128)(2,1)S(1)} %pad_maximum_fusion.11.refs_2_), channel_id=1, source_target_pairs={{0,1},{1,0},{2,3},{3,2},{4,5},{5,4},{6,7},{7,6},{8,9},{9,8},{10,11... | collective-permute-start | bytes 2359304 | tf_op jit(solution)/shard_map/ppermute | solution.py:106
  77.0 21.2 %collective-permute-start.13 = (bf16[2,2,24,4096]{3,2,1,0:T(8,128)(2,1)S(1)}, bf16[2,2,24,4096]{3,2,1,0:T(8,128)(2,1)S(1)}, u32[]{:S(2)}, u32[]{:S(2)}) collective-permute-start(bf16[2,2,24,4096]{3,2,1,0:T(8,128)(2,1)S(1)} %pad_maximum_fusion.10.refs_0_), channel_id=1, source_target_pairs={{0,16},{1,17},{2,18},{3,19},{4,20},{5,21},{6,22},{7,23},{8,24},{9,... | collective-permute-start | bytes 2359304 | tf_op jit(solution)/shard_map/ppermute | solution.py:106
  77.2 20.4 %collective-permute-start.7 = (bf16[2,2,24,3072]{3,2,1,0:T(8,128)(2,1)S(1)}, bf16[2,2,24,3072]{3,2,1,0:T(8,128)(2,1)S(1)}, u32[]{:S(2)}, u32[]{:S(2)}) collective-permute-start(bf16[2,2,24,3072]{3,2,1,0:T(8,128)(2,1)S(1)} %pad_maximum_fusion.12.refs_0_), channel_id=1, source_target_pairs={{0,8},{1,9},{2,10},{3,11},{4,12},{5,13},{6,14},{7,15},{8,0},{9,1},... | collective-permute-start | bytes 1769480 | tf_op jit(solution)/shard_map/ppermute | solution.py:106
  77.2 21.4 %collective-permute-start.10 = (bf16[2,2,24,3072]{3,2,1,0:T(8,128)(2,1)S(1)}, bf16[2,2,24,3072]{3,2,1,0:T(8,128)(2,1)S(1)}, u32[]{:S(2)}, u32[]{:S(2)}) collective-permute-start(bf16[2,2,24,3072]{3,2,1,0:T(8,128)(2,1)S(1)} %collective-permute-done.6.refs_3_), channel_id=1, source_target_pairs={{0,8},{1,9},{2,10},{3,11},{4,12},{5,13},{6,14},{7,15},{8,0},{9,1},... | collective-permute-start | bytes 1769480 | tf_op jit(solution)/shard_map/ppermute | solution.py:106
  77.7 21.0 %collective-permute-start.8 = (bf16[2,2,24,3072]{3,2,1,0:T(8,128)(2,1)S(1)}, bf16[2,2,24,3072]{3,2,1,0:T(8,128)(2,1)S(1)}, u32[]{:S(2)}, u32[]{:S(2)}) collective-permute-start(bf16[2,2,24,3072]{3,2,1,0:T(8,128)(2,1)S(1)} %collective-permute-done.2.refs_1_), channel_id=1, source_target_pairs={{0,8},{1,9},{2,10},{3,11},{4,12},{5,13},{6,14},{7,15},{8,0},{9,1},... | collective-permute-start | bytes 1769480 | tf_op jit(solution)/shard_map/ppermute | solution.py:106
  97.6 66.9 %collective-permute-start.20 = (bf16[2,2,24,4096]{3,2,1,0:T(8,128)(2,1)S(1)}, bf16[2,2,24,4096]{3,2,1,0:T(8,128)(2,1)}, u32[]{:S(2)}, u32[]{:S(2)}) collective-permute-start(bf16[2,2,24,4096]{3,2,1,0:T(8,128)(2,1)S(1)} %pad_maximum_fusion.11.refs_2_), channel_id=1, source_target_pairs={{0,8},{1,9},{2,10},{3,11},{4,12},{5,13},{6,14},{7,15},{8,0},{9,1},... | collective-permute-start | bytes 2359304 | tf_op jit(solution)/shard_map/ppermute | solution.py:106
  98.1 66.4 %collective-permute-start.18 = (bf16[2,2,24,4096]{3,2,1,0:T(8,128)(2,1)S(1)}, bf16[2,2,24,4096]{3,2,1,0:T(8,128)(2,1)}, u32[]{:S(2)}, u32[]{:S(2)}) collective-permute-start(bf16[2,2,24,4096]{3,2,1,0:T(8,128)(2,1)S(1)} %pad_maximum_fusion.10.refs_0_), channel_id=1, source_target_pairs={{0,8},{1,9},{2,10},{3,11},{4,12},{5,13},{6,14},{7,15},{8,0},{9,1},... | collective-permute-start | bytes 2359304 | tf_op jit(solution)/shard_map/ppermute | solution.py:106
  98.2 66.3 %collective-permute-start.21 = (bf16[2,2,24,4096]{3,2,1,0:T(8,128)(2,1)S(1)}, bf16[2,2,24,4096]{3,2,1,0:T(8,128)(2,1)}, u32[]{:S(2)}, u32[]{:S(2)}) collective-permute-start(bf16[2,2,24,4096]{3,2,1,0:T(8,128)(2,1)S(1)} %collective-permute-done.17.refs_3_), channel_id=1, source_target_pairs={{0,8},{1,9},{2,10},{3,11},{4,12},{5,13},{6,14},{7,15},{8,0},{9,1},... | collective-permute-start | bytes 2359304 | tf_op jit(solution)/shard_map/ppermute | solution.py:106
  98.6 65.9 %collective-permute-start.19 = (bf16[2,2,24,4096]{3,2,1,0:T(8,128)(2,1)S(1)}, bf16[2,2,24,4096]{3,2,1,0:T(8,128)(2,1)}, u32[]{:S(2)}, u32[]{:S(2)}) collective-permute-start(bf16[2,2,24,4096]{3,2,1,0:T(8,128)(2,1)S(1)} %collective-permute-done.13.refs_1_), channel_id=1, source_target_pairs={{0,8},{1,9},{2,10},{3,11},{4,12},{5,13},{6,14},{7,15},{8,0},{9,1},... | collective-permute-start | bytes 2359304 | tf_op jit(solution)/shard_map/ppermute | solution.py:106
  318.2 21.5 %collective-permute-start.49 = (bf16[2,4,2,64,768]{4,3,1,2,0:T(8,128)(2,1)}, bf16[2,4,2,64,768]{4,3,1,2,0:T(8,128)(2,1)}, u32[]{:S(2)}, u32[]{:S(2)}) collective-permute-start(bf16[2,4,2,64,768]{4,3,1,2,0:T(8,128)(2,1)} %bitcast.276), channel_id=1, source_target_pairs={{0,8},{1,9},{2,10},{3,11},{4,12},{5,13},{6,14},{7,15},{8,0},{9,1},... | collective-permute-start | bytes 4718600 | tf_op jit(solution)/shard_map/ppermute | solution.py:106
  319.2 3.9 collective-permute-start.57
  323.1 4.9 %collective-permute-start.58 = (f32[1920]{0:T(1024)S(1)}, f32[1920]{0:T(1024)S(1)}, u32[]{:S(2)}, u32[]{:S(2)}) collective-permute-start(f32[1920]{0:T(1024)S(1)} %fusion.168), channel_id=1, source_target_pairs={{0,1},{1,0},{2,3},{3,2},{4,5},{5,4},{6,7},{7,6},{8,9},{9,8},{10,11... | collective-permute-start | bytes 23048 | tf_op jit(solution)/shard_map/ppermute | solution.py:106
  328.0 3.7 collective-permute-start.59
  329.0 35.2 %collective-permute-start.33 = (bf16[2,4,2,24,3072]{4,3,1,2,0:T(8,128)(2,1)S(1)}, bf16[2,4,2,24,3072]{4,3,1,2,0:T(8,128)(2,1)S(1)}, u32[]{:S(2)}, u32[]{:S(2)}) collective-permute-start(bf16[2,4,2,24,3072]{4,3,1,2,0:T(8,128)(2,1)S(1)} %bitcast.311), channel_id=1, source_target_pairs={{0,8},{1,9},{2,10},{3,11},{4,12},{5,13},{6,14},{7,15},{8,0},{9,1},... | collective-permute-start | bytes 7077896 | tf_op jit(solution)/shard_map/ppermute | solution.py:106
  331.7 6.4 %collective-permute-start.60 = (f32[1920]{0:T(1024)S(1)}, f32[1920]{0:T(1024)S(1)}, u32[]{:S(2)}, u32[]{:S(2)}) collective-permute-start(f32[1920]{0:T(1024)S(1)} %add.519), channel_id=1, source_target_pairs={{0,2},{1,3},{2,0},{3,1},{4,6},{5,7},{6,4},{7,5},{8,10},{9,11},{10,... | collective-permute-start | bytes 23048 | tf_op jit(solution)/shard_map/ppermute | solution.py:106
  338.1 12.9 %collective-permute-start.61 = (f32[1920]{0:T(1024)S(1)}, f32[1920]{0:T(1024)S(1)}, u32[]{:S(2)}, u32[]{:S(2)}) collective-permute-start(f32[1920]{0:T(1024)S(1)} %add.520), channel_id=1, source_target_pairs={{0,4},{1,5},{2,6},{3,7},{4,0},{5,1},{6,2},{7,3},{8,12},{9,13},{10,... | collective-permute-start | bytes 23048 | tf_op jit(solution)/shard_map/ppermute | solution.py:106
  341.8 9.2 %collective-permute-start.50 = (bf16[2,2,64,768]{3,2,1,0:T(8,128)(2,1)S(1)}, bf16[2,2,64,768]{3,2,1,0:T(8,128)(2,1)S(1)}, u32[]{:S(2)}, u32[]{:S(2)}) collective-permute-start(bf16[2,2,64,768]{3,2,1,0:T(8,128)(2,1)S(1)} %dynamic-slice_bitcast_fusion.5), channel_id=1, source_target_pairs={{0,1},{1,0},{2,3},{3,2},{4,5},{5,4},{6,7},{7,6},{8,9},{9,8},{10,11... | collective-permute-start | bytes 1179656 | tf_op jit(solution)/shard_map/ppermute | solution.py:106
  343.4 8.3 %collective-permute-start.52 = (bf16[2,2,64,768]{3,2,0,1:T(8,128)(2,1)S(1)}, bf16[2,2,64,768]{3,2,0,1:T(8,128)(2,1)S(1)}, u32[]{:S(2)}, u32[]{:S(2)}) collective-permute-start(bf16[2,2,64,768]{3,2,0,1:T(8,128)(2,1)S(1)} %dynamic-slice_bitcast_fusion.4), channel_id=1, source_target_pairs={{0,16},{1,17},{2,18},{3,19},{4,20},{5,21},{6,22},{7,23},{8,24},{9,... | collective-permute-start | bytes 1179656 | tf_op jit(solution)/shard_map/ppermute | solution.py:106
  351.0 39.8 %collective-permute-start.41 = (bf16[2,4,2,24,4096]{4,3,1,2,0:T(8,128)(2,1)}, bf16[2,4,2,24,4096]{4,3,1,2,0:T(8,128)(2,1)}, u32[]{:S(2)}, u32[]{:S(2)}) collective-permute-start(bf16[2,4,2,24,4096]{4,3,1,2,0:T(8,128)(2,1)} %bitcast.274), channel_id=1, source_target_pairs={{0,8},{1,9},{2,10},{3,11},{4,12},{5,13},{6,14},{7,15},{8,0},{9,1},... | collective-permute-start | bytes 9437192 | tf_op jit(solution)/shard_map/ppermute | solution.py:106
  351.2 7.4 %collective-permute-start.51 = (bf16[2,64,768]{2,1,0:T(8,128)(2,1)S(1)}, bf16[2,64,768]{2,1,0:T(8,128)(2,1)S(1)}, u32[]{:S(2)}, u32[]{:S(2)}) collective-permute-start(bf16[2,64,768]{2,1,0:T(8,128)(2,1)S(1)} %dynamic-slice_bitcast_fusion.11), channel_id=1, source_target_pairs={{0,16},{1,17},{2,18},{3,19},{4,20},{5,21},{6,22},{7,23},{8,24},{9,... | collective-permute-start | bytes 589832 | tf_op jit(solution)/shard_map/ppermute | solution.py:106
  351.9 7.1 %collective-permute-start.53 = (bf16[2,64,768]{2,1,0:T(8,128)(2,1)S(1)}, bf16[2,64,768]{2,1,0:T(8,128)(2,1)S(1)}, u32[]{:S(2)}, u32[]{:S(2)}) collective-permute-start(bf16[2,64,768]{2,1,0:T(8,128)(2,1)S(1)} %dynamic-slice_bitcast_fusion.10), channel_id=1, source_target_pairs={{0,1},{1,0},{2,3},{3,2},{4,5},{5,4},{6,7},{7,6},{8,9},{9,8},{10,11... | collective-permute-start | bytes 589832 | tf_op jit(solution)/shard_map/ppermute | solution.py:106
  359.8 9.3 %collective-permute-start.54 = (bf16[64,768]{1,0:T(8,128)(2,1)}, bf16[64,768]{1,0:T(8,128)(2,1)S(1)}, u32[]{:S(2)}, u32[]{:S(2)}) collective-permute-start(bf16[64,768]{1,0:T(8,128)(2,1)} %get-tuple-element.108), channel_id=1, source_target_pairs={{0,2},{1,3},{2,0},{3,1},{4,6},{5,7},{6,4},{7,5},{8,10},{9,11},{10,... | collective-permute-start | bytes 294920 | tf_op jit(solution)/shard_map/ppermute | solution.py:106
  361.8 9.6 %collective-permute-start.55 = (bf16[64,768]{1,0:T(8,128)(2,1)}, bf16[64,768]{1,0:T(8,128)(2,1)}, u32[]{:S(2)}, u32[]{:S(2)}) collective-permute-start(bf16[64,768]{1,0:T(8,128)(2,1)} %get-tuple-element.109), channel_id=1, source_target_pairs={{0,4},{1,5},{2,6},{3,7},{4,0},{5,1},{6,2},{7,3},{8,12},{9,13},{10,... | collective-permute-start | bytes 294920 | tf_op jit(solution)/shard_map/ppermute | solution.py:106
  362.6 8.8 %collective-permute-start.56 = (bf16[64,768]{1,0:T(8,128)(2,1)S(1)}, bf16[64,768]{1,0:T(8,128)(2,1)}, u32[]{:S(2)}, u32[]{:S(2)}) collective-permute-start(bf16[64,768]{1,0:T(8,128)(2,1)S(1)} %get-tuple-element.110), channel_id=1, source_target_pairs={{0,6},{1,7},{2,4},{3,5},{4,2},{5,3},{6,0},{7,1},{8,14},{9,15},{10,... | collective-permute-start | bytes 294920 | tf_op jit(solution)/shard_map/ppermute | solution.py:106
  365.4 14.2 %collective-permute-start.34 = (bf16[2,2,24,3072]{3,2,1,0:T(8,128)(2,1)S(1)}, bf16[2,2,24,3072]{3,2,1,0:T(8,128)(2,1)}, u32[]{:S(2)}, u32[]{:S(2)}) collective-permute-start(bf16[2,2,24,3072]{3,2,1,0:T(8,128)(2,1)S(1)} %dynamic-slice_bitcast_fusion.3), channel_id=1, source_target_pairs={{0,1},{1,0},{2,3},{3,2},{4,5},{5,4},{6,7},{7,6},{8,9},{9,8},{10,11... | collective-permute-start | bytes 1769480 | tf_op jit(solution)/shard_map/ppermute | solution.py:106
  373.2 16.3 %collective-permute-start.36 = (bf16[2,2,24,3072]{3,2,0,1:T(8,128)(2,1)S(1)}, bf16[2,2,24,3072]{3,2,0,1:T(8,128)(2,1)S(1)}, u32[]{:S(2)}, u32[]{:S(2)}) collective-permute-start(bf16[2,2,24,3072]{3,2,0,1:T(8,128)(2,1)S(1)} %dynamic-slice_bitcast_fusion.2), channel_id=1, source_target_pairs={{0,16},{1,17},{2,18},{3,19},{4,20},{5,21},{6,22},{7,23},{8,24},{9,... | collective-permute-start | bytes 1769480 | tf_op jit(solution)/shard_map/ppermute | solution.py:106
  380.9 15.1 %collective-permute-start.35 = (bf16[2,24,3072]{2,1,0:T(8,128)(2,1)S(1)}, bf16[2,24,3072]{2,1,0:T(8,128)(2,1)S(1)}, u32[]{:S(2)}, u32[]{:S(2)}) collective-permute-start(bf16[2,24,3072]{2,1,0:T(8,128)(2,1)S(1)} %dynamic-slice_bitcast_fusion.9), channel_id=1, source_target_pairs={{0,16},{1,17},{2,18},{3,19},{4,20},{5,21},{6,22},{7,23},{8,24},{9,... | collective-permute-start | bytes 884744 | tf_op jit(solution)/shard_map/ppermute | solution.py:106
  389.7 10.0 %collective-permute-start.37 = (bf16[2,24,3072]{2,1,0:T(8,128)(2,1)S(1)}, bf16[2,24,3072]{2,1,0:T(8,128)(2,1)S(1)}, u32[]{:S(2)}, u32[]{:S(2)}) collective-permute-start(bf16[2,24,3072]{2,1,0:T(8,128)(2,1)S(1)} %dynamic-slice_bitcast_fusion.8), channel_id=1, source_target_pairs={{0,1},{1,0},{2,3},{3,2},{4,5},{5,4},{6,7},{7,6},{8,9},{9,8},{10,11... | collective-permute-start | bytes 884744 | tf_op jit(solution)/shard_map/ppermute | solution.py:106
  394.0 18.1 %collective-permute-start.42 = (bf16[2,2,24,4096]{3,2,1,0:T(8,128)(2,1)S(1)}, bf16[2,2,24,4096]{3,2,1,0:T(8,128)(2,1)S(1)}, u32[]{:S(2)}, u32[]{:S(2)}) collective-permute-start(bf16[2,2,24,4096]{3,2,1,0:T(8,128)(2,1)S(1)} %dynamic-slice_bitcast_fusion.1), channel_id=1, source_target_pairs={{0,1},{1,0},{2,3},{3,2},{4,5},{5,4},{6,7},{7,6},{8,9},{9,8},{10,11... | collective-permute-start | bytes 2359304 | tf_op jit(solution)/shard_map/ppermute | solution.py:106
  395.0 19.8 %collective-permute-start.44 = (bf16[2,2,24,4096]{3,2,0,1:T(8,128)(2,1)S(1)}, bf16[2,2,24,4096]{3,2,0,1:T(8,128)(2,1)S(1)}, u32[]{:S(2)}, u32[]{:S(2)}) collective-permute-start(bf16[2,2,24,4096]{3,2,0,1:T(8,128)(2,1)S(1)} %dynamic-slice_bitcast_fusion), channel_id=1, source_target_pairs={{0,16},{1,17},{2,18},{3,19},{4,20},{5,21},{6,22},{7,23},{8,24},{9,... | collective-permute-start | bytes 2359304 | tf_op jit(solution)/shard_map/ppermute | solution.py:106
  399.9 26.4 %collective-permute-start.38 = (bf16[24,3072]{1,0:T(8,128)(2,1)S(1)}, bf16[24,3072]{1,0:T(8,128)(2,1)S(1)}, u32[]{:S(2)}, u32[]{:S(2)}) collective-permute-start(bf16[24,3072]{1,0:T(8,128)(2,1)S(1)} %get-tuple-element.105), channel_id=1, source_target_pairs={{0,2},{1,3},{2,0},{3,1},{4,6},{5,7},{6,4},{7,5},{8,10},{9,11},{10,... | collective-permute-start | bytes 442376 | tf_op jit(solution)/shard_map/ppermute | solution.py:106
  402.1 26.7 %collective-permute-start.39 = (bf16[24,3072]{1,0:T(8,128)(2,1)S(1)}, bf16[24,3072]{1,0:T(8,128)(2,1)S(1)}, u32[]{:S(2)}, u32[]{:S(2)}) collective-permute-start(bf16[24,3072]{1,0:T(8,128)(2,1)S(1)} %get-tuple-element.106), channel_id=1, source_target_pairs={{0,4},{1,5},{2,6},{3,7},{4,0},{5,1},{6,2},{7,3},{8,12},{9,13},{10,... | collective-permute-start | bytes 442376 | tf_op jit(solution)/shard_map/ppermute | solution.py:106
  402.1 26.7 %collective-permute-start.40 = (bf16[24,3072]{1,0:T(8,128)(2,1)S(1)}, bf16[24,3072]{1,0:T(8,128)(2,1)S(1)}, u32[]{:S(2)}, u32[]{:S(2)}) collective-permute-start(bf16[24,3072]{1,0:T(8,128)(2,1)S(1)} %get-tuple-element.107), channel_id=1, source_target_pairs={{0,6},{1,7},{2,4},{3,5},{4,2},{5,3},{6,0},{7,1},{8,14},{9,15},{10,... | collective-permute-start | bytes 442376 | tf_op jit(solution)/shard_map/ppermute | solution.py:106
  412.3 8.9 %collective-permute-start.43 = (bf16[2,24,4096]{2,1,0:T(8,128)(2,1)S(1)}, bf16[2,24,4096]{2,1,0:T(8,128)(2,1)S(1)}, u32[]{:S(2)}, u32[]{:S(2)}) collective-permute-start(bf16[2,24,4096]{2,1,0:T(8,128)(2,1)S(1)} %dynamic-slice_bitcast_fusion.7), channel_id=1, source_target_pairs={{0,16},{1,17},{2,18},{3,19},{4,20},{5,21},{6,22},{7,23},{8,24},{9,... | collective-permute-start | bytes 1179656 | tf_op jit(solution)/shard_map/ppermute | solution.py:106
  415.0 7.9 %collective-permute-start.45 = (bf16[2,24,4096]{2,1,0:T(8,128)(2,1)S(1)}, bf16[2,24,4096]{2,1,0:T(8,128)(2,1)S(1)}, u32[]{:S(2)}, u32[]{:S(2)}) collective-permute-start(bf16[2,24,4096]{2,1,0:T(8,128)(2,1)S(1)} %dynamic-slice_bitcast_fusion.6), channel_id=1, source_target_pairs={{0,1},{1,0},{2,3},{3,2},{4,5},{5,4},{6,7},{7,6},{8,9},{9,8},{10,11... | collective-permute-start | bytes 1179656 | tf_op jit(solution)/shard_map/ppermute | solution.py:106
  423.3 10.8 %collective-permute-start.46 = (bf16[24,4096]{1,0:T(8,128)(2,1)S(1)}, bf16[24,4096]{1,0:T(8,128)(2,1)S(1)}, u32[]{:S(2)}, u32[]{:S(2)}) collective-permute-start(bf16[24,4096]{1,0:T(8,128)(2,1)S(1)} %get-tuple-element.102), channel_id=1, source_target_pairs={{0,2},{1,3},{2,0},{3,1},{4,6},{5,7},{6,4},{7,5},{8,10},{9,11},{10,... | collective-permute-start | bytes 589832 | tf_op jit(solution)/shard_map/ppermute | solution.py:106
  426.3 13.6 %collective-permute-start.47 = (bf16[24,4096]{1,0:T(8,128)(2,1)S(1)}, bf16[24,4096]{1,0:T(8,128)(2,1)S(1)}, u32[]{:S(2)}, u32[]{:S(2)}) collective-permute-start(bf16[24,4096]{1,0:T(8,128)(2,1)S(1)} %get-tuple-element.103), channel_id=1, source_target_pairs={{0,4},{1,5},{2,6},{3,7},{4,0},{5,1},{6,2},{7,3},{8,12},{9,13},{10,... | collective-permute-start | bytes 589832 | tf_op jit(solution)/shard_map/ppermute | solution.py:106
  426.3 13.6 %collective-permute-start.48 = (bf16[24,4096]{1,0:T(8,128)(2,1)S(1)}, bf16[24,4096]{1,0:T(8,128)(2,1)S(1)}, u32[]{:S(2)}, u32[]{:S(2)}) collective-permute-start(bf16[24,4096]{1,0:T(8,128)(2,1)S(1)} %get-tuple-element.104), channel_id=1, source_target_pairs={{0,6},{1,7},{2,4},{3,5},{4,2},{5,3},{6,0},{7,1},{8,14},{9,15},{10,... | collective-permute-start | bytes 589832 | tf_op jit(solution)/shard_map/ppermute | solution.py:106
  (65 other events, 479.8 us)

commit v2 on v0

v2 whole, which is shorter than its diff:
```python
import functools

import jax
import jax.numpy as jnp
from jax import lax
from jax.experimental import pallas as pl
from jax.experimental.pallas import tpu as pltpu
from jax.sharding import PartitionSpec as P

both = ("dp", "fsdp")
epsilon = 1e-06
highest = lax.Precision.HIGHEST
anywhere = pl.BlockSpec(memory_space=pl.ANY)


def place_index(y, c, z, x):
    return ((y * 2 + c) * 4 + z) * 2 + x


def flip_pairs(dy=0, dc=0, dz=0, dx=0):
    pairs = []
    for y in range(2):
        for c in range(2):
            for z in range(4):
                for x in range(2):
                    pairs.append(
                        (place_index(y, c, z, x), place_index(y ^ dy, c ^ dc, z ^ dz, x ^ dx))
                    )
    return pairs


def swap(values, **flips):
    return lax.ppermute(values, both, flip_pairs(**flips))


def hand_routed():
    return (lax.axis_size("dp"), lax.axis_size("fsdp")) == (4, 8)


def own_place():
    outer = lax.axis_index("dp")
    inner = lax.axis_index("fsdp")
    return outer // 2, outer % 2, inner // 2, inner % 2


def after(values, *earlier):
    return lax.optimization_barrier((values, *earlier))[0]


def together(*values):
    return lax.optimization_barrier(values)


def fill_copies(place_ref, pieces, target, sems):
    if len(pieces) == 1:
        return [pltpu.make_async_copy(pieces[0], target, sems.at[0])]
    y, c, z, x = place_ref[0], place_ref[1], place_ref[2], place_ref[3]
    copies = []

    def add(piece, row, size):
        copies.append(
            pltpu.make_async_copy(
                piece, target.at[pl.ds(row, size)], sems.at[len(copies)]
            )
        )

    for number, piece in enumerate(pieces):
        core = c ^ (number // 4)
        kind = number % 4
        if kind < 2:
            add(piece, place_index(y ^ kind, core, z - z % 2, 0), 4)
        else:
            for outer in range(2):
                for inner in range(2):
                    row = place_index(outer, core, (z - z % 2) ^ 2, x ^ (kind - 2))
                    add(piece.at[pl.ds(2 * outer + inner, 1)], row + 2 * inner, 1)
    return copies


def filled(place_ref, pieces, full_ref, held, sems, body):
    step = pl.program_id(0)
    kept = pltpu.make_async_copy(held, full_ref, sems.at[32])

    @pl.when(step == 0)
    def _():
        copies = fill_copies(place_ref, pieces, held, sems)
        for copy in copies:
            copy.start()
        for copy in copies:
            copy.wait()
        kept.start()

    body()

    @pl.when(step == pl.num_programs(0) - 1)
    def _():
        kept.wait()


def gather_order(near, far, core_near, core_far):
    return (near[0], far[0], near[1], far[1], core_near[0], core_far[0], core_near[1], core_far[1])


def split_rows(full):
    return full.reshape(32, full.shape[0] // 32, full.shape[1])


def in_order(own, other, index):
    odd = index % 2 == 1
    return jnp.where(odd, other, own), jnp.where(odd, own, other)


def gather_column(shard):
    return tuple(swap(shard, dz=flip) for flip in (1, 2, 3))


def gather_plane(place, shard, column):
    first = jnp.stack(in_order(shard, column[0], place[2]))
    second = jnp.stack(in_order(column[1], column[2], place[2]))
    return first, second, swap(first, dx=1), swap(second, dy=1)


def gather_near(place, first, second, first_near, second_near):
    rows, columns = first.shape[1:]
    first = jnp.stack(in_order(first, first_near, place[3]), axis=1)
    second = jnp.stack(in_order(second, second_near, place[0]))
    return first.reshape(4, rows, columns), second.reshape(4, rows, columns)


def gather_far(first, second):
    return swap(first, dy=1), swap(second, dx=1)


def gather_core(*pieces):
    return tuple(swap(piece, dc=1) for piece in pieces)


def cut(values, places):
    start = [0 if place is None else place for place in places]
    sizes = [size if place is None else 1 for place, size in zip(places, values.shape)]
    kept = [size for place, size in zip(places, values.shape) if place is None]
    return lax.dynamic_slice(values, start, sizes).reshape(kept)


def summed(*terms):
    total = terms[0].astype(jnp.float32)
    for term in terms[1:]:
        total = total + term.astype(jnp.float32)
    return total


def low_sum(*terms):
    return summed(*terms).astype(jnp.bfloat16)


def joined_halves(kept, sent):
    return jnp.stack([kept, sent], axis=1).reshape(-1, kept.shape[2]).astype(jnp.float32)


class Scatter:
    def __init__(self, kept, sent, place):
        self.place = place
        self.shape = (2, 4, 2, kept.shape[1] // 8, kept.shape[2])
        self.kept = kept.reshape(self.shape)
        self.sent = sent

    def halves(self, got, cut_y, cut_x, half):
        y, c, z, x = self.place
        own = self.kept[:, 2 * half : 2 * half + 2]
        got = got[:, 2 * half : 2 * half + 2]
        places = (cut_y, None, cut_x, None, None)
        return cut(own, places), cut(got, places)

    def core(self):
        return swap(self.sent, dc=1).reshape(self.shape)

    def plane(self, got):
        y, c, z, x = self.place
        first = swap(low_sum(*self.halves(got, None, 1 - x, 0)), dx=1)
        second = swap(low_sum(*self.halves(got, 1 - y, None, 1)), dy=1)
        return first, second

    def far(self, got, near):
        y, c, z, x = self.place
        first = low_sum(
            *self.halves(got, 1 - y, x, 0), cut(near[0], (1 - y, None, None, None))
        )
        second = low_sum(
            *self.halves(got, y, 1 - x, 1), cut(near[1], (None, 1 - x, None, None))
        )
        return swap(first, dy=1), swap(second, dx=1)

    def column(self, got, near, far):
        y, c, z, x = self.place
        first = summed(*self.halves(got, y, x, 0), cut(near[0], (y, None, None, None)), far[0])
        second = summed(*self.halves(got, y, x, 1), cut(near[1], (None, x, None, None)), far[1])
        total = jnp.concatenate([first, second], axis=0)
        others = []
        for flip in (1, 2, 3):
            share = cut(total, (z ^ flip, None, None)).astype(jnp.bfloat16)
            others.append(swap(share, dz=flip))
        return cut(total, (z, None, None)), *others


def add_flipped(values, *steps):
    for flips in steps:
        values = values + swap(values, **flips)
    return values


count = 128


def relative_places():
    places = jnp.arange(4 * count, dtype=jnp.int32)
    return jnp.where(places < 3 * count, places - count, places - 5 * count)


def bucket_of(relative):
    distance = jnp.abs(relative)
    larger = jnp.zeros_like(distance)
    for threshold in (12, 16, 23, 32, 46, 64, 91):
        larger = larger + (distance >= threshold).astype(jnp.int32)
    bucket = jnp.where(distance < 8, distance, 8 + larger)
    return bucket + 16 * (relative > 0).astype(jnp.int32)


def lines_onehot(bucket_count):
    labels = jnp.arange(bucket_count, dtype=jnp.int32)
    return (bucket_of(relative_places())[:, None] == labels).astype(jnp.float32)


def own_lanes(head, shape):
    lanes = lax.broadcasted_iota(jnp.int32, shape, 1)
    return lanes < shape[1] // 2 if head == 0 else lanes >= shape[1] // 2


def keep_lanes(head, values):
    return jnp.where(own_lanes(head, values.shape), values, jnp.zeros_like(values))


def both_heads(values):
    return jnp.concatenate([keep_lanes(0, values), keep_lanes(1, values)], axis=0)


def joined(stacked):
    first, second = jnp.split(stacked, 2, axis=0)
    return jnp.where(own_lanes(0, first.shape), first, second).astype(jnp.bfloat16)


def softmax_rows(scores):
    raised = jnp.exp(scores - jnp.max(scores, axis=-1, keepdims=True))
    return raised * (1.0 / jnp.sum(raised, axis=-1, keepdims=True))


def dot_nt(left, right):
    return lax.dot_general(
        left, right, (((1,), (1,)), ((), ())), preferred_element_type=jnp.float32
    )


def dot_nn(left, right):
    return jnp.dot(left, right, preferred_element_type=jnp.float32)


def attend_kernel(
    docs, length, group, q_ref, k_ref, v_ref, line_ref, mask_ref, query_mask_ref,
    mixed_ref, doc_probs_ref, query_probs_ref, scores_scratch, probs_scratch,
):
    blocks = length // count
    query_start = docs * length
    query_blocks = (q_ref.shape[0] - query_start) // count
    row_group = lax.broadcasted_iota(jnp.int32, (count, count), 0) // group
    column_group = lax.broadcasted_iota(jnp.int32, (count, count), 1) // group
    bands, edges = [], []
    for head in range(2):
        line = line_ref[0, head : head + 1, :]
        band = pltpu.roll(
            jnp.broadcast_to(line, (count, 4 * count)), 0, 1, stride=1, stride_axis=0
        )
        bands.append(band)
        edges.append(
            (
                jnp.broadcast_to(line[:, 4 * count - 1 :], (1, count)),
                jnp.broadcast_to(line[:, 3 * count - 1 : 3 * count], (1, count)),
            )
        )
    for doc in range(docs):
        base = doc * length
        whole = slice(base, base + length)
        masking = mask_ref[doc : doc + 1, :]
        scores_scratch[...] = dot_nt(both_heads(q_ref[whole, :]), k_ref[whole, :])
        for head in range(2):
            for row in range(blocks):
                rows = slice(row * count, (row + 1) * count)
                stacked = slice(head * length + row * count, head * length + (row + 1) * count)
                shifted = []
                for column in range(blocks):
                    columns = slice(column * count, (column + 1) * count)
                    away = column - row
                    block = scores_scratch[stacked, columns]
                    if abs(away) > 1:
                        block = block + (edges[head][away > 0] + masking[:, columns])
                    else:
                        start = (away + 1) * count
                        block = block + bands[head][:, start : start + count]
                        block = block + masking[:, columns]
                    shifted.append(block)
                probs = softmax_rows(jnp.concatenate(shifted, axis=1))
                doc_probs_ref[head, base + row * count : base + (row + 1) * count, :] = probs
                probs_scratch[stacked, :] = probs.astype(jnp.bfloat16)
        mixed_ref[whole, :] = joined(dot_nn(probs_scratch[...], v_ref[whole, :]))
    for block in range(query_blocks):
        rows = slice(query_start + block * count, query_start + (block + 1) * count)
        masking = query_mask_ref[block]
        scores = dot_nt(both_heads(q_ref[rows, :]), k_ref[rows, :])
        low = []
        for head in range(2):
            bias = jnp.where(
                row_group == column_group, bands[head][:, count : 2 * count], -1e9
            )
            probs = softmax_rows(scores[head * count : (head + 1) * count, :] + bias + masking)
            query_probs_ref[head, block * count : (block + 1) * count, :] = probs
            low.append(probs.astype(jnp.bfloat16))
        mixed_ref[rows, :] = joined(dot_nn(jnp.concatenate(low, axis=0), v_ref[rows, :]))


def pair_spec(rows, offset):
    return pl.BlockSpec((rows, 2 * 64), lambda pair: (0, offset + pair))


def attend(projected, lines, doc_mask, query_mask, group):
    docs, length = doc_mask.shape
    rows, width = projected.shape[0], projected.shape[1] // 3
    pairs = lines.shape[0]
    query_rows = rows - docs * length
    return pl.pallas_call(
        functools.partial(attend_kernel, docs, length, group),
        grid=(pairs,),
        out_shape=(
            jax.ShapeDtypeStruct((rows, width), jnp.bfloat16),
            jax.ShapeDtypeStruct((2 * pairs, docs * length, length), jnp.float32),
            jax.ShapeDtypeStruct((2 * pairs, query_rows, count), jnp.float32),
        ),
        in_specs=[
            pair_spec(rows, 0),
            pair_spec(rows, pairs),
            pair_spec(rows, 2 * pairs),
            pl.BlockSpec((1, 2, 4 * count), lambda pair: (pair, 0, 0)),
            pl.BlockSpec((docs, length), lambda pair: (0, 0)),
            pl.BlockSpec(query_mask.shape, lambda pair: (0, 0, 0)),
        ],
        out_specs=(
            pair_spec(rows, 0),
            pl.BlockSpec((2, docs * length, length), lambda pair: (pair, 0, 0)),
            pl.BlockSpec((2, query_rows, count), lambda pair: (pair, 0, 0)),
        ),
        scratch_shapes=[
            pltpu.VMEM((2 * length, length), jnp.float32),
            pltpu.VMEM((2 * length, length), jnp.bfloat16),
        ],
        compiler_params=pltpu.CompilerParams(vmem_limit_bytes=40 * 2**20),
        cost_estimate=pl.CostEstimate(
            flops=2 * 2 * pairs * (docs * length * length + query_rows * count) * 128 * 2,
            bytes_accessed=rows * width * 8 + 8 * pairs * docs * length * length,
            transcendentals=2 * pairs * (docs * length * length + query_rows * count),
        ),
        name="attend",
    )(projected, projected, projected, lines, doc_mask, query_mask)


def attend_back_kernel(
    docs, length, q_ref, k_ref, v_ref, grad_ref, doc_probs_ref, query_probs_ref,
    out_ref, line_ref, grads_scratch, scores_scratch, probs_scratch,
):
    blocks = length // count
    query_start = docs * length
    query_blocks = (q_ref.shape[0] - query_start) // count
    low = jnp.bfloat16
    band = [[None] * 5, [None] * 5]

    def gather(head, place, block):
        held = band[head][place]
        band[head][place] = block if held is None else held + block

    def backward(probs, grad_probs):
        product = probs * grad_probs
        return product - probs * jnp.sum(product, axis=-1, keepdims=True)

    for doc in range(docs):
        base = doc * length
        whole = slice(base, base + length)
        grads_scratch[...] = dot_nt(both_heads(grad_ref[whole, :]), v_ref[whole, :])
        for head in range(2):
            for row in range(blocks):
                rows = slice(base + row * count, base + (row + 1) * count)
                stacked = slice(head * length + row * count, head * length + (row + 1) * count)
                probs = doc_probs_ref[head, rows, :]
                scores = backward(probs, grads_scratch[stacked, :])
                for column in range(blocks):
                    away = max(-2, min(2, column - row))
                    block = scores[:, column * count : (column + 1) * count]
                    if abs(away) == 2:
                        block = jnp.sum(block.reshape(count // 8, 8, count), axis=0)
                    gather(head, away + 2, block)
                scores_scratch[stacked, :] = scores.astype(low)
                probs_scratch[stacked, :] = probs.astype(low)
        out_ref[0, whole, :] = joined(dot_nn(scores_scratch[...], k_ref[whole, :]))
        q_turned = q_ref[whole, :].T
        grad_turned = grad_ref[whole, :].T
        half = q_turned.shape[0] // 2
        grad_k, grad_v = [], []
        for head in range(2):
            own = slice(head * half, (head + 1) * half)
            stacked = slice(head * length, (head + 1) * length)
            grad_k.append(dot_nn(q_turned[own, :], scores_scratch[stacked, :]))
            grad_v.append(dot_nn(grad_turned[own, :], probs_scratch[stacked, :]))
        out_ref[1, whole, :] = jnp.concatenate(grad_k, axis=0).astype(low).T
        out_ref[2, whole, :] = jnp.concatenate(grad_v, axis=0).astype(low).T
    for block in range(query_blocks):
        rows = slice(query_start + block * count, query_start + (block + 1) * count)
        grad_probs = dot_nt(both_heads(grad_ref[rows, :]), v_ref[rows, :])
        low_scores, low_probs = [], []
        for head in range(2):
            probs = query_probs_ref[head, block * count : (block + 1) * count, :]
            scores = backward(probs, grad_probs[head * count : (head + 1) * count, :])
            gather(head, 2, scores)
            low_scores.append(scores.astype(low))
            low_probs.append(probs.astype(low))
        out_ref[0, rows, :] = joined(dot_nn(jnp.concatenate(low_scores, axis=0), k_ref[rows, :]))
        turned = jnp.concatenate(low_scores, axis=1).T
        out_ref[1, rows, :] = joined(dot_nn(turned, q_ref[rows, :]))
        turned = jnp.concatenate(low_probs, axis=1).T
        out_ref[2, rows, :] = joined(dot_nn(turned, grad_ref[rows, :]))
    for head in range(2):
        below, before, middle, after, above = band[head]
        wide = jnp.concatenate([before, middle, after, jnp.zeros_like(middle)], axis=1)
        size = count
        while size > 1:
            size //= 2
            wide = wide[:size] + pltpu.roll(wide[size:], 4 * count - size, 1)
        far = jnp.concatenate(
            [
                jnp.zeros((1, 2 * count), jnp.float32),
                jnp.sum(above, axis=0, keepdims=True),
                jnp.sum(below, axis=0, keepdims=True),
            ],
            axis=1,
        )
        line_ref[0, head : head + 1, :] = wide + far


def attend_back(projected, grad_mixed, doc_probs, query_probs, length, *earlier):
    rows, width = grad_mixed.shape
    pairs = doc_probs.shape[0] // 2
    docs = doc_probs.shape[1] // length
    query_rows = query_probs.shape[1]

    def kernel(*refs):
        attend_back_kernel(docs, length, *refs[:6], *refs[6 + len(earlier) :])

    return pl.pallas_call(
        kernel,
        grid=(pairs,),
        out_shape=(
            jax.ShapeDtypeStruct((3, rows, width), jnp.bfloat16),
            jax.ShapeDtypeStruct((pairs, 2, 4 * count), jnp.float32),
        ),
        in_specs=[
            pair_spec(rows, 0),
            pair_spec(rows, pairs),
            pair_spec(rows, 2 * pairs),
            pair_spec(rows, 0),
            pl.BlockSpec((2, docs * length, length), lambda pair: (pair, 0, 0)),
            pl.BlockSpec((2, query_rows, count), lambda pair: (pair, 0, 0)),
        ]
        + [anywhere] * len(earlier),
        out_specs=(
            pl.BlockSpec((3, rows, 2 * 64), lambda pair: (0, 0, pair)),
            pl.BlockSpec((1, 2, 4 * count), lambda pair: (pair, 0, 0)),
        ),
        scratch_shapes=[
            pltpu.VMEM((2 * length, length), jnp.float32),
            pltpu.VMEM((2 * length, length), jnp.bfloat16),
            pltpu.VMEM((2 * length, length), jnp.bfloat16),
        ],
        compiler_params=pltpu.CompilerParams(vmem_limit_bytes=40 * 2**20),
        cost_estimate=pl.CostEstimate(
            flops=2 * 2 * pairs * (docs * length * length + query_rows * count) * 128 * 4,
            bytes_accessed=rows * width * 14 + 8 * pairs * docs * length * length,
            transcendentals=0,
        ),
        name="attend_back",
    )(projected, projected, projected, grad_mixed, doc_probs, query_probs, *earlier)


def dot_tn(left, right):
    return lax.dot_general(
        left, right, (((0,), (0,)), ((), ())), preferred_element_type=jnp.float32
    )


tile = 512
row_parts = 2
gate_parts = 4
curve = 0.044715
slope = 0.7978845608028654


def turned_rows(place_ref, values, turned):
    quarter = values.shape[1] // 4
    flipped = values[...].T
    for outer in range(2):
        for core in range(2):
            kept = core ^ 1 ^ place_ref[1]
            start = pl.multiple_of((2 * kept + outer) * quarter, 16)
            block = flipped[(2 * outer + core) * quarter : (2 * outer + core + 1) * quarter, :]
            turned[pl.ds(start, quarter), :] = block


def split_store(values, kept_ref, sent_ref):
    quarter = values.shape[0] // 4
    low = values.astype(jnp.bfloat16)
    for outer in range(2):
        sent_ref[outer] = low[outer * quarter : (outer + 1) * quarter, :]
        kept_ref[outer] = low[(2 + outer) * quarter : (3 + outer) * quarter, :]


def gate_kernel(place_ref, n2_ref, weight, cot_ref, act_ref, by_gate_ref, by_up_ref, kept_ref, sent_ref):
    rows, width = n2_ref.shape
    hidden = weight.shape[2] // 2
    start = pl.multiple_of(pl.program_id(0) * tile, 128)
    gate_weight = weight[:, :, pl.ds(start, tile)].reshape(width, tile)
    up_weight = weight[:, :, pl.ds(hidden + start, tile)].reshape(width, tile)
    part = rows // gate_parts
    for start in range(0, rows, part):
        places = slice(start, start + part)
        gate = dot_nn(n2_ref[places, :], gate_weight)
        up = dot_nn(n2_ref[places, :], up_weight)
        square = gate * gate
        turned = jnp.tanh(slope * gate * (1.0 + curve * square))
        halved = 0.5 * (1.0 + turned)
        value = gate * halved
        steep = halved + 0.5 * gate * (1.0 - turned * turned) * slope * (1.0 + 3.0 * curve * square)
        act_ref[places, :] = (value * up).astype(jnp.bfloat16)
        by_gate_ref[places, :] = up * steep
        by_up_ref[places, :] = value
    grad = dot_tn(act_ref[...], cot_ref[...]).astype(jnp.bfloat16)
    core = pl.program_id(0) % 2

    @pl.when(core == place_ref[1])
    def _():
        kept_ref[0] = grad

    @pl.when(core != place_ref[1])
    def _():
        sent_ref[0] = grad


def gate_forward(place, pieces, normed_two, cot_low):
    rows, width = normed_two.shape
    columns = pieces[0].shape[-1]
    hidden = columns // 2
    number = len(pieces)
    whole = pl.BlockSpec((rows, width), lambda step: (0, 0))
    column = pl.BlockSpec((rows, tile), lambda step: (0, step))
    half = pl.BlockSpec((1, tile, width), lambda step: (step // 2, 0, 0))
    assert hidden == 4 * tile

    def kernel(place_ref, *refs):
        n2_ref, cot_ref, *outs, full_ref, held, sems = refs[number:]
        filled(
            place_ref, refs[:number], full_ref, held, sems,
            lambda: gate_kernel(place_ref, n2_ref, held, cot_ref, *outs),
        )

    *results, full = pl.pallas_call(
        kernel,
        grid=(hidden // tile,),
        out_shape=(
            jax.ShapeDtypeStruct((rows, hidden), jnp.bfloat16),
            jax.ShapeDtypeStruct((rows, hidden), jnp.float32),
            jax.ShapeDtypeStruct((rows, hidden), jnp.float32),
            jax.ShapeDtypeStruct((2, tile, width), jnp.bfloat16),
            jax.ShapeDtypeStruct((2, tile, width), jnp.bfloat16),
            jax.ShapeDtypeStruct((32, width // 32, columns), jnp.bfloat16),
        ),
        in_specs=[scalars()] + [anywhere] * number + [whole, whole],
        out_specs=(column, column, column, half, half, anywhere),
        scratch_shapes=[
            pltpu.VMEM((32, width // 32, columns), jnp.bfloat16),
            pltpu.SemaphoreType.DMA((33,)),
        ],
        compiler_params=pltpu.CompilerParams(vmem_limit_bytes=48 * 2**20),
        cost_estimate=pl.CostEstimate(
            flops=6 * rows * width * hidden,
            bytes_accessed=rows * hidden * 10 + 8 * width * hidden,
            transcendentals=rows * hidden,
        ),
        name="gate_forward",
    )(place, *pieces, normed_two, cot_low)
    return (*results, full.reshape(width, columns))


def gate_back_kernel(
    place_ref, n2_ref, cot_ref, ff, by_gate_ref, by_up_ref, out_ref, kept_ref, sent_ref, turned
):
    step = pl.program_id(0)

    @pl.when(step == 0)
    def _():
        turned_rows(place_ref, n2_ref, turned)

    per = tile // ff.shape[1]
    weight = ff[pl.ds(step * per, per)].reshape(tile, ff.shape[2])
    incoming = dot_nt(cot_ref[...], weight)
    by_gate = (incoming * by_gate_ref[...]).astype(jnp.bfloat16)
    by_up = (incoming * by_up_ref[...]).astype(jnp.bfloat16)
    out_ref[0] = by_gate
    out_ref[1] = by_up
    split_store(dot_nn(turned[...], by_gate), kept_ref.at[:, :, :tile], sent_ref.at[:, :, :tile])
    split_store(dot_nn(turned[...], by_up), kept_ref.at[:, :, tile:], sent_ref.at[:, :, tile:])


def gate_back(place, pieces, normed_two, cot_low, by_gate, by_up):
    rows, width = normed_two.shape
    hidden = by_gate.shape[1]
    number = len(pieces)
    whole = pl.BlockSpec((rows, width), lambda step: (0, 0))
    column = pl.BlockSpec((rows, tile), lambda step: (0, step))
    half = pl.BlockSpec((2, width // 4, 2 * tile), lambda step: (0, 0, step))

    def kernel(place_ref, *refs):
        n2_ref, cot_ref, gate_ref, up_ref, *outs, full_ref, held, turned, sems = refs[number:]
        filled(
            place_ref, refs[:number], full_ref, held, sems,
            lambda: gate_back_kernel(
                place_ref, n2_ref, cot_ref, held, gate_ref, up_ref, *outs, turned
            ),
        )

    *results, full = pl.pallas_call(
        kernel,
        grid=(hidden // tile,),
        out_shape=(
            jax.ShapeDtypeStruct((2, rows, hidden), jnp.bfloat16),
            jax.ShapeDtypeStruct((2, width // 4, 2 * hidden), jnp.bfloat16),
            jax.ShapeDtypeStruct((2, width // 4, 2 * hidden), jnp.bfloat16),
            jax.ShapeDtypeStruct((32, hidden // 32, width), jnp.bfloat16),
        ),
        in_specs=[scalars()] + [anywhere] * number + [whole, whole, column, column],
        out_specs=(
            pl.BlockSpec((2, rows, tile), lambda step: (0, 0, step)),
            half,
            half,
            anywhere,
        ),
        scratch_shapes=[
            pltpu.VMEM((32, hidden // 32, width), jnp.bfloat16),
            pltpu.VMEM((width, rows), jnp.bfloat16),
            pltpu.SemaphoreType.DMA((33,)),
        ],
        compiler_params=pltpu.CompilerParams(vmem_limit_bytes=48 * 2**20),
        cost_estimate=pl.CostEstimate(
            flops=6 * rows * width * hidden,
            bytes_accessed=rows * hidden * 12 + 8 * width * hidden,
            transcendentals=0,
        ),
        name="gate_back",
    )(place, *pieces, normed_two, cot_low, by_gate, by_up)
    return (*results, full.reshape(hidden, width))


def norm_back(grads, values, gain, residual):
    spread = lax.rsqrt(jnp.mean(values * values, axis=-1, keepdims=True) + epsilon)
    scaled = grads * gain
    inner = jnp.mean(scaled * values, axis=-1, keepdims=True)
    gain_grad = jnp.sum(grads * (values * spread), axis=0, keepdims=True)
    return residual + spread * scaled - values * (spread * spread * spread * inner), gain_grad


def middle_back_kernel(
    gates_ref, weight_ref, middle_ref, cot_ref, gain_ref, out_weight_ref,
    grad_ref, low_ref, mixed_ref, gain_grad_ref,
):
    hidden = gates_ref.shape[2]
    total = dot_nt(gates_ref[0], weight_ref[:, :hidden])
    total = total + dot_nt(gates_ref[1], weight_ref[:, hidden:])
    grad, gain_grad = norm_back(total, middle_ref[...], gain_ref[...], cot_ref[...])
    grad_ref[...] = grad
    low_ref[...] = grad.astype(jnp.bfloat16)

    @pl.when(pl.program_id(0) == 0)
    def _():
        gain_grad_ref[...] = gain_grad

    @pl.when(pl.program_id(0) > 0)
    def _():
        gain_grad_ref[...] += gain_grad

    mixed_ref[...] = dot_nt(low_ref[...], out_weight_ref[...]).astype(jnp.bfloat16)


def middle_back(gates, full_in, middle, cotangent, gain, full_attention, *earlier):
    rows, width = middle.shape
    hidden = gates.shape[2]
    part = rows // row_parts
    block = pl.BlockSpec((part, width), lambda step: (step, 0))

    def kernel(*refs):
        middle_back_kernel(*refs[:6], *refs[6 + len(earlier) :])

    return pl.pallas_call(
        kernel,
        grid=(row_parts,),
        out_shape=(
            jax.ShapeDtypeStruct((rows, width), jnp.float32),
            jax.ShapeDtypeStruct((rows, width), jnp.bfloat16),
            jax.ShapeDtypeStruct((rows, width), jnp.bfloat16),
            jax.ShapeDtypeStruct((1, width), jnp.float32),
        ),
        in_specs=[
            pl.BlockSpec((2, part, hidden), lambda step: (0, step, 0)),
            pl.BlockSpec((width, 2 * hidden), lambda step: (0, 0)),
            block,
            block,
            pl.BlockSpec((1, width), lambda step: (0, 0)),
            pl.BlockSpec((width, width), lambda step: (0, 3)),
        ]
        + [anywhere] * len(earlier),
        out_specs=(block, block, block, pl.BlockSpec((1, width), lambda step: (0, 0))),
        compiler_params=pltpu.CompilerParams(vmem_limit_bytes=56 * 2**20),
        cost_estimate=pl.CostEstimate(
            flops=4 * rows * width * hidden + 2 * rows * width * width,
            bytes_accessed=rows * hidden * 4 + 4 * width * hidden + 18 * rows * width,
            transcendentals=0,
        ),
        name="middle_back",
    )(gates, full_in, middle, cotangent, gain.reshape(1, -1), full_attention, *earlier)


def scalars():
    return pl.BlockSpec(memory_space=pltpu.SMEM)


def project(place, pieces, normed):
    rows, width = normed.shape
    columns = pieces[0].shape[-1]
    number = len(pieces)

    def kernel(place_ref, *refs):
        normed_ref, out_ref, full_ref, held, sems = refs[number:]

        def body():
            start = pl.multiple_of(pl.program_id(0) * width, 128)
            weight = held[:, :, pl.ds(start, width)].reshape(width, width)
            out_ref[...] = dot_nn(normed_ref[...], weight).astype(jnp.bfloat16)

        filled(place_ref, refs[:number], full_ref, held, sems, body)

    projected, full = pl.pallas_call(
        kernel,
        grid=(3,),
        out_shape=(
            jax.ShapeDtypeStruct((rows, 3 * width), jnp.bfloat16),
            jax.ShapeDtypeStruct((32, width // 32, columns), jnp.bfloat16),
        ),
        in_specs=[scalars()]
        + [anywhere] * number
        + [pl.BlockSpec((rows, width), lambda step: (0, 0))],
        out_specs=(pl.BlockSpec((rows, width), lambda step: (0, step)), anywhere),
        scratch_shapes=[
            pltpu.VMEM((32, width // 32, columns), jnp.bfloat16),
            pltpu.SemaphoreType.DMA((33,)),
        ],
        compiler_params=pltpu.CompilerParams(vmem_limit_bytes=32 * 2**20),
        cost_estimate=pl.CostEstimate(
            flops=6 * rows * width * width,
            bytes_accessed=8 * rows * width + 4 * columns * width,
            transcendentals=0,
        ),
        name="project",
    )(place, *pieces, normed)
    return projected, full.reshape(width, columns)


def middle_kernel(rows_ref, mixed_ref, weight_ref, gain_ref, middle_ref, normed_ref):
    middle = rows_ref[...] + dot_nn(mixed_ref[...], weight_ref[...])
    spread = lax.rsqrt(jnp.mean(middle * middle, axis=-1, keepdims=True) + epsilon)
    middle_ref[...] = middle
    normed_ref[...] = (middle * spread * gain_ref[...]).astype(jnp.bfloat16)


def middle_forward(values, mixed, full_attention, gain, *earlier):
    rows, width = values.shape
    part = rows // 2
    block = pl.BlockSpec((part, width), lambda step: (step, 0))

    def kernel(*refs):
        middle_kernel(*refs[:4], *refs[4 + len(earlier) :])

    return pl.pallas_call(
        kernel,
        grid=(2,),
        out_shape=(
            jax.ShapeDtypeStruct((rows, width), jnp.float32),
            jax.ShapeDtypeStruct((rows, width), jnp.bfloat16),
        ),
        in_specs=[
            block,
            block,
            pl.BlockSpec((width, width), lambda step: (0, 3)),
            pl.BlockSpec((1, width), lambda step: (0, 0)),
        ]
        + [anywhere] * len(earlier),
        out_specs=(block, block),
        compiler_params=pltpu.CompilerParams(vmem_limit_bytes=32 * 2**20),
        cost_estimate=pl.CostEstimate(
            flops=2 * rows * width * width,
            bytes_accessed=12 * rows * width + 2 * width * width,
            transcendentals=0,
        ),
        name="middle_forward",
    )(values, mixed, full_attention, gain.reshape(1, -1), *earlier)


def attention_grads_kernel(
    place_ref, normed_ref, grads_ref, mixed_ref, low_ref, kept_ref, sent_ref, turned
):
    step = pl.program_id(0)
    last = pl.num_programs(0) - 1

    @pl.when(step == 0)
    def _():
        turned_rows(place_ref, normed_ref, turned)

    @pl.when(step < last)
    def _():
        split_store(dot_nn(turned[...], grads_ref[0]), kept_ref, sent_ref)

    @pl.when(step == last)
    def _():
        turned_rows(place_ref, mixed_ref, turned)
        split_store(dot_nn(turned[...], low_ref[...]), kept_ref, sent_ref)


def attention_grads(place, normed, grad_projected, mixed, grad_low):
    rows, width = normed.shape
    whole = pl.BlockSpec((rows, width), lambda step: (0, 0))
    half = pl.BlockSpec((2, width // 4, width), lambda step: (0, 0, step))
    shape = jax.ShapeDtypeStruct((2, width // 4, 4 * width), jnp.bfloat16)
    return pl.pallas_call(
        attention_grads_kernel,
        grid=(4,),
        out_shape=(shape, shape),
        in_specs=[
            scalars(),
            whole,
            pl.BlockSpec((1, rows, width), lambda step: (jnp.minimum(step, 2), 0, 0)),
            whole,
            whole,
        ],
        out_specs=(half, half),
        scratch_shapes=[pltpu.VMEM((width, rows), jnp.bfloat16)],
        compiler_params=pltpu.CompilerParams(vmem_limit_bytes=32 * 2**20),
        cost_estimate=pl.CostEstimate(
            flops=8 * rows * width * width,
            bytes_accessed=12 * rows * width + 8 * width * width,
            transcendentals=0,
        ),
        name="attention_grads",
    )(place, normed, grad_projected, mixed, grad_low)


def input_back_kernel(grads_ref, weight_ref, rows_ref, residual_ref, gain_ref, out_ref, gain_grad_ref):
    width = rows_ref.shape[1]
    total = dot_nt(grads_ref[0], weight_ref[:, :width])
    for part in (1, 2):
        total = total + dot_nt(grads_ref[part], weight_ref[:, part * width : (part + 1) * width])
    grad, gain_grad = norm_back(total, rows_ref[...], gain_ref[...], residual_ref[...])
    out_ref[...] = grad

    @pl.when(pl.program_id(0) == 0)
    def _():
        gain_grad_ref[...] = gain_grad

    @pl.when(pl.program_id(0) > 0)
    def _():
        gain_grad_ref[...] += gain_grad


def input_back(grad_projected, full_attention, values, residual, gain, *earlier):
    rows, width = values.shape
    part = rows // 2
    block = pl.BlockSpec((part, width), lambda step: (step, 0))

    def kernel(*refs):
        input_back_kernel(*refs[:5], *refs[5 + len(earlier) :])

    return pl.pallas_call(
        kernel,
        grid=(2,),
        out_shape=(
            jax.ShapeDtypeStruct((rows, width), jnp.float32),
            jax.ShapeDtypeStruct((1, width), jnp.float32),
        ),
        in_specs=[
            pl.BlockSpec((3, part, width), lambda step: (0, step, 0)),
            pl.BlockSpec((width, 3 * width), lambda step: (0, 0)),
            block,
            block,
            pl.BlockSpec((1, width), lambda step: (0, 0)),
        ]
        + [anywhere] * len(earlier),
        out_specs=(block, pl.BlockSpec((1, width), lambda step: (0, 0))),
        compiler_params=pltpu.CompilerParams(vmem_limit_bytes=40 * 2**20),
        cost_estimate=pl.CostEstimate(
            flops=6 * rows * width * width,
            bytes_accessed=18 * rows * width + 6 * width * width,
            transcendentals=0,
        ),
        name="input_back",
    )(grad_projected, full_attention, values, residual, gain.reshape(1, -1), *earlier)


def body(
    doc_inputs,
    query_inputs,
    doc_mask,
    query_lengths,
    doc_cotangent,
    query_cotangent,
    qkv_weight,
    out_weight,
    in_weight,
    ff_weight,
    attn_gain,
    ffn_gain,
    bias_table,
):
    doc_count, doc_length, model_width = doc_inputs.shape
    group_count, group_length = (query_inputs.shape[0], query_inputs.shape[1])
    head_count = bias_table.shape[1]
    doc_rows = doc_count * doc_length
    low = jnp.bfloat16
    routed = hand_routed()
    place = own_place() if routed else (0, 0, 0, 0)
    place_vector = jnp.stack([jnp.asarray(index, jnp.int32) for index in place])

    attention_shard = jnp.concatenate([qkv_weight, out_weight], axis=1).astype(low)
    in_shard = in_weight.astype(low)
    ff_shard = ff_weight.astype(low)

    values = jnp.concatenate(
        [doc_inputs.reshape(doc_rows, model_width), query_inputs.reshape(-1, model_width)], axis=0
    )
    cotangent = jnp.concatenate(
        [doc_cotangent.reshape(doc_rows, model_width), query_cotangent.reshape(-1, model_width)],
        axis=0,
    )
    cot_low = cotangent.astype(low)
    spread = lax.rsqrt(jnp.mean(values * values, axis=-1, keepdims=True) + epsilon)
    normed = (values * spread * attn_gain).astype(low)
    places = jnp.arange(group_length, dtype=jnp.int32)
    query_mask = places[None, :] < query_lengths[:, None]
    onehot = lines_onehot(bias_table.shape[0])
    lines = jnp.einsum("pn,nh->hp", onehot, bias_table, precision=highest)
    lines = lines.reshape(head_count // 2, 2, 4 * count)
    doc_masking = jnp.where(doc_mask > 0, 0.0, -1e9).astype(jnp.float32)
    query_masking = jnp.where(query_mask, 0.0, -1e9).astype(jnp.float32)
    query_masking = query_masking.reshape(-1, 1, count)

    if routed:
        column_a = gather_column(attention_shard)
        column_a, normed, lines, doc_masking, query_masking, cotangent, cot_low, in_shard = together(
            column_a, normed, lines, doc_masking, query_masking, cotangent, cot_low, in_shard
        )
        near_a = gather_near(place, *gather_plane(place, attention_shard, column_a))
        column_i = gather_column(in_shard)
        core_a = gather_core(*near_a)
        far_a = gather_far(*near_a)
        column_i, far_a, core_a, ff_shard = together(column_i, far_a, core_a, ff_shard)
        pieces = gather_order(near_a, far_a, core_a, gather_core(*far_a))
        plane_i = gather_plane(place, in_shard, column_i)
    else:
        pieces = (split_rows(lax.all_gather(attention_shard, both, axis=0, tiled=True)),)
    projected, full_attention = project(place_vector, pieces, normed)
    if routed:
        plane_i, projected, ff_shard = together(plane_i, projected, ff_shard)
        near_i = gather_near(place, *plane_i)
        far_i = gather_far(*near_i)
        column_f = gather_column(ff_shard)
        core_i = gather_core(*near_i)
    mixed, doc_probs, query_probs = attend(
        projected, lines, doc_masking, query_masking, group_length
    )
    if routed:
        mixed, far_i, column_f = together(mixed, far_i, column_f)
        plane_f = gather_plane(place, ff_shard, column_f)
        pieces = gather_order(near_i, far_i, core_i, gather_core(*far_i))
    else:
        pieces = (split_rows(lax.all_gather(in_shard, both, axis=0, tiled=True)),)
    middle, normed_two = middle_forward(values, mixed, full_attention, ffn_gain)
    if routed:
        pieces, normed_two, plane_f = together(pieces, normed_two, plane_f)
        near_f = gather_near(place, *plane_f)
        far_f = gather_far(*near_f)
    activated, by_gate, by_up, kept, sent, full_in = gate_forward(
        place_vector, pieces, normed_two, cot_low
    )
    if routed:
        far_f, by_gate, kept, sent = together(far_f, by_gate, kept, sent)
        pieces = gather_order(near_f, far_f, gather_core(*near_f), gather_core(*far_f))
        ff_grads = Scatter(kept, sent, place)
        got_f = ff_grads.core()
    else:
        pieces = (split_rows(lax.all_gather(ff_shard, both, axis=0, tiled=True)),)
        grad_ff = joined_halves(kept, sent)
    gates, kept, sent, full_ff = gate_back(
        place_vector, pieces, normed_two, cot_low, by_gate, by_up
    )
    if routed:
        gates, kept, sent, got_f = together(gates, kept, sent, got_f)
        in_grads = Scatter(kept, sent, place)
        near_f = ff_grads.plane(got_f)
        got_i = in_grads.core()
    else:
        grad_in = joined_halves(kept, sent)
    grad_middle, grad_middle_low, grad_mixed, grad_ffn_gain = middle_back(
        gates, full_in, middle, cotangent, ffn_gain, full_attention
    )
    if routed:
        grad_mixed, near_f, got_i = together(grad_mixed, near_f, got_i)
        far_f = ff_grads.far(got_f, near_f)
        near_i = in_grads.plane(got_i)
    grad_projected, grad_lines = attend_back(
        projected, grad_mixed, doc_probs, query_probs, doc_length
    )
    if routed:
        grad_projected, grad_lines, far_f, near_i = together(
            grad_projected, grad_lines, far_f, near_i
        )
        far_i = in_grads.far(got_i, near_i)
        shares_f = ff_grads.column(got_f, near_f, far_f)
    kept, sent = attention_grads(place_vector, normed, grad_projected, mixed, grad_middle_low)
    if routed:
        kept, sent, far_i = together(kept, sent, far_i)
        attention = Scatter(kept, sent, place)
        got_a = attention.core()
        got_a, shares_f, grad_projected, grad_lines = together(
            got_a, shares_f, grad_projected, grad_lines
        )
        near_a = attention.plane(got_a)
        shares_i = in_grads.column(got_i, near_i, far_i)
    grad_inputs, grad_attn_gain = input_back(
        grad_projected, full_attention, values, grad_middle, attn_gain
    )
    grad_table = jnp.einsum(
        "pn,hp->nh", onehot, grad_lines.reshape(head_count, 4 * count), precision=highest
    )
    small = jnp.concatenate([grad_attn_gain[0], grad_ffn_gain[0], grad_table.reshape(-1)])
    if routed:
        near_a, small, activated = together(near_a, small, activated)
        far_a = attention.far(got_a, near_a)
        small = add_flipped(small, {"dc": 1}, {"dz": 1})
    outputs = middle + dot_nn(activated, full_ff)
    if routed:
        far_a, small, outputs, shares_i = together(far_a, small, outputs, shares_i)
        shares_a = attention.column(got_a, near_a, far_a)
        small = add_flipped(small, {"dx": 1}, {"dy": 1}, {"dz": 2})
        ff_grad_shard = summed(*shares_f)
        in_grad_shard = summed(*shares_i)
        attention_grad_shard = summed(*shares_a)
    else:
        scatter = functools.partial(
            lax.psum_scatter, axis_name=both, scatter_dimension=0, tiled=True
        )
        ff_grad_shard = scatter(grad_ff)
        in_grad_shard = scatter(grad_in)
        attention_grad_shard = scatter(joined_halves(kept, sent))
        small = lax.psum(small, both)
    in_grad_shard = in_grad_shard.reshape(in_weight.shape[0], -1, 2, tile)
    in_grad_shard = jnp.swapaxes(in_grad_shard, 1, 2).reshape(in_weight.shape)
    return (
        outputs[:doc_rows].reshape(doc_inputs.shape),
        outputs[doc_rows:].reshape(query_inputs.shape),
        grad_inputs[:doc_rows].reshape(doc_inputs.shape),
        grad_inputs[doc_rows:].reshape(query_inputs.shape),
        attention_grad_shard[:, : 3 * model_width],
        attention_grad_shard[:, 3 * model_width :],
        in_grad_shard,
        ff_grad_shard,
        small[:model_width],
        small[model_width : 2 * model_width],
        small[2 * model_width :].reshape(bias_table.shape),
    )


def solution(mesh):
    placed = (
        P(("dp", "fsdp"), None, None),
        P(("dp", "fsdp"), None, None),
        P(("dp", "fsdp"), None),
        P(("dp", "fsdp")),
        P(("dp", "fsdp"), None, None),
        P(("dp", "fsdp"), None, None),
        P(("dp", "fsdp"), None),
        P(("dp", "fsdp"), None),
        P(("dp", "fsdp"), None),
        P(("dp", "fsdp"), None),
        P(),
        P(),
        P(),
    )
    return jax.shard_map(
        body,
        mesh=mesh,
        in_specs=placed,
        out_specs=(
            P(("dp", "fsdp"), None, None),
            P(("dp", "fsdp"), None, None),
            P(("dp", "fsdp"), None, None),
            P(("dp", "fsdp"), None, None),
            P(("dp", "fsdp"), None),
            P(("dp", "fsdp"), None),
            P(("dp", "fsdp"), None),
            P(("dp", "fsdp"), None),
            P(),
            P(),
            P(),
        ),
        check_vma=False,
    )
```

time: 822 us -> 316 us (0.38)
  waiting for transfers between devices: 511 us -> 54.1 us
  matrix products: 167 us -> 5.76 us
  Pallas kernels: 0 us -> 115 us
  starting transfers between devices: 0.33 us -> 65.3 us
  blocking collectives: 38.3 us -> 0 us
  local copies, waits for them, and re-layouts: 60.4 us -> 33.9 us
  between operations: 15 us -> 2.45 us
  other arithmetic: 25.9 us -> 36 us
    reduce_scatter x4 -> x0, waiting for transfers between devices: 349 us -> none  [the longest x1 163 us: body(): lax.psum_scatter(grad_in, ('dp', 'fsdp'), scatter_dimension=0, tiled=True)]
    all_gather x4 -> x0, waiting for transfers between devices: 162 us -> none  [the longest x1 66.9 us: body(): lax.all_gather(shards[2], ('dp', 'fsdp'), axis=0, tiled=True)]
    dot_general x28 -> x3, matrix products: 167 us -> 5.76 us  [the longest x1 5.08 us: dot_nn(): return jnp.dot(left, right, preferred_element_type=jnp.float32)]
    pallas_call x0 -> x9, Pallas kernels: none -> 115 us  [the longest x1 22.2 us: gate_forward(): pl.pallas_call(kernel, grid=(hidden // tile,), out_shape=(jax.ShapeDtypeS...]
    ppermute x0 -> x62, starting transfers between devices: none -> 65.3 us  [swap(): return lax.ppermute(values, both, flip_pairs(**flips))]
    ppermute x0 -> x62, waiting for transfers between devices: none -> 54.1 us  [swap(): return lax.ppermute(values, both, flip_pairs(**flips))]
    psum x1 -> x0, blocking collectives: 38.3 us -> none  [body(): lax.psum((grad_attn_gain, grad_ffn_gain, doc_table + query_table), ('dp',...]
    convert_element_type x3 -> x0, local copies, waits for them, and re-layouts: 12.3 us -> none  [the longest x2 10.6 us: attend_backward(): return (stacked.astype(jnp.bfloat16), grad_table)]
  transfers between devices with their start and end apart: 8 -> 62, of which waited for: 7 -> 20; matrix products, arithmetic and copies ran while one was open for 24% -> 17% of each run, Pallas kernels for 0% -> 37%
where the time goes in v2:
time: 316 us; the launch traced here: 312 us
  Pallas kernels  115 us (36%)
  starting transfers between devices  65.3 us (21%)
  waiting for transfers between devices  54.1 us (17%)
  other arithmetic  36 us (11%)
  local copies, waits for them, and re-layouts  33.9 us (11%)
  matrix products  5.76 us (2%)
    ppermute x62, starting transfers between devices, swap(): return lax.ppermute(values, both, flip_pairs(**flips))  65.3 us
    ppermute x62, waiting for transfers between devices, swap(): return lax.ppermute(values, both, flip_pairs(**flips))  54.1 us
    pallas_call x1, Pallas kernels, gate_forward(): pl.pallas_call(kernel, grid=(hidden // tile,), out_shape=(jax.ShapeDtypeS...  22.2 us
    pallas_call x1, Pallas kernels, gate_back(): pl.pallas_call(kernel, grid=(hidden // tile,), out_shape=(jax.ShapeDtypeS...  19.6 us
    pallas_call x1, Pallas kernels, attend_back(): pl.pallas_call(kernel, grid=(pairs,), out_shape=(jax.ShapeDtypeStruct((3,...  18.1 us
    pallas_call x1, Pallas kernels, middle_back(): pl.pallas_call(kernel, grid=(row_parts,), out_shape=(jax.ShapeDtypeStruct...  17.5 us
    pallas_call x1, Pallas kernels, attend(): pl.pallas_call(functools.partial(attend_kernel, docs, length, group), gri...  13.5 us
    unnamed x131, local copies, waits for them, and re-layouts  12.2 us
  transfers between devices with their start and end apart: 62, of which 20 were waited for; matrix products, arithmetic and copies ran while one was open for 17% of the time, Pallas kernels for 37%

profile of v2, /device:TPU:0, one launch (start us, length us, event | category | flops | bytes accessed | tf_op | source)
XLA Modules:
  0.0 312.3 jit_solution(3440009120481271719)
XLA Ops:
  2.5 3.1 collective-permute-start
  5.6 2.6 collective-permute-start.1
  8.3 2.2 pad_maximum_fusion
  11.2 5.1 %pad_maximum_fusion.1 = (f32[896,768]{1,0:T(8,128)}, bf16[896,768]{1,0:T(8,128)(2,1)}) fusion(f32[384,768]{1,0:T(8,128)} %bitcast.249, f32[512,768]{1,0:T(8,128)} %bitcast.245, f32[768]{0:T(1024)S(1)} %copy-done.56, f32[896]{0:T(1024)S(1)} %add_rsqrt_fusion, f32[384,768]{1,0:T(8,128)} %bitcast.248, f32[512,768]{1,0:T(8,128)} %bitcast.244), kind=kLoop, calls=%fused_computation.1 | loop fusion | flops 3440640 | bytes 9640448 | tf_op jit(solution)/shard_map/concatenate | solution.py:957
  17.1 3.0 fusion.64.refs_9_
  21.1 1.8 collective-permute-start.8
  23.9 1.6 collective-permute-start.6
  25.5 1.7 collective-permute-start.3
  27.2 2.2 collective-permute-done.8
  29.6 1.6 collective-permute-start.9
  33.8 2.6 collective-permute-start.4
  36.3 9.7 %collective-permute-done.4 = bf16[24,4096]{1,0:T(8,128)(2,1)} collective-permute-done((bf16[24,4096]{1,0:T(8,128)(2,1)}, bf16[24,4096]{1,0:T(8,128)(2,1)}, u32[]{:S(2)}, u32[]{:S(2)}) %collective-permute-start.4) | collective-permute-done | bytes 196640 | tf_op jit(solution)/shard_map/ppermute | solution.py:33
  46.1 3.5 %collective-permute-start.5 = (bf16[24,4096]{1,0:T(8,128)(2,1)}, bf16[24,4096]{1,0:T(8,128)(2,1)}, u32[]{:S(2)}, u32[]{:S(2)}) collective-permute-start(bf16[24,4096]{1,0:T(8,128)(2,1)} %convert_element_type.456), channel_id=1, source_target_pairs={{0,6},{1,7},{2,4},{3,5},{4,2},{5,3},{6,0},{7,1},{8,14},{9,15},{10,... | collective-permute-start | bytes 589832 | tf_op jit(solution)/shard_map/ppermute | solution.py:33
  50.5 4.6 %collective-permute-done.5 = bf16[24,4096]{1,0:T(8,128)(2,1)} collective-permute-done((bf16[24,4096]{1,0:T(8,128)(2,1)}, bf16[24,4096]{1,0:T(8,128)(2,1)}, u32[]{:S(2)}, u32[]{:S(2)}) %collective-permute-start.5) | collective-permute-done | bytes 196640 | tf_op jit(solution)/shard_map/ppermute | solution.py:33
  59.0 1.6 collective-permute-start.12
  60.7 7.8 %project.1 = (bf16[896,2304]{1,0:T(8,128)(2,1)S(1)}, bf16[32,24,3072]{2,1,0:T(8,128)(2,1)S(1)}) custom-call(s32[4]{0:T(128)S(1)} %pad_add_fusion.place_ref, bf16[4,24,3072]{2,1,0:T(8,128)(2,1)} %bitcast.13.refs_0_, bf16[4,24,3072]{2,1,0:T(8,128)(2,1)} %collective-permute-done.7.refs_1_, bf16[4,24,3072]{2,1,0:T(8,128)(2,1)S(1)} %bitcast.236, ...), custom_call_target="tpu_custom_call" | custom-call | flops 3170893824 | bytes 14942208 | tf_op jit(solution)/shard_map/project/pallas_call | solution.py:761
  68.4 1.4 collective-permute-done.12
  70.0 1.6 collective-permute-start.17
  72.4 3.0 collective-permute-start.18
  76.5 1.3 collective-permute-start.20
  77.8 1.7 collective-permute-done.18
  79.5 13.5 %attend.1 = (bf16[896,768]{1,0:T(8,128)(2,1)S(1)}, f32[12,512,512]{2,1,0:T(8,128)}, f32[12,384,128]{2,1,0:T(8,128)S(1)}) custom-call(bf16[896,2304]{1,0:T(8,128)(2,1)S(1)} %get-tuple-element.137.q_ref.k_ref.v_ref.refs_0_.refs_1_.refs_2_, bf16[896,2304]{1,0:T(8,128)(2,1)S(1)} %get-tuple-element.137.q_ref.k_ref.v_ref.refs_0_.refs_1_.refs_2_, ...), custom_call_target="tpu_custom_call" | custom-call | flops 1912602624 | bytes 18087936 | tf_op jit(solution)/shard_map/attend/pallas_call | solution.py:337
  94.2 1.6 collective-permute-start.26
  96.5 1.9 middle_forward.1
  98.4 1.5 copy-done.17
  101.2 1.4 collective-permute-done.25
  105.9 22.2 %gate_forward.1 = (bf16[896,2048]{1,0:T(8,128)(2,1)}, f32[896,2048]{1,0:T(8,128)}, f32[896,2048]{1,0:T(8,128)}, bf16[2,512,768]{2,1,0:T(8,128)(2,1)}, bf16[2,512...) custom-call(s32[4]{0:T(128)S(1)} %pad_add_fusion.place_ref, bf16[4,24,4096]{2,1,0:T(8,128)(2,1)S(1)} %bitcast.233, ...), custom_call_target="tpu_custom_call" | custom-call | flops 8455716864 | bytes 30932992 | tf_op jit(solution)/shard_map/gate_forward/pallas_call | solution.py:577
  129.2 2.5 collective-permute-done.31.refs_6_
  133.8 19.6 %gate_back.1 = (bf16[2,896,2048]{2,1,0:T(8,128)(2,1)}, bf16[2,192,4096]{2,1,0:T(8,128)(2,1)}, bf16[2,192,4096]{2,1,0:T(8,128)(2,1)}, bf16[32,64,768]{2,1,0:T(8,128)(2,1)}) custom-call(s32[4]{0:T(128)S(1)} %pad_add_fusion.place_ref, bf16[4,64,768]{2,1,0:T(8,128)(2,1)S(1)} %bitcast.242, bf16[4,64,768]{2,1,0:T(8,128)(2,1)S(1)} %collective-permute-done.27.refs_1_, ...), custom_call_target="tpu_custom_call" | custom-call | flops 8455716864 | bytes 34603008 | tf_op jit(solution)/shard_map/gate_back/pallas_call | solution.py:642
  153.6 1.5 fusion.69
  155.1 2.1 fusion.68
  158.7 1.3 collective-permute-start.34
  160.3 17.5 %middle_back.1 = (f32[896,768]{1,0:T(8,128)}, bf16[896,768]{1,0:T(8,128)(2,1)}, bf16[896,768]{1,0:T(8,128)(2,1)}, f32[1,768]{1,0:T(1,128)}) custom-call(bf16[2,896,2048]{2,1,0:T(8,128)(2,1)} %get-tuple-element.180.refs_0_, bf16[768,4096]{1,0:T(8,128)(2,1)} %bitcast.257, f32[896,768]{1,0:T(8,128)} %copy-done.17, f32[896,768]{1,0:T(8,128)} %get-tuple-element.183.refs_3_, ...), custom_call_target="tpu_custom_call" | custom-call | flops 6694109184 | bytes 26017792 | tf_op jit(solution)/shard_map/middle_back/pallas_call | solution.py:713
  177.8 1.8 slice.104
  179.7 2.8 copy.50
  187.8 1.3 fusion.25
  191.2 1.4 collective-permute-start.37
  192.6 2.2 copy-done.3
  194.8 1.7 copy-done.9
  196.5 18.1 %attend_back.1 = (bf16[3,896,768]{2,1,0:T(8,128)(2,1)S(1)}, f32[6,2,512]{2,1,0:T(2,128)S(1)}) custom-call(bf16[896,2304]{1,0:T(8,128)(2,1)S(1)} %copy-done.3, bf16[896,2304]{1,0:T(8,128)(2,1)S(1)} %copy-done.3, bf16[896,2304]{1,0:T(8,128)(2,1)S(1)} %copy-done.3, bf16[896,768]{1,0:T(8,128)(2,1)S(1)} %copy-done.10, ...), custom_call_target="tpu_custom_call" | custom-call | flops 3825205248 | bytes 22216704 | tf_op jit(solution)/shard_map/attend_back/pallas_call | solution.py:462
  214.7 1.3 fusion.5
  219.1 1.3 fusion.23
  220.4 1.3 fusion.24
  222.9 1.7 collective-permute-start.45
  224.6 1.6 collective-permute-start.46
  226.3 7.7 %attention_grads.1 = (bf16[2,192,3072]{2,1,0:T(8,128)(2,1)S(1)}, bf16[2,192,3072]{2,1,0:T(8,128)(2,1)S(1)}) custom-call(s32[4]{0:T(128)S(1)} %pad_add_fusion.place_ref, bf16[896,768]{1,0:T(8,128)(2,1)S(1)} %copy-done.15, bf16[3,896,768]{2,1,0:T(8,128)(2,1)S(1)} %get-tuple-element.209.grads_ref.refs_0_, bf16[896,768]{1,0:T(8,128)(2,1)S(1)} %copy-done.12, ...), custom_call_target="tpu_custom_call" | custom-call | flops 4227858432 | bytes 12976128 | tf_op jit(solution)/shard_map/attention_grads/pallas_call | solution.py:852
  237.5 1.6 fusion.67
  240.1 2.6 collective-permute-start.54
  242.6 1.6 collective-permute-start.55
  244.3 1.4 copy-done.45
  245.7 6.8 %input_back.1 = (f32[896,768]{1,0:T(8,128)S(1)}, f32[1,768]{1,0:T(1,128)S(1)}) custom-call(bf16[3,896,768]{2,1,0:T(8,128)(2,1)S(1)} %get-tuple-element.209.grads_ref.refs_0_, bf16[768,3072]{1,0:T(8,128)(2,1)} %bitcast.226, f32[896,768]{1,0:T(8,128)S(1)} %get-tuple-element.248.refs_0_.refs_2_, f32[896,768]{1,0:T(8,128)S(1)} %copy-done.7, ...), custom_call_target="tpu_custom_call" | custom-call | flops 3170893824 | bytes 15925248 | tf_op jit(solution)/shard_map/input_back/pallas_call | solution.py:900
  252.5 1.5 copy-done.5
  254.6 1.9 fusion.66
  258.1 1.3 collective-permute-start.47
  262.5 9.3 %collective-permute-done.48 = bf16[2,2,24,3072]{3,2,0,1:T(8,128)(2,1)S(1)} collective-permute-done((bf16[2,2,24,3072]{3,2,0,1:T(8,128)(2,1)S(1)}, bf16[2,2,24,3072]{3,2,0,1:T(8,128)(2,1)S(1)}, u32[]{:S(2)}, u32[]{:S(2)}) %collective-permute-start.48) | collective-permute-done | bytes 589856 | tf_op jit(solution)/shard_map/ppermute | solution.py:33
  272.9 1.3 collective-permute-start.50
  274.3 3.5 %collective-permute-done.52 = f32[1920]{0:T(1024)S(1)} collective-permute-done((f32[1920]{0:T(1024)S(1)}, f32[1920]{0:T(1024)S(1)}, u32[]{:S(2)}, u32[]{:S(2)}) %collective-permute-start.52) | collective-permute-done | bytes 7712 | tf_op jit(solution)/shard_map/ppermute | solution.py:33
  278.6 5.1 %convolution_add_fusion = f32[896,768]{1,0:T(8,128)S(1)} fusion(f32[896,768]{1,0:T(8,128)S(1)} %copy-done.18, bf16[896,2048]{1,0:T(8,128)(2,1)} %get-tuple-element.218, bf16[2048,768]{1,0:T(8,128)(2,1)S(1)} %bitcast.258), kind=kOutput, calls=%fused_computation.20 | convolution fusion | flops 2819260416 | bytes 12320768 | tf_op jit(solution)/shard_map/dot_general | solution.py:263
  283.7 2.4 collective-permute-done.49
  290.6 2.8 collective-permute-done.60
  298.2 1.7 collective-permute-start.56
  300.4 2.2 collective-permute-start.58
  304.0 1.8 collective-permute-done.56
  305.8 4.6 %collective-permute-done.57 = bf16[24,3072]{1,0:T(8,128)(2,1)S(1)} collective-permute-done((bf16[24,3072]{1,0:T(8,128)(2,1)S(1)}, bf16[24,3072]{1,0:T(8,128)(2,1)S(1)}, u32[]{:S(2)}, u32[]{:S(2)}) %collective-permute-start.57) | collective-permute-done | bytes 147488 | tf_op jit(solution)/shard_map/ppermute | solution.py:33
  (307 shorter events, 62.6 us)
Async XLA Ops:
  2.5 17.5 %collective-permute-start = (bf16[24,3072]{1,0:T(8,128)(2,1)S(1)}, bf16[24,3072]{1,0:T(8,128)(2,1)}, u32[]{:S(2)}, u32[]{:S(2)}) collective-permute-start(bf16[24,3072]{1,0:T(8,128)(2,1)S(1)} %pad_maximum_fusion.14), channel_id=1, source_target_pairs={{0,2},{1,3},{2,0},{3,1},{4,6},{5,7},{6,4},{7,5},{8,10},{9,11},{10,... | collective-permute-start | bytes 442376 | tf_op jit(solution)/shard_map/ppermute | solution.py:33
  5.6 14.4 %collective-permute-start.1 = (bf16[24,3072]{1,0:T(8,128)(2,1)S(1)}, bf16[24,3072]{1,0:T(8,128)(2,1)}, u32[]{:S(2)}, u32[]{:S(2)}) collective-permute-start(bf16[24,3072]{1,0:T(8,128)(2,1)S(1)} %pad_maximum_fusion.14), channel_id=1, source_target_pairs={{0,4},{1,5},{2,6},{3,7},{4,0},{5,1},{6,2},{7,3},{8,12},{9,13},{10,... | collective-permute-start | bytes 442376 | tf_op jit(solution)/shard_map/ppermute | solution.py:33
  8.2 11.9 %collective-permute-start.2 = (bf16[24,3072]{1,0:T(8,128)(2,1)S(1)}, bf16[24,3072]{1,0:T(8,128)(2,1)}, u32[]{:S(2)}, u32[]{:S(2)}) collective-permute-start(bf16[24,3072]{1,0:T(8,128)(2,1)S(1)} %pad_maximum_fusion.14), channel_id=1, source_target_pairs={{0,6},{1,7},{2,4},{3,5},{4,2},{5,3},{6,0},{7,1},{8,14},{9,15},{10,... | collective-permute-start | bytes 442376 | tf_op jit(solution)/shard_map/ppermute | solution.py:33
  21.1 8.3 %collective-permute-start.8 = (bf16[2,24,3072]{2,1,0:T(8,128)(2,1)S(1)}, bf16[2,24,3072]{2,1,0:T(8,128)(2,1)S(1)}, u32[]{:S(2)}, u32[]{:S(2)}) collective-permute-start(bf16[2,24,3072]{2,1,0:T(8,128)(2,1)S(1)} %pad_maximum_fusion.11), channel_id=1, source_target_pairs={{0,16},{1,17},{2,18},{3,19},{4,20},{5,21},{6,22},{7,23},{8,24},{9,... | collective-permute-start | bytes 884744 | tf_op jit(solution)/shard_map/ppermute | solution.py:33
  23.9 7.8 %collective-permute-start.6 = (bf16[2,24,3072]{2,1,0:T(8,128)(2,1)S(1)}, bf16[2,24,3072]{2,1,0:T(8,128)(2,1)S(1)}, u32[]{:S(2)}, u32[]{:S(2)}) collective-permute-start(bf16[2,24,3072]{2,1,0:T(8,128)(2,1)S(1)} %pad_maximum_fusion.10), channel_id=1, source_target_pairs={{0,1},{1,0},{2,3},{3,2},{4,5},{5,4},{6,7},{7,6},{8,9},{9,8},{10,11... | collective-permute-start | bytes 884744 | tf_op jit(solution)/shard_map/ppermute | solution.py:33
  25.5 8.3 %collective-permute-start.3 = (bf16[24,4096]{1,0:T(8,128)(2,1)}, bf16[24,4096]{1,0:T(8,128)(2,1)}, u32[]{:S(2)}, u32[]{:S(2)}) collective-permute-start(bf16[24,4096]{1,0:T(8,128)(2,1)} %convert_element_type.456), channel_id=1, source_target_pairs={{0,2},{1,3},{2,0},{3,1},{4,6},{5,7},{6,4},{7,5},{8,10},{9,11},{10,... | collective-permute-start | bytes 589832 | tf_op jit(solution)/shard_map/ppermute | solution.py:33
  29.5 25.6 %collective-permute-start.11 = (bf16[4,24,3072]{2,1,0:T(8,128)(2,1)S(1)}, bf16[4,24,3072]{2,1,0:T(8,128)(2,1)}, u32[]{:S(2)}, u32[]{:S(2)}) collective-permute-start(bf16[4,24,3072]{2,1,0:T(8,128)(2,1)S(1)} %bitcast.234), channel_id=1, source_target_pairs={{0,8},{1,9},{2,10},{3,11},{4,12},{5,13},{6,14},{7,15},{8,0},{9,1},... | collective-permute-start | bytes 1769480 | tf_op jit(solution)/shard_map/ppermute | solution.py:33
  29.6 25.5 %collective-permute-start.9 = (bf16[4,24,3072]{2,1,0:T(8,128)(2,1)S(1)}, bf16[4,24,3072]{2,1,0:T(8,128)(2,1)}, u32[]{:S(2)}, u32[]{:S(2)}) collective-permute-start(bf16[4,24,3072]{2,1,0:T(8,128)(2,1)S(1)} %bitcast.235), channel_id=1, source_target_pairs={{0,1},{1,0},{2,3},{3,2},{4,5},{5,4},{6,7},{7,6},{8,9},{9,8},{10,11... | collective-permute-start | bytes 1769480 | tf_op jit(solution)/shard_map/ppermute | solution.py:33
  32.6 22.4 %collective-permute-start.10 = (bf16[4,24,3072]{2,1,0:T(8,128)(2,1)}, bf16[4,24,3072]{2,1,0:T(8,128)(2,1)}, u32[]{:S(2)}, u32[]{:S(2)}) collective-permute-start(bf16[4,24,3072]{2,1,0:T(8,128)(2,1)} %bitcast.13.refs_0_), channel_id=1, source_target_pairs={{0,8},{1,9},{2,10},{3,11},{4,12},{5,13},{6,14},{7,15},{8,0},{9,1},... | collective-permute-start | bytes 1769480 | tf_op jit(solution)/shard_map/ppermute | solution.py:33
  32.6 22.4 %collective-permute-start.7 = (bf16[4,24,3072]{2,1,0:T(8,128)(2,1)}, bf16[4,24,3072]{2,1,0:T(8,128)(2,1)}, u32[]{:S(2)}, u32[]{:S(2)}) collective-permute-start(bf16[4,24,3072]{2,1,0:T(8,128)(2,1)} %bitcast.13.refs_0_), channel_id=1, source_target_pairs={{0,16},{1,17},{2,18},{3,19},{4,20},{5,21},{6,22},{7,23},{8,24},{9,... | collective-permute-start | bytes 1769480 | tf_op jit(solution)/shard_map/ppermute | solution.py:33
  33.8 12.3 %collective-permute-start.4 = (bf16[24,4096]{1,0:T(8,128)(2,1)}, bf16[24,4096]{1,0:T(8,128)(2,1)}, u32[]{:S(2)}, u32[]{:S(2)}) collective-permute-start(bf16[24,4096]{1,0:T(8,128)(2,1)} %convert_element_type.456), channel_id=1, source_target_pairs={{0,4},{1,5},{2,6},{3,7},{4,0},{5,1},{6,2},{7,3},{8,12},{9,13},{10,... | collective-permute-start | bytes 589832 | tf_op jit(solution)/shard_map/ppermute | solution.py:33
  46.1 9.0 %collective-permute-start.5 = (bf16[24,4096]{1,0:T(8,128)(2,1)}, bf16[24,4096]{1,0:T(8,128)(2,1)}, u32[]{:S(2)}, u32[]{:S(2)}) collective-permute-start(bf16[24,4096]{1,0:T(8,128)(2,1)} %convert_element_type.456), channel_id=1, source_target_pairs={{0,6},{1,7},{2,4},{3,5},{4,2},{5,3},{6,0},{7,1},{8,14},{9,15},{10,... | collective-permute-start | bytes 589832 | tf_op jit(solution)/shard_map/ppermute | solution.py:33
  55.1 5.6 %collective-permute-start.14 = (bf16[4,24,3072]{2,1,0:T(8,128)(2,1)}, bf16[4,24,3072]{2,1,0:T(8,128)(2,1)S(1)}, u32[]{:S(2)}, u32[]{:S(2)}) collective-permute-start(bf16[4,24,3072]{2,1,0:T(8,128)(2,1)} %collective-permute-done.7.refs_1_), channel_id=1, source_target_pairs={{0,8},{1,9},{2,10},{3,11},{4,12},{5,13},{6,14},{7,15},{8,0},{9,1},... | collective-permute-start | bytes 1769480 | tf_op jit(solution)/shard_map/ppermute | solution.py:33
  55.2 5.5 %collective-permute-start.15 = (bf16[4,24,3072]{2,1,0:T(8,128)(2,1)}, bf16[4,24,3072]{2,1,0:T(8,128)(2,1)S(1)}, u32[]{:S(2)}, u32[]{:S(2)}) collective-permute-start(bf16[4,24,3072]{2,1,0:T(8,128)(2,1)} %collective-permute-done.9.refs_3_), channel_id=1, source_target_pairs={{0,8},{1,9},{2,10},{3,11},{4,12},{5,13},{6,14},{7,15},{8,0},{9,1},... | collective-permute-start | bytes 1769480 | tf_op jit(solution)/shard_map/ppermute | solution.py:33
  56.8 11.7 %collective-permute-start.13 = (bf16[2,24,4096]{2,1,0:T(8,128)(2,1)S(1)}, bf16[2,24,4096]{2,1,0:T(8,128)(2,1)S(1)}, u32[]{:S(2)}, u32[]{:S(2)}) collective-permute-start(bf16[2,24,4096]{2,1,0:T(8,128)(2,1)S(1)} %pad_maximum_fusion.7), channel_id=1, source_target_pairs={{0,16},{1,17},{2,18},{3,19},{4,20},{5,21},{6,22},{7,23},{8,24},{9,... | collective-permute-start | bytes 1179656 | tf_op jit(solution)/shard_map/ppermute | solution.py:33
  59.0 10.9 %collective-permute-start.12 = (bf16[2,24,4096]{2,1,0:T(8,128)(2,1)S(1)}, bf16[2,24,4096]{2,1,0:T(8,128)(2,1)S(1)}, u32[]{:S(2)}, u32[]{:S(2)}) collective-permute-start(bf16[2,24,4096]{2,1,0:T(8,128)(2,1)S(1)} %pad_maximum_fusion.6), channel_id=1, source_target_pairs={{0,1},{1,0},{2,3},{3,2},{4,5},{5,4},{6,7},{7,6},{8,9},{9,8},{10,11... | collective-permute-start | bytes 1179656 | tf_op jit(solution)/shard_map/ppermute | solution.py:33
  70.0 23.5 %collective-permute-start.17 = (bf16[4,24,4096]{2,1,0:T(8,128)(2,1)S(1)}, bf16[4,24,4096]{2,1,0:T(8,128)(2,1)S(1)}, u32[]{:S(2)}, u32[]{:S(2)}) collective-permute-start(bf16[4,24,4096]{2,1,0:T(8,128)(2,1)S(1)} %bitcast.228), channel_id=1, source_target_pairs={{0,1},{1,0},{2,3},{3,2},{4,5},{5,4},{6,7},{7,6},{8,9},{9,8},{10,11... | collective-permute-start | bytes 2359304 | tf_op jit(solution)/shard_map/ppermute | solution.py:33
  71.8 21.8 %collective-permute-start.16 = (bf16[4,24,4096]{2,1,0:T(8,128)(2,1)S(1)}, bf16[4,24,4096]{2,1,0:T(8,128)(2,1)S(1)}, u32[]{:S(2)}, u32[]{:S(2)}) collective-permute-start(bf16[4,24,4096]{2,1,0:T(8,128)(2,1)S(1)} %bitcast.231), channel_id=1, source_target_pairs={{0,16},{1,17},{2,18},{3,19},{4,20},{5,21},{6,22},{7,23},{8,24},{9,... | collective-permute-start | bytes 2359304 | tf_op jit(solution)/shard_map/ppermute | solution.py:33
  72.4 7.1 %collective-permute-start.18 = (bf16[64,768]{1,0:T(8,128)(2,1)S(1)}, bf16[64,768]{1,0:T(8,128)(2,1)S(1)}, u32[]{:S(2)}, u32[]{:S(2)}) collective-permute-start(bf16[64,768]{1,0:T(8,128)(2,1)S(1)} %convert_element_type.457), channel_id=1, source_target_pairs={{0,2},{1,3},{2,0},{3,1},{4,6},{5,7},{6,4},{7,5},{8,10},{9,11},{10,... | collective-permute-start | bytes 294920 | tf_op jit(solution)/shard_map/ppermute | solution.py:33
  75.4 17.6 %collective-permute-start.19 = (bf16[64,768]{1,0:T(8,128)(2,1)S(1)}, bf16[64,768]{1,0:T(8,128)(2,1)S(1)}, u32[]{:S(2)}, u32[]{:S(2)}) collective-permute-start(bf16[64,768]{1,0:T(8,128)(2,1)S(1)} %convert_element_type.457), channel_id=1, source_target_pairs={{0,4},{1,5},{2,6},{3,7},{4,0},{5,1},{6,2},{7,3},{8,12},{9,13},{10,... | collective-permute-start | bytes 294920 | tf_op jit(solution)/shard_map/ppermute | solution.py:33
  76.5 17.1 %collective-permute-start.20 = (bf16[64,768]{1,0:T(8,128)(2,1)S(1)}, bf16[64,768]{1,0:T(8,128)(2,1)S(1)}, u32[]{:S(2)}, u32[]{:S(2)}) collective-permute-start(bf16[64,768]{1,0:T(8,128)(2,1)S(1)} %convert_element_type.457), channel_id=1, source_target_pairs={{0,6},{1,7},{2,4},{3,5},{4,2},{5,3},{6,0},{7,1},{8,14},{9,15},{10,... | collective-permute-start | bytes 294920 | tf_op jit(solution)/shard_map/ppermute | solution.py:33
  79.5 16.4 %collective-permute-start.23 = (bf16[4,24,4096]{2,1,0:T(8,128)(2,1)S(1)}, bf16[4,24,4096]{2,1,0:T(8,128)(2,1)S(1)}, u32[]{:S(2)}, u32[]{:S(2)}) collective-permute-start(bf16[4,24,4096]{2,1,0:T(8,128)(2,1)S(1)} %bitcast.229), channel_id=1, source_target_pairs={{0,8},{1,9},{2,10},{3,11},{4,12},{5,13},{6,14},{7,15},{8,0},{9,1},... | collective-permute-start | bytes 2359304 | tf_op jit(solution)/shard_map/ppermute | solution.py:33
  93.0 7.0 %collective-permute-start.21 = (bf16[4,24,4096]{2,1,0:T(8,128)(2,1)S(1)}, bf16[4,24,4096]{2,1,0:T(8,128)(2,1)S(1)}, u32[]{:S(2)}, u32[]{:S(2)}) collective-permute-start(bf16[4,24,4096]{2,1,0:T(8,128)(2,1)S(1)} %bitcast.232), channel_id=1, source_target_pairs={{0,8},{1,9},{2,10},{3,11},{4,12},{5,13},{6,14},{7,15},{8,0},{9,1},... | collective-permute-start | bytes 2359304 | tf_op jit(solution)/shard_map/ppermute | solution.py:33
  93.6 9.0 %collective-permute-start.22 = (bf16[4,24,4096]{2,1,0:T(8,128)(2,1)S(1)}, bf16[4,24,4096]{2,1,0:T(8,128)(2,1)S(1)}, u32[]{:S(2)}, u32[]{:S(2)}) collective-permute-start(bf16[4,24,4096]{2,1,0:T(8,128)(2,1)S(1)} %collective-permute-done.16.refs_1_), channel_id=1, source_target_pairs={{0,8},{1,9},{2,10},{3,11},{4,12},{5,13},{6,14},{7,15},{8,0},{9,1},... | collective-permute-start | bytes 2359304 | tf_op jit(solution)/shard_map/ppermute | solution.py:33
  93.7 8.9 %collective-permute-start.24 = (bf16[4,24,4096]{2,1,0:T(8,128)(2,1)S(1)}, bf16[4,24,4096]{2,1,0:T(8,128)(2,1)S(1)}, u32[]{:S(2)}, u32[]{:S(2)}) collective-permute-start(bf16[4,24,4096]{2,1,0:T(8,128)(2,1)S(1)} %collective-permute-done.17.refs_3_), channel_id=1, source_target_pairs={{0,8},{1,9},{2,10},{3,11},{4,12},{5,13},{6,14},{7,15},{8,0},{9,1},... | collective-permute-start | bytes 2359304 | tf_op jit(solution)/shard_map/ppermute | solution.py:33
  94.2 7.0 %collective-permute-start.26 = (bf16[2,64,768]{2,1,0:T(8,128)(2,1)S(1)}, bf16[2,64,768]{2,1,0:T(8,128)(2,1)S(1)}, u32[]{:S(2)}, u32[]{:S(2)}) collective-permute-start(bf16[2,64,768]{2,1,0:T(8,128)(2,1)S(1)} %pad_maximum_fusion.13), channel_id=1, source_target_pairs={{0,16},{1,17},{2,18},{3,19},{4,20},{5,21},{6,22},{7,23},{8,24},{9,... | collective-permute-start | bytes 589832 | tf_op jit(solution)/shard_map/ppermute | solution.py:33
  95.9 6.7 %collective-permute-start.25 = (bf16[2,64,768]{2,1,0:T(8,128)(2,1)S(1)}, bf16[2,64,768]{2,1,0:T(8,128)(2,1)S(1)}, u32[]{:S(2)}, u32[]{:S(2)}) collective-permute-start(bf16[2,64,768]{2,1,0:T(8,128)(2,1)S(1)} %pad_maximum_fusion.12), channel_id=1, source_target_pairs={{0,1},{1,0},{2,3},{3,2},{4,5},{5,4},{6,7},{7,6},{8,9},{9,8},{10,11... | collective-permute-start | bytes 589832 | tf_op jit(solution)/shard_map/ppermute | solution.py:33
  102.7 25.3 %collective-permute-start.28 = (bf16[4,64,768]{2,1,0:T(8,128)(2,1)S(1)}, bf16[4,64,768]{2,1,0:T(8,128)(2,1)S(1)}, u32[]{:S(2)}, u32[]{:S(2)}) collective-permute-start(bf16[4,64,768]{2,1,0:T(8,128)(2,1)S(1)} %bitcast.237), channel_id=1, source_target_pairs={{0,1},{1,0},{2,3},{3,2},{4,5},{5,4},{6,7},{7,6},{8,9},{9,8},{10,11... | collective-permute-start | bytes 1179656 | tf_op jit(solution)/shard_map/ppermute | solution.py:33
  103.7 30.1 %copy-start.13 = (bf16[896,768]{1,0:T(8,128)(2,1)S(1)}, bf16[896,768]{1,0:T(8,128)(2,1)}, u32[]{:S(2)}) copy-start(bf16[896,768]{1,0:T(8,128)(2,1)} %fusion.64.refs_9_) | copy-start | bytes 4128772
  103.8 24.3 %collective-permute-start.27 = (bf16[4,64,768]{2,1,0:T(8,128)(2,1)S(1)}, bf16[4,64,768]{2,1,0:T(8,128)(2,1)S(1)}, u32[]{:S(2)}, u32[]{:S(2)}) collective-permute-start(bf16[4,64,768]{2,1,0:T(8,128)(2,1)S(1)} %bitcast.240), channel_id=1, source_target_pairs={{0,16},{1,17},{2,18},{3,19},{4,20},{5,21},{6,22},{7,23},{8,24},{9,... | collective-permute-start | bytes 1179656 | tf_op jit(solution)/shard_map/ppermute | solution.py:33
  128.1 25.4 %collective-permute-start.33 = (bf16[2,512,768]{2,1,0:T(8,128)(2,1)}, bf16[2,512,768]{2,1,0:T(8,128)(2,1)}, u32[]{:S(2)}, u32[]{:S(2)}) collective-permute-start(bf16[2,512,768]{2,1,0:T(8,128)(2,1)} %get-tuple-element.179), channel_id=1, source_target_pairs={{0,8},{1,9},{2,10},{3,11},{4,12},{5,13},{6,14},{7,15},{8,0},{9,1},... | collective-permute-start | bytes 4718600 | tf_op jit(solution)/shard_map/ppermute | solution.py:33
  128.1 3.6 %collective-permute-start.31 = (bf16[4,64,768]{2,1,0:T(8,128)(2,1)S(1)}, bf16[4,64,768]{2,1,0:T(8,128)(2,1)S(1)}, u32[]{:S(2)}, u32[]{:S(2)}) collective-permute-start(bf16[4,64,768]{2,1,0:T(8,128)(2,1)S(1)} %bitcast.238), channel_id=1, source_target_pairs={{0,8},{1,9},{2,10},{3,11},{4,12},{5,13},{6,14},{7,15},{8,0},{9,1},... | collective-permute-start | bytes 1179656 | tf_op jit(solution)/shard_map/ppermute | solution.py:33
  128.6 3.7 %collective-permute-start.29 = (bf16[4,64,768]{2,1,0:T(8,128)(2,1)S(1)}, bf16[4,64,768]{2,1,0:T(8,128)(2,1)S(1)}, u32[]{:S(2)}, u32[]{:S(2)}) collective-permute-start(bf16[4,64,768]{2,1,0:T(8,128)(2,1)S(1)} %bitcast.241), channel_id=1, source_target_pairs={{0,8},{1,9},{2,10},{3,11},{4,12},{5,13},{6,14},{7,15},{8,0},{9,1},... | collective-permute-start | bytes 1179656 | tf_op jit(solution)/shard_map/ppermute | solution.py:33
  128.7 4.5 %collective-permute-start.30 = (bf16[4,64,768]{2,1,0:T(8,128)(2,1)S(1)}, bf16[4,64,768]{2,1,0:T(8,128)(2,1)S(1)}, u32[]{:S(2)}, u32[]{:S(2)}) collective-permute-start(bf16[4,64,768]{2,1,0:T(8,128)(2,1)S(1)} %collective-permute-done.27.refs_1_), channel_id=1, source_target_pairs={{0,8},{1,9},{2,10},{3,11},{4,12},{5,13},{6,14},{7,15},{8,0},{9,1},... | collective-permute-start | bytes 1179656 | tf_op jit(solution)/shard_map/ppermute | solution.py:33
  129.2 4.6 %collective-permute-start.32 = (bf16[4,64,768]{2,1,0:T(8,128)(2,1)S(1)}, bf16[4,64,768]{2,1,0:T(8,128)(2,1)S(1)}, u32[]{:S(2)}, u32[]{:S(2)}) collective-permute-start(bf16[4,64,768]{2,1,0:T(8,128)(2,1)S(1)} %collective-permute-done.28.refs_3_), channel_id=1, source_target_pairs={{0,8},{1,9},{2,10},{3,11},{4,12},{5,13},{6,14},{7,15},{8,0},{9,1},... | collective-permute-start | bytes 1179656 | tf_op jit(solution)/shard_map/ppermute | solution.py:33
  153.4 24.4 %collective-permute-start.36 = (bf16[2,192,4096]{2,1,0:T(8,128)(2,1)}, bf16[2,192,4096]{2,1,0:T(8,128)(2,1)}, u32[]{:S(2)}, u32[]{:S(2)}) collective-permute-start(bf16[2,192,4096]{2,1,0:T(8,128)(2,1)} %get-tuple-element.187), channel_id=1, source_target_pairs={{0,8},{1,9},{2,10},{3,11},{4,12},{5,13},{6,14},{7,15},{8,0},{9,1},... | collective-permute-start | bytes 9437192 | tf_op jit(solution)/shard_map/ppermute | solution.py:33
  155.1 35.0 %copy-start.41 = (bf16[2,2,2,64,768]{4,3,2,1,0:T(8,128)(2,1)}, bf16[2,2,2,64,768]{4,3,2,1,0:T(8,128)(2,1)S(1)}, u32[]{:S(2)}) copy-start(bf16[2,2,2,64,768]{4,3,2,1,0:T(8,128)(2,1)S(1)} %get-tuple-element.260) | copy-start | bytes 2359300
  157.4 20.4 %collective-permute-start.35 = (bf16[2,2,64,768]{3,2,0,1:T(8,128)(2,1)S(1)}, bf16[2,2,64,768]{3,2,0,1:T(8,128)(2,1)S(1)}, u32[]{:S(2)}, u32[]{:S(2)}) collective-permute-start(bf16[2,2,64,768]{3,2,0,1:T(8,128)(2,1)S(1)} %fusion.14), channel_id=1, source_target_pairs={{0,16},{1,17},{2,18},{3,19},{4,20},{5,21},{6,22},{7,23},{8,24},{9,... | collective-permute-start | bytes 1179656 | tf_op jit(solution)/shard_map/ppermute | solution.py:33
  158.7 19.1 %collective-permute-start.34 = (bf16[2,2,64,768]{3,2,1,0:T(8,128)(2,1)S(1)}, bf16[2,2,64,768]{3,2,1,0:T(8,128)(2,1)S(1)}, u32[]{:S(2)}, u32[]{:S(2)}) collective-permute-start(bf16[2,2,64,768]{3,2,1,0:T(8,128)(2,1)S(1)} %fusion.13), channel_id=1, source_target_pairs={{0,1},{1,0},{2,3},{3,2},{4,5},{5,4},{6,7},{7,6},{8,9},{9,8},{10,11... | collective-permute-start | bytes 1179656 | tf_op jit(solution)/shard_map/ppermute | solution.py:33
  183.6 31.0 %collective-permute-start.40 = (bf16[2,2,24,4096]{3,2,0,1:T(8,128)(2,1)}, bf16[2,2,24,4096]{3,2,0,1:T(8,128)(2,1)}, u32[]{:S(2)}, u32[]{:S(2)}) collective-permute-start(bf16[2,2,24,4096]{3,2,0,1:T(8,128)(2,1)} %fusion.1), channel_id=1, source_target_pairs={{0,16},{1,17},{2,18},{3,19},{4,20},{5,21},{6,22},{7,23},{8,24},{9,... | collective-permute-start | bytes 2359304 | tf_op jit(solution)/shard_map/ppermute | solution.py:33
  186.7 27.9 %collective-permute-start.39 = (bf16[2,2,24,4096]{3,2,1,0:T(8,128)(2,1)}, bf16[2,2,24,4096]{3,2,1,0:T(8,128)(2,1)}, u32[]{:S(2)}, u32[]{:S(2)}) collective-permute-start(bf16[2,2,24,4096]{3,2,1,0:T(8,128)(2,1)} %fusion), channel_id=1, source_target_pairs={{0,1},{1,0},{2,3},{3,2},{4,5},{5,4},{6,7},{7,6},{8,9},{9,8},{10,11... | collective-permute-start | bytes 2359304 | tf_op jit(solution)/shard_map/ppermute | solution.py:33
  189.1 25.5 %collective-permute-start.38 = (bf16[2,64,768]{2,1,0:T(8,128)(2,1)S(1)}, bf16[2,64,768]{2,1,0:T(8,128)(2,1)S(1)}, u32[]{:S(2)}, u32[]{:S(2)}) collective-permute-start(bf16[2,64,768]{2,1,0:T(8,128)(2,1)S(1)} %fusion.25), channel_id=1, source_target_pairs={{0,1},{1,0},{2,3},{3,2},{4,5},{5,4},{6,7},{7,6},{8,9},{9,8},{10,11... | collective-permute-start | bytes 589832 | tf_op jit(solution)/shard_map/ppermute | solution.py:33
  191.2 23.4 %collective-permute-start.37 = (bf16[2,64,768]{2,1,0:T(8,128)(2,1)S(1)}, bf16[2,64,768]{2,1,0:T(8,128)(2,1)S(1)}, u32[]{:S(2)}, u32[]{:S(2)}) collective-permute-start(bf16[2,64,768]{2,1,0:T(8,128)(2,1)S(1)} %fusion.26), channel_id=1, source_target_pairs={{0,16},{1,17},{2,18},{3,19},{4,20},{5,21},{6,22},{7,23},{8,24},{9,... | collective-permute-start | bytes 589832 | tf_op jit(solution)/shard_map/ppermute | solution.py:33
  216.0 18.0 %collective-permute-start.42 = (bf16[2,24,4096]{2,1,0:T(8,128)(2,1)S(1)}, bf16[2,24,4096]{2,1,0:T(8,128)(2,1)S(1)}, u32[]{:S(2)}, u32[]{:S(2)}) collective-permute-start(bf16[2,24,4096]{2,1,0:T(8,128)(2,1)S(1)} %fusion.5), channel_id=1, source_target_pairs={{0,1},{1,0},{2,3},{3,2},{4,5},{5,4},{6,7},{7,6},{8,9},{9,8},{10,11... | collective-permute-start | bytes 1179656 | tf_op jit(solution)/shard_map/ppermute | solution.py:33
  218.1 16.0 %collective-permute-start.41 = (bf16[2,24,4096]{2,1,0:T(8,128)(2,1)S(1)}, bf16[2,24,4096]{2,1,0:T(8,128)(2,1)S(1)}, u32[]{:S(2)}, u32[]{:S(2)}) collective-permute-start(bf16[2,24,4096]{2,1,0:T(8,128)(2,1)S(1)} %fusion.6), channel_id=1, source_target_pairs={{0,16},{1,17},{2,18},{3,19},{4,20},{5,21},{6,22},{7,23},{8,24},{9,... | collective-permute-start | bytes 1179656 | tf_op jit(solution)/shard_map/ppermute | solution.py:33
  221.8 18.3 %collective-permute-start.44 = (bf16[64,768]{1,0:T(8,128)(2,1)S(1)}, bf16[64,768]{1,0:T(8,128)(2,1)S(1)}, u32[]{:S(2)}, u32[]{:S(2)}) collective-permute-start(bf16[64,768]{1,0:T(8,128)(2,1)S(1)} %get-tuple-element.265), channel_id=1, source_target_pairs={{0,2},{1,3},{2,0},{3,1},{4,6},{5,7},{6,4},{7,5},{8,10},{9,11},{10,... | collective-permute-start | bytes 294920 | tf_op jit(solution)/shard_map/ppermute | solution.py:33
  222.9 19.7 %collective-permute-start.45 = (bf16[64,768]{1,0:T(8,128)(2,1)S(1)}, bf16[64,768]{1,0:T(8,128)(2,1)S(1)}, u32[]{:S(2)}, u32[]{:S(2)}) collective-permute-start(bf16[64,768]{1,0:T(8,128)(2,1)S(1)} %get-tuple-element.266), channel_id=1, source_target_pairs={{0,4},{1,5},{2,6},{3,7},{4,0},{5,1},{6,2},{7,3},{8,12},{9,13},{10,... | collective-permute-start | bytes 294920 | tf_op jit(solution)/shard_map/ppermute | solution.py:33
  224.6 19.7 %collective-permute-start.46 = (bf16[64,768]{1,0:T(8,128)(2,1)S(1)}, bf16[64,768]{1,0:T(8,128)(2,1)S(1)}, u32[]{:S(2)}, u32[]{:S(2)}) collective-permute-start(bf16[64,768]{1,0:T(8,128)(2,1)S(1)} %get-tuple-element.264), channel_id=1, source_target_pairs={{0,6},{1,7},{2,4},{3,5},{4,2},{5,3},{6,0},{7,1},{8,14},{9,15},{10,... | collective-permute-start | bytes 294920 | tf_op jit(solution)/shard_map/ppermute | solution.py:33
  235.3 9.0 %collective-permute-start.43 = (bf16[2,192,3072]{2,1,0:T(8,128)(2,1)S(1)}, bf16[2,192,3072]{2,1,0:T(8,128)(2,1)S(1)}, u32[]{:S(2)}, u32[]{:S(2)}) collective-permute-start(bf16[2,192,3072]{2,1,0:T(8,128)(2,1)S(1)} %get-tuple-element.204), channel_id=1, source_target_pairs={{0,8},{1,9},{2,10},{3,11},{4,12},{5,13},{6,14},{7,15},{8,0},{9,1},... | collective-permute-start | bytes 7077896 | tf_op jit(solution)/shard_map/ppermute | solution.py:33
  239.9 43.8 %collective-permute-start.53 = (bf16[24,4096]{1,0:T(8,128)(2,1)}, bf16[24,4096]{1,0:T(8,128)(2,1)}, u32[]{:S(2)}, u32[]{:S(2)}) collective-permute-start(bf16[24,4096]{1,0:T(8,128)(2,1)} %get-tuple-element.255), channel_id=1, source_target_pairs={{0,2},{1,3},{2,0},{3,1},{4,6},{5,7},{6,4},{7,5},{8,10},{9,11},{10,... | collective-permute-start | bytes 589832 | tf_op jit(solution)/shard_map/ppermute | solution.py:33
  240.1 43.6 %collective-permute-start.54 = (bf16[24,4096]{1,0:T(8,128)(2,1)S(1)}, bf16[24,4096]{1,0:T(8,128)(2,1)}, u32[]{:S(2)}, u32[]{:S(2)}) collective-permute-start(bf16[24,4096]{1,0:T(8,128)(2,1)S(1)} %get-tuple-element.256), channel_id=1, source_target_pairs={{0,4},{1,5},{2,6},{3,7},{4,0},{5,1},{6,2},{7,3},{8,12},{9,13},{10,... | collective-permute-start | bytes 589832 | tf_op jit(solution)/shard_map/ppermute | solution.py:33
  242.6 41.1 %collective-permute-start.55 = (bf16[24,4096]{1,0:T(8,128)(2,1)S(1)}, bf16[24,4096]{1,0:T(8,128)(2,1)}, u32[]{:S(2)}, u32[]{:S(2)}) collective-permute-start(bf16[24,4096]{1,0:T(8,128)(2,1)S(1)} %get-tuple-element.254), channel_id=1, source_target_pairs={{0,6},{1,7},{2,4},{3,5},{4,2},{5,3},{6,0},{7,1},{8,14},{9,15},{10,... | collective-permute-start | bytes 589832 | tf_op jit(solution)/shard_map/ppermute | solution.py:33
  256.8 14.9 %collective-permute-start.48 = (bf16[2,2,24,3072]{3,2,0,1:T(8,128)(2,1)S(1)}, bf16[2,2,24,3072]{3,2,0,1:T(8,128)(2,1)S(1)}, u32[]{:S(2)}, u32[]{:S(2)}) collective-permute-start(bf16[2,2,24,3072]{3,2,0,1:T(8,128)(2,1)S(1)} %fusion.8), channel_id=1, source_target_pairs={{0,16},{1,17},{2,18},{3,19},{4,20},{5,21},{6,22},{7,23},{8,24},{9,... | collective-permute-start | bytes 1769480 | tf_op jit(solution)/shard_map/ppermute | solution.py:33
  258.1 14.7 %collective-permute-start.47 = (bf16[2,2,24,3072]{3,2,1,0:T(8,128)(2,1)S(1)}, bf16[2,2,24,3072]{3,2,1,0:T(8,128)(2,1)S(1)}, u32[]{:S(2)}, u32[]{:S(2)}) collective-permute-start(bf16[2,2,24,3072]{3,2,1,0:T(8,128)(2,1)S(1)} %fusion.7), channel_id=1, source_target_pairs={{0,1},{1,0},{2,3},{3,2},{4,5},{5,4},{6,7},{7,6},{8,9},{9,8},{10,11... | collective-permute-start | bytes 1769480 | tf_op jit(solution)/shard_map/ppermute | solution.py:33
  272.8 1.4 collective-permute-start.51
  272.9 10.8 %collective-permute-start.50 = (bf16[2,24,3072]{2,1,0:T(8,128)(2,1)S(1)}, bf16[2,24,3072]{2,1,0:T(8,128)(2,1)S(1)}, u32[]{:S(2)}, u32[]{:S(2)}) collective-permute-start(bf16[2,24,3072]{2,1,0:T(8,128)(2,1)S(1)} %fusion.11), channel_id=1, source_target_pairs={{0,1},{1,0},{2,3},{3,2},{4,5},{5,4},{6,7},{7,6},{8,9},{9,8},{10,11... | collective-permute-start | bytes 884744 | tf_op jit(solution)/shard_map/ppermute | solution.py:33
  274.2 3.7 %collective-permute-start.52 = (f32[1920]{0:T(1024)S(1)}, f32[1920]{0:T(1024)S(1)}, u32[]{:S(2)}, u32[]{:S(2)}) collective-permute-start(f32[1920]{0:T(1024)S(1)} %add.472), channel_id=1, source_target_pairs={{0,2},{1,3},{2,0},{3,1},{4,6},{5,7},{6,4},{7,5},{8,10},{9,11},{10,... | collective-permute-start | bytes 23048 | tf_op jit(solution)/shard_map/ppermute | solution.py:33
  277.8 8.3 %collective-permute-start.49 = (bf16[2,24,3072]{2,1,0:T(8,128)(2,1)S(1)}, bf16[2,24,3072]{2,1,0:T(8,128)(2,1)S(1)}, u32[]{:S(2)}, u32[]{:S(2)}) collective-permute-start(bf16[2,24,3072]{2,1,0:T(8,128)(2,1)S(1)} %fusion.12), channel_id=1, source_target_pairs={{0,16},{1,17},{2,18},{3,19},{4,20},{5,21},{6,22},{7,23},{8,24},{9,... | collective-permute-start | bytes 884744 | tf_op jit(solution)/shard_map/ppermute | solution.py:33
  286.1 3.7 %collective-permute-start.59 = (f32[1920]{0:T(1024)S(1)}, f32[1920]{0:T(1024)S(1)}, u32[]{:S(2)}, u32[]{:S(2)}) collective-permute-start(f32[1920]{0:T(1024)S(1)} %add.473), channel_id=1, source_target_pairs={{0,1},{1,0},{2,3},{3,2},{4,5},{5,4},{6,7},{7,6},{8,9},{9,8},{10,11... | collective-permute-start | bytes 23048 | tf_op jit(solution)/shard_map/ppermute | solution.py:33
  289.8 3.7 %collective-permute-start.60 = (f32[1920]{0:T(1024)S(1)}, f32[1920]{0:T(1024)S(1)}, u32[]{:S(2)}, u32[]{:S(2)}) collective-permute-start(f32[1920]{0:T(1024)S(1)} %add.500), channel_id=1, source_target_pairs={{0,16},{1,17},{2,18},{3,19},{4,20},{5,21},{6,22},{7,23},{8,24},{9,... | collective-permute-start | bytes 23048 | tf_op jit(solution)/shard_map/ppermute | solution.py:33
  293.4 9.2 %collective-permute-start.61 = (f32[1920]{0:T(1024)S(1)}, f32[1920]{0:T(1024)S(1)}, u32[]{:S(2)}, u32[]{:S(2)}) collective-permute-start(f32[1920]{0:T(1024)S(1)} %add.501), channel_id=1, source_target_pairs={{0,4},{1,5},{2,6},{3,7},{4,0},{5,1},{6,2},{7,3},{8,12},{9,13},{10,... | collective-permute-start | bytes 23048 | tf_op jit(solution)/shard_map/ppermute | solution.py:33
  298.2 7.6 %collective-permute-start.56 = (bf16[24,3072]{1,0:T(8,128)(2,1)S(1)}, bf16[24,3072]{1,0:T(8,128)(2,1)S(1)}, u32[]{:S(2)}, u32[]{:S(2)}) collective-permute-start(bf16[24,3072]{1,0:T(8,128)(2,1)S(1)} %get-tuple-element.261), channel_id=1, source_target_pairs={{0,2},{1,3},{2,0},{3,1},{4,6},{5,7},{6,4},{7,5},{8,10},{9,11},{10,... | collective-permute-start | bytes 442376 | tf_op jit(solution)/shard_map/ppermute | solution.py:33
  300.0 10.5 %collective-permute-start.57 = (bf16[24,3072]{1,0:T(8,128)(2,1)S(1)}, bf16[24,3072]{1,0:T(8,128)(2,1)S(1)}, u32[]{:S(2)}, u32[]{:S(2)}) collective-permute-start(bf16[24,3072]{1,0:T(8,128)(2,1)S(1)} %get-tuple-element.262), channel_id=1, source_target_pairs={{0,4},{1,5},{2,6},{3,7},{4,0},{5,1},{6,2},{7,3},{8,12},{9,13},{10,... | collective-permute-start | bytes 442376 | tf_op jit(solution)/shard_map/ppermute | solution.py:33
  300.4 10.0 %collective-permute-start.58 = (bf16[24,3072]{1,0:T(8,128)(2,1)S(1)}, bf16[24,3072]{1,0:T(8,128)(2,1)S(1)}, u32[]{:S(2)}, u32[]{:S(2)}) collective-permute-start(bf16[24,3072]{1,0:T(8,128)(2,1)S(1)} %get-tuple-element.263), channel_id=1, source_target_pairs={{0,6},{1,7},{2,4},{3,5},{4,2},{5,3},{6,0},{7,1},{8,14},{9,15},{10,... | collective-permute-start | bytes 442376 | tf_op jit(solution)/shard_map/ppermute | solution.py:33
  (63 other events, 417.0 us)

commit v3 on v2

--- a/solution.py
+++ b/solution.py
@@ -1,4 +1,5 @@
 import functools
+import math
 
 import jax
 import jax.numpy as jnp
@@ -47,6 +48,10 @@
     return lax.optimization_barrier((values, *earlier))[0]
 
 
+def in_hbm(*values):
+    return [pltpu.with_memory_space_constraint(value, pltpu.HBM) for value in values]
+
+
 def together(*values):
     return lax.optimization_barrier(values)
 
@@ -56,30 +61,21 @@
         return [pltpu.make_async_copy(pieces[0], target, sems.at[0])]
     y, c, z, x = place_ref[0], place_ref[1], place_ref[2], place_ref[3]
     copies = []
-
-    def add(piece, row, size):
-        copies.append(
-            pltpu.make_async_copy(
-                piece, target.at[pl.ds(row, size)], sems.at[len(copies)]
-            )
-        )
-
+    even = z - z % 2
     for number, piece in enumerate(pieces):
         core = c ^ (number // 4)
         kind = number % 4
         if kind < 2:
-            add(piece, place_index(y ^ kind, core, z - z % 2, 0), 4)
+            where = target.at[y ^ kind, core, pl.ds(even, 2)]
         else:
-            for outer in range(2):
-                for inner in range(2):
-                    row = place_index(outer, core, (z - z % 2) ^ 2, x ^ (kind - 2))
-                    add(piece.at[pl.ds(2 * outer + inner, 1)], row + 2 * inner, 1)
+            where = target.at[:, core, pl.ds(even ^ 2, 2), x ^ (kind - 2)]
+        copies.append(pltpu.make_async_copy(piece, where, sems.at[number]))
     return copies
 
 
 def filled(place_ref, pieces, full_ref, held, sems, body):
     step = pl.program_id(0)
-    kept = pltpu.make_async_copy(held, full_ref, sems.at[32])
+    kept = pltpu.make_async_copy(held, full_ref, sems.at[8])
 
     @pl.when(step == 0)
     def _():
@@ -97,12 +93,44 @@
         kept.wait()
 
 
+def emit(slots, targets, sems):
+    step, rows = pl.program_id(0), slots.shape[1]
+    copies = []
+    for number in range(slots.shape[0]):
+        start = 0
+        for target in targets:
+            low = max(number * rows, start)
+            high = min((number + 1) * rows, start + target.shape[0])
+            if low < high:
+                source = slots.at[number, pl.ds(low - number * rows, high - low)]
+                where = target.at[pl.ds(low - start, high - low)]
+                copy = pltpu.make_async_copy(source, where, sems.at[len(copies)])
+                copies.append((number, copy))
+            start += target.shape[0]
+    for number in range(slots.shape[0]):
+
+        @pl.when(step == number)
+        def _():
+            for owner, copy in copies:
+                if owner == number:
+                    copy.start()
+
+    @pl.when(step == slots.shape[0] - 1)
+    def _():
+        for _, copy in copies:
+            copy.wait()
+
+
 def gather_order(near, far, core_near, core_far):
     return (near[0], far[0], near[1], far[1], core_near[0], core_far[0], core_near[1], core_far[1])
 
 
+def slab(columns, rows):
+    return (2, 2, 4, 2, rows // 32, columns)
+
+
 def split_rows(full):
-    return full.reshape(32, full.shape[0] // 32, full.shape[1])
+    return full.reshape(slab(full.shape[1], full.shape[0]))
 
 
 def in_order(own, other, index):
@@ -121,10 +149,10 @@
 
 
 def gather_near(place, first, second, first_near, second_near):
-    rows, columns = first.shape[1:]
-    first = jnp.stack(in_order(first, first_near, place[3]), axis=1)
+    even, odd = in_order(first, first_near, place[3])
+    first = jnp.stack([even[0], odd[0], even[1], odd[1]]).reshape(2, 2, *first.shape[1:])
     second = jnp.stack(in_order(second, second_near, place[0]))
-    return first.reshape(4, rows, columns), second.reshape(4, rows, columns)
+    return first, second
 
 
 def gather_far(first, second):
@@ -133,13 +161,6 @@
 
 def gather_core(*pieces):
     return tuple(swap(piece, dc=1) for piece in pieces)
-
-
-def cut(values, places):
-    start = [0 if place is None else place for place in places]
-    sizes = [size if place is None else 1 for place, size in zip(places, values.shape)]
-    kept = [size for place, size in zip(places, values.shape) if place is None]
-    return lax.dynamic_slice(values, start, sizes).reshape(kept)
 
 
 def summed(*terms):
@@ -149,57 +170,161 @@
     return total
 
 
-def low_sum(*terms):
-    return summed(*terms).astype(jnp.bfloat16)
-
-
 def joined_halves(kept, sent):
     return jnp.stack([kept, sent], axis=1).reshape(-1, kept.shape[2]).astype(jnp.float32)
+
+
+def route(name, place, sources, targets, body, scratch=()):
+    def spec(array, lead, pick):
+        block = (*lead, *array.shape[-2:])
+        return pl.BlockSpec(block, lambda step, where: (*pick(where), 0, 0))
+
+    return pl.pallas_call(
+        body,
+        grid_spec=pltpu.PrefetchScalarGridSpec(
+            num_scalar_prefetch=1,
+            grid=(1,),
+            in_specs=[spec(*source) for source in sources],
+            out_specs=[spec(*target) for target in targets],
+            scratch_shapes=scratch,
+        ),
+        out_shape=[target[0] for target in targets],
+        compiler_params=pltpu.CompilerParams(vmem_limit_bytes=20 * 2**20),
+        cost_estimate=pl.CostEstimate(
+            flops=0,
+            bytes_accessed=8 * len(sources) * math.prod(sources[0][0].shape[-2:]),
+            transcendentals=0,
+        ),
+        name=name,
+    )(place, *[source[0] for source in sources])
+
+
+def whole_block(target):
+    lead = target.shape[:-2]
+    return target, lead, lambda where: (0,) * len(lead)
+
+
+def store_sum(out_ref, *refs):
+    blocks = math.prod(refs[0].shape[:-2])
+    for number in range(blocks):
+        terms = []
+        for ref in (out_ref, *refs):
+            index, rest = [], number
+            for size in reversed(ref.shape[:-2]):
+                index.insert(0, rest % size)
+                rest //= size
+            terms.append(ref.at[tuple(index)])
+        terms[0][...] = summed(*[term[...] for term in terms[1:]]).astype(out_ref.dtype)
 
 
 class Scatter:
     def __init__(self, kept, sent, place):
         self.place = place
-        self.shape = (2, 4, 2, kept.shape[1] // 8, kept.shape[2])
+        self.block = (kept.shape[1] // 8, kept.shape[2])
+        self.shape = (2, 4, 2, *self.block)
         self.kept = kept.reshape(self.shape)
         self.sent = sent
 
-    def halves(self, got, cut_y, cut_x, half):
-        y, c, z, x = self.place
-        own = self.kept[:, 2 * half : 2 * half + 2]
-        got = got[:, 2 * half : 2 * half + 2]
-        places = (cut_y, None, cut_x, None, None)
-        return cut(own, places), cut(got, places)
+    def target(self, *lead, dtype=jnp.bfloat16):
+        return jax.ShapeDtypeStruct((*lead, *self.block), dtype)
+
+    def both(self, got, lead, pick):
+        return [(in_hbm(self.kept)[0], lead, pick), (got, lead, pick)]
 
     def core(self):
         return swap(self.sent, dc=1).reshape(self.shape)
 
     def plane(self, got):
-        y, c, z, x = self.place
-        first = swap(low_sum(*self.halves(got, None, 1 - x, 0)), dx=1)
-        second = swap(low_sum(*self.halves(got, 1 - y, None, 1)), dy=1)
-        return first, second
+        def body(place_ref, *refs):
+            store_sum(refs[4], *refs[0:2])
+            store_sum(refs[5], *refs[2:4])
+
+        sources = self.both(got, (2, 2, 1), lambda where: (0, 0, 1 - where[3]))
+        sources += self.both(got, (1, 2, 2), lambda where: (1 - where[0], 1, 0))
+        target = whole_block(self.target(2, 2))
+        one, two = route("plane", self.place, sources, [target, target], body)
+        return swap(one, dx=1), swap(two, dy=1)
 
     def far(self, got, near):
-        y, c, z, x = self.place
-        first = low_sum(
-            *self.halves(got, 1 - y, x, 0), cut(near[0], (1 - y, None, None, None))
-        )
-        second = low_sum(
-            *self.halves(got, y, 1 - x, 1), cut(near[1], (None, 1 - x, None, None))
-        )
-        return swap(first, dy=1), swap(second, dx=1)
-
-    def column(self, got, near, far):
-        y, c, z, x = self.place
-        first = summed(*self.halves(got, y, x, 0), cut(near[0], (y, None, None, None)), far[0])
-        second = summed(*self.halves(got, y, x, 1), cut(near[1], (None, x, None, None)), far[1])
-        total = jnp.concatenate([first, second], axis=0)
-        others = []
-        for flip in (1, 2, 3):
-            share = cut(total, (z ^ flip, None, None)).astype(jnp.bfloat16)
-            others.append(swap(share, dz=flip))
-        return cut(total, (z, None, None)), *others
+        def body(place_ref, *refs):
+            store_sum(refs[6], *refs[0:3])
+            store_sum(refs[7], *refs[3:6])
+
+        sources = [
+            *self.both(got, (1, 2, 1), lambda where: (1 - where[0], 0, where[3])),
+            (near[0], (1, 2), lambda where: (1 - where[0], 0)),
+            *self.both(got, (1, 2, 1), lambda where: (where[0], 1, 1 - where[3])),
+            (near[1], (2, 1), lambda where: (0, 1 - where[3])),
+        ]
+        target = whole_block(self.target(2))
+        one, two = route("far", self.place, sources, [target, target], body)
+        return swap(one, dy=1), swap(two, dx=1)
+
+    def column_sources(self, near, far):
+        return [
+            (near[0], (1, 2), lambda where: (where[0], 0)),
+            (far[0], (2,), lambda where: (0,)),
+            (near[1], (2, 1), lambda where: (0, where[3])),
+            (far[1], (2,), lambda where: (0,)),
+        ]
+
+    def column_terms(self, row, refs):
+        if row < 2:
+            return refs[0].at[0, row], refs[1].at[row]
+        return refs[2].at[row - 2, 0], refs[3].at[row - 2]
+
+    def column_sums(self, got, near, far):
+        sources = self.both(got, (1, 4, 1), lambda where: (where[0], 0, where[3]))
+        sources += self.column_sources(near, far)
+        number = len(sources)
+
+        def body(place_ref, *refs):
+            *outs, total = refs[number:]
+            for row in range(4):
+                terms = (refs[0].at[0, row, 0], refs[1].at[0, row, 0])
+                terms += self.column_terms(row, refs[2:number])
+                total[row] = summed(*[term[...] for term in terms])
+            for flip, out in enumerate(outs):
+                out[...] = total[place_ref[2] ^ flip].astype(out.dtype)
+
+        targets = [self.target(dtype=jnp.float32)] + [self.target()] * 3
+        targets = [whole_block(target) for target in targets]
+        scratch = [pltpu.VMEM((4, *self.block), jnp.float32)]
+        return tuple(route("column", self.place, sources, targets, body, scratch))
+
+    def column(self, sums):
+        return sums[0], *[swap(share, dz=flip) for flip, share in zip((1, 2, 3), sums[1:])]
+
+
+class NarrowScatter(Scatter):
+    def plane(self, got):
+        def body(place_ref, *refs):
+            store_sum(refs[2], *refs[0:2])
+
+        sources = self.both(got, (2, 4, 1), lambda where: (0, 0, 1 - where[3]))
+        target = whole_block(self.target(2, 4))
+        (sums,) = route("plane", self.place, sources, [target], body)
+        return swap(sums, dx=1)
+
+    def far_sums(self, got, near):
+        def body(place_ref, *refs):
+            store_sum(refs[3], *refs[0:3])
+
+        sources = self.both(got, (1, 4, 1), lambda where: (1 - where[0], 0, where[3]))
+        sources.append((near, (1, 4), lambda where: (1 - where[0], 0)))
+        return route("far", self.place, sources, [whole_block(self.target(4))], body)[0]
+
+    def far(self, sums):
+        return swap(sums, dy=1)
+
+    def column_sources(self, near, far):
+        return [
+            (near, (1, 4), lambda where: (where[0], 0)),
+            (far, (4,), lambda where: (0,)),
+        ]
+
+    def column_terms(self, row, refs):
+        return refs[0].at[0, row], refs[1].at[row]
 
 
 def add_flipped(values, *steps):
@@ -338,9 +463,9 @@
         functools.partial(attend_kernel, docs, length, group),
         grid=(pairs,),
         out_shape=(
-            jax.ShapeDtypeStruct((rows, width), jnp.bfloat16),
-            jax.ShapeDtypeStruct((2 * pairs, docs * length, length), jnp.float32),
-            jax.ShapeDtypeStruct((2 * pairs, query_rows, count), jnp.float32),
+            pltpu.HBM((rows, width), jnp.bfloat16),
+            pltpu.HBM((2 * pairs, docs * length, length), jnp.float32),
+            pltpu.HBM((2 * pairs, query_rows, count), jnp.float32),
         ),
         in_specs=[
             pair_spec(rows, 0),
@@ -359,24 +484,25 @@
             pltpu.VMEM((2 * length, length), jnp.float32),
             pltpu.VMEM((2 * length, length), jnp.bfloat16),
         ],
-        compiler_params=pltpu.CompilerParams(vmem_limit_bytes=40 * 2**20),
+        compiler_params=pltpu.CompilerParams(vmem_limit_bytes=18 * 2**20),
         cost_estimate=pl.CostEstimate(
             flops=2 * 2 * pairs * (docs * length * length + query_rows * count) * 128 * 2,
             bytes_accessed=rows * width * 8 + 8 * pairs * docs * length * length,
             transcendentals=2 * pairs * (docs * length * length + query_rows * count),
         ),
         name="attend",
-    )(projected, projected, projected, lines, doc_mask, query_mask)
+    )(*in_hbm(projected, projected, projected), lines, doc_mask, query_mask)
 
 
 def attend_back_kernel(
-    docs, length, q_ref, k_ref, v_ref, grad_ref, doc_probs_ref, query_probs_ref,
-    out_ref, line_ref, grads_scratch, scores_scratch, probs_scratch,
+    docs, length, q_ref, k_ref, v_ref, grad_ref, doc_probs_ref, query_probs_ref, onehot_ref,
+    out_ref, table_ref, grads_scratch, scores_scratch, probs_scratch, lines_scratch,
 ):
     blocks = length // count
     query_start = docs * length
     query_blocks = (q_ref.shape[0] - query_start) // count
     low = jnp.bfloat16
+    half = q_ref.shape[1] // 2
     band = [[None] * 5, [None] * 5]
 
     def gather(head, place, block):
@@ -408,7 +534,6 @@
         out_ref[0, whole, :] = joined(dot_nn(scores_scratch[...], k_ref[whole, :]))
         q_turned = q_ref[whole, :].T
         grad_turned = grad_ref[whole, :].T
-        half = q_turned.shape[0] // 2
         grad_k, grad_v = [], []
         for head in range(2):
             own = slice(head * half, (head + 1) * half)
@@ -429,16 +554,29 @@
             low_probs.append(probs.astype(low))
         out_ref[0, rows, :] = joined(dot_nn(jnp.concatenate(low_scores, axis=0), k_ref[rows, :]))
         turned = jnp.concatenate(low_scores, axis=1).T
-        out_ref[1, rows, :] = joined(dot_nn(turned, q_ref[rows, :]))
-        turned = jnp.concatenate(low_probs, axis=1).T
-        out_ref[2, rows, :] = joined(dot_nn(turned, grad_ref[rows, :]))
+        turned = jnp.concatenate([turned, jnp.concatenate(low_probs, axis=1).T], axis=1)
+        empty = jnp.zeros((count, 2 * half), low)
+        weights = jnp.concatenate(
+            [
+                jnp.concatenate([q_ref[rows, :], empty], axis=1),
+                jnp.concatenate([empty, grad_ref[rows, :]], axis=1),
+            ],
+            axis=0,
+        )
+        both_grads = dot_nn(turned, weights)
+        out_ref[1, rows, :] = joined(both_grads[:, : 2 * half])
+        out_ref[2, rows, :] = joined(both_grads[:, 2 * half :])
+    lines = []
     for head in range(2):
         below, before, middle, after, above = band[head]
         wide = jnp.concatenate([before, middle, after, jnp.zeros_like(middle)], axis=1)
-        size = count
-        while size > 1:
-            size //= 2
-            wide = wide[:size] + pltpu.roll(wide[size:], 4 * count - size, 1)
+        eights = [wide[:8]]
+        for start in range(8, count, 8):
+            eights.append(pltpu.roll(wide[start : start + 8], 4 * count - start, 1))
+        wide = sum(eights)
+        wide = jnp.concatenate([wide[7 - row : 8 - row] for row in range(8)], axis=0)
+        wide = pltpu.roll(wide, 4 * count - 7, 1, stride=1, stride_axis=0)
+        wide = jnp.sum(wide, axis=0, keepdims=True)
         far = jnp.concatenate(
             [
                 jnp.zeros((1, 2 * count), jnp.float32),
@@ -447,24 +585,32 @@
             ],
             axis=1,
         )
-        line_ref[0, head : head + 1, :] = wide + far
-
-
-def attend_back(projected, grad_mixed, doc_probs, query_probs, length, *earlier):
+        lines.append(wide + far)
+    pair = pl.program_id(0)
+    lines_scratch[pair] = jnp.concatenate(lines, axis=0)
+
+    @pl.when(pair == pl.num_programs(0) - 1)
+    def _():
+        table_ref[...] = jnp.dot(
+            lines_scratch[...].reshape(-1, 4 * count),
+            onehot_ref[...],
+            precision=highest,
+            preferred_element_type=jnp.float32,
+        ).reshape(table_ref.shape)
+
+
+def attend_back(projected, grad_mixed, doc_probs, query_probs, onehot, length):
     rows, width = grad_mixed.shape
     pairs = doc_probs.shape[0] // 2
     docs = doc_probs.shape[1] // length
     query_rows = query_probs.shape[1]
 
-    def kernel(*refs):
-        attend_back_kernel(docs, length, *refs[:6], *refs[6 + len(earlier) :])
-
     return pl.pallas_call(
-        kernel,
+        functools.partial(attend_back_kernel, docs, length),
         grid=(pairs,),
         out_shape=(
-            jax.ShapeDtypeStruct((3, rows, width), jnp.bfloat16),
-            jax.ShapeDtypeStruct((pairs, 2, 4 * count), jnp.float32),
+            pltpu.HBM((3, rows, width), jnp.bfloat16),
+            pltpu.HBM((pairs, 2, onehot.shape[1]), jnp.float32),
         ),
         in_specs=[
             pair_spec(rows, 0),
@@ -473,25 +619,26 @@
             pair_spec(rows, 0),
             pl.BlockSpec((2, docs * length, length), lambda pair: (pair, 0, 0)),
             pl.BlockSpec((2, query_rows, count), lambda pair: (pair, 0, 0)),
-        ]
-        + [anywhere] * len(earlier),
+            pl.BlockSpec(onehot.shape, lambda pair: (0, 0)),
+        ],
         out_specs=(
             pl.BlockSpec((3, rows, 2 * 64), lambda pair: (0, 0, pair)),
-            pl.BlockSpec((1, 2, 4 * count), lambda pair: (pair, 0, 0)),
+            pl.BlockSpec((pairs, 2, onehot.shape[1]), lambda pair: (0, 0, 0)),
         ),
         scratch_shapes=[
             pltpu.VMEM((2 * length, length), jnp.float32),
             pltpu.VMEM((2 * length, length), jnp.bfloat16),
             pltpu.VMEM((2 * length, length), jnp.bfloat16),
+            pltpu.VMEM((pairs, 2, 4 * count), jnp.float32),
         ],
-        compiler_params=pltpu.CompilerParams(vmem_limit_bytes=40 * 2**20),
+        compiler_params=pltpu.CompilerParams(vmem_limit_bytes=22 * 2**20),
         cost_estimate=pl.CostEstimate(
             flops=2 * 2 * pairs * (docs * length * length + query_rows * count) * 128 * 4,
             bytes_accessed=rows * width * 14 + 8 * pairs * docs * length * length,
             transcendentals=0,
         ),
         name="attend_back",
-    )(projected, projected, projected, grad_mixed, doc_probs, query_probs, *earlier)
+    )(*in_hbm(projected, projected, projected, grad_mixed, doc_probs, query_probs), onehot)
 
 
 def dot_tn(left, right):
@@ -502,7 +649,6 @@
 
 tile = 512
 row_parts = 2
-gate_parts = 4
 curve = 0.044715
 slope = 0.7978845608028654
 
@@ -528,23 +674,30 @@
 
 def gate_kernel(place_ref, n2_ref, weight, cot_ref, act_ref, by_gate_ref, by_up_ref, kept_ref, sent_ref):
     rows, width = n2_ref.shape
-    hidden = weight.shape[2] // 2
+    hidden = weight.shape[-1] // 2
     start = pl.multiple_of(pl.program_id(0) * tile, 128)
-    gate_weight = weight[:, :, pl.ds(start, tile)].reshape(width, tile)
-    up_weight = weight[:, :, pl.ds(hidden + start, tile)].reshape(width, tile)
-    part = rows // gate_parts
-    for start in range(0, rows, part):
-        places = slice(start, start + part)
-        gate = dot_nn(n2_ref[places, :], gate_weight)
-        up = dot_nn(n2_ref[places, :], up_weight)
+    gate_weight = weight[..., pl.ds(start, tile)].reshape(width, tile)
+    up_weight = weight[..., pl.ds(hidden + start, tile)].reshape(width, tile)
+
+    def finish(places, gate, up):
         square = gate * gate
-        turned = jnp.tanh(slope * gate * (1.0 + curve * square))
-        halved = 0.5 * (1.0 + turned)
+        bent = slope + (slope * curve) * square
+        halved = 0.5 + 0.5 * jnp.tanh(gate * bent)
         value = gate * halved
-        steep = halved + 0.5 * gate * (1.0 - turned * turned) * slope * (1.0 + 3.0 * curve * square)
+        steep = halved + gate * (6.0 * bent - 4.0 * slope) * (halved - halved * halved)
         act_ref[places, :] = (value * up).astype(jnp.bfloat16)
         by_gate_ref[places, :] = up * steep
         by_up_ref[places, :] = value
+
+    held = None
+    for start in range(0, rows, 128):
+        places = slice(start, start + 128)
+        gate = dot_nn(n2_ref[places, :], gate_weight)
+        up = dot_nn(n2_ref[places, :], up_weight)
+        if held is not None:
+            finish(*held)
+        held = (places, gate, up)
+    finish(*held)
     grad = dot_tn(act_ref[...], cot_ref[...]).astype(jnp.bfloat16)
     core = pl.program_id(0) % 2
 
@@ -578,27 +731,27 @@
         kernel,
         grid=(hidden // tile,),
         out_shape=(
-            jax.ShapeDtypeStruct((rows, hidden), jnp.bfloat16),
-            jax.ShapeDtypeStruct((rows, hidden), jnp.float32),
-            jax.ShapeDtypeStruct((rows, hidden), jnp.float32),
-            jax.ShapeDtypeStruct((2, tile, width), jnp.bfloat16),
-            jax.ShapeDtypeStruct((2, tile, width), jnp.bfloat16),
-            jax.ShapeDtypeStruct((32, width // 32, columns), jnp.bfloat16),
+            pltpu.HBM((rows, hidden), jnp.bfloat16),
+            pltpu.HBM((rows, hidden), jnp.float32),
+            pltpu.HBM((rows, hidden), jnp.float32),
+            pltpu.HBM((2, tile, width), jnp.bfloat16),
+            pltpu.HBM((2, tile, width), jnp.bfloat16),
+            pltpu.HBM(slab(columns, width), jnp.bfloat16),
         ),
         in_specs=[scalars()] + [anywhere] * number + [whole, whole],
         out_specs=(column, column, column, half, half, anywhere),
         scratch_shapes=[
-            pltpu.VMEM((32, width // 32, columns), jnp.bfloat16),
-            pltpu.SemaphoreType.DMA((33,)),
+            pltpu.VMEM(slab(columns, width), jnp.bfloat16),
+            pltpu.SemaphoreType.DMA((9,)),
         ],
-        compiler_params=pltpu.CompilerParams(vmem_limit_bytes=48 * 2**20),
+        compiler_params=pltpu.CompilerParams(vmem_limit_bytes=34 * 2**20),
         cost_estimate=pl.CostEstimate(
             flops=6 * rows * width * hidden,
             bytes_accessed=rows * hidden * 10 + 8 * width * hidden,
             transcendentals=rows * hidden,
         ),
         name="gate_forward",
-    )(place, *pieces, normed_two, cot_low)
+    )(place, *pieces, normed_two, *in_hbm(cot_low))
     return (*results, full.reshape(width, columns))
 
 
@@ -611,8 +764,7 @@
     def _():
         turned_rows(place_ref, n2_ref, turned)
 
-    per = tile // ff.shape[1]
-    weight = ff[pl.ds(step * per, per)].reshape(tile, ff.shape[2])
+    weight = ff[step // 2, step % 2].reshape(tile, ff.shape[-1])
     incoming = dot_nt(cot_ref[...], weight)
     by_gate = (incoming * by_gate_ref[...]).astype(jnp.bfloat16)
     by_up = (incoming * by_up_ref[...]).astype(jnp.bfloat16)
@@ -643,10 +795,10 @@
         kernel,
         grid=(hidden // tile,),
         out_shape=(
-            jax.ShapeDtypeStruct((2, rows, hidden), jnp.bfloat16),
-            jax.ShapeDtypeStruct((2, width // 4, 2 * hidden), jnp.bfloat16),
-            jax.ShapeDtypeStruct((2, width // 4, 2 * hidden), jnp.bfloat16),
-            jax.ShapeDtypeStruct((32, hidden // 32, width), jnp.bfloat16),
+            pltpu.HBM((2, rows, hidden), jnp.bfloat16),
+            pltpu.HBM((2, width // 4, 2 * hidden), jnp.bfloat16),
+            pltpu.HBM((2, width // 4, 2 * hidden), jnp.bfloat16),
+            pltpu.HBM(slab(width, hidden), jnp.bfloat16),
         ),
         in_specs=[scalars()] + [anywhere] * number + [whole, whole, column, column],
         out_specs=(
@@ -656,18 +808,18 @@
             anywhere,
         ),
         scratch_shapes=[
-            pltpu.VMEM((32, hidden // 32, width), jnp.bfloat16),
+            pltpu.VMEM(slab(width, hidden), jnp.bfloat16),
             pltpu.VMEM((width, rows), jnp.bfloat16),
-            pltpu.SemaphoreType.DMA((33,)),
+            pltpu.SemaphoreType.DMA((9,)),
         ],
-        compiler_params=pltpu.CompilerParams(vmem_limit_bytes=48 * 2**20),
+        compiler_params=pltpu.CompilerParams(vmem_limit_bytes=38 * 2**20),
         cost_estimate=pl.CostEstimate(
             flops=6 * rows * width * hidden,
             bytes_accessed=rows * hidden * 12 + 8 * width * hidden,
             transcendentals=0,
         ),
         name="gate_back",
-    )(place, *pieces, normed_two, cot_low, by_gate, by_up)
+    )(place, *pieces, *in_hbm(normed_two, cot_low, by_gate, by_up))
     return (*results, full.reshape(hidden, width))
 
 
@@ -714,10 +866,10 @@
         kernel,
         grid=(row_parts,),
         out_shape=(
-            jax.ShapeDtypeStruct((rows, width), jnp.float32),
-            jax.ShapeDtypeStruct((rows, width), jnp.bfloat16),
-            jax.ShapeDtypeStruct((rows, width), jnp.bfloat16),
-            jax.ShapeDtypeStruct((1, width), jnp.float32),
+            pltpu.HBM((rows, width), jnp.float32),
+            pltpu.HBM((rows, width), jnp.bfloat16),
+            pltpu.HBM((rows, width), jnp.bfloat16),
+            pltpu.HBM((1, width), jnp.float32),
         ),
         in_specs=[
             pl.BlockSpec((2, part, hidden), lambda step: (0, step, 0)),
@@ -729,14 +881,18 @@
         ]
         + [anywhere] * len(earlier),
         out_specs=(block, block, block, pl.BlockSpec((1, width), lambda step: (0, 0))),
-        compiler_params=pltpu.CompilerParams(vmem_limit_bytes=56 * 2**20),
+        compiler_params=pltpu.CompilerParams(vmem_limit_bytes=46 * 2**20),
         cost_estimate=pl.CostEstimate(
             flops=4 * rows * width * hidden + 2 * rows * width * width,
             bytes_accessed=rows * hidden * 4 + 4 * width * hidden + 18 * rows * width,
             transcendentals=0,
         ),
         name="middle_back",
-    )(gates, full_in, middle, cotangent, gain.reshape(1, -1), full_attention, *earlier)
+    )(
+        *in_hbm(gates, full_in, middle, cotangent),
+        gain.reshape(1, -1),
+        *in_hbm(full_attention),
+    )
 
 
 def scalars():
@@ -753,7 +909,7 @@
 
         def body():
             start = pl.multiple_of(pl.program_id(0) * width, 128)
-            weight = held[:, :, pl.ds(start, width)].reshape(width, width)
+            weight = held[..., pl.ds(start, width)].reshape(width, width)
             out_ref[...] = dot_nn(normed_ref[...], weight).astype(jnp.bfloat16)
 
         filled(place_ref, refs[:number], full_ref, held, sems, body)
@@ -762,18 +918,18 @@
         kernel,
         grid=(3,),
         out_shape=(
-            jax.ShapeDtypeStruct((rows, 3 * width), jnp.bfloat16),
-            jax.ShapeDtypeStruct((32, width // 32, columns), jnp.bfloat16),
+            pltpu.HBM((rows, 3 * width), jnp.bfloat16),
+            pltpu.HBM(slab(columns, width), jnp.bfloat16),
         ),
         in_specs=[scalars()]
         + [anywhere] * number
         + [pl.BlockSpec((rows, width), lambda step: (0, 0))],
         out_specs=(pl.BlockSpec((rows, width), lambda step: (0, step)), anywhere),
         scratch_shapes=[
-            pltpu.VMEM((32, width // 32, columns), jnp.bfloat16),
-            pltpu.SemaphoreType.DMA((33,)),
+            pltpu.VMEM(slab(columns, width), jnp.bfloat16),
+            pltpu.SemaphoreType.DMA((9,)),
         ],
-        compiler_params=pltpu.CompilerParams(vmem_limit_bytes=32 * 2**20),
+        compiler_params=pltpu.CompilerParams(vmem_limit_bytes=14 * 2**20),
         cost_estimate=pl.CostEstimate(
             flops=6 * rows * width * width,
             bytes_accessed=8 * rows * width + 4 * columns * width,
@@ -803,7 +959,7 @@
         kernel,
         grid=(2,),
         out_shape=(
-            jax.ShapeDtypeStruct((rows, width), jnp.float32),
+            pltpu.HBM((rows, width), jnp.float32),
             jax.ShapeDtypeStruct((rows, width), jnp.bfloat16),
         ),
         in_specs=[
@@ -814,95 +970,122 @@
         ]
         + [anywhere] * len(earlier),
         out_specs=(block, block),
-        compiler_params=pltpu.CompilerParams(vmem_limit_bytes=32 * 2**20),
+        compiler_params=pltpu.CompilerParams(vmem_limit_bytes=15 * 2**20),
         cost_estimate=pl.CostEstimate(
             flops=2 * rows * width * width,
             bytes_accessed=12 * rows * width + 2 * width * width,
             transcendentals=0,
         ),
         name="middle_forward",
-    )(values, mixed, full_attention, gain.reshape(1, -1), *earlier)
+    )(*in_hbm(values, mixed, full_attention), gain.reshape(1, -1), *earlier)
 
 
 def attention_grads_kernel(
-    place_ref, normed_ref, grads_ref, mixed_ref, low_ref, kept_ref, sent_ref, turned
+    place_ref, normed_ref, grads_ref, mixed_hbm, low_hbm, weight_ref, gain_ref,
+    kept_ref, sent_ref, gain_grad_ref, turned, held, column, mixed_ref, low_ref, sems,
 ):
     step = pl.program_id(0)
     last = pl.num_programs(0) - 1
+    quarter = held.shape[0] // 4
+    copies = [
+        pltpu.make_async_copy(mixed_hbm, mixed_ref, sems.at[0]),
+        pltpu.make_async_copy(low_hbm, low_ref, sems.at[1]),
+    ]
 
     @pl.when(step == 0)
     def _():
+        for copy in copies:
+            copy.start()
         turned_rows(place_ref, normed_ref, turned)
+        column[...] = jnp.zeros_like(column)
 
     @pl.when(step < last)
     def _():
-        split_store(dot_nn(turned[...], grads_ref[0]), kept_ref, sent_ref)
+        held[...] = dot_nn(turned[...], grads_ref[0])
+        split_store(held[...], kept_ref, sent_ref)
+        for outer in range(2):
+            for core in range(2):
+                kept = core ^ 1 ^ place_ref[1]
+                start = pl.multiple_of((2 * kept + outer) * quarter, 16)
+                rows = slice((2 * outer + core) * quarter, (2 * outer + core + 1) * quarter)
+                product = held[pl.ds(start, quarter), :] * weight_ref[rows, :].astype(jnp.float32)
+                parts = [product[:, lane : lane + 128] for lane in range(0, held.shape[1], 128)]
+                column[rows, :] += sum(parts)
 
     @pl.when(step == last)
     def _():
+        for copy in copies:
+            copy.wait()
         turned_rows(place_ref, mixed_ref, turned)
         split_store(dot_nn(turned[...], low_ref[...]), kept_ref, sent_ref)
-
-
-def attention_grads(place, normed, grad_projected, mixed, grad_low):
+        gain_grad_ref[...] = jnp.sum(column[...].T, axis=0, keepdims=True) / gain_ref[...]
+
+
+def attention_grads(place, normed, grad_projected, mixed, grad_low, full_attention, gain):
     rows, width = normed.shape
     whole = pl.BlockSpec((rows, width), lambda step: (0, 0))
+    line = pl.BlockSpec((1, width), lambda step: (0, 0))
     half = pl.BlockSpec((2, width // 4, width), lambda step: (0, 0, step))
-    shape = jax.ShapeDtypeStruct((2, width // 4, 4 * width), jnp.bfloat16)
+    shape = pltpu.HBM((2, width // 4, 4 * width), jnp.bfloat16)
     return pl.pallas_call(
         attention_grads_kernel,
         grid=(4,),
-        out_shape=(shape, shape),
+        out_shape=(shape, shape, pltpu.HBM((1, width), jnp.float32)),
         in_specs=[
             scalars(),
             whole,
             pl.BlockSpec((1, rows, width), lambda step: (jnp.minimum(step, 2), 0, 0)),
-            whole,
-            whole,
+            anywhere,
+            anywhere,
+            pl.BlockSpec((width, width), lambda step: (0, jnp.minimum(step, 2))),
+            line,
         ],
-        out_specs=(half, half),
-        scratch_shapes=[pltpu.VMEM((width, rows), jnp.bfloat16)],
-        compiler_params=pltpu.CompilerParams(vmem_limit_bytes=32 * 2**20),
+        out_specs=(half, half, line),
+        scratch_shapes=[
+            pltpu.VMEM((width, rows), jnp.bfloat16),
+            pltpu.VMEM((width, width), jnp.float32),
+            pltpu.VMEM((width, 128), jnp.float32),
+            pltpu.VMEM((rows, width), jnp.bfloat16),
+            pltpu.VMEM((rows, width), jnp.bfloat16),
+            pltpu.SemaphoreType.DMA((2,)),
+        ],
+        compiler_params=pltpu.CompilerParams(vmem_limit_bytes=36 * 2**20),
         cost_estimate=pl.CostEstimate(
             flops=8 * rows * width * width,
-            bytes_accessed=12 * rows * width + 8 * width * width,
+            bytes_accessed=12 * rows * width + 14 * width * width,
             transcendentals=0,
         ),
         name="attention_grads",
-    )(place, normed, grad_projected, mixed, grad_low)
-
-
-def input_back_kernel(grads_ref, weight_ref, rows_ref, residual_ref, gain_ref, out_ref, gain_grad_ref):
-    width = rows_ref.shape[1]
-    total = dot_nt(grads_ref[0], weight_ref[:, :width])
-    for part in (1, 2):
-        total = total + dot_nt(grads_ref[part], weight_ref[:, part * width : (part + 1) * width])
-    grad, gain_grad = norm_back(total, rows_ref[...], gain_ref[...], residual_ref[...])
-    out_ref[...] = grad
-
-    @pl.when(pl.program_id(0) == 0)
-    def _():
-        gain_grad_ref[...] = gain_grad
-
-    @pl.when(pl.program_id(0) > 0)
-    def _():
-        gain_grad_ref[...] += gain_grad
-
-
-def input_back(grad_projected, full_attention, values, residual, gain, *earlier):
+    )(
+        place,
+        *in_hbm(normed, grad_projected, mixed, grad_low, full_attention),
+        gain.reshape(1, -1),
+    )
+
+
+def input_back(grad_projected, full_qkv, values, residual, gain, doc_rows):
     rows, width = values.shape
-    part = rows // 2
+    part = rows // row_parts
     block = pl.BlockSpec((part, width), lambda step: (step, 0))
 
-    def kernel(*refs):
-        input_back_kernel(*refs[:5], *refs[5 + len(earlier) :])
+    def kernel(
+        grads_ref, weight_ref, rows_ref, residual_ref, gain_ref,
+        doc_ref, query_ref, slots, sems,
+    ):
+        step = pl.program_id(0)
+        total = dot_nt(grads_ref[0], weight_ref[:, :width])
+        for third in (1, 2):
+            columns = slice(third * width, (third + 1) * width)
+            total = total + dot_nt(grads_ref[third], weight_ref[:, columns])
+        slots[step], _ = norm_back(total, rows_ref[...], gain_ref[...], residual_ref[...])
+        emit(slots, (doc_ref, query_ref), sems)
 
     return pl.pallas_call(
         kernel,
-        grid=(2,),
+        grid=(row_parts,),
         out_shape=(
-            jax.ShapeDtypeStruct((rows, width), jnp.float32),
-            jax.ShapeDtypeStruct((1, width), jnp.float32),
+            jax.ShapeDtypeStruct((doc_rows, width), jnp.float32),
+            jax.ShapeDtypeStruct((rows - doc_rows, width), jnp.float32),
         ),
         in_specs=[
             pl.BlockSpec((3, part, width), lambda step: (0, step, 0)),
@@ -910,17 +1093,56 @@
             block,
             block,
             pl.BlockSpec((1, width), lambda step: (0, 0)),
-        ]
-        + [anywhere] * len(earlier),
-        out_specs=(block, pl.BlockSpec((1, width), lambda step: (0, 0))),
-        compiler_params=pltpu.CompilerParams(vmem_limit_bytes=40 * 2**20),
+        ],
+        out_specs=(anywhere, anywhere),
+        scratch_shapes=[
+            pltpu.VMEM((row_parts, part, width), jnp.float32),
+            pltpu.SemaphoreType.DMA((row_parts + 1,)),
+        ],
+        compiler_params=pltpu.CompilerParams(vmem_limit_bytes=30 * 2**20),
         cost_estimate=pl.CostEstimate(
             flops=6 * rows * width * width,
             bytes_accessed=18 * rows * width + 6 * width * width,
             transcendentals=0,
         ),
         name="input_back",
-    )(grad_projected, full_attention, values, residual, gain.reshape(1, -1), *earlier)
+    )(*in_hbm(grad_projected, full_qkv, values, residual), gain.reshape(1, -1))
+
+
+def layer_outputs(middle, activated, full_ff, doc_rows):
+    rows, width = middle.shape
+    hidden = activated.shape[1]
+    part = rows // row_parts
+
+    def kernel(middle_ref, act_ref, weight_ref, doc_ref, query_ref, slots, sems):
+        slots[pl.program_id(0)] = middle_ref[...] + dot_nn(act_ref[...], weight_ref[...])
+        emit(slots, (doc_ref, query_ref), sems)
+
+    return pl.pallas_call(
+        kernel,
+        grid=(row_parts,),
+        out_shape=(
+            jax.ShapeDtypeStruct((doc_rows, width), jnp.float32),
+            jax.ShapeDtypeStruct((rows - doc_rows, width), jnp.float32),
+        ),
+        in_specs=[
+            pl.BlockSpec((part, width), lambda step: (step, 0)),
+            pl.BlockSpec((part, hidden), lambda step: (step, 0)),
+            pl.BlockSpec((hidden, width), lambda step: (0, 0)),
+        ],
+        out_specs=(anywhere, anywhere),
+        scratch_shapes=[
+            pltpu.VMEM((row_parts, part, width), jnp.float32),
+            pltpu.SemaphoreType.DMA((row_parts + 1,)),
+        ],
+        compiler_params=pltpu.CompilerParams(vmem_limit_bytes=24 * 2**20),
+        cost_estimate=pl.CostEstimate(
+            flops=2 * rows * width * hidden,
+            bytes_accessed=8 * rows * width + 2 * hidden * (rows + width),
+            transcendentals=0,
+        ),
+        name="layer_outputs",
+    )(*in_hbm(middle, activated, full_ff))
 
 
 def body(
@@ -977,10 +1199,9 @@
         )
         near_a = gather_near(place, *gather_plane(place, attention_shard, column_a))
         column_i = gather_column(in_shard)
-        core_a = gather_core(*near_a)
         far_a = gather_far(*near_a)
-        column_i, far_a, core_a, ff_shard = together(column_i, far_a, core_a, ff_shard)
-        pieces = gather_order(near_a, far_a, core_a, gather_core(*far_a))
+        column_i, far_a, ff_shard = together(column_i, far_a, ff_shard)
+        pieces = gather_order(near_a, far_a, gather_core(*near_a), gather_core(*far_a))
         plane_i = gather_plane(place, in_shard, column_i)
     else:
         pieces = (split_rows(lax.all_gather(attention_shard, both, axis=0, tiled=True)),)
@@ -990,14 +1211,13 @@
         near_i = gather_near(place, *plane_i)
         far_i = gather_far(*near_i)
         column_f = gather_column(ff_shard)
-        core_i = gather_core(*near_i)
     mixed, doc_probs, query_probs = attend(
         projected, lines, doc_masking, query_masking, group_length
     )
     if routed:
         mixed, far_i, column_f = together(mixed, far_i, column_f)
         plane_f = gather_plane(place, ff_shard, column_f)
-        pieces = gather_order(near_i, far_i, core_i, gather_core(*far_i))
+        pieces = gather_order(near_i, far_i, gather_core(*near_i), gather_core(*far_i))
     else:
         pieces = (split_rows(lax.all_gather(in_shard, both, axis=0, tiled=True)),)
     middle, normed_two = middle_forward(values, mixed, full_attention, ffn_gain)
@@ -1005,14 +1225,17 @@
         pieces, normed_two, plane_f = together(pieces, normed_two, plane_f)
         near_f = gather_near(place, *plane_f)
         far_f = gather_far(*near_f)
+        core_f = gather_core(*near_f)
     activated, by_gate, by_up, kept, sent, full_in = gate_forward(
         place_vector, pieces, normed_two, cot_low
     )
     if routed:
-        far_f, by_gate, kept, sent = together(far_f, by_gate, kept, sent)
-        pieces = gather_order(near_f, far_f, gather_core(*near_f), gather_core(*far_f))
-        ff_grads = Scatter(kept, sent, place)
+        far_f, core_f, by_gate, kept, sent = together(far_f, core_f, by_gate, kept, sent)
+        pieces = gather_order(near_f, far_f, core_f, gather_core(*far_f))
+        ff_grads = NarrowScatter(kept, sent, place_vector)
         got_f = ff_grads.core()
+        pieces, got_f = together(pieces, got_f)
+        near_f = ff_grads.plane(got_f)
     else:
         pieces = (split_rows(lax.all_gather(ff_shard, both, axis=0, tiled=True)),)
         grad_ff = joined_halves(kept, sent)
@@ -1020,9 +1243,9 @@
         place_vector, pieces, normed_two, cot_low, by_gate, by_up
     )
     if routed:
-        gates, kept, sent, got_f = together(gates, kept, sent, got_f)
-        in_grads = Scatter(kept, sent, place)
-        near_f = ff_grads.plane(got_f)
+        gates, kept, sent, near_f = together(gates, kept, sent, near_f)
+        in_grads = Scatter(kept, sent, place_vector)
+        far_f = ff_grads.far(ff_grads.far_sums(got_f, near_f))
         got_i = in_grads.core()
     else:
         grad_in = joined_halves(kept, sent)
@@ -1030,69 +1253,84 @@
         gates, full_in, middle, cotangent, ffn_gain, full_attention
     )
     if routed:
-        grad_mixed, near_f, got_i = together(grad_mixed, near_f, got_i)
-        far_f = ff_grads.far(got_f, near_f)
+        grad_mixed, far_f, got_i = together(grad_mixed, far_f, got_i)
         near_i = in_grads.plane(got_i)
-    grad_projected, grad_lines = attend_back(
-        projected, grad_mixed, doc_probs, query_probs, doc_length
+        shares_f = ff_grads.column(ff_grads.column_sums(got_f, near_f, far_f))
+    grad_projected, grad_table = attend_back(
+        projected, grad_mixed, doc_probs, query_probs, onehot, doc_length
     )
     if routed:
-        grad_projected, grad_lines, far_f, near_i = together(
-            grad_projected, grad_lines, far_f, near_i
+        grad_projected, grad_table, shares_f, near_i = together(
+            grad_projected, grad_table, shares_f, near_i
         )
         far_i = in_grads.far(got_i, near_i)
-        shares_f = ff_grads.column(got_f, near_f, far_f)
-    kept, sent = attention_grads(place_vector, normed, grad_projected, mixed, grad_middle_low)
+    kept, sent, grad_attn_gain = attention_grads(
+        place_vector, normed, grad_projected, mixed, grad_middle_low, full_attention, attn_gain
+    )
+    small = (grad_attn_gain, grad_ffn_gain, grad_table)
+    small = jnp.concatenate([part.reshape(-1) for part in small])
     if routed:
-        kept, sent, far_i = together(kept, sent, far_i)
-        attention = Scatter(kept, sent, place)
+        kept, sent, far_i, small, grad_projected, shares_f, activated = together(
+            kept, sent, far_i, small, grad_projected, shares_f, activated
+        )
+        attention = Scatter(kept, sent, place_vector)
         got_a = attention.core()
-        got_a, shares_f, grad_projected, grad_lines = together(
-            got_a, shares_f, grad_projected, grad_lines
+        small = add_flipped(small, {"dc": 1})
+        sums_i = in_grads.column_sums(got_i, near_i, far_i)
+        got_a, sums_i, small, grad_projected, shares_f, activated = together(
+            got_a, sums_i, small, grad_projected, shares_f, activated
         )
         near_a = attention.plane(got_a)
-        shares_i = in_grads.column(got_i, near_i, far_i)
-    grad_inputs, grad_attn_gain = input_back(
-        grad_projected, full_attention, values, grad_middle, attn_gain
-    )
-    grad_table = jnp.einsum(
-        "pn,hp->nh", onehot, grad_lines.reshape(head_count, 4 * count), precision=highest
-    )
-    small = jnp.concatenate([grad_attn_gain[0], grad_ffn_gain[0], grad_table.reshape(-1)])
+        shares_i = in_grads.column(sums_i)
+        small = add_flipped(small, {"dz": 1})
+    grad_inputs = input_back(
+        grad_projected, full_attention, values, grad_middle, attn_gain, doc_rows
+    )
     if routed:
-        near_a, small, activated = together(near_a, small, activated)
+        near_a, grad_inputs, small, shares_f, shares_i, activated = together(
+            near_a, grad_inputs, small, shares_f, shares_i, activated
+        )
         far_a = attention.far(got_a, near_a)
-        small = add_flipped(small, {"dc": 1}, {"dz": 1})
-    outputs = middle + dot_nn(activated, full_ff)
+        small = add_flipped(small, {"dz": 2})
+        far_a, small, shares_f, shares_i, activated = together(
+            far_a, small, shares_f, shares_i, activated
+        )
+        sums_a = attention.column_sums(got_a, near_a, far_a)
+        sums_a, small, shares_f, shares_i, activated = together(
+            sums_a, small, shares_f, shares_i, activated
+        )
+        shares_a = attention.column(sums_a)
+        small = add_flipped(small, {"dx": 1}, {"dy": 1})
+    outputs = layer_outputs(middle, activated, full_ff, doc_rows)
     if routed:
-        far_a, small, outputs, shares_i = together(far_a, small, outputs, shares_i)
-        shares_a = attention.column(got_a, near_a, far_a)
-        small = add_flipped(small, {"dx": 1}, {"dy": 1}, {"dz": 2})
         ff_grad_shard = summed(*shares_f)
         in_grad_shard = summed(*shares_i)
-        attention_grad_shard = summed(*shares_a)
+        grad_qkv = summed(*[share[:, : 3 * model_width] for share in shares_a])
+        grad_out = summed(*[share[:, 3 * model_width :] for share in shares_a])
     else:
         scatter = functools.partial(
             lax.psum_scatter, axis_name=both, scatter_dimension=0, tiled=True
         )
         ff_grad_shard = scatter(grad_ff)
         in_grad_shard = scatter(grad_in)
-        attention_grad_shard = scatter(joined_halves(kept, sent))
+        grad_attention = scatter(joined_halves(kept, sent))
+        grad_qkv = grad_attention[:, : 3 * model_width]
+        grad_out = grad_attention[:, 3 * model_width :]
         small = lax.psum(small, both)
     in_grad_shard = in_grad_shard.reshape(in_weight.shape[0], -1, 2, tile)
     in_grad_shard = jnp.swapaxes(in_grad_shard, 1, 2).reshape(in_weight.shape)
     return (
-        outputs[:doc_rows].reshape(doc_inputs.shape),
-        outputs[doc_rows:].reshape(query_inputs.shape),
-        grad_inputs[:doc_rows].reshape(doc_inputs.shape),
-        grad_inputs[doc_rows:].reshape(query_inputs.shape),
-        attention_grad_shard[:, : 3 * model_width],
-        attention_grad_shard[:, 3 * model_width :],
+        outputs[0].reshape(doc_inputs.shape),
+        outputs[1].reshape(query_inputs.shape),
+        grad_inputs[0].reshape(doc_inputs.shape),
+        grad_inputs[1].reshape(query_inputs.shape),
+        grad_qkv,
+        grad_out,
         in_grad_shard,
         ff_grad_shard,
         small[:model_width],
         small[model_width : 2 * model_width],
-        small[2 * model_width :].reshape(bias_table.shape),
+        small[2 * model_width :].reshape(head_count, -1).T,
     )
 
 

time: 316 us -> 271 us (0.86)
  local copies, waits for them, and re-layouts: 33.9 us -> 8.23 us
  Pallas kernels: 115 us -> 139 us
  waiting for transfers between devices: 54.1 us -> 35 us
  other arithmetic: 36 us -> 22 us
  matrix products: 5.76 us -> 0.31 us
    pallas_call x7 -> x17, Pallas kernels: 93.8 us -> 114 us  [the longest x9 20.1 us: route(): pl.pallas_call(body, grid_spec=pltpu.PrefetchScalarGridSpec(num_scalar_pr...]
    ppermute x62 -> x60, waiting for transfers between devices: 54.1 us -> 35 us  [swap(): return lax.ppermute(values, both, flip_pairs(**flips))]
    slice x13 -> x8, local copies, waits for them, and re-layouts: 13 us -> 0.81 us  [the longest x2 0.68 us: body(): small[2 * model_width:].reshape(head_count, -1)]
    unnamed x131 -> x50, local copies, waits for them, and re-layouts: 12.2 us -> 3.65 us
    concatenate x3 -> x1, other arithmetic: 7.27 us -> 0.69 us  [body(): small = jnp.concatenate([part.reshape(-1) for part in small])]
    dot_general x2 -> x0, matrix products: 5.44 us -> none  [the longest x1 5.08 us: dot_nn(): return jnp.dot(left, right, preferred_element_type=jnp.float32)]
    add x9 -> x4, other arithmetic: 7.35 us -> 2.18 us  [summed(): total = total + term.astype(jnp.float32)]
    convert_element_type x15 -> x2, other arithmetic: 8.95 us -> 5.04 us  [the longest x1 4.91 us: body(): normed = (values * spread * attn_gain).astype(low)]
  transfers between devices with their start and end apart: 62 -> 60, of which waited for: 20 -> 18; matrix products, arithmetic and copies ran while one was open for 17% -> 8% of each run, Pallas kernels for 37% -> 46%
where the time goes in v3:
time: 271 us; the launch traced here: 270 us
  Pallas kernels  139 us (51%)
  starting transfers between devices  64.1 us (24%)
  waiting for transfers between devices  35 us (13%)
  other arithmetic  22 us (8%)
  local copies, waits for them, and re-layouts  8.23 us (3%)
    ppermute x60, starting transfers between devices, swap(): return lax.ppermute(values, both, flip_pairs(**flips))  64.1 us
    ppermute x60, waiting for transfers between devices, swap(): return lax.ppermute(values, both, flip_pairs(**flips))  35 us
    pallas_call x9, Pallas kernels, route(): pl.pallas_call(body, grid_spec=pltpu.PrefetchScalarGridSpec(num_scalar_pr...  20.1 us
    pallas_call x1, Pallas kernels, gate_back(): pl.pallas_call(kernel, grid=(hidden // tile,), out_shape=(pltpu.HBM((2, r...  17.9 us
    pallas_call x1, Pallas kernels, gate_forward(): pl.pallas_call(kernel, grid=(hidden // tile,), out_shape=(pltpu.HBM((rows...  16.3 us
    pallas_call x1, Pallas kernels, middle_back(): pl.pallas_call(kernel, grid=(row_parts,), out_shape=(pltpu.HBM((rows, wid...  16.1 us
    pallas_call x1, Pallas kernels, attend_back(): pl.pallas_call(functools.partial(attend_back_kernel, docs, length), grid=...  16 us
    pallas_call x1, Pallas kernels, attend(): pl.pallas_call(functools.partial(attend_kernel, docs, length, group), gri...  13.6 us
  transfers between devices with their start and end apart: 60, of which 18 were waited for; matrix products, arithmetic and copies ran while one was open for 8% of the time, Pallas kernels for 46%

profile of v3, /device:TPU:0, one launch (start us, length us, event | category | flops | bytes accessed | tf_op | source)
XLA Modules:
  0.0 270.4 jit_solution(12595447317088794570)
XLA Ops:
  2.7 3.1 %collective-permute-start = (bf16[24,3072]{1,0:T(8,128)(2,1)S(1)}, bf16[24,3072]{1,0:T(8,128)(2,1)}, u32[]{:S(2)}, u32[]{:S(2)}) collective-permute-start(bf16[24,3072]{1,0:T(8,128)(2,1)S(1)} %pad_maximum_fusion.14), channel_id=1, source_target_pairs={{0,2},{1,3},{2,0},{3,1},{4,6},{5,7},{6,4},{7,5},{8,10},{9,11},{10,... | collective-permute-start | bytes 442376 | tf_op jit(solution)/shard_map/ppermute | solution.py:34
  5.8 2.6 collective-permute-start.1
  8.4 2.0 multiply_reduce_fusion
  11.2 4.9 %multiply_convert_fusion = (bf16[896,768]{1,0:T(8,128)(2,1)S(1)}, f32[896,768]{1,0:T(8,128)}, f32[896,768]{1,0:T(8,128)}) fusion(f32[768]{0:T(1024)S(1)} %copy-done.20, f32[896]{0:T(1024)S(1)} %add_rsqrt_fusion, f32[384,768]{1,0:T(8,128)} %bitcast.109, f32[512,768]{1,0:T(8,128)S(1)} %bitcast.105, f32[384,768]{1,0:T(8,128)} %bitcast.110, f32[512,768]{1,0:T(8,128)} %bitcast.106), kind=kLoop, calls=%fused_computation.2 | loop fusion | flops 3440640 | bytes 12392960 | tf_op jit(solution)/shard_map/convert_element_type | solution.py:1185
  16.2 3.5 %fusion.6.refs_9_ = bf16[896,768]{1,0:T(8,128)(2,1)} fusion(f32[384,768]{1,0:T(8,128)} %bitcast.111, f32[512,768]{1,0:T(8,128)} %bitcast.107), kind=kLoop, calls=%fused_computation.62 | loop fusion | flops 2752512 | bytes 4128768 | tf_op jit(solution)/shard_map/convert_element_type | solution.py:1183
  20.9 1.6 collective-permute-start.6
  23.5 1.6 collective-permute-start.8
  25.1 3.8 %collective-permute-done.6 = bf16[2,24,3072]{2,1,0:T(8,128)(2,1)S(1)} collective-permute-done((bf16[2,24,3072]{2,1,0:T(8,128)(2,1)S(1)}, bf16[2,24,3072]{2,1,0:T(8,128)(2,1)S(1)}, u32[]{:S(2)}, u32[]{:S(2)}) %collective-permute-start.6) | collective-permute-done | bytes 294944 | tf_op jit(solution)/shard_map/ppermute | solution.py:34
  29.1 1.6 collective-permute-start.7
  30.7 1.8 collective-permute-done.8
  32.7 2.4 collective-permute-start.3
  35.1 1.9 collective-permute-start.4
  38.5 1.7 collective-permute-done.3
  40.2 9.3 %collective-permute-done.4 = bf16[24,4096]{1,0:T(8,128)(2,1)} collective-permute-done((bf16[24,4096]{1,0:T(8,128)(2,1)S(1)}, bf16[24,4096]{1,0:T(8,128)(2,1)}, u32[]{:S(2)}, u32[]{:S(2)}) %collective-permute-start.4) | collective-permute-done | bytes 196640 | tf_op jit(solution)/shard_map/ppermute | solution.py:34
  50.6 1.1 collective-permute-start.10
  53.4 1.6 collective-permute-start.11
  55.1 7.3 %project.1 = (bf16[896,2304]{1,0:T(8,128)(2,1)}, bf16[2,2,4,2,24,3072]{5,4,3,2,1,0:T(8,128)(2,1)}) custom-call(s32[4]{0:T(128)S(1)} %pad_add_fusion.place_ref, bf16[2,2,24,3072]{3,2,1,0:T(8,128)(2,1)S(1)} %bitcast.83, bf16[2,2,24,3072]{3,2,1,0:T(8,128)(2,1)S(1)} %collective-permute-done.7.refs_1_, bf16[2,2,24,3072]{3,2,1,0:T(8,128)(2,1)S(1)} %pad_maximum_fusion.5.refs_2_, ...), custom_call_target="tpu_custom_call" | custom-call | flops 3170893824 | bytes 14942208 | tf_op jit(solution)/shard_map/project/pallas_call | solution.py:917
  62.3 2.3 collective-permute-done.11
  64.9 1.6 collective-permute-start.16
  67.3 2.4 collective-permute-start.18
  69.7 1.4 collective-permute-start.19
  71.1 1.5 collective-permute-start.20
  73.3 13.6 %attend.1 = (bf16[896,768]{1,0:T(8,128)(2,1)}, f32[12,512,512]{2,1,0:T(8,128)}, f32[12,384,128]{2,1,0:T(8,128)}) custom-call(bf16[896,2304]{1,0:T(8,128)(2,1)} %get-tuple-element.208.q_ref.k_ref.v_ref, bf16[896,2304]{1,0:T(8,128)(2,1)} %get-tuple-element.208.q_ref.k_ref.v_ref, bf16[896,2304]{1,0:T(8,128)(2,1)} %get-tuple-element.208.q_ref.k_ref.v_ref, ...), custom_call_target="tpu_custom_call" | custom-call | flops 1912602624 | bytes 18087936 | tf_op jit(solution)/shard_map/attend/pallas_call | solution.py:462
  88.1 1.5 collective-permute-start.25
  90.3 4.7 %middle_forward.1 = (f32[896,768]{1,0:T(8,128)}, bf16[896,768]{1,0:T(8,128)(2,1)S(1)}) custom-call(f32[896,768]{1,0:T(8,128)} %get-tuple-element.382.refs_0_.rows_ref, bf16[896,768]{1,0:T(8,128)(2,1)} %get-tuple-element.218.refs_1_.mixed_hbm, bf16[768,3072]{1,0:T(8,128)(2,1)} %bitcast.97, f32[1,768]{1,0:T(1,128)S(1)} %reshape.212.refs_3_.refs_4_), custom_call_target="tpu_custom_call" | custom-call | flops 1056964608 | bytes 9437184 | tf_op jit(solution)/shard_map/middle_forward/pallas_call | solution.py:958
  95.1 1.3 collective-permute-done.26
  98.5 16.3 %gate_forward.1 = (bf16[896,2048]{1,0:T(8,128)(2,1)}, f32[896,2048]{1,0:T(8,128)}, f32[896,2048]{1,0:T(8,128)}, bf16[2,512,768]{2,1,0:T(8,128)(2,1)}, bf16[2,512...) custom-call(s32[4]{0:T(128)S(1)} %pad_add_fusion.place_ref, bf16[2,2,24,4096]{3,2,1,0:T(8,128)(2,1)S(1)} %bitcast.80, ...), custom_call_target="tpu_custom_call" | custom-call | flops 8455716864 | bytes 30932992 | tf_op jit(solution)/shard_map/gate_forward/pallas_call | solution.py:730
  115.7 3.2 %collective-permute-done.31.refs_5_ = bf16[2,2,64,768]{3,2,1,0:T(8,128)(2,1)S(1)} collective-permute-done((bf16[2,2,64,768]{3,2,1,0:T(8,128)(2,1)S(1)}, bf16[2,2,64,768]{3,2,1,0:T(8,128)(2,1)S(1)}, u32[]{:S(2)}, u32[]{:S(2)}) %collective-permute-start.31) | collective-permute-done | bytes 393248 | tf_op jit(solution)/shard_map/ppermute | solution.py:34
  119.4 1.9 plane.3
  121.3 1.1 collective-permute-start.34
  122.4 17.9 %gate_back.1 = (bf16[2,896,2048]{2,1,0:T(8,128)(2,1)}, bf16[2,192,4096]{2,1,0:T(8,128)(2,1)}, bf16[2,192,4096]{2,1,0:T(8,128)(2,1)}, bf16[2,2,4,2,64,768]{5,4,3,2,1,0:T(8,128)(2,1)}) custom-call(s32[4]{0:T(128)S(1)} %pad_add_fusion.place_ref, bf16[2,2,64,768]{3,2,1,0:T(8,128)(2,1)S(1)} %bitcast.86, ...), custom_call_target="tpu_custom_call" | custom-call | flops 8455716864 | bytes 34603008 | tf_op jit(solution)/shard_map/gate_back/pallas_call | solution.py:794
  141.1 1.7 far.3
  142.8 1.2 collective-permute-start.35
  144.0 16.1 %middle_back.1 = (f32[896,768]{1,0:T(8,128)}, bf16[896,768]{1,0:T(8,128)(2,1)}, bf16[896,768]{1,0:T(8,128)(2,1)}, f32[1,768]{1,0:T(1,128)}) custom-call(bf16[2,896,2048]{2,1,0:T(8,128)(2,1)} %get-tuple-element.264.refs_0_, bf16[768,4096]{1,0:T(8,128)(2,1)} %bitcast.116, f32[896,768]{1,0:T(8,128)} %get-tuple-element.220.refs_2_.middle_ref, ...), custom_call_target="tpu_custom_call" | custom-call | flops 6694109184 | bytes 26017792 | tf_op jit(solution)/shard_map/middle_back/pallas_call | solution.py:865
  160.1 3.3 %plane.4 = (bf16[2,2,24,4096]{3,2,1,0:T(8,128)(2,1)}, bf16[2,2,24,4096]{3,2,1,0:T(8,128)(2,1)}) custom-call(s32[4]{0:T(128)S(1)} %pad_add_fusion.place_ref, bf16[2,4,2,24,4096]{4,3,2,1,0:T(8,128)(2,1)} %bitcast.87, bf16[2,4,2,24,4096]{4,3,2,1,0:T(8,128)(2,1)S(1)} %bitcast.65, bf16[2,4,2,24,4096]{4,3,2,1,0:T(8,128)(2,1)} %bitcast.88, ...), custom_call_target="tpu_custom_call" | custom-call | bytes 3145728 | tf_op jit(solution)/shard_map/plane/pallas_call | solution.py:182
  163.4 1.5 collective-permute-start.40
  165.6 1.4 copy-done.3
  167.0 1.1 copy-done.5
  169.1 1.8 column.3
  170.9 2.1 collective-permute-start.37
  173.0 1.3 collective-permute-start.38
  174.3 1.4 collective-permute-start.39
  175.6 16.0 %attend_back.1 = (bf16[3,896,768]{2,1,0:T(8,128)(2,1)}, f32[6,2,32]{2,1,0:T(2,128)}) custom-call(bf16[896,2304]{1,0:T(8,128)(2,1)} %get-tuple-element.208.q_ref.k_ref.v_ref, bf16[896,2304]{1,0:T(8,128)(2,1)} %get-tuple-element.208.q_ref.k_ref.v_ref, bf16[896,2304]{1,0:T(8,128)(2,1)} %get-tuple-element.208.q_ref.k_ref.v_ref, ...), custom_call_target="tpu_custom_call" | custom-call | flops 3825205248 | bytes 22216704 | tf_op jit(solution)/shard_map/attend_back/pallas_call | solution.py:608
  191.8 2.9 %far.4 = (bf16[2,24,4096]{2,1,0:T(8,128)(2,1)}, bf16[2,24,4096]{2,1,0:T(8,128)(2,1)}) custom-call(s32[4]{0:T(128)S(1)} %pad_add_fusion.place_ref, bf16[2,4,2,24,4096]{4,3,2,1,0:T(8,128)(2,1)} %bitcast.89, bf16[2,4,2,24,4096]{4,3,2,1,0:T(8,128)(2,1)S(1)} %bitcast.67, bf16[2,2,24,4096]{3,2,1,0:T(8,128)(2,1)} %collective-permute-done.40.refs_2_, ...), custom_call_target="tpu_custom_call" | custom-call | bytes 4718592 | tf_op jit(solution)/shard_map/far/pallas_call | solution.py:182
  194.7 1.6 collective-permute-start.42
  196.8 1.4 reshape.221
  198.2 11.3 %attention_grads.1 = (bf16[2,192,3072]{2,1,0:T(8,128)(2,1)}, bf16[2,192,3072]{2,1,0:T(8,128)(2,1)}, f32[1,768]{1,0:T(1,128)}) custom-call(s32[4]{0:T(128)S(1)} %pad_add_fusion.place_ref, bf16[896,768]{1,0:T(8,128)(2,1)} %copy-done.6, bf16[3,896,768]{2,1,0:T(8,128)(2,1)} %get-tuple-element.318.grads_ref, ...), custom_call_target="tpu_custom_call" | custom-call | flops 4227858432 | bytes 16515072 | tf_op jit(solution)/shard_map/attention_grads/pallas_call | solution.py:1030
  211.4 2.6 column.4
  214.1 1.1 collective-permute-done.45
  215.7 2.1 plane.5
  217.8 1.6 collective-permute-start.46
  220.7 1.2 collective-permute-start.49
  221.9 2.0 collective-permute-start.50
  223.9 2.1 collective-permute-start.51
  226.0 8.6 %input_back.1 = (f32[512,768]{1,0:T(8,128)}, f32[384,768]{1,0:T(8,128)}) custom-call(bf16[3,896,768]{2,1,0:T(8,128)(2,1)} %get-tuple-element.318.grads_ref, bf16[768,3072]{1,0:T(8,128)(2,1)} %bitcast.100, f32[896,768]{1,0:T(8,128)} %get-tuple-element.382.refs_0_.rows_ref, f32[896,768]{1,0:T(8,128)} %get-tuple-element.319.residual_ref, ...), custom_call_target="tpu_custom_call" | custom-call | flops 3170893824 | bytes 15925248 | tf_op jit(solution)/shard_map/input_back/pallas_call | solution.py:1083
  234.7 4.4 %collective-permute-done.50 = bf16[24,4096]{1,0:T(8,128)(2,1)S(1)} collective-permute-done((bf16[24,4096]{1,0:T(8,128)(2,1)S(1)}, bf16[24,4096]{1,0:T(8,128)(2,1)S(1)}, u32[]{:S(2)}, u32[]{:S(2)}) %collective-permute-start.50) | collective-permute-done | bytes 196640 | tf_op jit(solution)/shard_map/ppermute | solution.py:34
  239.1 1.8 far.5
  240.9 1.6 collective-permute-start.52
  243.0 3.8 %collective-permute-start.54 = (f32[1920]{0:T(1024)S(1)}, f32[1920]{0:T(1024)S(1)}, u32[]{:S(2)}, u32[]{:S(2)}) collective-permute-start(f32[1920]{0:T(1024)S(1)} %add.187), channel_id=1, source_target_pairs={{0,4},{1,5},{2,6},{3,7},{4,0},{5,1},{6,2},{7,3},{8,12},{9,13},{10,... | collective-permute-start | bytes 23048 | tf_op jit(solution)/shard_map/ppermute | solution.py:34
  246.8 1.6 collective-permute-done.54
  249.2 2.0 column.5
  251.2 2.2 collective-permute-start.57
  253.5 2.2 collective-permute-start.56
  256.7 7.3 %layer_outputs.1 = (f32[512,768]{1,0:T(8,128)}, f32[384,768]{1,0:T(8,128)}) custom-call(f32[896,768]{1,0:T(8,128)} %get-tuple-element.220.refs_2_.middle_ref, bf16[896,2048]{1,0:T(8,128)(2,1)} %get-tuple-element.362.act_ref, bf16[2048,768]{1,0:T(8,128)(2,1)} %bitcast.117), custom_call_target="tpu_custom_call" | custom-call | flops 2818572288 | bytes 12320768 | tf_op jit(solution)/shard_map/layer_outputs/pallas_call | solution.py:1121
  (197 shorter events, 32.1 us)
Async XLA Ops:
  2.7 17.0 %collective-permute-start = (bf16[24,3072]{1,0:T(8,128)(2,1)S(1)}, bf16[24,3072]{1,0:T(8,128)(2,1)}, u32[]{:S(2)}, u32[]{:S(2)}) collective-permute-start(bf16[24,3072]{1,0:T(8,128)(2,1)S(1)} %pad_maximum_fusion.14), channel_id=1, source_target_pairs={{0,2},{1,3},{2,0},{3,1},{4,6},{5,7},{6,4},{7,5},{8,10},{9,11},{10,... | collective-permute-start | bytes 442376 | tf_op jit(solution)/shard_map/ppermute | solution.py:34
  5.8 14.1 %collective-permute-start.1 = (bf16[24,3072]{1,0:T(8,128)(2,1)S(1)}, bf16[24,3072]{1,0:T(8,128)(2,1)}, u32[]{:S(2)}, u32[]{:S(2)}) collective-permute-start(bf16[24,3072]{1,0:T(8,128)(2,1)S(1)} %pad_maximum_fusion.14), channel_id=1, source_target_pairs={{0,4},{1,5},{2,6},{3,7},{4,0},{5,1},{6,2},{7,3},{8,12},{9,13},{10,... | collective-permute-start | bytes 442376 | tf_op jit(solution)/shard_map/ppermute | solution.py:34
  8.4 11.5 %collective-permute-start.2 = (bf16[24,3072]{1,0:T(8,128)(2,1)S(1)}, bf16[24,3072]{1,0:T(8,128)(2,1)}, u32[]{:S(2)}, u32[]{:S(2)}) collective-permute-start(bf16[24,3072]{1,0:T(8,128)(2,1)S(1)} %pad_maximum_fusion.14), channel_id=1, source_target_pairs={{0,6},{1,7},{2,4},{3,5},{4,2},{5,3},{6,0},{7,1},{8,14},{9,15},{10,... | collective-permute-start | bytes 442376 | tf_op jit(solution)/shard_map/ppermute | solution.py:34
  16.2 38.9 %copy-start.6 = (bf16[896,768]{1,0:T(8,128)(2,1)}, bf16[896,768]{1,0:T(8,128)(2,1)S(1)}, u32[]{:S(2)}) copy-start(bf16[896,768]{1,0:T(8,128)(2,1)S(1)} %get-tuple-element.205.refs_8_.normed_ref) | copy-start | bytes 4128772
  20.9 8.1 %collective-permute-start.6 = (bf16[2,24,3072]{2,1,0:T(8,128)(2,1)S(1)}, bf16[2,24,3072]{2,1,0:T(8,128)(2,1)S(1)}, u32[]{:S(2)}, u32[]{:S(2)}) collective-permute-start(bf16[2,24,3072]{2,1,0:T(8,128)(2,1)S(1)} %pad_maximum_fusion.10), channel_id=1, source_target_pairs={{0,1},{1,0},{2,3},{3,2},{4,5},{5,4},{6,7},{7,6},{8,9},{9,8},{10,11... | collective-permute-start | bytes 884744 | tf_op jit(solution)/shard_map/ppermute | solution.py:34
  23.5 9.0 %collective-permute-start.8 = (bf16[2,24,3072]{2,1,0:T(8,128)(2,1)S(1)}, bf16[2,24,3072]{2,1,0:T(8,128)(2,1)S(1)}, u32[]{:S(2)}, u32[]{:S(2)}) collective-permute-start(bf16[2,24,3072]{2,1,0:T(8,128)(2,1)S(1)} %pad_maximum_fusion.11), channel_id=1, source_target_pairs={{0,16},{1,17},{2,18},{3,19},{4,20},{5,21},{6,22},{7,23},{8,24},{9,... | collective-permute-start | bytes 884744 | tf_op jit(solution)/shard_map/ppermute | solution.py:34
  29.1 20.4 %collective-permute-start.7 = (bf16[2,2,24,3072]{3,2,1,0:T(8,128)(2,1)S(1)}, bf16[2,2,24,3072]{3,2,1,0:T(8,128)(2,1)S(1)}, u32[]{:S(2)}, u32[]{:S(2)}) collective-permute-start(bf16[2,2,24,3072]{3,2,1,0:T(8,128)(2,1)S(1)} %bitcast.81), channel_id=1, source_target_pairs={{0,16},{1,17},{2,18},{3,19},{4,20},{5,21},{6,22},{7,23},{8,24},{9,... | collective-permute-start | bytes 1769480 | tf_op jit(solution)/shard_map/ppermute | solution.py:34
  32.6 17.0 %collective-permute-start.9 = (bf16[2,2,24,3072]{3,2,1,0:T(8,128)(2,1)S(1)}, bf16[2,2,24,3072]{3,2,1,0:T(8,128)(2,1)}, u32[]{:S(2)}, u32[]{:S(2)}) collective-permute-start(bf16[2,2,24,3072]{3,2,1,0:T(8,128)(2,1)S(1)} %pad_maximum_fusion.5.refs_2_), channel_id=1, source_target_pairs={{0,1},{1,0},{2,3},{3,2},{4,5},{5,4},{6,7},{7,6},{8,9},{9,8},{10,11... | collective-permute-start | bytes 1769480 | tf_op jit(solution)/shard_map/ppermute | solution.py:34
  32.7 7.5 %collective-permute-start.3 = (bf16[24,4096]{1,0:T(8,128)(2,1)S(1)}, bf16[24,4096]{1,0:T(8,128)(2,1)}, u32[]{:S(2)}, u32[]{:S(2)}) collective-permute-start(bf16[24,4096]{1,0:T(8,128)(2,1)S(1)} %convert_element_type.125), channel_id=1, source_target_pairs={{0,2},{1,3},{2,0},{3,1},{4,6},{5,7},{6,4},{7,5},{8,10},{9,11},{10,... | collective-permute-start | bytes 589832 | tf_op jit(solution)/shard_map/ppermute | solution.py:34
  35.1 14.5 %collective-permute-start.4 = (bf16[24,4096]{1,0:T(8,128)(2,1)S(1)}, bf16[24,4096]{1,0:T(8,128)(2,1)}, u32[]{:S(2)}, u32[]{:S(2)}) collective-permute-start(bf16[24,4096]{1,0:T(8,128)(2,1)S(1)} %convert_element_type.125), channel_id=1, source_target_pairs={{0,4},{1,5},{2,6},{3,7},{4,0},{5,1},{6,2},{7,3},{8,12},{9,13},{10,... | collective-permute-start | bytes 589832 | tf_op jit(solution)/shard_map/ppermute | solution.py:34
  37.0 12.6 %collective-permute-start.5 = (bf16[24,4096]{1,0:T(8,128)(2,1)S(1)}, bf16[24,4096]{1,0:T(8,128)(2,1)}, u32[]{:S(2)}, u32[]{:S(2)}) collective-permute-start(bf16[24,4096]{1,0:T(8,128)(2,1)S(1)} %convert_element_type.125), channel_id=1, source_target_pairs={{0,6},{1,7},{2,4},{3,5},{4,2},{5,3},{6,0},{7,1},{8,14},{9,15},{10,... | collective-permute-start | bytes 589832 | tf_op jit(solution)/shard_map/ppermute | solution.py:34
  40.2 13.1 %collective-permute-start.12 = (bf16[2,2,24,3072]{3,2,1,0:T(8,128)(2,1)S(1)}, bf16[2,2,24,3072]{3,2,1,0:T(8,128)(2,1)S(1)}, u32[]{:S(2)}, u32[]{:S(2)}) collective-permute-start(bf16[2,2,24,3072]{3,2,1,0:T(8,128)(2,1)S(1)} %bitcast.82), channel_id=1, source_target_pairs={{0,8},{1,9},{2,10},{3,11},{4,12},{5,13},{6,14},{7,15},{8,0},{9,1},... | collective-permute-start | bytes 1769480 | tf_op jit(solution)/shard_map/ppermute | solution.py:34
  49.6 5.5 %collective-permute-start.14 = (bf16[2,2,24,3072]{3,2,1,0:T(8,128)(2,1)S(1)}, bf16[2,2,24,3072]{3,2,1,0:T(8,128)(2,1)S(1)}, u32[]{:S(2)}, u32[]{:S(2)}) collective-permute-start(bf16[2,2,24,3072]{3,2,1,0:T(8,128)(2,1)S(1)} %pad_maximum_fusion.5.refs_2_), channel_id=1, source_target_pairs={{0,8},{1,9},{2,10},{3,11},{4,12},{5,13},{6,14},{7,15},{8,0},{9,1},... | collective-permute-start | bytes 1769480 | tf_op jit(solution)/shard_map/ppermute | solution.py:34
  50.6 11.7 %collective-permute-start.10 = (bf16[2,24,4096]{2,1,0:T(8,128)(2,1)S(1)}, bf16[2,24,4096]{2,1,0:T(8,128)(2,1)S(1)}, u32[]{:S(2)}, u32[]{:S(2)}) collective-permute-start(bf16[2,24,4096]{2,1,0:T(8,128)(2,1)S(1)} %pad_maximum_fusion.6), channel_id=1, source_target_pairs={{0,1},{1,0},{2,3},{3,2},{4,5},{5,4},{6,7},{7,6},{8,9},{9,8},{10,11... | collective-permute-start | bytes 1179656 | tf_op jit(solution)/shard_map/ppermute | solution.py:34
  51.7 3.3 %collective-permute-start.13 = (bf16[2,2,24,3072]{3,2,1,0:T(8,128)(2,1)S(1)}, bf16[2,2,24,3072]{3,2,1,0:T(8,128)(2,1)S(1)}, u32[]{:S(2)}, u32[]{:S(2)}) collective-permute-start(bf16[2,2,24,3072]{3,2,1,0:T(8,128)(2,1)S(1)} %collective-permute-done.7.refs_1_), channel_id=1, source_target_pairs={{0,8},{1,9},{2,10},{3,11},{4,12},{5,13},{6,14},{7,15},{8,0},{9,1},... | collective-permute-start | bytes 1769480 | tf_op jit(solution)/shard_map/ppermute | solution.py:34
  52.0 3.1 %collective-permute-start.15 = (bf16[2,2,24,3072]{3,2,1,0:T(8,128)(2,1)}, bf16[2,2,24,3072]{3,2,1,0:T(8,128)(2,1)S(1)}, u32[]{:S(2)}, u32[]{:S(2)}) collective-permute-start(bf16[2,2,24,3072]{3,2,1,0:T(8,128)(2,1)} %collective-permute-done.9.refs_3_), channel_id=1, source_target_pairs={{0,8},{1,9},{2,10},{3,11},{4,12},{5,13},{6,14},{7,15},{8,0},{9,1},... | collective-permute-start | bytes 1769480 | tf_op jit(solution)/shard_map/ppermute | solution.py:34
  53.4 11.3 %collective-permute-start.11 = (bf16[2,24,4096]{2,1,0:T(8,128)(2,1)S(1)}, bf16[2,24,4096]{2,1,0:T(8,128)(2,1)S(1)}, u32[]{:S(2)}, u32[]{:S(2)}) collective-permute-start(bf16[2,24,4096]{2,1,0:T(8,128)(2,1)S(1)} %pad_maximum_fusion.7), channel_id=1, source_target_pairs={{0,16},{1,17},{2,18},{3,19},{4,20},{5,21},{6,22},{7,23},{8,24},{9,... | collective-permute-start | bytes 1179656 | tf_op jit(solution)/shard_map/ppermute | solution.py:34
  64.9 22.6 %collective-permute-start.16 = (bf16[2,2,24,4096]{3,2,1,0:T(8,128)(2,1)S(1)}, bf16[2,2,24,4096]{3,2,1,0:T(8,128)(2,1)S(1)}, u32[]{:S(2)}, u32[]{:S(2)}) collective-permute-start(bf16[2,2,24,4096]{3,2,1,0:T(8,128)(2,1)S(1)} %bitcast.78), channel_id=1, source_target_pairs={{0,16},{1,17},{2,18},{3,19},{4,20},{5,21},{6,22},{7,23},{8,24},{9,... | collective-permute-start | bytes 2359304 | tf_op jit(solution)/shard_map/ppermute | solution.py:34
  66.6 23.7 %copy-start.21 = (f32[768]{0:T(1024)S(1)}, f32[768]{0:T(1024)}, u32[]{:S(2)}) copy-start(f32[768]{0:T(1024)} %param.24) | copy-start | bytes 9220
  66.7 20.8 %collective-permute-start.17 = (bf16[2,2,24,4096]{3,2,1,0:T(8,128)(2,1)S(1)}, bf16[2,2,24,4096]{3,2,1,0:T(8,128)(2,1)S(1)}, u32[]{:S(2)}, u32[]{:S(2)}) collective-permute-start(bf16[2,2,24,4096]{3,2,1,0:T(8,128)(2,1)S(1)} %pad_maximum_fusion.3.refs_2_), channel_id=1, source_target_pairs={{0,1},{1,0},{2,3},{3,2},{4,5},{5,4},{6,7},{7,6},{8,9},{9,8},{10,11... | collective-permute-start | bytes 2359304 | tf_op jit(solution)/shard_map/ppermute | solution.py:34
  67.3 6.1 %collective-permute-start.18 = (bf16[64,768]{1,0:T(8,128)(2,1)S(1)}, bf16[64,768]{1,0:T(8,128)(2,1)S(1)}, u32[]{:S(2)}, u32[]{:S(2)}) collective-permute-start(bf16[64,768]{1,0:T(8,128)(2,1)S(1)} %convert_element_type.126), channel_id=1, source_target_pairs={{0,2},{1,3},{2,0},{3,1},{4,6},{5,7},{6,4},{7,5},{8,10},{9,11},{10,... | collective-permute-start | bytes 294920 | tf_op jit(solution)/shard_map/ppermute | solution.py:34
  69.7 17.2 %collective-permute-start.19 = (bf16[64,768]{1,0:T(8,128)(2,1)S(1)}, bf16[64,768]{1,0:T(8,128)(2,1)S(1)}, u32[]{:S(2)}, u32[]{:S(2)}) collective-permute-start(bf16[64,768]{1,0:T(8,128)(2,1)S(1)} %convert_element_type.126), channel_id=1, source_target_pairs={{0,4},{1,5},{2,6},{3,7},{4,0},{5,1},{6,2},{7,3},{8,12},{9,13},{10,... | collective-permute-start | bytes 294920 | tf_op jit(solution)/shard_map/ppermute | solution.py:34
  71.1 16.4 %collective-permute-start.20 = (bf16[64,768]{1,0:T(8,128)(2,1)S(1)}, bf16[64,768]{1,0:T(8,128)(2,1)S(1)}, u32[]{:S(2)}, u32[]{:S(2)}) collective-permute-start(bf16[64,768]{1,0:T(8,128)(2,1)S(1)} %convert_element_type.126), channel_id=1, source_target_pairs={{0,6},{1,7},{2,4},{3,5},{4,2},{5,3},{6,0},{7,1},{8,14},{9,15},{10,... | collective-permute-start | bytes 294920 | tf_op jit(solution)/shard_map/ppermute | solution.py:34
  73.3 16.4 %collective-permute-start.21 = (bf16[2,2,24,4096]{3,2,1,0:T(8,128)(2,1)S(1)}, bf16[2,2,24,4096]{3,2,1,0:T(8,128)(2,1)S(1)}, u32[]{:S(2)}, u32[]{:S(2)}) collective-permute-start(bf16[2,2,24,4096]{3,2,1,0:T(8,128)(2,1)S(1)} %bitcast.79), channel_id=1, source_target_pairs={{0,8},{1,9},{2,10},{3,11},{4,12},{5,13},{6,14},{7,15},{8,0},{9,1},... | collective-permute-start | bytes 2359304 | tf_op jit(solution)/shard_map/ppermute | solution.py:34
  86.9 8.1 %collective-permute-start.23 = (bf16[2,2,24,4096]{3,2,1,0:T(8,128)(2,1)S(1)}, bf16[2,2,24,4096]{3,2,1,0:T(8,128)(2,1)S(1)}, u32[]{:S(2)}, u32[]{:S(2)}) collective-permute-start(bf16[2,2,24,4096]{3,2,1,0:T(8,128)(2,1)S(1)} %pad_maximum_fusion.3.refs_2_), channel_id=1, source_target_pairs={{0,8},{1,9},{2,10},{3,11},{4,12},{5,13},{6,14},{7,15},{8,0},{9,1},... | collective-permute-start | bytes 2359304 | tf_op jit(solution)/shard_map/ppermute | solution.py:34
  87.5 8.9 %collective-permute-start.22 = (bf16[2,2,24,4096]{3,2,1,0:T(8,128)(2,1)S(1)}, bf16[2,2,24,4096]{3,2,1,0:T(8,128)(2,1)S(1)}, u32[]{:S(2)}, u32[]{:S(2)}) collective-permute-start(bf16[2,2,24,4096]{3,2,1,0:T(8,128)(2,1)S(1)} %collective-permute-done.16.refs_1_), channel_id=1, source_target_pairs={{0,8},{1,9},{2,10},{3,11},{4,12},{5,13},{6,14},{7,15},{8,0},{9,1},... | collective-permute-start | bytes 2359304 | tf_op jit(solution)/shard_map/ppermute | solution.py:34
  87.6 8.8 %collective-permute-start.24 = (bf16[2,2,24,4096]{3,2,1,0:T(8,128)(2,1)S(1)}, bf16[2,2,24,4096]{3,2,1,0:T(8,128)(2,1)S(1)}, u32[]{:S(2)}, u32[]{:S(2)}) collective-permute-start(bf16[2,2,24,4096]{3,2,1,0:T(8,128)(2,1)S(1)} %collective-permute-done.17.refs_3_), channel_id=1, source_target_pairs={{0,8},{1,9},{2,10},{3,11},{4,12},{5,13},{6,14},{7,15},{8,0},{9,1},... | collective-permute-start | bytes 2359304 | tf_op jit(solution)/shard_map/ppermute | solution.py:34
  88.1 7.0 %collective-permute-start.25 = (bf16[2,64,768]{2,1,0:T(8,128)(2,1)S(1)}, bf16[2,64,768]{2,1,0:T(8,128)(2,1)S(1)}, u32[]{:S(2)}, u32[]{:S(2)}) collective-permute-start(bf16[2,64,768]{2,1,0:T(8,128)(2,1)S(1)} %pad_maximum_fusion.12), channel_id=1, source_target_pairs={{0,1},{1,0},{2,3},{3,2},{4,5},{5,4},{6,7},{7,6},{8,9},{9,8},{10,11... | collective-permute-start | bytes 589832 | tf_op jit(solution)/shard_map/ppermute | solution.py:34
  89.7 6.7 %collective-permute-start.26 = (bf16[2,64,768]{2,1,0:T(8,128)(2,1)S(1)}, bf16[2,64,768]{2,1,0:T(8,128)(2,1)S(1)}, u32[]{:S(2)}, u32[]{:S(2)}) collective-permute-start(bf16[2,64,768]{2,1,0:T(8,128)(2,1)S(1)} %pad_maximum_fusion.13), channel_id=1, source_target_pairs={{0,16},{1,17},{2,18},{3,19},{4,20},{5,21},{6,22},{7,23},{8,24},{9,... | collective-permute-start | bytes 589832 | tf_op jit(solution)/shard_map/ppermute | solution.py:34
  96.6 18.2 %collective-permute-start.27 = (bf16[2,2,64,768]{3,2,1,0:T(8,128)(2,1)S(1)}, bf16[2,2,64,768]{3,2,1,0:T(8,128)(2,1)S(1)}, u32[]{:S(2)}, u32[]{:S(2)}) collective-permute-start(bf16[2,2,64,768]{3,2,1,0:T(8,128)(2,1)S(1)} %bitcast.84), channel_id=1, source_target_pairs={{0,16},{1,17},{2,18},{3,19},{4,20},{5,21},{6,22},{7,23},{8,24},{9,... | collective-permute-start | bytes 1179656 | tf_op jit(solution)/shard_map/ppermute | solution.py:34
  97.1 17.7 %collective-permute-start.29 = (bf16[2,2,64,768]{3,2,1,0:T(8,128)(2,1)S(1)}, bf16[2,2,64,768]{3,2,1,0:T(8,128)(2,1)S(1)}, u32[]{:S(2)}, u32[]{:S(2)}) collective-permute-start(bf16[2,2,64,768]{3,2,1,0:T(8,128)(2,1)S(1)} %bitcast.85), channel_id=1, source_target_pairs={{0,8},{1,9},{2,10},{3,11},{4,12},{5,13},{6,14},{7,15},{8,0},{9,1},... | collective-permute-start | bytes 1179656 | tf_op jit(solution)/shard_map/ppermute | solution.py:34
  97.2 17.6 %collective-permute-start.28 = (bf16[2,2,64,768]{3,2,1,0:T(8,128)(2,1)S(1)}, bf16[2,2,64,768]{3,2,1,0:T(8,128)(2,1)S(1)}, u32[]{:S(2)}, u32[]{:S(2)}) collective-permute-start(bf16[2,2,64,768]{3,2,1,0:T(8,128)(2,1)S(1)} %pad_maximum_fusion.9.refs_2_), channel_id=1, source_target_pairs={{0,1},{1,0},{2,3},{3,2},{4,5},{5,4},{6,7},{7,6},{8,9},{9,8},{10,11... | collective-permute-start | bytes 1179656 | tf_op jit(solution)/shard_map/ppermute | solution.py:34
  98.2 16.6 %collective-permute-start.30 = (bf16[2,2,64,768]{3,2,1,0:T(8,128)(2,1)S(1)}, bf16[2,2,64,768]{3,2,1,0:T(8,128)(2,1)S(1)}, u32[]{:S(2)}, u32[]{:S(2)}) collective-permute-start(bf16[2,2,64,768]{3,2,1,0:T(8,128)(2,1)S(1)} %pad_maximum_fusion.9.refs_2_), channel_id=1, source_target_pairs={{0,8},{1,9},{2,10},{3,11},{4,12},{5,13},{6,14},{7,15},{8,0},{9,1},... | collective-permute-start | bytes 1179656 | tf_op jit(solution)/shard_map/ppermute | solution.py:34
  114.8 4.6 %collective-permute-start.33 = (bf16[2,512,768]{2,1,0:T(8,128)(2,1)}, bf16[2,512,768]{2,1,0:T(8,128)(2,1)S(1)}, u32[]{:S(2)}, u32[]{:S(2)}) collective-permute-start(bf16[2,512,768]{2,1,0:T(8,128)(2,1)} %get-tuple-element.248), channel_id=1, source_target_pairs={{0,8},{1,9},{2,10},{3,11},{4,12},{5,13},{6,14},{7,15},{8,0},{9,1},... | collective-permute-start | bytes 4718600 | tf_op jit(solution)/shard_map/ppermute | solution.py:34
  115.2 3.7 %collective-permute-start.31 = (bf16[2,2,64,768]{3,2,1,0:T(8,128)(2,1)S(1)}, bf16[2,2,64,768]{3,2,1,0:T(8,128)(2,1)S(1)}, u32[]{:S(2)}, u32[]{:S(2)}) collective-permute-start(bf16[2,2,64,768]{3,2,1,0:T(8,128)(2,1)S(1)} %collective-permute-done.27.refs_1_), channel_id=1, source_target_pairs={{0,8},{1,9},{2,10},{3,11},{4,12},{5,13},{6,14},{7,15},{8,0},{9,1},... | collective-permute-start | bytes 1179656 | tf_op jit(solution)/shard_map/ppermute | solution.py:34
  115.4 4.0 %collective-permute-start.32 = (bf16[2,2,64,768]{3,2,1,0:T(8,128)(2,1)S(1)}, bf16[2,2,64,768]{3,2,1,0:T(8,128)(2,1)S(1)}, u32[]{:S(2)}, u32[]{:S(2)}) collective-permute-start(bf16[2,2,64,768]{3,2,1,0:T(8,128)(2,1)S(1)} %collective-permute-done.28.refs_3_), channel_id=1, source_target_pairs={{0,8},{1,9},{2,10},{3,11},{4,12},{5,13},{6,14},{7,15},{8,0},{9,1},... | collective-permute-start | bytes 1179656 | tf_op jit(solution)/shard_map/ppermute | solution.py:34
  119.4 21.7 %copy-start.2 = (bf16[2,512,768]{2,1,0:T(8,128)(2,1)}, bf16[2,512,768]{2,1,0:T(8,128)(2,1)S(1)}, u32[]{:S(2)}) copy-start(bf16[2,512,768]{2,1,0:T(8,128)(2,1)S(1)} %collective-permute-done.33) | copy-start | bytes 4718596
  121.3 19.8 %collective-permute-start.34 = (bf16[2,4,64,768]{3,2,1,0:T(8,128)(2,1)S(1)}, bf16[2,4,64,768]{3,2,1,0:T(8,128)(2,1)S(1)}, u32[]{:S(2)}, u32[]{:S(2)}) collective-permute-start(bf16[2,4,64,768]{3,2,1,0:T(8,128)(2,1)S(1)} %plane.3), channel_id=1, source_target_pairs={{0,1},{1,0},{2,3},{3,2},{4,5},{5,4},{6,7},{7,6},{8,9},{9,8},{10,11... | collective-permute-start | bytes 2359304 | tf_op jit(solution)/shard_map/ppermute | solution.py:34
  141.1 19.0 %collective-permute-start.36 = (bf16[2,192,4096]{2,1,0:T(8,128)(2,1)}, bf16[2,192,4096]{2,1,0:T(8,128)(2,1)S(1)}, u32[]{:S(2)}, u32[]{:S(2)}) collective-permute-start(bf16[2,192,4096]{2,1,0:T(8,128)(2,1)} %get-tuple-element.269), channel_id=1, source_target_pairs={{0,8},{1,9},{2,10},{3,11},{4,12},{5,13},{6,14},{7,15},{8,0},{9,1},... | collective-permute-start | bytes 9437192 | tf_op jit(solution)/shard_map/ppermute | solution.py:34
  142.8 17.3 %collective-permute-start.35 = (bf16[4,64,768]{2,1,0:T(8,128)(2,1)S(1)}, bf16[4,64,768]{2,1,0:T(8,128)(2,1)S(1)}, u32[]{:S(2)}, u32[]{:S(2)}) collective-permute-start(bf16[4,64,768]{2,1,0:T(8,128)(2,1)S(1)} %far.3), channel_id=1, source_target_pairs={{0,16},{1,17},{2,18},{3,19},{4,20},{5,21},{6,22},{7,23},{8,24},{9,... | collective-permute-start | bytes 1179656 | tf_op jit(solution)/shard_map/ppermute | solution.py:34
  163.4 28.3 %collective-permute-start.40 = (bf16[2,2,24,4096]{3,2,1,0:T(8,128)(2,1)}, bf16[2,2,24,4096]{3,2,1,0:T(8,128)(2,1)}, u32[]{:S(2)}, u32[]{:S(2)}) collective-permute-start(bf16[2,2,24,4096]{3,2,1,0:T(8,128)(2,1)} %get-tuple-element.282), channel_id=1, source_target_pairs={{0,1},{1,0},{2,3},{3,2},{4,5},{5,4},{6,7},{7,6},{8,9},{9,8},{10,11... | collective-permute-start | bytes 2359304 | tf_op jit(solution)/shard_map/ppermute | solution.py:34
  164.9 26.9 %collective-permute-start.41 = (bf16[2,2,24,4096]{3,2,1,0:T(8,128)(2,1)}, bf16[2,2,24,4096]{3,2,1,0:T(8,128)(2,1)}, u32[]{:S(2)}, u32[]{:S(2)}) collective-permute-start(bf16[2,2,24,4096]{3,2,1,0:T(8,128)(2,1)} %get-tuple-element.283), channel_id=1, source_target_pairs={{0,16},{1,17},{2,18},{3,19},{4,20},{5,21},{6,22},{7,23},{8,24},{9,... | collective-permute-start | bytes 2359304 | tf_op jit(solution)/shard_map/ppermute | solution.py:34
  170.9 20.8 %copy-start.9 = (f32[64,768]{1,0:T(8,128)}, f32[64,768]{1,0:T(8,128)S(1)}, u32[]{:S(2)}) copy-start(f32[64,768]{1,0:T(8,128)S(1)} %get-tuple-element.376) | copy-start | bytes 589828
  170.9 20.8 %collective-permute-start.37 = (bf16[64,768]{1,0:T(8,128)(2,1)S(1)}, bf16[64,768]{1,0:T(8,128)(2,1)S(1)}, u32[]{:S(2)}, u32[]{:S(2)}) collective-permute-start(bf16[64,768]{1,0:T(8,128)(2,1)S(1)} %get-tuple-element.277), channel_id=1, source_target_pairs={{0,2},{1,3},{2,0},{3,1},{4,6},{5,7},{6,4},{7,5},{8,10},{9,11},{10,... | collective-permute-start | bytes 294920 | tf_op jit(solution)/shard_map/ppermute | solution.py:34
  173.0 18.7 %collective-permute-start.38 = (bf16[64,768]{1,0:T(8,128)(2,1)S(1)}, bf16[64,768]{1,0:T(8,128)(2,1)S(1)}, u32[]{:S(2)}, u32[]{:S(2)}) collective-permute-start(bf16[64,768]{1,0:T(8,128)(2,1)S(1)} %get-tuple-element.278), channel_id=1, source_target_pairs={{0,4},{1,5},{2,6},{3,7},{4,0},{5,1},{6,2},{7,3},{8,12},{9,13},{10,... | collective-permute-start | bytes 294920 | tf_op jit(solution)/shard_map/ppermute | solution.py:34
  174.3 17.5 %collective-permute-start.39 = (bf16[64,768]{1,0:T(8,128)(2,1)S(1)}, bf16[64,768]{1,0:T(8,128)(2,1)S(1)}, u32[]{:S(2)}, u32[]{:S(2)}) collective-permute-start(bf16[64,768]{1,0:T(8,128)(2,1)S(1)} %get-tuple-element.279), channel_id=1, source_target_pairs={{0,6},{1,7},{2,4},{3,5},{4,2},{5,3},{6,0},{7,1},{8,14},{9,15},{10,... | collective-permute-start | bytes 294920 | tf_op jit(solution)/shard_map/ppermute | solution.py:34
  194.7 16.1 %collective-permute-start.42 = (bf16[2,24,4096]{2,1,0:T(8,128)(2,1)}, bf16[2,24,4096]{2,1,0:T(8,128)(2,1)S(1)}, u32[]{:S(2)}, u32[]{:S(2)}) collective-permute-start(bf16[2,24,4096]{2,1,0:T(8,128)(2,1)} %get-tuple-element.290), channel_id=1, source_target_pairs={{0,16},{1,17},{2,18},{3,19},{4,20},{5,21},{6,22},{7,23},{8,24},{9,... | collective-permute-start | bytes 1179656 | tf_op jit(solution)/shard_map/ppermute | solution.py:34
  196.3 14.5 %collective-permute-start.43 = (bf16[2,24,4096]{2,1,0:T(8,128)(2,1)}, bf16[2,24,4096]{2,1,0:T(8,128)(2,1)}, u32[]{:S(2)}, u32[]{:S(2)}) collective-permute-start(bf16[2,24,4096]{2,1,0:T(8,128)(2,1)} %get-tuple-element.291), channel_id=1, source_target_pairs={{0,1},{1,0},{2,3},{3,2},{4,5},{5,4},{6,7},{7,6},{8,9},{9,8},{10,11... | collective-permute-start | bytes 1179656 | tf_op jit(solution)/shard_map/ppermute | solution.py:34
  210.9 4.8 %collective-permute-start.44 = (bf16[2,192,3072]{2,1,0:T(8,128)(2,1)}, bf16[2,192,3072]{2,1,0:T(8,128)(2,1)S(1)}, u32[]{:S(2)}, u32[]{:S(2)}) collective-permute-start(bf16[2,192,3072]{2,1,0:T(8,128)(2,1)} %get-tuple-element.301), channel_id=1, source_target_pairs={{0,8},{1,9},{2,10},{3,11},{4,12},{5,13},{6,14},{7,15},{8,0},{9,1},... | collective-permute-start | bytes 7077896 | tf_op jit(solution)/shard_map/ppermute | solution.py:34
  210.9 4.2 %collective-permute-start.45 = (f32[1920]{0:T(1024)S(1)}, f32[1920]{0:T(1024)S(1)}, u32[]{:S(2)}, u32[]{:S(2)}) collective-permute-start(f32[1920]{0:T(1024)S(1)} %pad_maximum_fusion.15), channel_id=1, source_target_pairs={{0,8},{1,9},{2,10},{3,11},{4,12},{5,13},{6,14},{7,15},{8,0},{9,1},... | collective-permute-start | bytes 23048 | tf_op jit(solution)/shard_map/ppermute | solution.py:34
  217.8 21.3 %collective-permute-start.46 = (bf16[2,2,24,3072]{3,2,1,0:T(8,128)(2,1)S(1)}, bf16[2,2,24,3072]{3,2,1,0:T(8,128)(2,1)S(1)}, u32[]{:S(2)}, u32[]{:S(2)}) collective-permute-start(bf16[2,2,24,3072]{3,2,1,0:T(8,128)(2,1)S(1)} %get-tuple-element.316), channel_id=1, source_target_pairs={{0,1},{1,0},{2,3},{3,2},{4,5},{5,4},{6,7},{7,6},{8,9},{9,8},{10,11... | collective-permute-start | bytes 1769480 | tf_op jit(solution)/shard_map/ppermute | solution.py:34
  219.4 19.7 %collective-permute-start.47 = (bf16[2,2,24,3072]{3,2,1,0:T(8,128)(2,1)S(1)}, bf16[2,2,24,3072]{3,2,1,0:T(8,128)(2,1)S(1)}, u32[]{:S(2)}, u32[]{:S(2)}) collective-permute-start(bf16[2,2,24,3072]{3,2,1,0:T(8,128)(2,1)S(1)} %get-tuple-element.317), channel_id=1, source_target_pairs={{0,16},{1,17},{2,18},{3,19},{4,20},{5,21},{6,22},{7,23},{8,24},{9,... | collective-permute-start | bytes 1769480 | tf_op jit(solution)/shard_map/ppermute | solution.py:34
  219.9 4.0 %collective-permute-start.48 = (f32[1920]{0:T(1024)S(1)}, f32[1920]{0:T(1024)S(1)}, u32[]{:S(2)}, u32[]{:S(2)}) collective-permute-start(f32[1920]{0:T(1024)S(1)} %add.186), channel_id=1, source_target_pairs={{0,2},{1,3},{2,0},{3,1},{4,6},{5,7},{6,4},{7,5},{8,10},{9,11},{10,... | collective-permute-start | bytes 23048 | tf_op jit(solution)/shard_map/ppermute | solution.py:34
  220.7 14.0 %collective-permute-start.49 = (bf16[24,4096]{1,0:T(8,128)(2,1)S(1)}, bf16[24,4096]{1,0:T(8,128)(2,1)S(1)}, u32[]{:S(2)}, u32[]{:S(2)}) collective-permute-start(bf16[24,4096]{1,0:T(8,128)(2,1)S(1)} %get-tuple-element.328), channel_id=1, source_target_pairs={{0,2},{1,3},{2,0},{3,1},{4,6},{5,7},{6,4},{7,5},{8,10},{9,11},{10,... | collective-permute-start | bytes 589832 | tf_op jit(solution)/shard_map/ppermute | solution.py:34
  221.9 17.2 %collective-permute-start.50 = (bf16[24,4096]{1,0:T(8,128)(2,1)S(1)}, bf16[24,4096]{1,0:T(8,128)(2,1)S(1)}, u32[]{:S(2)}, u32[]{:S(2)}) collective-permute-start(bf16[24,4096]{1,0:T(8,128)(2,1)S(1)} %get-tuple-element.329), channel_id=1, source_target_pairs={{0,4},{1,5},{2,6},{3,7},{4,0},{5,1},{6,2},{7,3},{8,12},{9,13},{10,... | collective-permute-start | bytes 589832 | tf_op jit(solution)/shard_map/ppermute | solution.py:34
  223.9 15.2 %collective-permute-start.51 = (bf16[24,4096]{1,0:T(8,128)(2,1)S(1)}, bf16[24,4096]{1,0:T(8,128)(2,1)S(1)}, u32[]{:S(2)}, u32[]{:S(2)}) collective-permute-start(bf16[24,4096]{1,0:T(8,128)(2,1)S(1)} %get-tuple-element.330), channel_id=1, source_target_pairs={{0,6},{1,7},{2,4},{3,5},{4,2},{5,3},{6,0},{7,1},{8,14},{9,15},{10,... | collective-permute-start | bytes 589832 | tf_op jit(solution)/shard_map/ppermute | solution.py:34
  240.9 7.6 %collective-permute-start.52 = (bf16[2,24,3072]{2,1,0:T(8,128)(2,1)S(1)}, bf16[2,24,3072]{2,1,0:T(8,128)(2,1)S(1)}, u32[]{:S(2)}, u32[]{:S(2)}) collective-permute-start(bf16[2,24,3072]{2,1,0:T(8,128)(2,1)S(1)} %get-tuple-element.334), channel_id=1, source_target_pairs={{0,16},{1,17},{2,18},{3,19},{4,20},{5,21},{6,22},{7,23},{8,24},{9,... | collective-permute-start | bytes 884744 | tf_op jit(solution)/shard_map/ppermute | solution.py:34
  242.5 6.7 %collective-permute-start.53 = (bf16[2,24,3072]{2,1,0:T(8,128)(2,1)S(1)}, bf16[2,24,3072]{2,1,0:T(8,128)(2,1)S(1)}, u32[]{:S(2)}, u32[]{:S(2)}) collective-permute-start(bf16[2,24,3072]{2,1,0:T(8,128)(2,1)S(1)} %get-tuple-element.335), channel_id=1, source_target_pairs={{0,1},{1,0},{2,3},{3,2},{4,5},{5,4},{6,7},{7,6},{8,9},{9,8},{10,11... | collective-permute-start | bytes 884744 | tf_op jit(solution)/shard_map/ppermute | solution.py:34
  243.0 5.4 %collective-permute-start.54 = (f32[1920]{0:T(1024)S(1)}, f32[1920]{0:T(1024)S(1)}, u32[]{:S(2)}, u32[]{:S(2)}) collective-permute-start(f32[1920]{0:T(1024)S(1)} %add.187), channel_id=1, source_target_pairs={{0,4},{1,5},{2,6},{3,7},{4,0},{5,1},{6,2},{7,3},{8,12},{9,13},{10,... | collective-permute-start | bytes 23048 | tf_op jit(solution)/shard_map/ppermute | solution.py:34
  251.2 17.7 %collective-permute-start.57 = (bf16[24,3072]{1,0:T(8,128)(2,1)S(1)}, bf16[24,3072]{1,0:T(8,128)(2,1)S(1)}, u32[]{:S(2)}, u32[]{:S(2)}) collective-permute-start(bf16[24,3072]{1,0:T(8,128)(2,1)S(1)} %get-tuple-element.371), channel_id=1, source_target_pairs={{0,6},{1,7},{2,4},{3,5},{4,2},{5,3},{6,0},{7,1},{8,14},{9,15},{10,... | collective-permute-start | bytes 442376 | tf_op jit(solution)/shard_map/ppermute | solution.py:34
  253.5 15.5 %collective-permute-start.56 = (bf16[24,3072]{1,0:T(8,128)(2,1)S(1)}, bf16[24,3072]{1,0:T(8,128)(2,1)S(1)}, u32[]{:S(2)}, u32[]{:S(2)}) collective-permute-start(bf16[24,3072]{1,0:T(8,128)(2,1)S(1)} %get-tuple-element.370), channel_id=1, source_target_pairs={{0,4},{1,5},{2,6},{3,7},{4,0},{5,1},{6,2},{7,3},{8,12},{9,13},{10,... | collective-permute-start | bytes 442376 | tf_op jit(solution)/shard_map/ppermute | solution.py:34
  255.6 13.4 %collective-permute-start.55 = (bf16[24,3072]{1,0:T(8,128)(2,1)S(1)}, bf16[24,3072]{1,0:T(8,128)(2,1)S(1)}, u32[]{:S(2)}, u32[]{:S(2)}) collective-permute-start(bf16[24,3072]{1,0:T(8,128)(2,1)S(1)} %get-tuple-element.369), channel_id=1, source_target_pairs={{0,2},{1,3},{2,0},{3,1},{4,6},{5,7},{6,4},{7,5},{8,10},{9,11},{10,... | collective-permute-start | bytes 442376 | tf_op jit(solution)/shard_map/ppermute | solution.py:34
  256.0 7.9 %collective-permute-start.58 = (f32[1920]{0:T(1024)S(1)}, f32[1920]{0:T(1024)S(1)}, u32[]{:S(2)}, u32[]{:S(2)}) collective-permute-start(f32[1920]{0:T(1024)S(1)} %add.188), channel_id=1, source_target_pairs={{0,1},{1,0},{2,3},{3,2},{4,5},{5,4},{6,7},{7,6},{8,9},{9,8},{10,11... | collective-permute-start | bytes 23048 | tf_op jit(solution)/shard_map/ppermute | solution.py:34
  264.0 3.7 %collective-permute-start.59 = (f32[1920]{0:T(1024)S(1)}, f32[1920]{0:T(1024)S(1)}, u32[]{:S(2)}, u32[]{:S(2)}) collective-permute-start(f32[1920]{0:T(1024)S(1)} %add.201), channel_id=1, source_target_pairs={{0,16},{1,17},{2,18},{3,19},{4,20},{5,21},{6,22},{7,23},{8,24},{9,... | collective-permute-start | bytes 23048 | tf_op jit(solution)/shard_map/ppermute | solution.py:34
  (21 other events, 145.8 us)

commit v4 on v3

--- a/solution.py
+++ b/solution.py
@@ -56,7 +56,7 @@
     return lax.optimization_barrier(values)
 
 
-def fill_copies(place_ref, pieces, target, sems):
+def fill_copies(place_ref, pieces, target, sems, by_column):
     if len(pieces) == 1:
         return [pltpu.make_async_copy(pieces[0], target, sems.at[0])]
     y, c, z, x = place_ref[0], place_ref[1], place_ref[2], place_ref[3]
@@ -65,7 +65,9 @@
     for number, piece in enumerate(pieces):
         core = c ^ (number // 4)
         kind = number % 4
-        if kind < 2:
+        if by_column:
+            where = target.at[:, core, z ^ kind]
+        elif kind < 2:
             where = target.at[y ^ kind, core, pl.ds(even, 2)]
         else:
             where = target.at[:, core, pl.ds(even ^ 2, 2), x ^ (kind - 2)]
@@ -73,15 +75,17 @@
     return copies
 
 
-def filled(place_ref, pieces, full_ref, held, sems, body):
+def filled(place_ref, pieces, full_ref, held, sems, body, meanwhile=None, by_column=False):
     step = pl.program_id(0)
     kept = pltpu.make_async_copy(held, full_ref, sems.at[8])
 
     @pl.when(step == 0)
     def _():
-        copies = fill_copies(place_ref, pieces, held, sems)
+        copies = fill_copies(place_ref, pieces, held, sems, by_column)
         for copy in copies:
             copy.start()
+        if meanwhile is not None:
+            meanwhile()
         for copy in copies:
             copy.wait()
         kept.start()
@@ -139,7 +143,8 @@
 
 
 def gather_column(shard):
-    return tuple(swap(shard, dz=flip) for flip in (1, 2, 3))
+    two, three, one = [swap(shard, dz=flip) for flip in (2, 3, 1)]
+    return one, two, three
 
 
 def gather_plane(place, shard, column):
@@ -157,6 +162,10 @@
 
 def gather_far(first, second):
     return swap(first, dy=1), swap(second, dx=1)
+
+
+def gather_others(own, second):
+    return swap(own, dz=1), swap(second, dz=1)
 
 
 def gather_core(*pieces):
@@ -229,7 +238,7 @@
         return jax.ShapeDtypeStruct((*lead, *self.block), dtype)
 
     def both(self, got, lead, pick):
-        return [(in_hbm(self.kept)[0], lead, pick), (got, lead, pick)]
+        return [(*in_hbm(self.kept), lead, pick), (got, lead, pick)]
 
     def core(self):
         return swap(self.sent, dc=1).reshape(self.shape)
@@ -297,11 +306,15 @@
 
 
 class NarrowScatter(Scatter):
+    def both(self, got, lead, pick, pinned=True):
+        got = in_hbm(got)[0] if pinned else got
+        return [(*in_hbm(self.kept), lead, pick), (got, lead, pick)]
+
     def plane(self, got):
         def body(place_ref, *refs):
             store_sum(refs[2], *refs[0:2])
 
-        sources = self.both(got, (2, 4, 1), lambda where: (0, 0, 1 - where[3]))
+        sources = self.both(got, (2, 4, 1), lambda where: (0, 0, 1 - where[3]), False)
         target = whole_block(self.target(2, 4))
         (sums,) = route("plane", self.place, sources, [target], body)
         return swap(sums, dx=1)
@@ -463,7 +476,7 @@
         functools.partial(attend_kernel, docs, length, group),
         grid=(pairs,),
         out_shape=(
-            pltpu.HBM((rows, width), jnp.bfloat16),
+            jax.ShapeDtypeStruct((rows, width), jnp.bfloat16),
             pltpu.HBM((2 * pairs, docs * length, length), jnp.float32),
             pltpu.HBM((2 * pairs, query_rows, count), jnp.float32),
         ),
@@ -759,11 +772,6 @@
     place_ref, n2_ref, cot_ref, ff, by_gate_ref, by_up_ref, out_ref, kept_ref, sent_ref, turned
 ):
     step = pl.program_id(0)
-
-    @pl.when(step == 0)
-    def _():
-        turned_rows(place_ref, n2_ref, turned)
-
     weight = ff[step // 2, step % 2].reshape(tile, ff.shape[-1])
     incoming = dot_nt(cot_ref[...], weight)
     by_gate = (incoming * by_gate_ref[...]).astype(jnp.bfloat16)
@@ -789,6 +797,7 @@
             lambda: gate_back_kernel(
                 place_ref, n2_ref, cot_ref, held, gate_ref, up_ref, *outs, turned
             ),
+            lambda: turned_rows(place_ref, n2_ref, turned), True,
         )
 
     *results, full = pl.pallas_call(
@@ -832,55 +841,91 @@
 
 
 def middle_back_kernel(
-    gates_ref, weight_ref, middle_ref, cot_ref, gain_ref, out_weight_ref,
-    grad_ref, low_ref, mixed_ref, gain_grad_ref,
+    gates_hbm, weight_hbm, out_weight_hbm, middle_hbm, cot_hbm, gain_ref,
+    grad_hbm, low_hbm, mixed_hbm, gain_grad_ref,
+    gates, weight, out_weight, middle, cot, total, low, mixed, sems,
 ):
-    hidden = gates_ref.shape[2]
-    total = dot_nt(gates_ref[0], weight_ref[:, :hidden])
-    total = total + dot_nt(gates_ref[1], weight_ref[:, hidden:])
-    grad, gain_grad = norm_back(total, middle_ref[...], gain_ref[...], cot_ref[...])
-    grad_ref[...] = grad
-    low_ref[...] = grad.astype(jnp.bfloat16)
-
-    @pl.when(pl.program_id(0) == 0)
-    def _():
-        gain_grad_ref[...] = gain_grad
-
-    @pl.when(pl.program_id(0) > 0)
-    def _():
-        gain_grad_ref[...] += gain_grad
-
-    mixed_ref[...] = dot_nt(low_ref[...], out_weight_ref[...]).astype(jnp.bfloat16)
-
-
-def middle_back(gates, full_in, middle, cotangent, gain, full_attention, *earlier):
+    rows, width = total.shape
+    hidden = gates.shape[2]
+    wide = hidden // 2
+    arrivals = []
+
+    def bring(source, target):
+        copy = pltpu.make_async_copy(source, target, sems.at[len(arrivals)])
+        copy.start()
+        arrivals.append(copy)
+
+    for part in range(4):
+        columns = pl.ds(part % 2 * wide, wide)
+        bring(gates_hbm.at[part // 2, :, columns], gates.at[part // 2, :, columns])
+        columns = pl.ds(part * wide, wide)
+        bring(weight_hbm.at[:, columns], weight.at[:, columns])
+    bring(middle_hbm, middle)
+    bring(cot_hbm, cot)
+    bring(out_weight_hbm.at[:, pl.ds(3 * width, width)], out_weight)
+    for part in range(4):
+        arrivals[2 * part].wait()
+        arrivals[2 * part + 1].wait()
+        columns = slice(part % 2 * wide, part % 2 * wide + wide)
+        product = dot_nt(
+            gates[part // 2, :, columns], weight[:, part * wide : part * wide + wide]
+        )
+        if part == 0:
+            total[...] = product
+        else:
+            total[...] += product
+    for copy in arrivals[8:]:
+        copy.wait()
+    leaving = []
+    for half in range(2):
+        places = slice(half * rows // 2, (half + 1) * rows // 2)
+        grad, gain_grad = norm_back(
+            total[places, :], middle[places, :], gain_ref[...], cot[places, :]
+        )
+        total[places, :] = grad
+        low[places, :] = grad.astype(jnp.bfloat16)
+        if half == 0:
+            gain_grad_ref[...] = gain_grad
+        else:
+            gain_grad_ref[...] += gain_grad
+        mixed[places, :] = dot_nt(low[places, :], out_weight[...]).astype(jnp.bfloat16)
+        places = pl.ds(half * rows // 2, rows // 2)
+        for source, target in ((total, grad_hbm), (low, low_hbm), (mixed, mixed_hbm)):
+            copy = pltpu.make_async_copy(
+                source.at[places], target.at[places], sems.at[len(arrivals) + len(leaving)]
+            )
+            copy.start()
+            leaving.append(copy)
+    for copy in leaving:
+        copy.wait()
+
+
+def middle_back(gates, full_in, middle, cotangent, gain, full_attention):
     rows, width = middle.shape
     hidden = gates.shape[2]
-    part = rows // row_parts
-    block = pl.BlockSpec((part, width), lambda step: (step, 0))
-
-    def kernel(*refs):
-        middle_back_kernel(*refs[:6], *refs[6 + len(earlier) :])
-
+    low = jnp.bfloat16
+    line = pl.BlockSpec(memory_space=pltpu.VMEM)
     return pl.pallas_call(
-        kernel,
-        grid=(row_parts,),
+        middle_back_kernel,
         out_shape=(
             pltpu.HBM((rows, width), jnp.float32),
-            pltpu.HBM((rows, width), jnp.bfloat16),
-            pltpu.HBM((rows, width), jnp.bfloat16),
-            pltpu.HBM((1, width), jnp.float32),
-        ),
-        in_specs=[
-            pl.BlockSpec((2, part, hidden), lambda step: (0, step, 0)),
-            pl.BlockSpec((width, 2 * hidden), lambda step: (0, 0)),
-            block,
-            block,
-            pl.BlockSpec((1, width), lambda step: (0, 0)),
-            pl.BlockSpec((width, width), lambda step: (0, 3)),
-        ]
-        + [anywhere] * len(earlier),
-        out_specs=(block, block, block, pl.BlockSpec((1, width), lambda step: (0, 0))),
+            pltpu.HBM((rows, width), low),
+            pltpu.HBM((rows, width), low),
+            jax.ShapeDtypeStruct((1, width), jnp.float32),
+        ),
+        in_specs=[anywhere] * 5 + [line],
+        out_specs=(anywhere, anywhere, anywhere, line),
+        scratch_shapes=[
+            pltpu.VMEM((2, rows, hidden), low),
+            pltpu.VMEM((width, 2 * hidden), low),
+            pltpu.VMEM((width, width), low),
+            pltpu.VMEM((rows, width), jnp.float32),
+            pltpu.VMEM((rows, width), jnp.float32),
+            pltpu.VMEM((rows, width), jnp.float32),
+            pltpu.VMEM((rows, width), low),
+            pltpu.VMEM((rows, width), low),
+            pltpu.SemaphoreType.DMA((17,)),
+        ],
         compiler_params=pltpu.CompilerParams(vmem_limit_bytes=46 * 2**20),
         cost_estimate=pl.CostEstimate(
             flops=4 * rows * width * hidden + 2 * rows * width * width,
@@ -888,15 +933,55 @@
             transcendentals=0,
         ),
         name="middle_back",
-    )(
-        *in_hbm(gates, full_in, middle, cotangent),
-        gain.reshape(1, -1),
-        *in_hbm(full_attention),
-    )
+    )(*in_hbm(gates, full_in, full_attention, middle, cotangent), gain.reshape(1, -1))
 
 
 def scalars():
     return pl.BlockSpec(memory_space=pltpu.SMEM)
+
+
+def by_parts(name, first, second, kinds, body, *extra):
+    width = first.shape[1]
+    rows = first.shape[0] + second.shape[0]
+    starts = first.shape[0] // count
+
+    def kernel(first_ref, second_ref, *refs):
+        @pl.when(pl.program_id(0) < starts)
+        def _():
+            body(first_ref, *refs)
+
+        @pl.when(pl.program_id(0) >= starts)
+        def _():
+            body(second_ref, *refs)
+
+    return pl.pallas_call(
+        kernel,
+        grid=(rows // count,),
+        out_shape=[pltpu.HBM((rows, width), kind) for kind in kinds],
+        in_specs=[
+            pl.BlockSpec((count, width), lambda step: (jnp.minimum(step, starts - 1), 0)),
+            pl.BlockSpec((count, width), lambda step: (jnp.maximum(step - starts, 0), 0)),
+        ]
+        + [pl.BlockSpec(line.shape, lambda step: (0, 0)) for line in extra],
+        out_specs=[pl.BlockSpec((count, width), lambda step: (step, 0))] * len(kinds),
+        compiler_params=pltpu.CompilerParams(vmem_limit_bytes=20 * 2**20),
+        cost_estimate=pl.CostEstimate(
+            flops=4 * rows * width, bytes_accessed=10 * rows * width, transcendentals=rows
+        ),
+        name=name,
+    )(*in_hbm(first, second), *extra)
+
+
+def norm_body(rows_ref, gain_ref, values_ref, normed_ref):
+    values = rows_ref[...]
+    spread = lax.rsqrt(jnp.mean(values * values, axis=-1, keepdims=True) + epsilon)
+    values_ref[...] = values
+    normed_ref[...] = (values * spread * gain_ref[...]).astype(jnp.bfloat16)
+
+
+def round_body(rows_ref, values_ref, low_ref):
+    values_ref[...] = rows_ref[...]
+    low_ref[...] = rows_ref[...].astype(jnp.bfloat16)
 
 
 def project(place, pieces, normed):
@@ -977,16 +1062,17 @@
             transcendentals=0,
         ),
         name="middle_forward",
-    )(*in_hbm(values, mixed, full_attention), gain.reshape(1, -1), *earlier)
+    )(*in_hbm(values), mixed, *in_hbm(full_attention), gain.reshape(1, -1), *earlier)
 
 
 def attention_grads_kernel(
-    place_ref, normed_ref, grads_ref, mixed_hbm, low_hbm, weight_ref, gain_ref,
-    kept_ref, sent_ref, gain_grad_ref, turned, held, column, mixed_ref, low_ref, sems,
+    place_ref, normed_ref, grads_ref, mixed_hbm, low_hbm, weight_0, weight_1, weight_2, weight_3,
+    gain_ref, ffn_ref, table_ref, kept_ref, sent_ref, small_ref,
+    turned, column, ordered, mixed_ref, low_ref, sems,
 ):
     step = pl.program_id(0)
     last = pl.num_programs(0) - 1
-    quarter = held.shape[0] // 4
+    quarter = column.shape[0] // 4
     copies = [
         pltpu.make_async_copy(mixed_hbm, mixed_ref, sems.at[0]),
         pltpu.make_async_copy(low_hbm, low_ref, sems.at[1]),
@@ -1001,16 +1087,13 @@
 
     @pl.when(step < last)
     def _():
-        held[...] = dot_nn(turned[...], grads_ref[0])
-        split_store(held[...], kept_ref, sent_ref)
-        for outer in range(2):
-            for core in range(2):
-                kept = core ^ 1 ^ place_ref[1]
-                start = pl.multiple_of((2 * kept + outer) * quarter, 16)
-                rows = slice((2 * outer + core) * quarter, (2 * outer + core + 1) * quarter)
-                product = held[pl.ds(start, quarter), :] * weight_ref[rows, :].astype(jnp.float32)
-                parts = [product[:, lane : lane + 128] for lane in range(0, held.shape[1], 128)]
-                column[rows, :] += sum(parts)
+        grads = dot_nn(turned[...], grads_ref[0])
+        split_store(grads, kept_ref, sent_ref)
+        for number, weight in enumerate((weight_0, weight_1, weight_2, weight_3)):
+            rows = slice(number * quarter, (number + 1) * quarter)
+            product = grads[rows, :] * weight[...].astype(jnp.float32)
+            parts = [product[:, lane : lane + 128] for lane in range(0, grads.shape[1], 128)]
+            column[rows, :] += sum(parts)
 
     @pl.when(step == last)
     def _():
@@ -1018,37 +1101,71 @@
             copy.wait()
         turned_rows(place_ref, mixed_ref, turned)
         split_store(dot_nn(turned[...], low_ref[...]), kept_ref, sent_ref)
-        gain_grad_ref[...] = jnp.sum(column[...].T, axis=0, keepdims=True) / gain_ref[...]
-
-
-def attention_grads(place, normed, grad_projected, mixed, grad_low, full_attention, gain):
+        for number in range(4):
+            row = quarter_owner(number, place_ref[1])
+            start = pl.multiple_of(row * quarter, 16)
+            ordered[pl.ds(start, quarter), :] = column[number * quarter : (number + 1) * quarter, :]
+        gain_grad = jnp.sum(ordered[...].T, axis=0, keepdims=True) / gain_ref[...]
+        small_ref[...] = jnp.zeros_like(small_ref)
+        lines = gain_grad.shape[1] // 128
+        for number, line in enumerate((gain_grad, ffn_ref[...])):
+            for part in range(lines):
+                row = number * lines + part
+                small_ref[row : row + 1, :] = line[:, part * 128 : (part + 1) * 128]
+        table = table_ref[...].reshape(-1, table_ref.shape[2])
+        small_ref[2 * lines :, : table.shape[1]] = table
+
+
+def quarter_owner(number, core):
+    return 2 * (number % 2) + (core if number >= 2 else 1 - core)
+
+
+def attention_grads(
+    place, normed, grad_projected, mixed, grad_low, full_attention, gain, ffn_grad, table
+):
     rows, width = normed.shape
-    whole = pl.BlockSpec((rows, width), lambda step: (0, 0))
-    line = pl.BlockSpec((1, width), lambda step: (0, 0))
-    half = pl.BlockSpec((2, width // 4, width), lambda step: (0, 0, step))
+    lines = 2 * (width // 128) + 2 * table.shape[0]
+
+    def fixed(step, where):
+        return 0, 0
+
+    def column(step, where):
+        return 0, 0, step
+
+    def weight_spec(number):
+        return pl.BlockSpec(
+            (width // 4, width),
+            lambda step, where: (quarter_owner(number, where[1]), jnp.minimum(step, 2)),
+        )
+
     shape = pltpu.HBM((2, width // 4, 4 * width), jnp.bfloat16)
+    half = pl.BlockSpec((2, width // 4, width), column)
     return pl.pallas_call(
         attention_grads_kernel,
-        grid=(4,),
-        out_shape=(shape, shape, pltpu.HBM((1, width), jnp.float32)),
-        in_specs=[
-            scalars(),
-            whole,
-            pl.BlockSpec((1, rows, width), lambda step: (jnp.minimum(step, 2), 0, 0)),
-            anywhere,
-            anywhere,
-            pl.BlockSpec((width, width), lambda step: (0, jnp.minimum(step, 2))),
-            line,
-        ],
-        out_specs=(half, half, line),
-        scratch_shapes=[
-            pltpu.VMEM((width, rows), jnp.bfloat16),
-            pltpu.VMEM((width, width), jnp.float32),
-            pltpu.VMEM((width, 128), jnp.float32),
-            pltpu.VMEM((rows, width), jnp.bfloat16),
-            pltpu.VMEM((rows, width), jnp.bfloat16),
-            pltpu.SemaphoreType.DMA((2,)),
-        ],
+        grid_spec=pltpu.PrefetchScalarGridSpec(
+            num_scalar_prefetch=1,
+            grid=(4,),
+            in_specs=[
+                pl.BlockSpec((rows, width), fixed),
+                pl.BlockSpec((1, rows, width), lambda step, where: (jnp.minimum(step, 2), 0, 0)),
+                anywhere,
+                anywhere,
+                *[weight_spec(number) for number in range(4)],
+                pl.BlockSpec((1, width), fixed),
+                pl.BlockSpec((1, width), fixed),
+                pl.BlockSpec(table.shape, lambda step, where: (0, 0, 0)),
+            ],
+            out_specs=(half, half, pl.BlockSpec((lines, 128), fixed)),
+            scratch_shapes=[
+                pltpu.VMEM((width, rows), jnp.bfloat16),
+                pltpu.VMEM((width, 128), jnp.float32),
+                pltpu.VMEM((width, 128), jnp.float32),
+                pltpu.VMEM((rows, width), jnp.bfloat16),
+                pltpu.VMEM((rows, width), jnp.bfloat16),
+                pltpu.SemaphoreType.DMA((2,)),
+            ],
+        ),
+        out_shape=(shape, shape, jax.ShapeDtypeStruct((lines, 128), jnp.float32)),
         compiler_params=pltpu.CompilerParams(vmem_limit_bytes=36 * 2**20),
         cost_estimate=pl.CostEstimate(
             flops=8 * rows * width * width,
@@ -1058,8 +1175,10 @@
         name="attention_grads",
     )(
         place,
-        *in_hbm(normed, grad_projected, mixed, grad_low, full_attention),
+        *in_hbm(normed, grad_projected, mixed, grad_low, *[full_attention] * 4),
         gain.reshape(1, -1),
+        ffn_grad,
+        table,
     )
 
 
@@ -1173,16 +1292,19 @@
     in_shard = in_weight.astype(low)
     ff_shard = ff_weight.astype(low)
 
-    values = jnp.concatenate(
-        [doc_inputs.reshape(doc_rows, model_width), query_inputs.reshape(-1, model_width)], axis=0
+    kinds = (jnp.float32, low)
+    values, normed = by_parts(
+        "norm_rows",
+        doc_inputs.reshape(doc_rows, model_width),
+        query_inputs.reshape(-1, model_width),
+        kinds,
+        norm_body,
+        attn_gain.reshape(1, -1),
     )
-    cotangent = jnp.concatenate(
-        [doc_cotangent.reshape(doc_rows, model_width), query_cotangent.reshape(-1, model_width)],
-        axis=0,
+    cotangent_parts = (
+        doc_cotangent.reshape(doc_rows, model_width),
+        query_cotangent.reshape(-1, model_width),
     )
-    cot_low = cotangent.astype(low)
-    spread = lax.rsqrt(jnp.mean(values * values, axis=-1, keepdims=True) + epsilon)
-    normed = (values * spread * attn_gain).astype(low)
     places = jnp.arange(group_length, dtype=jnp.int32)
     query_mask = places[None, :] < query_lengths[:, None]
     onehot = lines_onehot(bias_table.shape[0])
@@ -1194,44 +1316,54 @@
 
     if routed:
         column_a = gather_column(attention_shard)
-        column_a, normed, lines, doc_masking, query_masking, cotangent, cot_low, in_shard = together(
-            column_a, normed, lines, doc_masking, query_masking, cotangent, cot_low, in_shard
-        )
-        near_a = gather_near(place, *gather_plane(place, attention_shard, column_a))
+        row_f = jnp.stack(in_order(ff_shard, swap(ff_shard, dx=1), place[3]))
+        column_a, row_f, normed, lines, doc_masking, query_masking, in_shard, cotangent_parts = (
+            together(
+                column_a, row_f, normed, lines, doc_masking, query_masking, in_shard,
+                cotangent_parts,
+            )
+        )
+        plane_a = gather_plane(place, attention_shard, column_a)
+        cotangent, cot_low = by_parts("round_rows", *cotangent_parts, kinds, round_body)
+        plane_a, cotangent, cot_low = together(plane_a, cotangent, cot_low)
+        near_a = gather_near(place, *plane_a)
         column_i = gather_column(in_shard)
         far_a = gather_far(*near_a)
-        column_i, far_a, ff_shard = together(column_i, far_a, ff_shard)
+        far_f = swap(row_f, dy=1)
+        column_i, far_a, far_f = together(column_i, far_a, far_f)
+        plane_f = jnp.stack(in_order(row_f, far_f, place[0]))
         pieces = gather_order(near_a, far_a, gather_core(*near_a), gather_core(*far_a))
         plane_i = gather_plane(place, in_shard, column_i)
     else:
+        cotangent, cot_low = by_parts("round_rows", *cotangent_parts, kinds, round_body)
         pieces = (split_rows(lax.all_gather(attention_shard, both, axis=0, tiled=True)),)
     projected, full_attention = project(place_vector, pieces, normed)
     if routed:
-        plane_i, projected, ff_shard = together(plane_i, projected, ff_shard)
+        plane_i, projected = together(plane_i, projected)
         near_i = gather_near(place, *plane_i)
         far_i = gather_far(*near_i)
-        column_f = gather_column(ff_shard)
+        second_f = swap(plane_f, dz=2)
     mixed, doc_probs, query_probs = attend(
         projected, lines, doc_masking, query_masking, group_length
     )
     if routed:
-        mixed, far_i, column_f = together(mixed, far_i, column_f)
-        plane_f = gather_plane(place, ff_shard, column_f)
+        mixed, far_i, second_f = together(mixed, far_i, second_f)
+        others_f = gather_others(plane_f, second_f)
         pieces = gather_order(near_i, far_i, gather_core(*near_i), gather_core(*far_i))
     else:
         pieces = (split_rows(lax.all_gather(in_shard, both, axis=0, tiled=True)),)
     middle, normed_two = middle_forward(values, mixed, full_attention, ffn_gain)
     if routed:
-        pieces, normed_two, plane_f = together(pieces, normed_two, plane_f)
-        near_f = gather_near(place, *plane_f)
-        far_f = gather_far(*near_f)
-        core_f = gather_core(*near_f)
+        pieces, normed_two = together(pieces, normed_two)
+        core_f = gather_core(plane_f, second_f)
     activated, by_gate, by_up, kept, sent, full_in = gate_forward(
         place_vector, pieces, normed_two, cot_low
     )
     if routed:
-        far_f, core_f, by_gate, kept, sent = together(far_f, core_f, by_gate, kept, sent)
-        pieces = gather_order(near_f, far_f, core_f, gather_core(*far_f))
+        others_f, core_f, by_gate, kept, sent = together(others_f, core_f, by_gate, kept, sent)
+        core_others = gather_core(*others_f)
+        pieces = (plane_f, others_f[0], second_f, others_f[1])
+        pieces += (core_f[0], core_others[0], core_f[1], core_others[1])
         ff_grads = NarrowScatter(kept, sent, place_vector)
         got_f = ff_grads.core()
         pieces, got_f = together(pieces, got_f)
@@ -1264,11 +1396,10 @@
             grad_projected, grad_table, shares_f, near_i
         )
         far_i = in_grads.far(got_i, near_i)
-    kept, sent, grad_attn_gain = attention_grads(
-        place_vector, normed, grad_projected, mixed, grad_middle_low, full_attention, attn_gain
+    kept, sent, small = attention_grads(
+        place_vector, normed, grad_projected, mixed, grad_middle_low, full_attention, attn_gain,
+        grad_ffn_gain, grad_table,
     )
-    small = (grad_attn_gain, grad_ffn_gain, grad_table)
-    small = jnp.concatenate([part.reshape(-1) for part in small])
     if routed:
         kept, sent, far_i, small, grad_projected, shares_f, activated = together(
             kept, sent, far_i, small, grad_projected, shares_f, activated
@@ -1317,6 +1448,7 @@
         grad_qkv = grad_attention[:, : 3 * model_width]
         grad_out = grad_attention[:, 3 * model_width :]
         small = lax.psum(small, both)
+    width_lines = model_width // 128
     in_grad_shard = in_grad_shard.reshape(in_weight.shape[0], -1, 2, tile)
     in_grad_shard = jnp.swapaxes(in_grad_shard, 1, 2).reshape(in_weight.shape)
     return (
@@ -1328,9 +1460,9 @@
         grad_out,
         in_grad_shard,
         ff_grad_shard,
-        small[:model_width],
-        small[model_width : 2 * model_width],
-        small[2 * model_width :].reshape(head_count, -1).T,
+        small[:width_lines].reshape(model_width),
+        small[width_lines : 2 * width_lines].reshape(model_width),
+        small[2 * width_lines :, : bias_table.shape[0]].T,
     )
 
 

time: 271 us -> 259 us (0.956)
  other arithmetic: 22 us -> 11.6 us
  Pallas kernels: 139 us -> 147 us
  local copies, waits for them, and re-layouts: 8.23 us -> 4.5 us
  starting transfers between devices: 64.1 us -> 60.7 us
  waiting for transfers between devices: 35 us -> 32.2 us
    pallas_call x2 -> x4, Pallas kernels: 27.4 us -> 37.3 us  [the longest x1 14.2 us: middle_back(): pl.pallas_call(middle_back_kernel, out_shape=(pltpu.HBM((rows, width), jn...]
    convert_element_type x2 -> x0, other arithmetic: 8.38 us -> none  [the longest x1 4.91 us: body(): normed = (values * spread * attn_gain).astype(low)]
    unnamed x50 -> x18, local copies, waits for them, and re-layouts: 3.65 us -> 0.05 us
    ppermute x60 -> x58, starting transfers between devices: 64.1 us -> 60.7 us  [swap(): return lax.ppermute(values, both, flip_pairs(**flips))]
    ppermute x60 -> x58, waiting for transfers between devices: 35 us -> 32.2 us  [swap(): return lax.ppermute(values, both, flip_pairs(**flips))]
  transfers between devices with their start and end apart: 60 -> 58, of which waited for: 18 -> 17; matrix products, arithmetic and copies ran while one was open for 8% -> 5% of each run, Pallas kernels for 46% -> 52%
where the time goes in v4:
time: 259 us; the launch traced here: 257 us
  Pallas kernels  147 us (57%)
  starting transfers between devices  60.7 us (23%)
  waiting for transfers between devices  32.2 us (12%)
  other arithmetic  11.6 us (4%)
  local copies, waits for them, and re-layouts  4.5 us (2%)
    ppermute x58, starting transfers between devices, swap(): return lax.ppermute(values, both, flip_pairs(**flips))  60.7 us
    ppermute x58, waiting for transfers between devices, swap(): return lax.ppermute(values, both, flip_pairs(**flips))  32.2 us
    pallas_call x9, Pallas kernels, route(): pl.pallas_call(body, grid_spec=pltpu.PrefetchScalarGridSpec(num_scalar_pr...  18 us
    pallas_call x1, Pallas kernels, gate_back(): pl.pallas_call(kernel, grid=(hidden // tile,), out_shape=(pltpu.HBM((2, r...  17.7 us
    pallas_call x1, Pallas kernels, attend_back(): pl.pallas_call(functools.partial(attend_back_kernel, docs, length), grid=...  16 us
    pallas_call x1, Pallas kernels, gate_forward(): pl.pallas_call(kernel, grid=(hidden // tile,), out_shape=(pltpu.HBM((rows...  16 us
    pallas_call x1, Pallas kernels, attend(): pl.pallas_call(functools.partial(attend_kernel, docs, length, group), gri...  14.3 us
    pallas_call x1, Pallas kernels, middle_back(): pl.pallas_call(middle_back_kernel, out_shape=(pltpu.HBM((rows, width), jn...  14.2 us
  transfers between devices with their start and end apart: 58, of which 17 were waited for; matrix products, arithmetic and copies ran while one was open for 5% of the time, Pallas kernels for 52%

profile of v4, /device:TPU:0, one launch (start us, length us, event | category | flops | bytes accessed | tf_op | source)
XLA Modules:
  0.0 257.4 jit_solution(1721476056544968281)
XLA Ops:
  1.6 0.9 convert.6
  2.6 3.1 %collective-permute-start = (bf16[24,3072]{1,0:T(8,128)(2,1)S(1)}, bf16[24,3072]{1,0:T(8,128)(2,1)S(1)}, u32[]{:S(2)}, u32[]{:S(2)}) collective-permute-start(bf16[24,3072]{1,0:T(8,128)(2,1)S(1)} %pad_maximum_fusion.10), channel_id=1, source_target_pairs={{0,2},{1,3},{2,0},{3,1},{4,6},{5,7},{6,4},{7,5},{8,10},{9,11},{10,... | collective-permute-start | bytes 442376 | tf_op jit(solution)/shard_map/ppermute | solution.py:34
  5.7 2.6 %collective-permute-start.1 = (bf16[24,3072]{1,0:T(8,128)(2,1)S(1)}, bf16[24,3072]{1,0:T(8,128)(2,1)S(1)}, u32[]{:S(2)}, u32[]{:S(2)}) collective-permute-start(bf16[24,3072]{1,0:T(8,128)(2,1)S(1)} %pad_maximum_fusion.10), channel_id=1, source_target_pairs={{0,4},{1,5},{2,6},{3,7},{4,0},{5,1},{6,2},{7,3},{8,12},{9,13},{10,... | collective-permute-start | bytes 442376 | tf_op jit(solution)/shard_map/ppermute | solution.py:34
  9.2 1.8 collective-permute-start.3
  13.8 1.7 convert_element_type.118
  15.5 6.1 %norm_rows.1 = (f32[896,768]{1,0:T(8,128)}, bf16[896,768]{1,0:T(8,128)(2,1)}) custom-call(f32[512,768]{1,0:T(8,128)} %bitcast.104, f32[384,768]{1,0:T(8,128)} %bitcast.107, f32[1,768]{1,0:T(1,128)S(1)} %reshape.185.refs_0_.gain_ref), custom_call_target="tpu_custom_call" | custom-call | flops 2752512 | bytes 6881280 | tf_op jit(solution)/shard_map/norm_rows/pallas_call | solution.py:957
  22.2 1.8 collective-permute-start.8
  24.0 5.8 %round_rows.1 = (f32[896,768]{1,0:T(8,128)}, bf16[896,768]{1,0:T(8,128)(2,1)}) custom-call(f32[512,768]{1,0:T(8,128)} %bitcast.106, f32[384,768]{1,0:T(8,128)} %bitcast.108), custom_call_target="tpu_custom_call" | custom-call | flops 2752512 | bytes 6881280 | tf_op jit(solution)/shard_map/round_rows/pallas_call | solution.py:957
  30.1 1.6 collective-permute-start.9
  31.8 1.6 collective-permute-start.10
  34.0 3.5 %collective-permute-start.5 = (bf16[24,4096]{1,0:T(8,128)(2,1)}, bf16[24,4096]{1,0:T(8,128)(2,1)}, u32[]{:S(2)}, u32[]{:S(2)}) collective-permute-start(bf16[24,4096]{1,0:T(8,128)(2,1)} %convert_element_type.118), channel_id=1, source_target_pairs={{0,4},{1,5},{2,6},{3,7},{4,0},{5,1},{6,2},{7,3},{8,12},{9,13},{10,... | collective-permute-start | bytes 589832 | tf_op jit(solution)/shard_map/ppermute | solution.py:34
  37.8 1.9 collective-permute-done.4
  39.7 1.3 collective-permute-start.11
  40.9 9.2 %collective-permute-done.5 = bf16[24,4096]{1,0:T(8,128)(2,1)} collective-permute-done((bf16[24,4096]{1,0:T(8,128)(2,1)}, bf16[24,4096]{1,0:T(8,128)(2,1)}, u32[]{:S(2)}, u32[]{:S(2)}) %collective-permute-start.5) | collective-permute-done | bytes 196640 | tf_op jit(solution)/shard_map/ppermute | solution.py:34
  50.6 1.1 select_bitcast_fusion.9
  52.8 1.1 select_bitcast_fusion.7
  54.0 1.1 collective-permute-start.13
  55.4 7.1 %project.1 = (bf16[896,2304]{1,0:T(8,128)(2,1)}, bf16[2,2,4,2,24,3072]{5,4,3,2,1,0:T(8,128)(2,1)}) custom-call(s32[4]{0:T(128)S(1)} %pad_add_fusion.place_ref, bf16[2,2,24,3072]{3,2,1,0:T(8,128)(2,1)S(1)} %bitcast.83, bf16[2,2,24,3072]{3,2,1,0:T(8,128)(2,1)S(1)} %collective-permute-done.9.refs_1_, bf16[2,2,24,3072]{3,2,1,0:T(8,128)(2,1)S(1)} %pad_maximum_fusion.3.refs_2_, ...), custom_call_target="tpu_custom_call" | custom-call | flops 3170893824 | bytes 14942208 | tf_op jit(solution)/shard_map/project/pallas_call | solution.py:1002
  62.8 2.2 collective-permute-done.13
  65.3 1.1 collective-permute-start.18
  66.5 1.6 collective-permute-start.19
  68.2 1.0 select_bitcast_fusion.5
  69.2 3.4 %collective-permute-start.20 = (bf16[2,2,64,768]{3,2,1,0:T(8,128)(2,1)S(1)}, bf16[2,2,64,768]{3,2,1,0:T(8,128)(2,1)S(1)}, u32[]{:S(2)}, u32[]{:S(2)}) collective-permute-start(bf16[2,2,64,768]{3,2,1,0:T(8,128)(2,1)S(1)} %pad_maximum_fusion.6.refs_0_), channel_id=1, source_target_pairs={{0,4},{1,5},{2,6},{3,7},{4,0},{5,1},{6,2},{7,3},{8,12},{9,13},{10,... | collective-permute-start | bytes 1179656 | tf_op jit(solution)/shard_map/ppermute | solution.py:34
  73.1 14.3 %attend.1 = (bf16[896,768]{1,0:T(8,128)(2,1)S(1)}, f32[12,512,512]{2,1,0:T(8,128)}, f32[12,384,128]{2,1,0:T(8,128)}) custom-call(bf16[896,2304]{1,0:T(8,128)(2,1)} %get-tuple-element.222.q_ref.k_ref.v_ref, bf16[896,2304]{1,0:T(8,128)(2,1)} %get-tuple-element.222.q_ref.k_ref.v_ref, bf16[896,2304]{1,0:T(8,128)(2,1)} %get-tuple-element.222.q_ref.k_ref.v_ref, ...), custom_call_target="tpu_custom_call" | custom-call | flops 1912602624 | bytes 18087936 | tf_op jit(solution)/shard_map/attend/pallas_call | solution.py:475
  87.4 1.8 collective-permute-done.20.refs_2_
  89.7 4.4 %middle_forward.1 = (f32[896,768]{1,0:T(8,128)}, bf16[896,768]{1,0:T(8,128)(2,1)S(1)}) custom-call(f32[896,768]{1,0:T(8,128)} %get-tuple-element.200.refs_0_.rows_ref, bf16[896,768]{1,0:T(8,128)(2,1)S(1)} %get-tuple-element.232.refs_1_.mixed_hbm, bf16[768,3072]{1,0:T(8,128)(2,1)} %bitcast.84, f32[1,768]{1,0:T(1,128)S(1)} %reshape.192.refs_3_.gain_ref), custom_call_target="tpu_custom_call" | custom-call | flops 1056964608 | bytes 9437184 | tf_op jit(solution)/shard_map/middle_forward/pallas_call | solution.py:1043
  94.3 2.0 collective-permute-start.22
  96.4 16.0 %gate_forward.1 = (bf16[896,2048]{1,0:T(8,128)(2,1)}, f32[896,2048]{1,0:T(8,128)}, f32[896,2048]{1,0:T(8,128)}, bf16[2,512,768]{2,1,0:T(8,128)(2,1)}, bf16[2,512...) custom-call(s32[4]{0:T(128)S(1)} %pad_add_fusion.place_ref, bf16[2,2,24,4096]{3,2,1,0:T(8,128)(2,1)S(1)} %bitcast.80, ...), custom_call_target="tpu_custom_call" | custom-call | flops 8455716864 | bytes 30932992 | tf_op jit(solution)/shard_map/gate_forward/pallas_call | solution.py:743
  113.4 3.2 %collective-permute-done.29.refs_5_ = bf16[2,2,64,768]{3,2,1,0:T(8,128)(2,1)S(1)} collective-permute-done((bf16[2,2,64,768]{3,2,1,0:T(8,128)(2,1)S(1)}, bf16[2,2,64,768]{3,2,1,0:T(8,128)(2,1)S(1)}, u32[]{:S(2)}, u32[]{:S(2)}) %collective-permute-start.29) | collective-permute-done | bytes 393248 | tf_op jit(solution)/shard_map/ppermute | solution.py:34
  117.1 1.9 plane.3
  119.6 17.7 %gate_back.1 = (bf16[2,896,2048]{2,1,0:T(8,128)(2,1)}, bf16[2,192,4096]{2,1,0:T(8,128)(2,1)}, bf16[2,192,4096]{2,1,0:T(8,128)(2,1)}, bf16[2,2,4,2,64,768]{5,4,3,2,1,0:T(8,128)(2,1)}) custom-call(s32[4]{0:T(128)S(1)} %pad_add_fusion.place_ref, bf16[2,2,64,768]{3,2,1,0:T(8,128)(2,1)S(1)} %pad_maximum_fusion.6.refs_0_, ...), custom_call_target="tpu_custom_call" | custom-call | flops 8455716864 | bytes 34603008 | tf_op jit(solution)/shard_map/gate_back/pallas_call | solution.py:803
  137.3 1.5 collective-permute-done.32.refs_2_
  138.8 1.8 far.3
  140.6 1.0 collective-permute-start.33
  141.6 14.2 %middle_back.1 = (f32[896,768]{1,0:T(8,128)}, bf16[896,768]{1,0:T(8,128)(2,1)}, bf16[896,768]{1,0:T(8,128)(2,1)}, f32[1,768]{1,0:T(1,128)S(1)}) custom-call(bf16[2,896,2048]{2,1,0:T(8,128)(2,1)} %get-tuple-element.272.gates_hbm, bf16[768,4096]{1,0:T(8,128)(2,1)} %bitcast.111, bf16[768,3072]{1,0:T(8,128)(2,1)} %bitcast.85, ...), custom_call_target="tpu_custom_call" | custom-call | flops 6694109184 | bytes 26017792 | tf_op jit(solution)/shard_map/middle_back/pallas_call | solution.py:908
  155.8 2.3 plane.4
  160.0 1.9 column.3
  162.1 1.9 collective-permute-start.36
  164.0 2.4 collective-permute-start.37
  166.4 16.0 %attend_back.1 = (bf16[3,896,768]{2,1,0:T(8,128)(2,1)}, f32[6,2,32]{2,1,0:T(2,128)}) custom-call(bf16[896,2304]{1,0:T(8,128)(2,1)} %get-tuple-element.222.q_ref.k_ref.v_ref, bf16[896,2304]{1,0:T(8,128)(2,1)} %get-tuple-element.222.q_ref.k_ref.v_ref, bf16[896,2304]{1,0:T(8,128)(2,1)} %get-tuple-element.222.q_ref.k_ref.v_ref, ...), custom_call_target="tpu_custom_call" | custom-call | flops 3825205248 | bytes 22216704 | tf_op jit(solution)/shard_map/attend_back/pallas_call | solution.py:621
  182.5 2.0 far.4
  184.4 1.2 collective-permute-start.40
  185.6 1.3 collective-permute-start.41
  186.9 11.2 %attention_grads.1 = (bf16[2,192,3072]{2,1,0:T(8,128)(2,1)}, bf16[2,192,3072]{2,1,0:T(8,128)(2,1)}, f32[24,128]{1,0:T(8,128)S(1)}) custom-call(s32[4]{0:T(128)S(1)} %pad_add_fusion.place_ref, bf16[896,768]{1,0:T(8,128)(2,1)} %get-tuple-element.220.refs_8_.normed_ref, bf16[3,896,768]{2,1,0:T(8,128)(2,1)} %get-tuple-element.326.grads_ref, ...), custom_call_target="tpu_custom_call" | custom-call | flops 4227858432 | bytes 16515072 | tf_op jit(solution)/shard_map/attention_grads/pallas_call | solution.py:1143
  198.7 2.3 column.4
  200.9 1.4 collective-permute-done.43
  202.9 2.1 plane.5
  206.8 2.0 collective-permute-start.47
  208.8 1.8 collective-permute-done.46
  210.6 1.4 collective-permute-start.49
  212.1 8.7 %input_back.1 = (f32[512,768]{1,0:T(8,128)}, f32[384,768]{1,0:T(8,128)}) custom-call(bf16[3,896,768]{2,1,0:T(8,128)(2,1)} %get-tuple-element.326.grads_ref, bf16[768,3072]{1,0:T(8,128)(2,1)} %bitcast.90, f32[896,768]{1,0:T(8,128)} %get-tuple-element.200.refs_0_.rows_ref, f32[896,768]{1,0:T(8,128)} %get-tuple-element.327.residual_ref, ...), custom_call_target="tpu_custom_call" | custom-call | flops 3170893824 | bytes 15925248 | tf_op jit(solution)/shard_map/input_back/pallas_call | solution.py:1202
  220.8 4.8 %collective-permute-done.48 = bf16[24,4096]{1,0:T(8,128)(2,1)S(1)} collective-permute-done((bf16[24,4096]{1,0:T(8,128)(2,1)S(1)}, bf16[24,4096]{1,0:T(8,128)(2,1)S(1)}, u32[]{:S(2)}, u32[]{:S(2)}) %collective-permute-start.48) | collective-permute-done | bytes 196640 | tf_op jit(solution)/shard_map/ppermute | solution.py:34
  225.6 1.8 far.5
  227.4 1.1 collective-permute-start.50
  228.5 1.4 collective-permute-start.51
  229.9 3.1 %collective-permute-start.52 = (f32[24,128]{1,0:T(8,128)S(1)}, f32[24,128]{1,0:T(8,128)S(1)}, u32[]{:S(2)}, u32[]{:S(2)}) collective-permute-start(f32[24,128]{1,0:T(8,128)S(1)} %add.172), channel_id=1, source_target_pairs={{0,4},{1,5},{2,6},{3,7},{4,0},{5,1},{6,2},{7,3},{8,12},{9,13},{10,... | collective-permute-start | bytes 36872 | tf_op jit(solution)/shard_map/ppermute | solution.py:34
  233.0 1.7 collective-permute-done.52
  235.2 2.0 column.5
  237.3 1.9 collective-permute-start.55
  239.2 3.3 %collective-permute-start.54 = (bf16[24,3072]{1,0:T(8,128)(2,1)S(1)}, bf16[24,3072]{1,0:T(8,128)(2,1)S(1)}, u32[]{:S(2)}, u32[]{:S(2)}) collective-permute-start(bf16[24,3072]{1,0:T(8,128)(2,1)S(1)} %get-tuple-element.378), channel_id=1, source_target_pairs={{0,4},{1,5},{2,6},{3,7},{4,0},{5,1},{6,2},{7,3},{8,12},{9,13},{10,... | collective-permute-start | bytes 442376 | tf_op jit(solution)/shard_map/ppermute | solution.py:34
  242.5 1.2 collective-permute-start.56
  243.8 7.2 %layer_outputs.1 = (f32[512,768]{1,0:T(8,128)}, f32[384,768]{1,0:T(8,128)}) custom-call(f32[896,768]{1,0:T(8,128)} %get-tuple-element.234.middle_hbm.middle_ref, bf16[896,2048]{1,0:T(8,128)(2,1)} %get-tuple-element.370.act_ref, bf16[2048,768]{1,0:T(8,128)(2,1)} %bitcast.112), custom_call_target="tpu_custom_call" | custom-call | flops 2818572288 | bytes 12320768 | tf_op jit(solution)/shard_map/layer_outputs/pallas_call | solution.py:1240
  251.0 1.2 collective-permute-start.57
  253.4 1.0 reshape.206
  (147 shorter events, 22.4 us)
Async XLA Ops:
  0.7 20.9 %copy-start.7 = (f32[64,768]{1,0:T(8,128)S(1)}, f32[64,768]{1,0:T(8,128)}, u32[]{:S(2)}) copy-start(f32[64,768]{1,0:T(8,128)} %param.22) | copy-start | bytes 589828
  2.6 19.1 %collective-permute-start = (bf16[24,3072]{1,0:T(8,128)(2,1)S(1)}, bf16[24,3072]{1,0:T(8,128)(2,1)S(1)}, u32[]{:S(2)}, u32[]{:S(2)}) collective-permute-start(bf16[24,3072]{1,0:T(8,128)(2,1)S(1)} %pad_maximum_fusion.10), channel_id=1, source_target_pairs={{0,2},{1,3},{2,0},{3,1},{4,6},{5,7},{6,4},{7,5},{8,10},{9,11},{10,... | collective-permute-start | bytes 442376 | tf_op jit(solution)/shard_map/ppermute | solution.py:34
  5.7 16.0 %collective-permute-start.1 = (bf16[24,3072]{1,0:T(8,128)(2,1)S(1)}, bf16[24,3072]{1,0:T(8,128)(2,1)S(1)}, u32[]{:S(2)}, u32[]{:S(2)}) collective-permute-start(bf16[24,3072]{1,0:T(8,128)(2,1)S(1)} %pad_maximum_fusion.10), channel_id=1, source_target_pairs={{0,4},{1,5},{2,6},{3,7},{4,0},{5,1},{6,2},{7,3},{8,12},{9,13},{10,... | collective-permute-start | bytes 442376 | tf_op jit(solution)/shard_map/ppermute | solution.py:34
  8.3 13.4 %collective-permute-start.2 = (bf16[24,3072]{1,0:T(8,128)(2,1)S(1)}, bf16[24,3072]{1,0:T(8,128)(2,1)S(1)}, u32[]{:S(2)}, u32[]{:S(2)}) collective-permute-start(bf16[24,3072]{1,0:T(8,128)(2,1)S(1)} %pad_maximum_fusion.10), channel_id=1, source_target_pairs={{0,6},{1,7},{2,4},{3,5},{4,2},{5,3},{6,0},{7,1},{8,14},{9,15},{10,... | collective-permute-start | bytes 442376 | tf_op jit(solution)/shard_map/ppermute | solution.py:34
  9.2 12.4 %collective-permute-start.3 = (bf16[64,768]{1,0:T(8,128)(2,1)S(1)}, bf16[64,768]{1,0:T(8,128)(2,1)S(1)}, u32[]{:S(2)}, u32[]{:S(2)}) collective-permute-start(bf16[64,768]{1,0:T(8,128)(2,1)S(1)} %convert_element_type.110), channel_id=1, source_target_pairs={{0,1},{1,0},{2,3},{3,2},{4,5},{5,4},{6,7},{7,6},{8,9},{9,8},{10,11... | collective-permute-start | bytes 294920 | tf_op jit(solution)/shard_map/ppermute | solution.py:34
  21.8 8.0 %collective-permute-start.7 = (bf16[2,24,3072]{2,1,0:T(8,128)(2,1)S(1)}, bf16[2,24,3072]{2,1,0:T(8,128)(2,1)S(1)}, u32[]{:S(2)}, u32[]{:S(2)}) collective-permute-start(bf16[2,24,3072]{2,1,0:T(8,128)(2,1)S(1)} %pad_maximum_fusion.7), channel_id=1, source_target_pairs={{0,1},{1,0},{2,3},{3,2},{4,5},{5,4},{6,7},{7,6},{8,9},{9,8},{10,11... | collective-permute-start | bytes 884744 | tf_op jit(solution)/shard_map/ppermute | solution.py:34
  22.2 7.7 %collective-permute-start.8 = (bf16[2,24,3072]{2,1,0:T(8,128)(2,1)S(1)}, bf16[2,24,3072]{2,1,0:T(8,128)(2,1)S(1)}, u32[]{:S(2)}, u32[]{:S(2)}) collective-permute-start(bf16[2,24,3072]{2,1,0:T(8,128)(2,1)S(1)} %pad_maximum_fusion.8), channel_id=1, source_target_pairs={{0,16},{1,17},{2,18},{3,19},{4,20},{5,21},{6,22},{7,23},{8,24},{9,... | collective-permute-start | bytes 884744 | tf_op jit(solution)/shard_map/ppermute | solution.py:34
  30.1 20.5 %collective-permute-start.9 = (bf16[2,2,24,3072]{3,2,1,0:T(8,128)(2,1)S(1)}, bf16[2,2,24,3072]{3,2,1,0:T(8,128)(2,1)S(1)}, u32[]{:S(2)}, u32[]{:S(2)}) collective-permute-start(bf16[2,2,24,3072]{3,2,1,0:T(8,128)(2,1)S(1)} %bitcast.81), channel_id=1, source_target_pairs={{0,16},{1,17},{2,18},{3,19},{4,20},{5,21},{6,22},{7,23},{8,24},{9,... | collective-permute-start | bytes 1769480 | tf_op jit(solution)/shard_map/ppermute | solution.py:34
  31.7 23.6 %copy-start.4 = (bf16[896,768]{1,0:T(8,128)(2,1)S(1)}, bf16[896,768]{1,0:T(8,128)(2,1)}, u32[]{:S(2)}) copy-start(bf16[896,768]{1,0:T(8,128)(2,1)} %get-tuple-element.220.refs_8_.normed_ref) | copy-start | bytes 4128772
  31.8 18.8 %collective-permute-start.10 = (bf16[2,2,24,3072]{3,2,1,0:T(8,128)(2,1)S(1)}, bf16[2,2,24,3072]{3,2,1,0:T(8,128)(2,1)}, u32[]{:S(2)}, u32[]{:S(2)}) collective-permute-start(bf16[2,2,24,3072]{3,2,1,0:T(8,128)(2,1)S(1)} %pad_maximum_fusion.3.refs_2_), channel_id=1, source_target_pairs={{0,1},{1,0},{2,3},{3,2},{4,5},{5,4},{6,7},{7,6},{8,9},{9,8},{10,11... | collective-permute-start | bytes 1769480 | tf_op jit(solution)/shard_map/ppermute | solution.py:34
  33.4 6.3 %collective-permute-start.4 = (bf16[24,4096]{1,0:T(8,128)(2,1)}, bf16[24,4096]{1,0:T(8,128)(2,1)}, u32[]{:S(2)}, u32[]{:S(2)}) collective-permute-start(bf16[24,4096]{1,0:T(8,128)(2,1)} %convert_element_type.118), channel_id=1, source_target_pairs={{0,2},{1,3},{2,0},{3,1},{4,6},{5,7},{6,4},{7,5},{8,10},{9,11},{10,... | collective-permute-start | bytes 589832 | tf_op jit(solution)/shard_map/ppermute | solution.py:34
  34.0 16.1 %collective-permute-start.5 = (bf16[24,4096]{1,0:T(8,128)(2,1)}, bf16[24,4096]{1,0:T(8,128)(2,1)}, u32[]{:S(2)}, u32[]{:S(2)}) collective-permute-start(bf16[24,4096]{1,0:T(8,128)(2,1)} %convert_element_type.118), channel_id=1, source_target_pairs={{0,4},{1,5},{2,6},{3,7},{4,0},{5,1},{6,2},{7,3},{8,12},{9,13},{10,... | collective-permute-start | bytes 589832 | tf_op jit(solution)/shard_map/ppermute | solution.py:34
  37.5 12.6 %collective-permute-start.6 = (bf16[24,4096]{1,0:T(8,128)(2,1)}, bf16[24,4096]{1,0:T(8,128)(2,1)}, u32[]{:S(2)}, u32[]{:S(2)}) collective-permute-start(bf16[24,4096]{1,0:T(8,128)(2,1)} %convert_element_type.118), channel_id=1, source_target_pairs={{0,6},{1,7},{2,4},{3,5},{4,2},{5,3},{6,0},{7,1},{8,14},{9,15},{10,... | collective-permute-start | bytes 589832 | tf_op jit(solution)/shard_map/ppermute | solution.py:34
  39.7 11.0 %collective-permute-start.11 = (bf16[2,64,768]{2,1,0:T(8,128)(2,1)S(1)}, bf16[2,64,768]{2,1,0:T(8,128)(2,1)}, u32[]{:S(2)}, u32[]{:S(2)}) collective-permute-start(bf16[2,64,768]{2,1,0:T(8,128)(2,1)S(1)} %pad_maximum_fusion.9), channel_id=1, source_target_pairs={{0,16},{1,17},{2,18},{3,19},{4,20},{5,21},{6,22},{7,23},{8,24},{9,... | collective-permute-start | bytes 589832 | tf_op jit(solution)/shard_map/ppermute | solution.py:34
  50.1 3.8 %collective-permute-start.14 = (bf16[2,2,24,3072]{3,2,1,0:T(8,128)(2,1)S(1)}, bf16[2,2,24,3072]{3,2,1,0:T(8,128)(2,1)S(1)}, u32[]{:S(2)}, u32[]{:S(2)}) collective-permute-start(bf16[2,2,24,3072]{3,2,1,0:T(8,128)(2,1)S(1)} %bitcast.82), channel_id=1, source_target_pairs={{0,8},{1,9},{2,10},{3,11},{4,12},{5,13},{6,14},{7,15},{8,0},{9,1},... | collective-permute-start | bytes 1769480 | tf_op jit(solution)/shard_map/ppermute | solution.py:34
  50.1 5.0 %collective-permute-start.16 = (bf16[2,2,24,3072]{3,2,1,0:T(8,128)(2,1)S(1)}, bf16[2,2,24,3072]{3,2,1,0:T(8,128)(2,1)S(1)}, u32[]{:S(2)}, u32[]{:S(2)}) collective-permute-start(bf16[2,2,24,3072]{3,2,1,0:T(8,128)(2,1)S(1)} %pad_maximum_fusion.3.refs_2_), channel_id=1, source_target_pairs={{0,8},{1,9},{2,10},{3,11},{4,12},{5,13},{6,14},{7,15},{8,0},{9,1},... | collective-permute-start | bytes 1769480 | tf_op jit(solution)/shard_map/ppermute | solution.py:34
  51.7 11.1 %collective-permute-start.12 = (bf16[2,24,4096]{2,1,0:T(8,128)(2,1)S(1)}, bf16[2,24,4096]{2,1,0:T(8,128)(2,1)S(1)}, u32[]{:S(2)}, u32[]{:S(2)}) collective-permute-start(bf16[2,24,4096]{2,1,0:T(8,128)(2,1)S(1)} %pad_maximum_fusion.4), channel_id=1, source_target_pairs={{0,1},{1,0},{2,3},{3,2},{4,5},{5,4},{6,7},{7,6},{8,9},{9,8},{10,11... | collective-permute-start | bytes 1179656 | tf_op jit(solution)/shard_map/ppermute | solution.py:34
  52.3 2.8 %collective-permute-start.15 = (bf16[2,2,24,3072]{3,2,1,0:T(8,128)(2,1)S(1)}, bf16[2,2,24,3072]{3,2,1,0:T(8,128)(2,1)S(1)}, u32[]{:S(2)}, u32[]{:S(2)}) collective-permute-start(bf16[2,2,24,3072]{3,2,1,0:T(8,128)(2,1)S(1)} %collective-permute-done.9.refs_1_), channel_id=1, source_target_pairs={{0,8},{1,9},{2,10},{3,11},{4,12},{5,13},{6,14},{7,15},{8,0},{9,1},... | collective-permute-start | bytes 1769480 | tf_op jit(solution)/shard_map/ppermute | solution.py:34
  52.3 3.1 %collective-permute-start.17 = (bf16[2,2,24,3072]{3,2,1,0:T(8,128)(2,1)}, bf16[2,2,24,3072]{3,2,1,0:T(8,128)(2,1)S(1)}, u32[]{:S(2)}, u32[]{:S(2)}) collective-permute-start(bf16[2,2,24,3072]{3,2,1,0:T(8,128)(2,1)} %collective-permute-done.10.refs_3_), channel_id=1, source_target_pairs={{0,8},{1,9},{2,10},{3,11},{4,12},{5,13},{6,14},{7,15},{8,0},{9,1},... | collective-permute-start | bytes 1769480 | tf_op jit(solution)/shard_map/ppermute | solution.py:34
  54.0 11.1 %collective-permute-start.13 = (bf16[2,24,4096]{2,1,0:T(8,128)(2,1)S(1)}, bf16[2,24,4096]{2,1,0:T(8,128)(2,1)S(1)}, u32[]{:S(2)}, u32[]{:S(2)}) collective-permute-start(bf16[2,24,4096]{2,1,0:T(8,128)(2,1)S(1)} %pad_maximum_fusion.5), channel_id=1, source_target_pairs={{0,16},{1,17},{2,18},{3,19},{4,20},{5,21},{6,22},{7,23},{8,24},{9,... | collective-permute-start | bytes 1179656 | tf_op jit(solution)/shard_map/ppermute | solution.py:34
  65.3 23.8 %collective-permute-start.18 = (bf16[2,2,24,4096]{3,2,1,0:T(8,128)(2,1)S(1)}, bf16[2,2,24,4096]{3,2,1,0:T(8,128)(2,1)S(1)}, u32[]{:S(2)}, u32[]{:S(2)}) collective-permute-start(bf16[2,2,24,4096]{3,2,1,0:T(8,128)(2,1)S(1)} %bitcast.78), channel_id=1, source_target_pairs={{0,16},{1,17},{2,18},{3,19},{4,20},{5,21},{6,22},{7,23},{8,24},{9,... | collective-permute-start | bytes 2359304 | tf_op jit(solution)/shard_map/ppermute | solution.py:34
  66.5 22.6 %collective-permute-start.19 = (bf16[2,2,24,4096]{3,2,1,0:T(8,128)(2,1)S(1)}, bf16[2,2,24,4096]{3,2,1,0:T(8,128)(2,1)S(1)}, u32[]{:S(2)}, u32[]{:S(2)}) collective-permute-start(bf16[2,2,24,4096]{3,2,1,0:T(8,128)(2,1)S(1)} %pad_maximum_fusion.1.refs_2_), channel_id=1, source_target_pairs={{0,1},{1,0},{2,3},{3,2},{4,5},{5,4},{6,7},{7,6},{8,9},{9,8},{10,11... | collective-permute-start | bytes 2359304 | tf_op jit(solution)/shard_map/ppermute | solution.py:34
  69.2 20.4 %copy-start.8 = (f32[768]{0:T(1024)S(1)}, f32[768]{0:T(1024)}, u32[]{:S(2)}) copy-start(f32[768]{0:T(1024)} %param.24) | copy-start | bytes 9220
  69.2 19.9 %collective-permute-start.20 = (bf16[2,2,64,768]{3,2,1,0:T(8,128)(2,1)S(1)}, bf16[2,2,64,768]{3,2,1,0:T(8,128)(2,1)S(1)}, u32[]{:S(2)}, u32[]{:S(2)}) collective-permute-start(bf16[2,2,64,768]{3,2,1,0:T(8,128)(2,1)S(1)} %pad_maximum_fusion.6.refs_0_), channel_id=1, source_target_pairs={{0,4},{1,5},{2,6},{3,7},{4,0},{5,1},{6,2},{7,3},{8,12},{9,13},{10,... | collective-permute-start | bytes 1179656 | tf_op jit(solution)/shard_map/ppermute | solution.py:34
  72.6 21.5 %collective-permute-start.25 = (bf16[2,2,24,4096]{3,2,1,0:T(8,128)(2,1)S(1)}, bf16[2,2,24,4096]{3,2,1,0:T(8,128)(2,1)S(1)}, u32[]{:S(2)}, u32[]{:S(2)}) collective-permute-start(bf16[2,2,24,4096]{3,2,1,0:T(8,128)(2,1)S(1)} %bitcast.79), channel_id=1, source_target_pairs={{0,8},{1,9},{2,10},{3,11},{4,12},{5,13},{6,14},{7,15},{8,0},{9,1},... | collective-permute-start | bytes 2359304 | tf_op jit(solution)/shard_map/ppermute | solution.py:34
  72.6 21.7 %collective-permute-start.27 = (bf16[2,2,24,4096]{3,2,1,0:T(8,128)(2,1)S(1)}, bf16[2,2,24,4096]{3,2,1,0:T(8,128)(2,1)S(1)}, u32[]{:S(2)}, u32[]{:S(2)}) collective-permute-start(bf16[2,2,24,4096]{3,2,1,0:T(8,128)(2,1)S(1)} %pad_maximum_fusion.1.refs_2_), channel_id=1, source_target_pairs={{0,8},{1,9},{2,10},{3,11},{4,12},{5,13},{6,14},{7,15},{8,0},{9,1},... | collective-permute-start | bytes 2359304 | tf_op jit(solution)/shard_map/ppermute | solution.py:34
  89.1 7.1 %collective-permute-start.26 = (bf16[2,2,24,4096]{3,2,1,0:T(8,128)(2,1)S(1)}, bf16[2,2,24,4096]{3,2,1,0:T(8,128)(2,1)S(1)}, u32[]{:S(2)}, u32[]{:S(2)}) collective-permute-start(bf16[2,2,24,4096]{3,2,1,0:T(8,128)(2,1)S(1)} %collective-permute-done.18.refs_1_), channel_id=1, source_target_pairs={{0,8},{1,9},{2,10},{3,11},{4,12},{5,13},{6,14},{7,15},{8,0},{9,1},... | collective-permute-start | bytes 2359304 | tf_op jit(solution)/shard_map/ppermute | solution.py:34
  89.1 7.3 %collective-permute-start.28 = (bf16[2,2,24,4096]{3,2,1,0:T(8,128)(2,1)S(1)}, bf16[2,2,24,4096]{3,2,1,0:T(8,128)(2,1)S(1)}, u32[]{:S(2)}, u32[]{:S(2)}) collective-permute-start(bf16[2,2,24,4096]{3,2,1,0:T(8,128)(2,1)S(1)} %collective-permute-done.19.refs_3_), channel_id=1, source_target_pairs={{0,8},{1,9},{2,10},{3,11},{4,12},{5,13},{6,14},{7,15},{8,0},{9,1},... | collective-permute-start | bytes 2359304 | tf_op jit(solution)/shard_map/ppermute | solution.py:34
  89.6 22.8 %collective-permute-start.21 = (bf16[2,2,64,768]{3,2,1,0:T(8,128)(2,1)S(1)}, bf16[2,2,64,768]{3,2,1,0:T(8,128)(2,1)S(1)}, u32[]{:S(2)}, u32[]{:S(2)}) collective-permute-start(bf16[2,2,64,768]{3,2,1,0:T(8,128)(2,1)S(1)} %pad_maximum_fusion.6.refs_0_), channel_id=1, source_target_pairs={{0,2},{1,3},{2,0},{3,1},{4,6},{5,7},{6,4},{7,5},{8,10},{9,11},{10,... | collective-permute-start | bytes 1179656 | tf_op jit(solution)/shard_map/ppermute | solution.py:34
  94.1 18.3 %copy-start.6 = (bf16[896,768]{1,0:T(8,128)(2,1)}, bf16[896,768]{1,0:T(8,128)(2,1)S(1)}, u32[]{:S(2)}) copy-start(bf16[896,768]{1,0:T(8,128)(2,1)S(1)} %get-tuple-element.247.refs_8_) | copy-start | bytes 4128772
  94.1 18.4 %collective-permute-start.23 = (bf16[2,2,64,768]{3,2,1,0:T(8,128)(2,1)S(1)}, bf16[2,2,64,768]{3,2,1,0:T(8,128)(2,1)S(1)}, u32[]{:S(2)}, u32[]{:S(2)}) collective-permute-start(bf16[2,2,64,768]{3,2,1,0:T(8,128)(2,1)S(1)} %pad_maximum_fusion.6.refs_0_), channel_id=1, source_target_pairs={{0,8},{1,9},{2,10},{3,11},{4,12},{5,13},{6,14},{7,15},{8,0},{9,1},... | collective-permute-start | bytes 1179656 | tf_op jit(solution)/shard_map/ppermute | solution.py:34
  94.3 18.2 %collective-permute-start.22 = (bf16[2,2,64,768]{3,2,1,0:T(8,128)(2,1)S(1)}, bf16[2,2,64,768]{3,2,1,0:T(8,128)(2,1)S(1)}, u32[]{:S(2)}, u32[]{:S(2)}) collective-permute-start(bf16[2,2,64,768]{3,2,1,0:T(8,128)(2,1)S(1)} %collective-permute-done.20.refs_2_), channel_id=1, source_target_pairs={{0,2},{1,3},{2,0},{3,1},{4,6},{5,7},{6,4},{7,5},{8,10},{9,11},{10,... | collective-permute-start | bytes 1179656 | tf_op jit(solution)/shard_map/ppermute | solution.py:34
  96.3 16.2 %collective-permute-start.24 = (bf16[2,2,64,768]{3,2,1,0:T(8,128)(2,1)S(1)}, bf16[2,2,64,768]{3,2,1,0:T(8,128)(2,1)S(1)}, u32[]{:S(2)}, u32[]{:S(2)}) collective-permute-start(bf16[2,2,64,768]{3,2,1,0:T(8,128)(2,1)S(1)} %collective-permute-done.20.refs_2_), channel_id=1, source_target_pairs={{0,8},{1,9},{2,10},{3,11},{4,12},{5,13},{6,14},{7,15},{8,0},{9,1},... | collective-permute-start | bytes 1179656 | tf_op jit(solution)/shard_map/ppermute | solution.py:34
  112.5 4.6 %collective-permute-start.31 = (bf16[2,512,768]{2,1,0:T(8,128)(2,1)}, bf16[2,512,768]{2,1,0:T(8,128)(2,1)S(1)}, u32[]{:S(2)}, u32[]{:S(2)}) collective-permute-start(bf16[2,512,768]{2,1,0:T(8,128)(2,1)} %get-tuple-element.256), channel_id=1, source_target_pairs={{0,8},{1,9},{2,10},{3,11},{4,12},{5,13},{6,14},{7,15},{8,0},{9,1},... | collective-permute-start | bytes 4718600 | tf_op jit(solution)/shard_map/ppermute | solution.py:34
  112.9 3.7 %collective-permute-start.29 = (bf16[2,2,64,768]{3,2,1,0:T(8,128)(2,1)S(1)}, bf16[2,2,64,768]{3,2,1,0:T(8,128)(2,1)S(1)}, u32[]{:S(2)}, u32[]{:S(2)}) collective-permute-start(bf16[2,2,64,768]{3,2,1,0:T(8,128)(2,1)S(1)} %collective-permute-done.21.refs_1_), channel_id=1, source_target_pairs={{0,8},{1,9},{2,10},{3,11},{4,12},{5,13},{6,14},{7,15},{8,0},{9,1},... | collective-permute-start | bytes 1179656 | tf_op jit(solution)/shard_map/ppermute | solution.py:34
  113.1 4.0 %collective-permute-start.30 = (bf16[2,2,64,768]{3,2,1,0:T(8,128)(2,1)S(1)}, bf16[2,2,64,768]{3,2,1,0:T(8,128)(2,1)S(1)}, u32[]{:S(2)}, u32[]{:S(2)}) collective-permute-start(bf16[2,2,64,768]{3,2,1,0:T(8,128)(2,1)S(1)} %collective-permute-done.22.refs_3_), channel_id=1, source_target_pairs={{0,8},{1,9},{2,10},{3,11},{4,12},{5,13},{6,14},{7,15},{8,0},{9,1},... | collective-permute-start | bytes 1179656 | tf_op jit(solution)/shard_map/ppermute | solution.py:34
  117.1 20.2 %copy-start.2 = (bf16[2,512,768]{2,1,0:T(8,128)(2,1)}, bf16[2,512,768]{2,1,0:T(8,128)(2,1)S(1)}, u32[]{:S(2)}) copy-start(bf16[2,512,768]{2,1,0:T(8,128)(2,1)S(1)} %collective-permute-done.31) | copy-start | bytes 4718596
  119.0 19.8 %collective-permute-start.32 = (bf16[2,4,64,768]{3,2,1,0:T(8,128)(2,1)S(1)}, bf16[2,4,64,768]{3,2,1,0:T(8,128)(2,1)S(1)}, u32[]{:S(2)}, u32[]{:S(2)}) collective-permute-start(bf16[2,4,64,768]{3,2,1,0:T(8,128)(2,1)S(1)} %plane.3), channel_id=1, source_target_pairs={{0,1},{1,0},{2,3},{3,2},{4,5},{5,4},{6,7},{7,6},{8,9},{9,8},{10,11... | collective-permute-start | bytes 2359304 | tf_op jit(solution)/shard_map/ppermute | solution.py:34
  138.8 17.1 %collective-permute-start.34 = (bf16[2,192,4096]{2,1,0:T(8,128)(2,1)}, bf16[2,192,4096]{2,1,0:T(8,128)(2,1)S(1)}, u32[]{:S(2)}, u32[]{:S(2)}) collective-permute-start(bf16[2,192,4096]{2,1,0:T(8,128)(2,1)} %get-tuple-element.277), channel_id=1, source_target_pairs={{0,8},{1,9},{2,10},{3,11},{4,12},{5,13},{6,14},{7,15},{8,0},{9,1},... | collective-permute-start | bytes 9437192 | tf_op jit(solution)/shard_map/ppermute | solution.py:34
  140.6 15.2 %collective-permute-start.33 = (bf16[4,64,768]{2,1,0:T(8,128)(2,1)S(1)}, bf16[4,64,768]{2,1,0:T(8,128)(2,1)S(1)}, u32[]{:S(2)}, u32[]{:S(2)}) collective-permute-start(bf16[4,64,768]{2,1,0:T(8,128)(2,1)S(1)} %far.3), channel_id=1, source_target_pairs={{0,16},{1,17},{2,18},{3,19},{4,20},{5,21},{6,22},{7,23},{8,24},{9,... | collective-permute-start | bytes 1179656 | tf_op jit(solution)/shard_map/ppermute | solution.py:34
  158.1 24.3 %collective-permute-start.38 = (bf16[2,2,24,4096]{3,2,1,0:T(8,128)(2,1)S(1)}, bf16[2,2,24,4096]{3,2,1,0:T(8,128)(2,1)S(1)}, u32[]{:S(2)}, u32[]{:S(2)}) collective-permute-start(bf16[2,2,24,4096]{3,2,1,0:T(8,128)(2,1)S(1)} %get-tuple-element.290), channel_id=1, source_target_pairs={{0,1},{1,0},{2,3},{3,2},{4,5},{5,4},{6,7},{7,6},{8,9},{9,8},{10,11... | collective-permute-start | bytes 2359304 | tf_op jit(solution)/shard_map/ppermute | solution.py:34
  158.9 23.5 %collective-permute-start.39 = (bf16[2,2,24,4096]{3,2,1,0:T(8,128)(2,1)S(1)}, bf16[2,2,24,4096]{3,2,1,0:T(8,128)(2,1)S(1)}, u32[]{:S(2)}, u32[]{:S(2)}) collective-permute-start(bf16[2,2,24,4096]{3,2,1,0:T(8,128)(2,1)S(1)} %get-tuple-element.291), channel_id=1, source_target_pairs={{0,16},{1,17},{2,18},{3,19},{4,20},{5,21},{6,22},{7,23},{8,24},{9,... | collective-permute-start | bytes 2359304 | tf_op jit(solution)/shard_map/ppermute | solution.py:34
  161.9 20.5 %collective-permute-start.35 = (bf16[64,768]{1,0:T(8,128)(2,1)S(1)}, bf16[64,768]{1,0:T(8,128)(2,1)S(1)}, u32[]{:S(2)}, u32[]{:S(2)}) collective-permute-start(bf16[64,768]{1,0:T(8,128)(2,1)S(1)} %get-tuple-element.285), channel_id=1, source_target_pairs={{0,2},{1,3},{2,0},{3,1},{4,6},{5,7},{6,4},{7,5},{8,10},{9,11},{10,... | collective-permute-start | bytes 294920 | tf_op jit(solution)/shard_map/ppermute | solution.py:34
  162.1 20.3 %collective-permute-start.36 = (bf16[64,768]{1,0:T(8,128)(2,1)S(1)}, bf16[64,768]{1,0:T(8,128)(2,1)S(1)}, u32[]{:S(2)}, u32[]{:S(2)}) collective-permute-start(bf16[64,768]{1,0:T(8,128)(2,1)S(1)} %get-tuple-element.286), channel_id=1, source_target_pairs={{0,4},{1,5},{2,6},{3,7},{4,0},{5,1},{6,2},{7,3},{8,12},{9,13},{10,... | collective-permute-start | bytes 294920 | tf_op jit(solution)/shard_map/ppermute | solution.py:34
  164.0 18.4 %collective-permute-start.37 = (bf16[64,768]{1,0:T(8,128)(2,1)S(1)}, bf16[64,768]{1,0:T(8,128)(2,1)S(1)}, u32[]{:S(2)}, u32[]{:S(2)}) collective-permute-start(bf16[64,768]{1,0:T(8,128)(2,1)S(1)} %get-tuple-element.287), channel_id=1, source_target_pairs={{0,6},{1,7},{2,4},{3,5},{4,2},{5,3},{6,0},{7,1},{8,14},{9,15},{10,... | collective-permute-start | bytes 294920 | tf_op jit(solution)/shard_map/ppermute | solution.py:34
  184.4 13.7 %collective-permute-start.40 = (bf16[2,24,4096]{2,1,0:T(8,128)(2,1)S(1)}, bf16[2,24,4096]{2,1,0:T(8,128)(2,1)S(1)}, u32[]{:S(2)}, u32[]{:S(2)}) collective-permute-start(bf16[2,24,4096]{2,1,0:T(8,128)(2,1)S(1)} %get-tuple-element.300), channel_id=1, source_target_pairs={{0,16},{1,17},{2,18},{3,19},{4,20},{5,21},{6,22},{7,23},{8,24},{9,... | collective-permute-start | bytes 1179656 | tf_op jit(solution)/shard_map/ppermute | solution.py:34
  185.6 12.5 %collective-permute-start.41 = (bf16[2,24,4096]{2,1,0:T(8,128)(2,1)S(1)}, bf16[2,24,4096]{2,1,0:T(8,128)(2,1)S(1)}, u32[]{:S(2)}, u32[]{:S(2)}) collective-permute-start(bf16[2,24,4096]{2,1,0:T(8,128)(2,1)S(1)} %get-tuple-element.301), channel_id=1, source_target_pairs={{0,1},{1,0},{2,3},{3,2},{4,5},{5,4},{6,7},{7,6},{8,9},{9,8},{10,11... | collective-permute-start | bytes 1179656 | tf_op jit(solution)/shard_map/ppermute | solution.py:34
  198.1 4.8 %collective-permute-start.42 = (bf16[2,192,3072]{2,1,0:T(8,128)(2,1)}, bf16[2,192,3072]{2,1,0:T(8,128)(2,1)S(1)}, u32[]{:S(2)}, u32[]{:S(2)}) collective-permute-start(bf16[2,192,3072]{2,1,0:T(8,128)(2,1)} %get-tuple-element.309), channel_id=1, source_target_pairs={{0,8},{1,9},{2,10},{3,11},{4,12},{5,13},{6,14},{7,15},{8,0},{9,1},... | collective-permute-start | bytes 7077896 | tf_op jit(solution)/shard_map/ppermute | solution.py:34
  198.2 4.2 %collective-permute-start.43 = (f32[24,128]{1,0:T(8,128)S(1)}, f32[24,128]{1,0:T(8,128)S(1)}, u32[]{:S(2)}, u32[]{:S(2)}) collective-permute-start(f32[24,128]{1,0:T(8,128)S(1)} %get-tuple-element.316), channel_id=1, source_target_pairs={{0,8},{1,9},{2,10},{3,11},{4,12},{5,13},{6,14},{7,15},{8,0},{9,1},... | collective-permute-start | bytes 36872 | tf_op jit(solution)/shard_map/ppermute | solution.py:34
  205.0 20.6 %collective-permute-start.44 = (bf16[2,2,24,3072]{3,2,1,0:T(8,128)(2,1)S(1)}, bf16[2,2,24,3072]{3,2,1,0:T(8,128)(2,1)S(1)}, u32[]{:S(2)}, u32[]{:S(2)}) collective-permute-start(bf16[2,2,24,3072]{3,2,1,0:T(8,128)(2,1)S(1)} %get-tuple-element.324), channel_id=1, source_target_pairs={{0,1},{1,0},{2,3},{3,2},{4,5},{5,4},{6,7},{7,6},{8,9},{9,8},{10,11... | collective-permute-start | bytes 1769480 | tf_op jit(solution)/shard_map/ppermute | solution.py:34
  205.8 19.8 %collective-permute-start.45 = (bf16[2,2,24,3072]{3,2,1,0:T(8,128)(2,1)S(1)}, bf16[2,2,24,3072]{3,2,1,0:T(8,128)(2,1)S(1)}, u32[]{:S(2)}, u32[]{:S(2)}) collective-permute-start(bf16[2,2,24,3072]{3,2,1,0:T(8,128)(2,1)S(1)} %get-tuple-element.325), channel_id=1, source_target_pairs={{0,16},{1,17},{2,18},{3,19},{4,20},{5,21},{6,22},{7,23},{8,24},{9,... | collective-permute-start | bytes 1769480 | tf_op jit(solution)/shard_map/ppermute | solution.py:34
  206.7 3.9 %collective-permute-start.46 = (f32[24,128]{1,0:T(8,128)S(1)}, f32[24,128]{1,0:T(8,128)S(1)}, u32[]{:S(2)}, u32[]{:S(2)}) collective-permute-start(f32[24,128]{1,0:T(8,128)S(1)} %add.171), channel_id=1, source_target_pairs={{0,2},{1,3},{2,0},{3,1},{4,6},{5,7},{6,4},{7,5},{8,10},{9,11},{10,... | collective-permute-start | bytes 36872 | tf_op jit(solution)/shard_map/ppermute | solution.py:34
  206.8 14.0 %collective-permute-start.47 = (bf16[24,4096]{1,0:T(8,128)(2,1)S(1)}, bf16[24,4096]{1,0:T(8,128)(2,1)S(1)}, u32[]{:S(2)}, u32[]{:S(2)}) collective-permute-start(bf16[24,4096]{1,0:T(8,128)(2,1)S(1)} %get-tuple-element.336), channel_id=1, source_target_pairs={{0,2},{1,3},{2,0},{3,1},{4,6},{5,7},{6,4},{7,5},{8,10},{9,11},{10,... | collective-permute-start | bytes 589832 | tf_op jit(solution)/shard_map/ppermute | solution.py:34
  208.8 16.8 %collective-permute-start.48 = (bf16[24,4096]{1,0:T(8,128)(2,1)S(1)}, bf16[24,4096]{1,0:T(8,128)(2,1)S(1)}, u32[]{:S(2)}, u32[]{:S(2)}) collective-permute-start(bf16[24,4096]{1,0:T(8,128)(2,1)S(1)} %get-tuple-element.337), channel_id=1, source_target_pairs={{0,4},{1,5},{2,6},{3,7},{4,0},{5,1},{6,2},{7,3},{8,12},{9,13},{10,... | collective-permute-start | bytes 589832 | tf_op jit(solution)/shard_map/ppermute | solution.py:34
  210.6 15.0 %collective-permute-start.49 = (bf16[24,4096]{1,0:T(8,128)(2,1)S(1)}, bf16[24,4096]{1,0:T(8,128)(2,1)S(1)}, u32[]{:S(2)}, u32[]{:S(2)}) collective-permute-start(bf16[24,4096]{1,0:T(8,128)(2,1)S(1)} %get-tuple-element.338), channel_id=1, source_target_pairs={{0,6},{1,7},{2,4},{3,5},{4,2},{5,3},{6,0},{7,1},{8,14},{9,15},{10,... | collective-permute-start | bytes 589832 | tf_op jit(solution)/shard_map/ppermute | solution.py:34
  227.4 7.3 %collective-permute-start.50 = (bf16[2,24,3072]{2,1,0:T(8,128)(2,1)S(1)}, bf16[2,24,3072]{2,1,0:T(8,128)(2,1)S(1)}, u32[]{:S(2)}, u32[]{:S(2)}) collective-permute-start(bf16[2,24,3072]{2,1,0:T(8,128)(2,1)S(1)} %get-tuple-element.342), channel_id=1, source_target_pairs={{0,16},{1,17},{2,18},{3,19},{4,20},{5,21},{6,22},{7,23},{8,24},{9,... | collective-permute-start | bytes 884744 | tf_op jit(solution)/shard_map/ppermute | solution.py:34
  228.5 6.7 %collective-permute-start.51 = (bf16[2,24,3072]{2,1,0:T(8,128)(2,1)S(1)}, bf16[2,24,3072]{2,1,0:T(8,128)(2,1)S(1)}, u32[]{:S(2)}, u32[]{:S(2)}) collective-permute-start(bf16[2,24,3072]{2,1,0:T(8,128)(2,1)S(1)} %get-tuple-element.343), channel_id=1, source_target_pairs={{0,1},{1,0},{2,3},{3,2},{4,5},{5,4},{6,7},{7,6},{8,9},{9,8},{10,11... | collective-permute-start | bytes 884744 | tf_op jit(solution)/shard_map/ppermute | solution.py:34
  229.9 4.8 %collective-permute-start.52 = (f32[24,128]{1,0:T(8,128)S(1)}, f32[24,128]{1,0:T(8,128)S(1)}, u32[]{:S(2)}, u32[]{:S(2)}) collective-permute-start(f32[24,128]{1,0:T(8,128)S(1)} %add.172), channel_id=1, source_target_pairs={{0,4},{1,5},{2,6},{3,7},{4,0},{5,1},{6,2},{7,3},{8,12},{9,13},{10,... | collective-permute-start | bytes 36872 | tf_op jit(solution)/shard_map/ppermute | solution.py:34
  237.3 18.7 %collective-permute-start.55 = (bf16[24,3072]{1,0:T(8,128)(2,1)S(1)}, bf16[24,3072]{1,0:T(8,128)(2,1)S(1)}, u32[]{:S(2)}, u32[]{:S(2)}) collective-permute-start(bf16[24,3072]{1,0:T(8,128)(2,1)S(1)} %get-tuple-element.379), channel_id=1, source_target_pairs={{0,6},{1,7},{2,4},{3,5},{4,2},{5,3},{6,0},{7,1},{8,14},{9,15},{10,... | collective-permute-start | bytes 442376 | tf_op jit(solution)/shard_map/ppermute | solution.py:34
  239.2 16.8 %collective-permute-start.54 = (bf16[24,3072]{1,0:T(8,128)(2,1)S(1)}, bf16[24,3072]{1,0:T(8,128)(2,1)S(1)}, u32[]{:S(2)}, u32[]{:S(2)}) collective-permute-start(bf16[24,3072]{1,0:T(8,128)(2,1)S(1)} %get-tuple-element.378), channel_id=1, source_target_pairs={{0,4},{1,5},{2,6},{3,7},{4,0},{5,1},{6,2},{7,3},{8,12},{9,13},{10,... | collective-permute-start | bytes 442376 | tf_op jit(solution)/shard_map/ppermute | solution.py:34
  242.5 13.5 %collective-permute-start.53 = (bf16[24,3072]{1,0:T(8,128)(2,1)S(1)}, bf16[24,3072]{1,0:T(8,128)(2,1)S(1)}, u32[]{:S(2)}, u32[]{:S(2)}) collective-permute-start(bf16[24,3072]{1,0:T(8,128)(2,1)S(1)} %get-tuple-element.377), channel_id=1, source_target_pairs={{0,2},{1,3},{2,0},{3,1},{4,6},{5,7},{6,4},{7,5},{8,10},{9,11},{10,... | collective-permute-start | bytes 442376 | tf_op jit(solution)/shard_map/ppermute | solution.py:34
  242.5 8.5 %collective-permute-start.56 = (f32[24,128]{1,0:T(8,128)S(1)}, f32[24,128]{1,0:T(8,128)S(1)}, u32[]{:S(2)}, u32[]{:S(2)}) collective-permute-start(f32[24,128]{1,0:T(8,128)S(1)} %add.173), channel_id=1, source_target_pairs={{0,1},{1,0},{2,3},{3,2},{4,5},{5,4},{6,7},{7,6},{8,9},{9,8},{10,11... | collective-permute-start | bytes 36872 | tf_op jit(solution)/shard_map/ppermute | solution.py:34
  243.8 13.6 %copy-start.1 = (f32[32,12]{0,1:T(8,128)S(1)}, f32[32,12]{0,1:T(8,128)}, u32[]{:S(2)}) copy-start(f32[32,12]{0,1:T(8,128)} %param.25) | copy-start | bytes 4612
  251.0 3.8 %collective-permute-start.57 = (f32[24,128]{1,0:T(8,128)S(1)}, f32[24,128]{1,0:T(8,128)S(1)}, u32[]{:S(2)}, u32[]{:S(2)}) collective-permute-start(f32[24,128]{1,0:T(8,128)S(1)} %add.186), channel_id=1, source_target_pairs={{0,16},{1,17},{2,18},{3,19},{4,20},{5,21},{6,22},{7,23},{8,24},{9,... | collective-permute-start | bytes 36872 | tf_op jit(solution)/shard_map/ppermute | solution.py:34
  (3 other events, 23.2 us)

commit v5 on v4

--- a/solution.py
+++ b/solution.py
@@ -227,8 +227,9 @@
 
 
 class Scatter:
-    def __init__(self, kept, sent, place):
+    def __init__(self, kept, sent, place, pinned=True):
         self.place = place
+        self.pinned = pinned
         self.block = (kept.shape[1] // 8, kept.shape[2])
         self.shape = (2, 4, 2, *self.block)
         self.kept = kept.reshape(self.shape)
@@ -238,7 +239,8 @@
         return jax.ShapeDtypeStruct((*lead, *self.block), dtype)
 
     def both(self, got, lead, pick):
-        return [(*in_hbm(self.kept), lead, pick), (got, lead, pick)]
+        kept = in_hbm(self.kept)[0] if self.pinned else self.kept
+        return [(kept, lead, pick), (got, lead, pick)]
 
     def core(self):
         return swap(self.sent, dc=1).reshape(self.shape)
@@ -307,8 +309,8 @@
 
 class NarrowScatter(Scatter):
     def both(self, got, lead, pick, pinned=True):
-        got = in_hbm(got)[0] if pinned else got
-        return [(*in_hbm(self.kept), lead, pick), (got, lead, pick)]
+        kept, got = in_hbm(self.kept, got) if pinned else (self.kept, got)
+        return [(kept, lead, pick), (got, lead, pick)]
 
     def plane(self, got):
         def body(place_ref, *refs):
@@ -427,8 +429,12 @@
         base = doc * length
         whole = slice(base, base + length)
         masking = mask_ref[doc : doc + 1, :]
-        scores_scratch[...] = dot_nt(both_heads(q_ref[whole, :]), k_ref[whole, :])
         for head in range(2):
+            own = slice(head * length, (head + 1) * length)
+            scores_scratch[own, :] = dot_nt(keep_lanes(head, q_ref[whole, :]), k_ref[whole, :])
+        halves = []
+        for head in range(2):
+            own = slice(head * length, (head + 1) * length)
             for row in range(blocks):
                 rows = slice(row * count, (row + 1) * count)
                 stacked = slice(head * length + row * count, head * length + (row + 1) * count)
@@ -447,7 +453,8 @@
                 probs = softmax_rows(jnp.concatenate(shifted, axis=1))
                 doc_probs_ref[head, base + row * count : base + (row + 1) * count, :] = probs
                 probs_scratch[stacked, :] = probs.astype(jnp.bfloat16)
-        mixed_ref[whole, :] = joined(dot_nn(probs_scratch[...], v_ref[whole, :]))
+            halves.append(dot_nn(probs_scratch[own, :], v_ref[whole, :]))
+        mixed_ref[whole, :] = joined(jnp.concatenate(halves, axis=0))
     for block in range(query_blocks):
         rows = slice(query_start + block * count, query_start + (block + 1) * count)
         masking = query_mask_ref[block]
@@ -529,8 +536,14 @@
     for doc in range(docs):
         base = doc * length
         whole = slice(base, base + length)
-        grads_scratch[...] = dot_nt(both_heads(grad_ref[whole, :]), v_ref[whole, :])
         for head in range(2):
+            own = slice(head * length, (head + 1) * length)
+            grads_scratch[own, :] = dot_nt(keep_lanes(head, grad_ref[whole, :]), v_ref[whole, :])
+        halves, grad_k, grad_v = [], [], []
+        q_turned = q_ref[whole, :].T
+        grad_turned = grad_ref[whole, :].T
+        for head in range(2):
+            own = slice(head * length, (head + 1) * length)
             for row in range(blocks):
                 rows = slice(base + row * count, base + (row + 1) * count)
                 stacked = slice(head * length + row * count, head * length + (row + 1) * count)
@@ -544,15 +557,11 @@
                     gather(head, away + 2, block)
                 scores_scratch[stacked, :] = scores.astype(low)
                 probs_scratch[stacked, :] = probs.astype(low)
-        out_ref[0, whole, :] = joined(dot_nn(scores_scratch[...], k_ref[whole, :]))
-        q_turned = q_ref[whole, :].T
-        grad_turned = grad_ref[whole, :].T
-        grad_k, grad_v = [], []
-        for head in range(2):
-            own = slice(head * half, (head + 1) * half)
-            stacked = slice(head * length, (head + 1) * length)
-            grad_k.append(dot_nn(q_turned[own, :], scores_scratch[stacked, :]))
-            grad_v.append(dot_nn(grad_turned[own, :], probs_scratch[stacked, :]))
+            halves.append(dot_nn(scores_scratch[own, :], k_ref[whole, :]))
+            part = slice(head * half, (head + 1) * half)
+            grad_k.append(dot_nn(q_turned[part, :], scores_scratch[own, :]))
+            grad_v.append(dot_nn(grad_turned[part, :], probs_scratch[own, :]))
+        out_ref[0, whole, :] = joined(jnp.concatenate(halves, axis=0))
         out_ref[1, whole, :] = jnp.concatenate(grad_k, axis=0).astype(low).T
         out_ref[2, whole, :] = jnp.concatenate(grad_v, axis=0).astype(low).T
     for block in range(query_blocks):
@@ -622,7 +631,7 @@
         functools.partial(attend_back_kernel, docs, length),
         grid=(pairs,),
         out_shape=(
-            pltpu.HBM((3, rows, width), jnp.bfloat16),
+            jax.ShapeDtypeStruct((3, rows, width), jnp.bfloat16),
             pltpu.HBM((pairs, 2, onehot.shape[1]), jnp.float32),
         ),
         in_specs=[
@@ -747,8 +756,8 @@
             pltpu.HBM((rows, hidden), jnp.bfloat16),
             pltpu.HBM((rows, hidden), jnp.float32),
             pltpu.HBM((rows, hidden), jnp.float32),
-            pltpu.HBM((2, tile, width), jnp.bfloat16),
-            pltpu.HBM((2, tile, width), jnp.bfloat16),
+            jax.ShapeDtypeStruct((2, tile, width), jnp.bfloat16),
+            jax.ShapeDtypeStruct((2, tile, width), jnp.bfloat16),
             pltpu.HBM(slab(columns, width), jnp.bfloat16),
         ),
         in_specs=[scalars()] + [anywhere] * number + [whole, whole],
@@ -805,8 +814,8 @@
         grid=(hidden // tile,),
         out_shape=(
             pltpu.HBM((2, rows, hidden), jnp.bfloat16),
-            pltpu.HBM((2, width // 4, 2 * hidden), jnp.bfloat16),
-            pltpu.HBM((2, width // 4, 2 * hidden), jnp.bfloat16),
+            jax.ShapeDtypeStruct((2, width // 4, 2 * hidden), jnp.bfloat16),
+            jax.ShapeDtypeStruct((2, width // 4, 2 * hidden), jnp.bfloat16),
             pltpu.HBM(slab(width, hidden), jnp.bfloat16),
         ),
         in_specs=[scalars()] + [anywhere] * number + [whole, whole, column, column],
@@ -1138,7 +1147,7 @@
             lambda step, where: (quarter_owner(number, where[1]), jnp.minimum(step, 2)),
         )
 
-    shape = pltpu.HBM((2, width // 4, 4 * width), jnp.bfloat16)
+    shape = jax.ShapeDtypeStruct((2, width // 4, 4 * width), jnp.bfloat16)
     half = pl.BlockSpec((2, width // 4, width), column)
     return pl.pallas_call(
         attention_grads_kernel,
@@ -1175,7 +1184,9 @@
         name="attention_grads",
     )(
         place,
-        *in_hbm(normed, grad_projected, mixed, grad_low, *[full_attention] * 4),
+        *in_hbm(normed),
+        grad_projected,
+        *in_hbm(mixed, grad_low, *[full_attention] * 4),
         gain.reshape(1, -1),
         ffn_grad,
         table,
@@ -1225,7 +1236,7 @@
             transcendentals=0,
         ),
         name="input_back",
-    )(*in_hbm(grad_projected, full_qkv, values, residual), gain.reshape(1, -1))
+    )(grad_projected, *in_hbm(full_qkv, values, residual), gain.reshape(1, -1))
 
 
 def layer_outputs(middle, activated, full_ff, doc_rows):
@@ -1329,9 +1340,8 @@
         near_a = gather_near(place, *plane_a)
         column_i = gather_column(in_shard)
         far_a = gather_far(*near_a)
-        far_f = swap(row_f, dy=1)
-        column_i, far_a, far_f = together(column_i, far_a, far_f)
-        plane_f = jnp.stack(in_order(row_f, far_f, place[0]))
+        plane_f = jnp.stack(in_order(row_f, swap(row_f, dy=1), place[0]))
+        column_i, far_a, plane_f = together(column_i, far_a, plane_f)
         pieces = gather_order(near_a, far_a, gather_core(*near_a), gather_core(*far_a))
         plane_i = gather_plane(place, in_shard, column_i)
     else:
@@ -1376,7 +1386,7 @@
     )
     if routed:
         gates, kept, sent, near_f = together(gates, kept, sent, near_f)
-        in_grads = Scatter(kept, sent, place_vector)
+        in_grads = Scatter(kept, sent, place_vector, pinned=False)
         far_f = ff_grads.far(ff_grads.far_sums(got_f, near_f))
         got_i = in_grads.core()
     else:
@@ -1404,7 +1414,7 @@
         kept, sent, far_i, small, grad_projected, shares_f, activated = together(
             kept, sent, far_i, small, grad_projected, shares_f, activated
         )
-        attention = Scatter(kept, sent, place_vector)
+        attention = Scatter(kept, sent, place_vector, pinned=False)
         got_a = attention.core()
         small = add_flipped(small, {"dc": 1})
         sums_i = in_grads.column_sums(got_i, near_i, far_i)

time: 259 us -> 249 us (0.961)
  Pallas kernels: 147 us -> 133 us
  starting transfers between devices: 60.7 us -> 67.9 us
  other arithmetic: 11.6 us -> 7.93 us
    pallas_call x9, Pallas kernels: 18 us -> 9.96 us  [route(): pl.pallas_call(body, grid_spec=pltpu.PrefetchScalarGridSpec(num_scalar_pr...]
    ppermute x58, starting transfers between devices: 60.7 us -> 67.9 us  [swap(): return lax.ppermute(values, both, flip_pairs(**flips))]
  transfers between devices with their start and end apart: 58 -> 58, of which waited for: 17 -> 14; matrix products, arithmetic and copies ran while one was open for 5% -> 4% of each run, Pallas kernels for 52% -> 51%
where the time goes in v5:
time: 249 us; the launch traced here: 248 us
  Pallas kernels  133 us (53%)
  starting transfers between devices  67.9 us (27%)
  waiting for transfers between devices  33.7 us (14%)
  other arithmetic  7.93 us (3%)
  local copies, waits for them, and re-layouts  4.51 us (2%)
    ppermute x58, starting transfers between devices, swap(): return lax.ppermute(values, both, flip_pairs(**flips))  67.9 us
    ppermute x58, waiting for transfers between devices, swap(): return lax.ppermute(values, both, flip_pairs(**flips))  33.7 us
    pallas_call x1, Pallas kernels, gate_back(): pl.pallas_call(kernel, grid=(hidden // tile,), out_shape=(pltpu.HBM((2, r...  16.8 us
    pallas_call x1, Pallas kernels, gate_forward(): pl.pallas_call(kernel, grid=(hidden // tile,), out_shape=(pltpu.HBM((rows...  15.6 us
    pallas_call x1, Pallas kernels, attend_back(): pl.pallas_call(functools.partial(attend_back_kernel, docs, length), grid=...  15 us
    pallas_call x1, Pallas kernels, middle_back(): pl.pallas_call(middle_back_kernel, out_shape=(pltpu.HBM((rows, width), jn...  14.2 us
    pallas_call x1, Pallas kernels, attend(): pl.pallas_call(functools.partial(attend_kernel, docs, length, group), gri...  13.6 us
    pallas_call x2, Pallas kernels, by_parts(): pl.pallas_call(kernel, grid=(rows // count,), out_shape=[pltpu.HBM((rows,...  11.8 us
  transfers between devices with their start and end apart: 58, of which 14 were waited for; matrix products, arithmetic and copies ran while one was open for 4% of the time, Pallas kernels for 51%

profile of v5, /device:TPU:0, one launch (start us, length us, event | category | flops | bytes accessed | tf_op | source)
XLA Modules:
  0.0 248.3 jit_solution(7152923751243278559)
XLA Ops:
  0.7 0.9 convert.7
  1.6 0.9 convert.6
  2.6 3.1 %collective-permute-start = (bf16[24,3072]{1,0:T(8,128)(2,1)S(1)}, bf16[24,3072]{1,0:T(8,128)(2,1)S(1)}, u32[]{:S(2)}, u32[]{:S(2)}) collective-permute-start(bf16[24,3072]{1,0:T(8,128)(2,1)S(1)} %pad_maximum_fusion.10), channel_id=1, source_target_pairs={{0,2},{1,3},{2,0},{3,1},{4,6},{5,7},{6,4},{7,5},{8,10},{9,11},{10,... | collective-permute-start | bytes 442376 | tf_op jit(solution)/shard_map/ppermute | solution.py:34
  5.7 2.6 %collective-permute-start.1 = (bf16[24,3072]{1,0:T(8,128)(2,1)S(1)}, bf16[24,3072]{1,0:T(8,128)(2,1)S(1)}, u32[]{:S(2)}, u32[]{:S(2)}) collective-permute-start(bf16[24,3072]{1,0:T(8,128)(2,1)S(1)} %pad_maximum_fusion.10), channel_id=1, source_target_pairs={{0,4},{1,5},{2,6},{3,7},{4,0},{5,1},{6,2},{7,3},{8,12},{9,13},{10,... | collective-permute-start | bytes 442376 | tf_op jit(solution)/shard_map/ppermute | solution.py:34
  8.3 0.9 convert_element_type.110
  9.2 1.8 collective-permute-start.3
  13.8 1.0 convert_element_type.118
  14.8 6.1 %norm_rows.1 = (f32[896,768]{1,0:T(8,128)}, bf16[896,768]{1,0:T(8,128)(2,1)}) custom-call(f32[512,768]{1,0:T(8,128)} %bitcast.104, f32[384,768]{1,0:T(8,128)} %bitcast.107, f32[1,768]{1,0:T(1,128)S(1)} %reshape.185.refs_0_.gain_ref), custom_call_target="tpu_custom_call" | custom-call | flops 2752512 | bytes 6881280 | tf_op jit(solution)/shard_map/norm_rows/pallas_call | solution.py:966
  21.6 1.8 collective-permute-start.8
  23.4 5.7 %round_rows.1 = (f32[896,768]{1,0:T(8,128)}, bf16[896,768]{1,0:T(8,128)(2,1)}) custom-call(f32[512,768]{1,0:T(8,128)} %bitcast.106, f32[384,768]{1,0:T(8,128)} %bitcast.108), custom_call_target="tpu_custom_call" | custom-call | flops 2752512 | bytes 6881280 | tf_op jit(solution)/shard_map/round_rows/pallas_call | solution.py:966
  29.5 1.6 collective-permute-start.9
  31.2 1.6 collective-permute-start.10
  33.2 0.9 collective-permute-start.4
  34.1 3.2 %collective-permute-start.5 = (bf16[24,4096]{1,0:T(8,128)(2,1)S(1)}, bf16[24,4096]{1,0:T(8,128)(2,1)S(1)}, u32[]{:S(2)}, u32[]{:S(2)}) collective-permute-start(bf16[24,4096]{1,0:T(8,128)(2,1)S(1)} %convert_element_type.118), channel_id=1, source_target_pairs={{0,4},{1,5},{2,6},{3,7},{4,0},{5,1},{6,2},{7,3},{8,12},{9,13},{10,... | collective-permute-start | bytes 589832 | tf_op jit(solution)/shard_map/ppermute | solution.py:34
  37.3 9.7 %collective-permute-done.11 = bf16[2,64,768]{2,1,0:T(8,128)(2,1)S(1)} collective-permute-done((bf16[2,64,768]{2,1,0:T(8,128)(2,1)S(1)}, bf16[2,64,768]{2,1,0:T(8,128)(2,1)S(1)}, u32[]{:S(2)}, u32[]{:S(2)}) %collective-permute-start.11) | collective-permute-done | bytes 196640 | tf_op jit(solution)/shard_map/ppermute | solution.py:34
  47.1 3.5 %collective-permute-start.6 = (bf16[24,4096]{1,0:T(8,128)(2,1)S(1)}, bf16[24,4096]{1,0:T(8,128)(2,1)S(1)}, u32[]{:S(2)}, u32[]{:S(2)}) collective-permute-start(bf16[24,4096]{1,0:T(8,128)(2,1)S(1)} %convert_element_type.118), channel_id=1, source_target_pairs={{0,6},{1,7},{2,4},{3,5},{4,2},{5,3},{6,0},{7,1},{8,14},{9,15},{10,... | collective-permute-start | bytes 589832 | tf_op jit(solution)/shard_map/ppermute | solution.py:34
  51.3 3.4 %collective-permute-done.6 = bf16[24,4096]{1,0:T(8,128)(2,1)S(1)} collective-permute-done((bf16[24,4096]{1,0:T(8,128)(2,1)S(1)}, bf16[24,4096]{1,0:T(8,128)(2,1)S(1)}, u32[]{:S(2)}, u32[]{:S(2)}) %collective-permute-start.6) | collective-permute-done | bytes 196640 | tf_op jit(solution)/shard_map/ppermute | solution.py:34
  54.7 1.6 collective-permute-start.12
  56.9 1.1 collective-permute-start.13
  58.3 0.8 collective-permute-done.17.refs_7_
  59.1 6.4 %project.1 = (bf16[896,2304]{1,0:T(8,128)(2,1)}, bf16[2,2,4,2,24,3072]{5,4,3,2,1,0:T(8,128)(2,1)}) custom-call(s32[4]{0:T(128)S(1)} %pad_add_fusion.place_ref, bf16[2,2,24,3072]{3,2,1,0:T(8,128)(2,1)S(1)} %bitcast.96, bf16[2,2,24,3072]{3,2,1,0:T(8,128)(2,1)S(1)} %collective-permute-done.9.refs_1_, bf16[2,2,24,3072]{3,2,1,0:T(8,128)(2,1)S(1)} %pad_maximum_fusion.3.refs_2_, ...), custom_call_target="tpu_custom_call" | custom-call | flops 3170893824 | bytes 14942208 | tf_op jit(solution)/shard_map/project/pallas_call | solution.py:1011
  65.6 2.4 collective-permute-done.13
  68.2 1.1 collective-permute-start.18
  70.0 3.3 %collective-permute-start.20 = (bf16[2,2,64,768]{3,2,1,0:T(8,128)(2,1)S(1)}, bf16[2,2,64,768]{3,2,1,0:T(8,128)(2,1)S(1)}, u32[]{:S(2)}, u32[]{:S(2)}) collective-permute-start(bf16[2,2,64,768]{3,2,1,0:T(8,128)(2,1)S(1)} %pad_maximum_fusion.4.refs_0_), channel_id=1, source_target_pairs={{0,4},{1,5},{2,6},{3,7},{4,0},{5,1},{6,2},{7,3},{8,12},{9,13},{10,... | collective-permute-start | bytes 1179656 | tf_op jit(solution)/shard_map/ppermute | solution.py:34
  73.9 13.6 %attend.1 = (bf16[896,768]{1,0:T(8,128)(2,1)S(1)}, f32[12,512,512]{2,1,0:T(8,128)}, f32[12,384,128]{2,1,0:T(8,128)}) custom-call(bf16[896,2304]{1,0:T(8,128)(2,1)} %get-tuple-element.222.q_ref.k_ref.v_ref, bf16[896,2304]{1,0:T(8,128)(2,1)} %get-tuple-element.222.q_ref.k_ref.v_ref, bf16[896,2304]{1,0:T(8,128)(2,1)} %get-tuple-element.222.q_ref.k_ref.v_ref, ...), custom_call_target="tpu_custom_call" | custom-call | flops 1912602624 | bytes 18087936 | tf_op jit(solution)/shard_map/attend/pallas_call | solution.py:482
  87.5 2.2 collective-permute-done.20.refs_2_
  90.2 4.4 %middle_forward.1 = (f32[896,768]{1,0:T(8,128)}, bf16[896,768]{1,0:T(8,128)(2,1)S(1)}) custom-call(f32[896,768]{1,0:T(8,128)} %get-tuple-element.200.refs_0_.rows_ref, bf16[896,768]{1,0:T(8,128)(2,1)S(1)} %get-tuple-element.232.refs_1_.mixed_hbm, bf16[768,3072]{1,0:T(8,128)(2,1)} %bitcast.97, f32[1,768]{1,0:T(1,128)S(1)} %reshape.192.refs_3_.gain_ref), custom_call_target="tpu_custom_call" | custom-call | flops 1056964608 | bytes 9437184 | tf_op jit(solution)/shard_map/middle_forward/pallas_call | solution.py:1052
  94.8 2.0 collective-permute-start.22
  97.0 15.6 %gate_forward.1 = (bf16[896,2048]{1,0:T(8,128)(2,1)}, f32[896,2048]{1,0:T(8,128)}, f32[896,2048]{1,0:T(8,128)}, bf16[2,512,768]{2,1,0:T(8,128)(2,1)S(1)}, bf16[2...) custom-call(s32[4]{0:T(128)S(1)} %pad_add_fusion.place_ref, bf16[2,2,24,4096]{3,2,1,0:T(8,128)(2,1)S(1)} %bitcast.93, ...), custom_call_target="tpu_custom_call" | custom-call | flops 8455716864 | bytes 30932992 | tf_op jit(solution)/shard_map/gate_forward/pallas_call | solution.py:752
  113.6 3.1 %collective-permute-done.29.refs_5_ = bf16[2,2,64,768]{3,2,1,0:T(8,128)(2,1)S(1)} collective-permute-done((bf16[2,2,64,768]{3,2,1,0:T(8,128)(2,1)S(1)}, bf16[2,2,64,768]{3,2,1,0:T(8,128)(2,1)S(1)}, u32[]{:S(2)}, u32[]{:S(2)}) %collective-permute-start.29) | collective-permute-done | bytes 393248 | tf_op jit(solution)/shard_map/ppermute | solution.py:34
  118.0 0.9 collective-permute-start.32
  118.8 16.8 %gate_back.1 = (bf16[2,896,2048]{2,1,0:T(8,128)(2,1)}, bf16[2,192,4096]{2,1,0:T(8,128)(2,1)S(1)}, bf16[2,192,4096]{2,1,0:T(8,128)(2,1)S(1)}, bf16[2,2,4,2,64,768]{5,4,3,2,1,0:T(8,128)(2,1)}) custom-call(s32[4]{0:T(128)S(1)} %pad_add_fusion.place_ref, bf16[2,2,64,768]{3,2,1,0:T(8,128)(2,1)S(1)} %pad_maximum_fusion.4.refs_0_, ...), custom_call_target="tpu_custom_call" | custom-call | flops 8455716864 | bytes 34603008 | tf_op jit(solution)/shard_map/gate_back/pallas_call | solution.py:812
  135.6 2.2 collective-permute-done.32.refs_2_
  137.8 1.8 far.3
  139.7 1.4 collective-permute-start.33
  141.0 14.2 %middle_back.1 = (f32[896,768]{1,0:T(8,128)}, bf16[896,768]{1,0:T(8,128)(2,1)}, bf16[896,768]{1,0:T(8,128)(2,1)}, f32[1,768]{1,0:T(1,128)S(1)}) custom-call(bf16[2,896,2048]{2,1,0:T(8,128)(2,1)} %get-tuple-element.272.gates_hbm, bf16[768,4096]{1,0:T(8,128)(2,1)} %bitcast.111, bf16[768,3072]{1,0:T(8,128)(2,1)} %bitcast.98, ...), custom_call_target="tpu_custom_call" | custom-call | flops 6694109184 | bytes 26017792 | tf_op jit(solution)/shard_map/middle_back/pallas_call | solution.py:917
  155.3 0.9 plane.4
  156.2 0.9 collective-permute-start.38
  157.9 1.9 column.3
  160.5 3.4 %collective-permute-start.36 = (bf16[64,768]{1,0:T(8,128)(2,1)S(1)}, bf16[64,768]{1,0:T(8,128)(2,1)S(1)}, u32[]{:S(2)}, u32[]{:S(2)}) collective-permute-start(bf16[64,768]{1,0:T(8,128)(2,1)S(1)} %get-tuple-element.286), channel_id=1, source_target_pairs={{0,4},{1,5},{2,6},{3,7},{4,0},{5,1},{6,2},{7,3},{8,12},{9,13},{10,... | collective-permute-start | bytes 294920 | tf_op jit(solution)/shard_map/ppermute | solution.py:34
  164.3 15.0 %attend_back.1 = (bf16[3,896,768]{2,1,0:T(8,128)(2,1)S(1)}, f32[6,2,32]{2,1,0:T(2,128)}) custom-call(bf16[896,2304]{1,0:T(8,128)(2,1)} %get-tuple-element.222.q_ref.k_ref.v_ref, bf16[896,2304]{1,0:T(8,128)(2,1)} %get-tuple-element.222.q_ref.k_ref.v_ref, bf16[896,2304]{1,0:T(8,128)(2,1)} %get-tuple-element.222.q_ref.k_ref.v_ref, ...), custom_call_target="tpu_custom_call" | custom-call | flops 3825205248 | bytes 22216704 | tf_op jit(solution)/shard_map/attend_back/pallas_call | solution.py:630
  179.4 0.8 far.4
  180.2 1.4 collective-permute-start.40
  181.6 1.2 collective-permute-start.41
  182.8 9.4 %attention_grads.1 = (bf16[2,192,3072]{2,1,0:T(8,128)(2,1)S(1)}, bf16[2,192,3072]{2,1,0:T(8,128)(2,1)S(1)}, f32[24,128]{1,0:T(8,128)S(1)}) custom-call(s32[4]{0:T(128)S(1)} %pad_add_fusion.place_ref, bf16[896,768]{1,0:T(8,128)(2,1)} %get-tuple-element.220.refs_8_.normed_ref, bf16[3,896,768]{2,1,0:T(8,128)(2,1)S(1)} %get-tuple-element.326.grads_ref, ...), custom_call_target="tpu_custom_call" | custom-call | flops 4227858432 | bytes 16515072 | tf_op jit(solution)/shard_map/attention_grads/pallas_call | solution.py:1152
  192.9 1.2 column.4
  194.0 2.9 %collective-permute-done.43 = f32[24,128]{1,0:T(8,128)S(1)} collective-permute-done((f32[24,128]{1,0:T(8,128)S(1)}, f32[24,128]{1,0:T(8,128)S(1)}, u32[]{:S(2)}, u32[]{:S(2)}) %collective-permute-start.43) | collective-permute-done | bytes 12320 | tf_op jit(solution)/shard_map/ppermute | solution.py:34
  196.9 0.8 plane.5
  197.7 0.9 collective-permute-start.44
  199.4 1.9 collective-permute-start.47
  201.3 1.9 collective-permute-start.48
  203.3 3.3 %collective-permute-start.49 = (bf16[24,4096]{1,0:T(8,128)(2,1)S(1)}, bf16[24,4096]{1,0:T(8,128)(2,1)S(1)}, u32[]{:S(2)}, u32[]{:S(2)}) collective-permute-start(bf16[24,4096]{1,0:T(8,128)(2,1)S(1)} %get-tuple-element.338), channel_id=1, source_target_pairs={{0,6},{1,7},{2,4},{3,5},{4,2},{5,3},{6,0},{7,1},{8,14},{9,15},{10,... | collective-permute-start | bytes 589832 | tf_op jit(solution)/shard_map/ppermute | solution.py:34
  206.6 8.2 %input_back.1 = (f32[512,768]{1,0:T(8,128)}, f32[384,768]{1,0:T(8,128)}) custom-call(bf16[3,896,768]{2,1,0:T(8,128)(2,1)S(1)} %get-tuple-element.326.grads_ref, bf16[768,3072]{1,0:T(8,128)(2,1)} %bitcast.103, f32[896,768]{1,0:T(8,128)} %get-tuple-element.200.refs_0_.rows_ref, f32[896,768]{1,0:T(8,128)} %get-tuple-element.327.residual_ref, ...), custom_call_target="tpu_custom_call" | custom-call | flops 3170893824 | bytes 15925248 | tf_op jit(solution)/shard_map/input_back/pallas_call | solution.py:1213
  214.8 3.7 %collective-permute-done.48 = bf16[24,4096]{1,0:T(8,128)(2,1)S(1)} collective-permute-done((bf16[24,4096]{1,0:T(8,128)(2,1)S(1)}, bf16[24,4096]{1,0:T(8,128)(2,1)S(1)}, u32[]{:S(2)}, u32[]{:S(2)}) %collective-permute-start.48) | collective-permute-done | bytes 196640 | tf_op jit(solution)/shard_map/ppermute | solution.py:34
  219.3 1.4 collective-permute-start.50
  220.7 1.2 collective-permute-start.51
  221.9 3.9 %collective-permute-start.52 = (f32[24,128]{1,0:T(8,128)S(1)}, f32[24,128]{1,0:T(8,128)S(1)}, u32[]{:S(2)}, u32[]{:S(2)}) collective-permute-start(f32[24,128]{1,0:T(8,128)S(1)} %add.172), channel_id=1, source_target_pairs={{0,4},{1,5},{2,6},{3,7},{4,0},{5,1},{6,2},{7,3},{8,12},{9,13},{10,... | collective-permute-start | bytes 36872 | tf_op jit(solution)/shard_map/ppermute | solution.py:34
  225.8 1.7 collective-permute-done.52
  227.5 1.0 column.5
  228.5 2.4 collective-permute-start.55
  230.9 2.9 %collective-permute-start.54 = (bf16[24,3072]{1,0:T(8,128)(2,1)S(1)}, bf16[24,3072]{1,0:T(8,128)(2,1)S(1)}, u32[]{:S(2)}, u32[]{:S(2)}) collective-permute-start(bf16[24,3072]{1,0:T(8,128)(2,1)S(1)} %get-tuple-element.378), channel_id=1, source_target_pairs={{0,4},{1,5},{2,6},{3,7},{4,0},{5,1},{6,2},{7,3},{8,12},{9,13},{10,... | collective-permute-start | bytes 442376 | tf_op jit(solution)/shard_map/ppermute | solution.py:34
  234.7 7.2 %layer_outputs.1 = (f32[512,768]{1,0:T(8,128)}, f32[384,768]{1,0:T(8,128)}) custom-call(f32[896,768]{1,0:T(8,128)} %get-tuple-element.234.middle_hbm.middle_ref, bf16[896,2048]{1,0:T(8,128)(2,1)} %get-tuple-element.370.act_ref, bf16[2048,768]{1,0:T(8,128)(2,1)} %bitcast.112), custom_call_target="tpu_custom_call" | custom-call | flops 2818572288 | bytes 12320768 | tf_op jit(solution)/shard_map/layer_outputs/pallas_call | solution.py:1251
  242.0 1.0 collective-permute-start.57
  244.2 1.0 reshape.206
  (149 shorter events, 19.8 us)
Async XLA Ops:
  0.7 20.2 %copy-start.8 = (f32[64,768]{1,0:T(8,128)S(1)}, f32[64,768]{1,0:T(8,128)}, u32[]{:S(2)}) copy-start(f32[64,768]{1,0:T(8,128)} %param.22) | copy-start | bytes 589828
  2.6 18.4 %collective-permute-start = (bf16[24,3072]{1,0:T(8,128)(2,1)S(1)}, bf16[24,3072]{1,0:T(8,128)(2,1)S(1)}, u32[]{:S(2)}, u32[]{:S(2)}) collective-permute-start(bf16[24,3072]{1,0:T(8,128)(2,1)S(1)} %pad_maximum_fusion.10), channel_id=1, source_target_pairs={{0,2},{1,3},{2,0},{3,1},{4,6},{5,7},{6,4},{7,5},{8,10},{9,11},{10,... | collective-permute-start | bytes 442376 | tf_op jit(solution)/shard_map/ppermute | solution.py:34
  5.7 15.3 %collective-permute-start.1 = (bf16[24,3072]{1,0:T(8,128)(2,1)S(1)}, bf16[24,3072]{1,0:T(8,128)(2,1)S(1)}, u32[]{:S(2)}, u32[]{:S(2)}) collective-permute-start(bf16[24,3072]{1,0:T(8,128)(2,1)S(1)} %pad_maximum_fusion.10), channel_id=1, source_target_pairs={{0,4},{1,5},{2,6},{3,7},{4,0},{5,1},{6,2},{7,3},{8,12},{9,13},{10,... | collective-permute-start | bytes 442376 | tf_op jit(solution)/shard_map/ppermute | solution.py:34
  8.3 12.7 %collective-permute-start.2 = (bf16[24,3072]{1,0:T(8,128)(2,1)S(1)}, bf16[24,3072]{1,0:T(8,128)(2,1)S(1)}, u32[]{:S(2)}, u32[]{:S(2)}) collective-permute-start(bf16[24,3072]{1,0:T(8,128)(2,1)S(1)} %pad_maximum_fusion.10), channel_id=1, source_target_pairs={{0,6},{1,7},{2,4},{3,5},{4,2},{5,3},{6,0},{7,1},{8,14},{9,15},{10,... | collective-permute-start | bytes 442376 | tf_op jit(solution)/shard_map/ppermute | solution.py:34
  9.2 11.7 %collective-permute-start.3 = (bf16[64,768]{1,0:T(8,128)(2,1)S(1)}, bf16[64,768]{1,0:T(8,128)(2,1)S(1)}, u32[]{:S(2)}, u32[]{:S(2)}) collective-permute-start(bf16[64,768]{1,0:T(8,128)(2,1)S(1)} %convert_element_type.110), channel_id=1, source_target_pairs={{0,1},{1,0},{2,3},{3,2},{4,5},{5,4},{6,7},{7,6},{8,9},{9,8},{10,11... | collective-permute-start | bytes 294920 | tf_op jit(solution)/shard_map/ppermute | solution.py:34
  21.2 8.0 %collective-permute-start.7 = (bf16[2,24,3072]{2,1,0:T(8,128)(2,1)S(1)}, bf16[2,24,3072]{2,1,0:T(8,128)(2,1)S(1)}, u32[]{:S(2)}, u32[]{:S(2)}) collective-permute-start(bf16[2,24,3072]{2,1,0:T(8,128)(2,1)S(1)} %pad_maximum_fusion.7), channel_id=1, source_target_pairs={{0,1},{1,0},{2,3},{3,2},{4,5},{5,4},{6,7},{7,6},{8,9},{9,8},{10,11... | collective-permute-start | bytes 884744 | tf_op jit(solution)/shard_map/ppermute | solution.py:34
  21.6 7.7 %collective-permute-start.8 = (bf16[2,24,3072]{2,1,0:T(8,128)(2,1)S(1)}, bf16[2,24,3072]{2,1,0:T(8,128)(2,1)S(1)}, u32[]{:S(2)}, u32[]{:S(2)}) collective-permute-start(bf16[2,24,3072]{2,1,0:T(8,128)(2,1)S(1)} %pad_maximum_fusion.8), channel_id=1, source_target_pairs={{0,16},{1,17},{2,18},{3,19},{4,20},{5,21},{6,22},{7,23},{8,24},{9,... | collective-permute-start | bytes 884744 | tf_op jit(solution)/shard_map/ppermute | solution.py:34
  29.5 25.2 %collective-permute-start.9 = (bf16[2,2,24,3072]{3,2,1,0:T(8,128)(2,1)S(1)}, bf16[2,2,24,3072]{3,2,1,0:T(8,128)(2,1)S(1)}, u32[]{:S(2)}, u32[]{:S(2)}) collective-permute-start(bf16[2,2,24,3072]{3,2,1,0:T(8,128)(2,1)S(1)} %bitcast.94), channel_id=1, source_target_pairs={{0,16},{1,17},{2,18},{3,19},{4,20},{5,21},{6,22},{7,23},{8,24},{9,... | collective-permute-start | bytes 1769480 | tf_op jit(solution)/shard_map/ppermute | solution.py:34
  31.2 23.5 %collective-permute-start.10 = (bf16[2,2,24,3072]{3,2,1,0:T(8,128)(2,1)S(1)}, bf16[2,2,24,3072]{3,2,1,0:T(8,128)(2,1)S(1)}, u32[]{:S(2)}, u32[]{:S(2)}) collective-permute-start(bf16[2,2,24,3072]{3,2,1,0:T(8,128)(2,1)S(1)} %pad_maximum_fusion.3.refs_2_), channel_id=1, source_target_pairs={{0,1},{1,0},{2,3},{3,2},{4,5},{5,4},{6,7},{7,6},{8,9},{9,8},{10,11... | collective-permute-start | bytes 1769480 | tf_op jit(solution)/shard_map/ppermute | solution.py:34
  32.7 14.3 %collective-permute-start.11 = (bf16[2,64,768]{2,1,0:T(8,128)(2,1)S(1)}, bf16[2,64,768]{2,1,0:T(8,128)(2,1)S(1)}, u32[]{:S(2)}, u32[]{:S(2)}) collective-permute-start(bf16[2,64,768]{2,1,0:T(8,128)(2,1)S(1)} %pad_maximum_fusion.9), channel_id=1, source_target_pairs={{0,16},{1,17},{2,18},{3,19},{4,20},{5,21},{6,22},{7,23},{8,24},{9,... | collective-permute-start | bytes 589832 | tf_op jit(solution)/shard_map/ppermute | solution.py:34
  33.2 25.9 %copy-start.5 = (bf16[896,768]{1,0:T(8,128)(2,1)S(1)}, bf16[896,768]{1,0:T(8,128)(2,1)}, u32[]{:S(2)}) copy-start(bf16[896,768]{1,0:T(8,128)(2,1)} %get-tuple-element.220.refs_8_.normed_ref) | copy-start | bytes 4128772
  33.2 17.5 %collective-permute-start.4 = (bf16[24,4096]{1,0:T(8,128)(2,1)S(1)}, bf16[24,4096]{1,0:T(8,128)(2,1)S(1)}, u32[]{:S(2)}, u32[]{:S(2)}) collective-permute-start(bf16[24,4096]{1,0:T(8,128)(2,1)S(1)} %convert_element_type.118), channel_id=1, source_target_pairs={{0,2},{1,3},{2,0},{3,1},{4,6},{5,7},{6,4},{7,5},{8,10},{9,11},{10,... | collective-permute-start | bytes 589832 | tf_op jit(solution)/shard_map/ppermute | solution.py:34
  34.1 16.7 %collective-permute-start.5 = (bf16[24,4096]{1,0:T(8,128)(2,1)S(1)}, bf16[24,4096]{1,0:T(8,128)(2,1)S(1)}, u32[]{:S(2)}, u32[]{:S(2)}) collective-permute-start(bf16[24,4096]{1,0:T(8,128)(2,1)S(1)} %convert_element_type.118), channel_id=1, source_target_pairs={{0,4},{1,5},{2,6},{3,7},{4,0},{5,1},{6,2},{7,3},{8,12},{9,13},{10,... | collective-permute-start | bytes 589832 | tf_op jit(solution)/shard_map/ppermute | solution.py:34
  47.1 7.6 %collective-permute-start.6 = (bf16[24,4096]{1,0:T(8,128)(2,1)S(1)}, bf16[24,4096]{1,0:T(8,128)(2,1)S(1)}, u32[]{:S(2)}, u32[]{:S(2)}) collective-permute-start(bf16[24,4096]{1,0:T(8,128)(2,1)S(1)} %convert_element_type.118), channel_id=1, source_target_pairs={{0,6},{1,7},{2,4},{3,5},{4,2},{5,3},{6,0},{7,1},{8,14},{9,15},{10,... | collective-permute-start | bytes 589832 | tf_op jit(solution)/shard_map/ppermute | solution.py:34
  50.7 6.2 %collective-permute-start.14 = (bf16[2,2,24,3072]{3,2,1,0:T(8,128)(2,1)S(1)}, bf16[2,2,24,3072]{3,2,1,0:T(8,128)(2,1)S(1)}, u32[]{:S(2)}, u32[]{:S(2)}) collective-permute-start(bf16[2,2,24,3072]{3,2,1,0:T(8,128)(2,1)S(1)} %bitcast.95), channel_id=1, source_target_pairs={{0,8},{1,9},{2,10},{3,11},{4,12},{5,13},{6,14},{7,15},{8,0},{9,1},... | collective-permute-start | bytes 1769480 | tf_op jit(solution)/shard_map/ppermute | solution.py:34
  50.8 7.3 %collective-permute-start.16 = (bf16[2,2,24,3072]{3,2,1,0:T(8,128)(2,1)S(1)}, bf16[2,2,24,3072]{3,2,1,0:T(8,128)(2,1)S(1)}, u32[]{:S(2)}, u32[]{:S(2)}) collective-permute-start(bf16[2,2,24,3072]{3,2,1,0:T(8,128)(2,1)S(1)} %pad_maximum_fusion.3.refs_2_), channel_id=1, source_target_pairs={{0,8},{1,9},{2,10},{3,11},{4,12},{5,13},{6,14},{7,15},{8,0},{9,1},... | collective-permute-start | bytes 1769480 | tf_op jit(solution)/shard_map/ppermute | solution.py:34
  54.7 10.8 %collective-permute-start.12 = (bf16[2,24,4096]{2,1,0:T(8,128)(2,1)S(1)}, bf16[2,24,4096]{2,1,0:T(8,128)(2,1)S(1)}, u32[]{:S(2)}, u32[]{:S(2)}) collective-permute-start(bf16[2,24,4096]{2,1,0:T(8,128)(2,1)S(1)} %pad_maximum_fusion.5), channel_id=1, source_target_pairs={{0,1},{1,0},{2,3},{3,2},{4,5},{5,4},{6,7},{7,6},{8,9},{9,8},{10,11... | collective-permute-start | bytes 1179656 | tf_op jit(solution)/shard_map/ppermute | solution.py:34
  56.3 2.0 collective-permute-start.15
  56.3 2.8 %collective-permute-start.17 = (bf16[2,2,24,3072]{3,2,1,0:T(8,128)(2,1)S(1)}, bf16[2,2,24,3072]{3,2,1,0:T(8,128)(2,1)S(1)}, u32[]{:S(2)}, u32[]{:S(2)}) collective-permute-start(bf16[2,2,24,3072]{3,2,1,0:T(8,128)(2,1)S(1)} %collective-permute-done.10.refs_3_), channel_id=1, source_target_pairs={{0,8},{1,9},{2,10},{3,11},{4,12},{5,13},{6,14},{7,15},{8,0},{9,1},... | collective-permute-start | bytes 1769480 | tf_op jit(solution)/shard_map/ppermute | solution.py:34
  56.9 11.1 %collective-permute-start.13 = (bf16[2,24,4096]{2,1,0:T(8,128)(2,1)S(1)}, bf16[2,24,4096]{2,1,0:T(8,128)(2,1)S(1)}, u32[]{:S(2)}, u32[]{:S(2)}) collective-permute-start(bf16[2,24,4096]{2,1,0:T(8,128)(2,1)S(1)} %pad_maximum_fusion.6), channel_id=1, source_target_pairs={{0,16},{1,17},{2,18},{3,19},{4,20},{5,21},{6,22},{7,23},{8,24},{9,... | collective-permute-start | bytes 1179656 | tf_op jit(solution)/shard_map/ppermute | solution.py:34
  68.2 21.5 %collective-permute-start.18 = (bf16[2,2,24,4096]{3,2,1,0:T(8,128)(2,1)S(1)}, bf16[2,2,24,4096]{3,2,1,0:T(8,128)(2,1)S(1)}, u32[]{:S(2)}, u32[]{:S(2)}) collective-permute-start(bf16[2,2,24,4096]{3,2,1,0:T(8,128)(2,1)S(1)} %bitcast.91), channel_id=1, source_target_pairs={{0,16},{1,17},{2,18},{3,19},{4,20},{5,21},{6,22},{7,23},{8,24},{9,... | collective-permute-start | bytes 2359304 | tf_op jit(solution)/shard_map/ppermute | solution.py:34
  69.4 20.8 %copy-start.9 = (f32[768]{0:T(1024)S(1)}, f32[768]{0:T(1024)}, u32[]{:S(2)}) copy-start(f32[768]{0:T(1024)} %param.24) | copy-start | bytes 9220
  69.4 20.2 %collective-permute-start.19 = (bf16[2,2,24,4096]{3,2,1,0:T(8,128)(2,1)S(1)}, bf16[2,2,24,4096]{3,2,1,0:T(8,128)(2,1)S(1)}, u32[]{:S(2)}, u32[]{:S(2)}) collective-permute-start(bf16[2,2,24,4096]{3,2,1,0:T(8,128)(2,1)S(1)} %pad_maximum_fusion.1.refs_2_), channel_id=1, source_target_pairs={{0,1},{1,0},{2,3},{3,2},{4,5},{5,4},{6,7},{7,6},{8,9},{9,8},{10,11... | collective-permute-start | bytes 2359304 | tf_op jit(solution)/shard_map/ppermute | solution.py:34
  70.0 19.6 %collective-permute-start.20 = (bf16[2,2,64,768]{3,2,1,0:T(8,128)(2,1)S(1)}, bf16[2,2,64,768]{3,2,1,0:T(8,128)(2,1)S(1)}, u32[]{:S(2)}, u32[]{:S(2)}) collective-permute-start(bf16[2,2,64,768]{3,2,1,0:T(8,128)(2,1)S(1)} %pad_maximum_fusion.4.refs_0_), channel_id=1, source_target_pairs={{0,4},{1,5},{2,6},{3,7},{4,0},{5,1},{6,2},{7,3},{8,12},{9,13},{10,... | collective-permute-start | bytes 1179656 | tf_op jit(solution)/shard_map/ppermute | solution.py:34
  73.4 21.3 %collective-permute-start.25 = (bf16[2,2,24,4096]{3,2,1,0:T(8,128)(2,1)S(1)}, bf16[2,2,24,4096]{3,2,1,0:T(8,128)(2,1)S(1)}, u32[]{:S(2)}, u32[]{:S(2)}) collective-permute-start(bf16[2,2,24,4096]{3,2,1,0:T(8,128)(2,1)S(1)} %bitcast.92), channel_id=1, source_target_pairs={{0,8},{1,9},{2,10},{3,11},{4,12},{5,13},{6,14},{7,15},{8,0},{9,1},... | collective-permute-start | bytes 2359304 | tf_op jit(solution)/shard_map/ppermute | solution.py:34
  73.4 21.4 %collective-permute-start.27 = (bf16[2,2,24,4096]{3,2,1,0:T(8,128)(2,1)S(1)}, bf16[2,2,24,4096]{3,2,1,0:T(8,128)(2,1)S(1)}, u32[]{:S(2)}, u32[]{:S(2)}) collective-permute-start(bf16[2,2,24,4096]{3,2,1,0:T(8,128)(2,1)S(1)} %pad_maximum_fusion.1.refs_2_), channel_id=1, source_target_pairs={{0,8},{1,9},{2,10},{3,11},{4,12},{5,13},{6,14},{7,15},{8,0},{9,1},... | collective-permute-start | bytes 2359304 | tf_op jit(solution)/shard_map/ppermute | solution.py:34
  89.7 7.1 %collective-permute-start.26 = (bf16[2,2,24,4096]{3,2,1,0:T(8,128)(2,1)S(1)}, bf16[2,2,24,4096]{3,2,1,0:T(8,128)(2,1)S(1)}, u32[]{:S(2)}, u32[]{:S(2)}) collective-permute-start(bf16[2,2,24,4096]{3,2,1,0:T(8,128)(2,1)S(1)} %collective-permute-done.18.refs_1_), channel_id=1, source_target_pairs={{0,8},{1,9},{2,10},{3,11},{4,12},{5,13},{6,14},{7,15},{8,0},{9,1},... | collective-permute-start | bytes 2359304 | tf_op jit(solution)/shard_map/ppermute | solution.py:34
  89.7 7.3 %collective-permute-start.28 = (bf16[2,2,24,4096]{3,2,1,0:T(8,128)(2,1)S(1)}, bf16[2,2,24,4096]{3,2,1,0:T(8,128)(2,1)S(1)}, u32[]{:S(2)}, u32[]{:S(2)}) collective-permute-start(bf16[2,2,24,4096]{3,2,1,0:T(8,128)(2,1)S(1)} %collective-permute-done.19.refs_3_), channel_id=1, source_target_pairs={{0,8},{1,9},{2,10},{3,11},{4,12},{5,13},{6,14},{7,15},{8,0},{9,1},... | collective-permute-start | bytes 2359304 | tf_op jit(solution)/shard_map/ppermute | solution.py:34
  90.2 22.4 %collective-permute-start.21 = (bf16[2,2,64,768]{3,2,1,0:T(8,128)(2,1)S(1)}, bf16[2,2,64,768]{3,2,1,0:T(8,128)(2,1)S(1)}, u32[]{:S(2)}, u32[]{:S(2)}) collective-permute-start(bf16[2,2,64,768]{3,2,1,0:T(8,128)(2,1)S(1)} %pad_maximum_fusion.4.refs_0_), channel_id=1, source_target_pairs={{0,2},{1,3},{2,0},{3,1},{4,6},{5,7},{6,4},{7,5},{8,10},{9,11},{10,... | collective-permute-start | bytes 1179656 | tf_op jit(solution)/shard_map/ppermute | solution.py:34
  94.7 17.9 %copy-start.7 = (bf16[896,768]{1,0:T(8,128)(2,1)}, bf16[896,768]{1,0:T(8,128)(2,1)S(1)}, u32[]{:S(2)}) copy-start(bf16[896,768]{1,0:T(8,128)(2,1)S(1)} %get-tuple-element.247.refs_8_) | copy-start | bytes 4128772
  94.7 17.9 %collective-permute-start.23 = (bf16[2,2,64,768]{3,2,1,0:T(8,128)(2,1)S(1)}, bf16[2,2,64,768]{3,2,1,0:T(8,128)(2,1)S(1)}, u32[]{:S(2)}, u32[]{:S(2)}) collective-permute-start(bf16[2,2,64,768]{3,2,1,0:T(8,128)(2,1)S(1)} %pad_maximum_fusion.4.refs_0_), channel_id=1, source_target_pairs={{0,8},{1,9},{2,10},{3,11},{4,12},{5,13},{6,14},{7,15},{8,0},{9,1},... | collective-permute-start | bytes 1179656 | tf_op jit(solution)/shard_map/ppermute | solution.py:34
  94.8 17.8 %collective-permute-start.22 = (bf16[2,2,64,768]{3,2,1,0:T(8,128)(2,1)S(1)}, bf16[2,2,64,768]{3,2,1,0:T(8,128)(2,1)S(1)}, u32[]{:S(2)}, u32[]{:S(2)}) collective-permute-start(bf16[2,2,64,768]{3,2,1,0:T(8,128)(2,1)S(1)} %collective-permute-done.20.refs_2_), channel_id=1, source_target_pairs={{0,2},{1,3},{2,0},{3,1},{4,6},{5,7},{6,4},{7,5},{8,10},{9,11},{10,... | collective-permute-start | bytes 1179656 | tf_op jit(solution)/shard_map/ppermute | solution.py:34
  96.8 15.8 %collective-permute-start.24 = (bf16[2,2,64,768]{3,2,1,0:T(8,128)(2,1)S(1)}, bf16[2,2,64,768]{3,2,1,0:T(8,128)(2,1)S(1)}, u32[]{:S(2)}, u32[]{:S(2)}) collective-permute-start(bf16[2,2,64,768]{3,2,1,0:T(8,128)(2,1)S(1)} %collective-permute-done.20.refs_2_), channel_id=1, source_target_pairs={{0,8},{1,9},{2,10},{3,11},{4,12},{5,13},{6,14},{7,15},{8,0},{9,1},... | collective-permute-start | bytes 1179656 | tf_op jit(solution)/shard_map/ppermute | solution.py:34
  112.6 23.0 %copy-start.2 = (bf16[2,512,768]{2,1,0:T(8,128)(2,1)}, bf16[2,512,768]{2,1,0:T(8,128)(2,1)S(1)}, u32[]{:S(2)}) copy-start(bf16[2,512,768]{2,1,0:T(8,128)(2,1)S(1)} %get-tuple-element.270) | copy-start | bytes 4718596
  112.6 4.6 %collective-permute-start.31 = (bf16[2,512,768]{2,1,0:T(8,128)(2,1)S(1)}, bf16[2,512,768]{2,1,0:T(8,128)(2,1)S(1)}, u32[]{:S(2)}, u32[]{:S(2)}) collective-permute-start(bf16[2,512,768]{2,1,0:T(8,128)(2,1)S(1)} %get-tuple-element.256), channel_id=1, source_target_pairs={{0,8},{1,9},{2,10},{3,11},{4,12},{5,13},{6,14},{7,15},{8,0},{9,1},... | collective-permute-start | bytes 4718600 | tf_op jit(solution)/shard_map/ppermute | solution.py:34
  113.0 3.6 %collective-permute-start.29 = (bf16[2,2,64,768]{3,2,1,0:T(8,128)(2,1)S(1)}, bf16[2,2,64,768]{3,2,1,0:T(8,128)(2,1)S(1)}, u32[]{:S(2)}, u32[]{:S(2)}) collective-permute-start(bf16[2,2,64,768]{3,2,1,0:T(8,128)(2,1)S(1)} %collective-permute-done.21.refs_1_), channel_id=1, source_target_pairs={{0,8},{1,9},{2,10},{3,11},{4,12},{5,13},{6,14},{7,15},{8,0},{9,1},... | collective-permute-start | bytes 1179656 | tf_op jit(solution)/shard_map/ppermute | solution.py:34
  113.2 4.0 %collective-permute-start.30 = (bf16[2,2,64,768]{3,2,1,0:T(8,128)(2,1)S(1)}, bf16[2,2,64,768]{3,2,1,0:T(8,128)(2,1)S(1)}, u32[]{:S(2)}, u32[]{:S(2)}) collective-permute-start(bf16[2,2,64,768]{3,2,1,0:T(8,128)(2,1)S(1)} %collective-permute-done.22.refs_3_), channel_id=1, source_target_pairs={{0,8},{1,9},{2,10},{3,11},{4,12},{5,13},{6,14},{7,15},{8,0},{9,1},... | collective-permute-start | bytes 1179656 | tf_op jit(solution)/shard_map/ppermute | solution.py:34
  117.2 18.4 %copy-start.3 = (bf16[2,512,768]{2,1,0:T(8,128)(2,1)}, bf16[2,512,768]{2,1,0:T(8,128)(2,1)S(1)}, u32[]{:S(2)}) copy-start(bf16[2,512,768]{2,1,0:T(8,128)(2,1)S(1)} %collective-permute-done.31) | copy-start | bytes 4718596
  118.0 19.9 %collective-permute-start.32 = (bf16[2,4,64,768]{3,2,1,0:T(8,128)(2,1)S(1)}, bf16[2,4,64,768]{3,2,1,0:T(8,128)(2,1)S(1)}, u32[]{:S(2)}, u32[]{:S(2)}) collective-permute-start(bf16[2,4,64,768]{3,2,1,0:T(8,128)(2,1)S(1)} %plane.3), channel_id=1, source_target_pairs={{0,1},{1,0},{2,3},{3,2},{4,5},{5,4},{6,7},{7,6},{8,9},{9,8},{10,11... | collective-permute-start | bytes 2359304 | tf_op jit(solution)/shard_map/ppermute | solution.py:34
  137.8 17.5 %collective-permute-start.34 = (bf16[2,192,4096]{2,1,0:T(8,128)(2,1)S(1)}, bf16[2,192,4096]{2,1,0:T(8,128)(2,1)S(1)}, u32[]{:S(2)}, u32[]{:S(2)}) collective-permute-start(bf16[2,192,4096]{2,1,0:T(8,128)(2,1)S(1)} %get-tuple-element.277), channel_id=1, source_target_pairs={{0,8},{1,9},{2,10},{3,11},{4,12},{5,13},{6,14},{7,15},{8,0},{9,1},... | collective-permute-start | bytes 9437192 | tf_op jit(solution)/shard_map/ppermute | solution.py:34
  139.7 15.6 %collective-permute-start.33 = (bf16[4,64,768]{2,1,0:T(8,128)(2,1)S(1)}, bf16[4,64,768]{2,1,0:T(8,128)(2,1)S(1)}, u32[]{:S(2)}, u32[]{:S(2)}) collective-permute-start(bf16[4,64,768]{2,1,0:T(8,128)(2,1)S(1)} %far.3), channel_id=1, source_target_pairs={{0,16},{1,17},{2,18},{3,19},{4,20},{5,21},{6,22},{7,23},{8,24},{9,... | collective-permute-start | bytes 1179656 | tf_op jit(solution)/shard_map/ppermute | solution.py:34
  156.2 23.1 %collective-permute-start.38 = (bf16[2,2,24,4096]{3,2,1,0:T(8,128)(2,1)S(1)}, bf16[2,2,24,4096]{3,2,1,0:T(8,128)(2,1)S(1)}, u32[]{:S(2)}, u32[]{:S(2)}) collective-permute-start(bf16[2,2,24,4096]{3,2,1,0:T(8,128)(2,1)S(1)} %get-tuple-element.290), channel_id=1, source_target_pairs={{0,1},{1,0},{2,3},{3,2},{4,5},{5,4},{6,7},{7,6},{8,9},{9,8},{10,11... | collective-permute-start | bytes 2359304 | tf_op jit(solution)/shard_map/ppermute | solution.py:34
  157.1 22.3 %collective-permute-start.39 = (bf16[2,2,24,4096]{3,2,1,0:T(8,128)(2,1)S(1)}, bf16[2,2,24,4096]{3,2,1,0:T(8,128)(2,1)S(1)}, u32[]{:S(2)}, u32[]{:S(2)}) collective-permute-start(bf16[2,2,24,4096]{3,2,1,0:T(8,128)(2,1)S(1)} %get-tuple-element.291), channel_id=1, source_target_pairs={{0,16},{1,17},{2,18},{3,19},{4,20},{5,21},{6,22},{7,23},{8,24},{9,... | collective-permute-start | bytes 2359304 | tf_op jit(solution)/shard_map/ppermute | solution.py:34
  159.9 19.5 %collective-permute-start.35 = (bf16[64,768]{1,0:T(8,128)(2,1)S(1)}, bf16[64,768]{1,0:T(8,128)(2,1)S(1)}, u32[]{:S(2)}, u32[]{:S(2)}) collective-permute-start(bf16[64,768]{1,0:T(8,128)(2,1)S(1)} %get-tuple-element.285), channel_id=1, source_target_pairs={{0,2},{1,3},{2,0},{3,1},{4,6},{5,7},{6,4},{7,5},{8,10},{9,11},{10,... | collective-permute-start | bytes 294920 | tf_op jit(solution)/shard_map/ppermute | solution.py:34
  160.5 18.8 %collective-permute-start.36 = (bf16[64,768]{1,0:T(8,128)(2,1)S(1)}, bf16[64,768]{1,0:T(8,128)(2,1)S(1)}, u32[]{:S(2)}, u32[]{:S(2)}) collective-permute-start(bf16[64,768]{1,0:T(8,128)(2,1)S(1)} %get-tuple-element.286), channel_id=1, source_target_pairs={{0,4},{1,5},{2,6},{3,7},{4,0},{5,1},{6,2},{7,3},{8,12},{9,13},{10,... | collective-permute-start | bytes 294920 | tf_op jit(solution)/shard_map/ppermute | solution.py:34
  163.9 15.5 %collective-permute-start.37 = (bf16[64,768]{1,0:T(8,128)(2,1)S(1)}, bf16[64,768]{1,0:T(8,128)(2,1)S(1)}, u32[]{:S(2)}, u32[]{:S(2)}) collective-permute-start(bf16[64,768]{1,0:T(8,128)(2,1)S(1)} %get-tuple-element.287), channel_id=1, source_target_pairs={{0,6},{1,7},{2,4},{3,5},{4,2},{5,3},{6,0},{7,1},{8,14},{9,15},{10,... | collective-permute-start | bytes 294920 | tf_op jit(solution)/shard_map/ppermute | solution.py:34
  180.2 12.1 %collective-permute-start.40 = (bf16[2,24,4096]{2,1,0:T(8,128)(2,1)S(1)}, bf16[2,24,4096]{2,1,0:T(8,128)(2,1)S(1)}, u32[]{:S(2)}, u32[]{:S(2)}) collective-permute-start(bf16[2,24,4096]{2,1,0:T(8,128)(2,1)S(1)} %get-tuple-element.300), channel_id=1, source_target_pairs={{0,16},{1,17},{2,18},{3,19},{4,20},{5,21},{6,22},{7,23},{8,24},{9,... | collective-permute-start | bytes 1179656 | tf_op jit(solution)/shard_map/ppermute | solution.py:34
  181.6 10.7 %collective-permute-start.41 = (bf16[2,24,4096]{2,1,0:T(8,128)(2,1)S(1)}, bf16[2,24,4096]{2,1,0:T(8,128)(2,1)S(1)}, u32[]{:S(2)}, u32[]{:S(2)}) collective-permute-start(bf16[2,24,4096]{2,1,0:T(8,128)(2,1)S(1)} %get-tuple-element.301), channel_id=1, source_target_pairs={{0,1},{1,0},{2,3},{3,2},{4,5},{5,4},{6,7},{7,6},{8,9},{9,8},{10,11... | collective-permute-start | bytes 1179656 | tf_op jit(solution)/shard_map/ppermute | solution.py:34
  192.3 4.6 %collective-permute-start.42 = (bf16[2,192,3072]{2,1,0:T(8,128)(2,1)S(1)}, bf16[2,192,3072]{2,1,0:T(8,128)(2,1)S(1)}, u32[]{:S(2)}, u32[]{:S(2)}) collective-permute-start(bf16[2,192,3072]{2,1,0:T(8,128)(2,1)S(1)} %get-tuple-element.309), channel_id=1, source_target_pairs={{0,8},{1,9},{2,10},{3,11},{4,12},{5,13},{6,14},{7,15},{8,0},{9,1},... | collective-permute-start | bytes 7077896 | tf_op jit(solution)/shard_map/ppermute | solution.py:34
  192.4 4.5 %collective-permute-start.43 = (f32[24,128]{1,0:T(8,128)S(1)}, f32[24,128]{1,0:T(8,128)S(1)}, u32[]{:S(2)}, u32[]{:S(2)}) collective-permute-start(f32[24,128]{1,0:T(8,128)S(1)} %get-tuple-element.316), channel_id=1, source_target_pairs={{0,8},{1,9},{2,10},{3,11},{4,12},{5,13},{6,14},{7,15},{8,0},{9,1},... | collective-permute-start | bytes 36872 | tf_op jit(solution)/shard_map/ppermute | solution.py:34
  197.7 20.8 %collective-permute-start.44 = (bf16[2,2,24,3072]{3,2,1,0:T(8,128)(2,1)S(1)}, bf16[2,2,24,3072]{3,2,1,0:T(8,128)(2,1)S(1)}, u32[]{:S(2)}, u32[]{:S(2)}) collective-permute-start(bf16[2,2,24,3072]{3,2,1,0:T(8,128)(2,1)S(1)} %get-tuple-element.324), channel_id=1, source_target_pairs={{0,1},{1,0},{2,3},{3,2},{4,5},{5,4},{6,7},{7,6},{8,9},{9,8},{10,11... | collective-permute-start | bytes 1769480 | tf_op jit(solution)/shard_map/ppermute | solution.py:34
  198.6 19.9 %collective-permute-start.45 = (bf16[2,2,24,3072]{3,2,1,0:T(8,128)(2,1)S(1)}, bf16[2,2,24,3072]{3,2,1,0:T(8,128)(2,1)S(1)}, u32[]{:S(2)}, u32[]{:S(2)}) collective-permute-start(bf16[2,2,24,3072]{3,2,1,0:T(8,128)(2,1)S(1)} %get-tuple-element.325), channel_id=1, source_target_pairs={{0,16},{1,17},{2,18},{3,19},{4,20},{5,21},{6,22},{7,23},{8,24},{9,... | collective-permute-start | bytes 1769480 | tf_op jit(solution)/shard_map/ppermute | solution.py:34
  199.3 4.0 %collective-permute-start.46 = (f32[24,128]{1,0:T(8,128)S(1)}, f32[24,128]{1,0:T(8,128)S(1)}, u32[]{:S(2)}, u32[]{:S(2)}) collective-permute-start(f32[24,128]{1,0:T(8,128)S(1)} %add.171), channel_id=1, source_target_pairs={{0,2},{1,3},{2,0},{3,1},{4,6},{5,7},{6,4},{7,5},{8,10},{9,11},{10,... | collective-permute-start | bytes 36872 | tf_op jit(solution)/shard_map/ppermute | solution.py:34
  199.4 15.3 %collective-permute-start.47 = (bf16[24,4096]{1,0:T(8,128)(2,1)S(1)}, bf16[24,4096]{1,0:T(8,128)(2,1)S(1)}, u32[]{:S(2)}, u32[]{:S(2)}) collective-permute-start(bf16[24,4096]{1,0:T(8,128)(2,1)S(1)} %get-tuple-element.336), channel_id=1, source_target_pairs={{0,2},{1,3},{2,0},{3,1},{4,6},{5,7},{6,4},{7,5},{8,10},{9,11},{10,... | collective-permute-start | bytes 589832 | tf_op jit(solution)/shard_map/ppermute | solution.py:34
  201.3 17.2 %collective-permute-start.48 = (bf16[24,4096]{1,0:T(8,128)(2,1)S(1)}, bf16[24,4096]{1,0:T(8,128)(2,1)S(1)}, u32[]{:S(2)}, u32[]{:S(2)}) collective-permute-start(bf16[24,4096]{1,0:T(8,128)(2,1)S(1)} %get-tuple-element.337), channel_id=1, source_target_pairs={{0,4},{1,5},{2,6},{3,7},{4,0},{5,1},{6,2},{7,3},{8,12},{9,13},{10,... | collective-permute-start | bytes 589832 | tf_op jit(solution)/shard_map/ppermute | solution.py:34
  203.3 15.2 %collective-permute-start.49 = (bf16[24,4096]{1,0:T(8,128)(2,1)S(1)}, bf16[24,4096]{1,0:T(8,128)(2,1)S(1)}, u32[]{:S(2)}, u32[]{:S(2)}) collective-permute-start(bf16[24,4096]{1,0:T(8,128)(2,1)S(1)} %get-tuple-element.338), channel_id=1, source_target_pairs={{0,6},{1,7},{2,4},{3,5},{4,2},{5,3},{6,0},{7,1},{8,14},{9,15},{10,... | collective-permute-start | bytes 589832 | tf_op jit(solution)/shard_map/ppermute | solution.py:34
  219.3 8.2 %collective-permute-start.50 = (bf16[2,24,3072]{2,1,0:T(8,128)(2,1)S(1)}, bf16[2,24,3072]{2,1,0:T(8,128)(2,1)S(1)}, u32[]{:S(2)}, u32[]{:S(2)}) collective-permute-start(bf16[2,24,3072]{2,1,0:T(8,128)(2,1)S(1)} %get-tuple-element.342), channel_id=1, source_target_pairs={{0,16},{1,17},{2,18},{3,19},{4,20},{5,21},{6,22},{7,23},{8,24},{9,... | collective-permute-start | bytes 884744 | tf_op jit(solution)/shard_map/ppermute | solution.py:34
  220.7 6.8 %collective-permute-start.51 = (bf16[2,24,3072]{2,1,0:T(8,128)(2,1)S(1)}, bf16[2,24,3072]{2,1,0:T(8,128)(2,1)S(1)}, u32[]{:S(2)}, u32[]{:S(2)}) collective-permute-start(bf16[2,24,3072]{2,1,0:T(8,128)(2,1)S(1)} %get-tuple-element.343), channel_id=1, source_target_pairs={{0,1},{1,0},{2,3},{3,2},{4,5},{5,4},{6,7},{7,6},{8,9},{9,8},{10,11... | collective-permute-start | bytes 884744 | tf_op jit(solution)/shard_map/ppermute | solution.py:34
  221.9 5.6 %collective-permute-start.52 = (f32[24,128]{1,0:T(8,128)S(1)}, f32[24,128]{1,0:T(8,128)S(1)}, u32[]{:S(2)}, u32[]{:S(2)}) collective-permute-start(f32[24,128]{1,0:T(8,128)S(1)} %add.172), channel_id=1, source_target_pairs={{0,4},{1,5},{2,6},{3,7},{4,0},{5,1},{6,2},{7,3},{8,12},{9,13},{10,... | collective-permute-start | bytes 36872 | tf_op jit(solution)/shard_map/ppermute | solution.py:34
  228.5 18.5 %collective-permute-start.55 = (bf16[24,3072]{1,0:T(8,128)(2,1)S(1)}, bf16[24,3072]{1,0:T(8,128)(2,1)S(1)}, u32[]{:S(2)}, u32[]{:S(2)}) collective-permute-start(bf16[24,3072]{1,0:T(8,128)(2,1)S(1)} %get-tuple-element.379), channel_id=1, source_target_pairs={{0,6},{1,7},{2,4},{3,5},{4,2},{5,3},{6,0},{7,1},{8,14},{9,15},{10,... | collective-permute-start | bytes 442376 | tf_op jit(solution)/shard_map/ppermute | solution.py:34
  230.9 16.0 %collective-permute-start.54 = (bf16[24,3072]{1,0:T(8,128)(2,1)S(1)}, bf16[24,3072]{1,0:T(8,128)(2,1)S(1)}, u32[]{:S(2)}, u32[]{:S(2)}) collective-permute-start(bf16[24,3072]{1,0:T(8,128)(2,1)S(1)} %get-tuple-element.378), channel_id=1, source_target_pairs={{0,4},{1,5},{2,6},{3,7},{4,0},{5,1},{6,2},{7,3},{8,12},{9,13},{10,... | collective-permute-start | bytes 442376 | tf_op jit(solution)/shard_map/ppermute | solution.py:34
  233.8 13.1 %collective-permute-start.53 = (bf16[24,3072]{1,0:T(8,128)(2,1)S(1)}, bf16[24,3072]{1,0:T(8,128)(2,1)S(1)}, u32[]{:S(2)}, u32[]{:S(2)}) collective-permute-start(bf16[24,3072]{1,0:T(8,128)(2,1)S(1)} %get-tuple-element.377), channel_id=1, source_target_pairs={{0,2},{1,3},{2,0},{3,1},{4,6},{5,7},{6,4},{7,5},{8,10},{9,11},{10,... | collective-permute-start | bytes 442376 | tf_op jit(solution)/shard_map/ppermute | solution.py:34
  234.3 7.6 %collective-permute-start.56 = (f32[24,128]{1,0:T(8,128)S(1)}, f32[24,128]{1,0:T(8,128)S(1)}, u32[]{:S(2)}, u32[]{:S(2)}) collective-permute-start(f32[24,128]{1,0:T(8,128)S(1)} %add.173), channel_id=1, source_target_pairs={{0,1},{1,0},{2,3},{3,2},{4,5},{5,4},{6,7},{7,6},{8,9},{9,8},{10,11... | collective-permute-start | bytes 36872 | tf_op jit(solution)/shard_map/ppermute | solution.py:34
  242.0 3.8 %collective-permute-start.57 = (f32[24,128]{1,0:T(8,128)S(1)}, f32[24,128]{1,0:T(8,128)S(1)}, u32[]{:S(2)}, u32[]{:S(2)}) collective-permute-start(f32[24,128]{1,0:T(8,128)S(1)} %add.186), channel_id=1, source_target_pairs={{0,16},{1,17},{2,18},{3,19},{4,20},{5,21},{6,22},{7,23},{8,24},{9,... | collective-permute-start | bytes 36872 | tf_op jit(solution)/shard_map/ppermute | solution.py:34
  (4 other events, 36.3 us)

commit v6 on v5

--- a/solution.py
+++ b/solution.py
@@ -308,7 +308,7 @@
 
 
 class NarrowScatter(Scatter):
-    def both(self, got, lead, pick, pinned=True):
+    def both(self, got, lead, pick, pinned=False):
         kept, got = in_hbm(self.kept, got) if pinned else (self.kept, got)
         return [(kept, lead, pick), (got, lead, pick)]
 
@@ -837,7 +837,7 @@
             transcendentals=0,
         ),
         name="gate_back",
-    )(place, *pieces, *in_hbm(normed_two, cot_low, by_gate, by_up))
+    )(place, *pieces, normed_two, cot_low, *in_hbm(by_gate, by_up))
     return (*results, full.reshape(hidden, width))
 
 

time: 249 us -> 247 us (level)
  Pallas kernels: 133 us -> 129 us
  transfers between devices with their start and end apart: 58 -> 58, of which waited for: 14 -> 15; matrix products, arithmetic and copies ran while one was open for 4% -> 4% of each run, Pallas kernels for 51% -> 51%
where the time goes in v6:
time: 247 us; the launch traced here: 246 us
  Pallas kernels  129 us (52%)
  starting transfers between devices  67.6 us (27%)
  waiting for transfers between devices  34.8 us (14%)
  other arithmetic  7.98 us (3%)
  local copies, waits for them, and re-layouts  4.5 us (2%)
    ppermute x58, starting transfers between devices, swap(): return lax.ppermute(values, both, flip_pairs(**flips))  67.6 us
    ppermute x58, waiting for transfers between devices, swap(): return lax.ppermute(values, both, flip_pairs(**flips))  34.8 us
    pallas_call x1, Pallas kernels, gate_back(): pl.pallas_call(kernel, grid=(hidden // tile,), out_shape=(pltpu.HBM((2, r...  15.9 us
    pallas_call x1, Pallas kernels, gate_forward(): pl.pallas_call(kernel, grid=(hidden // tile,), out_shape=(pltpu.HBM((rows...  15.4 us
    pallas_call x1, Pallas kernels, attend_back(): pl.pallas_call(functools.partial(attend_back_kernel, docs, length), grid=...  15 us
    pallas_call x1, Pallas kernels, middle_back(): pl.pallas_call(middle_back_kernel, out_shape=(pltpu.HBM((rows, width), jn...  14.3 us
    pallas_call x1, Pallas kernels, attend(): pl.pallas_call(functools.partial(attend_kernel, docs, length, group), gri...  13.6 us
    pallas_call x2, Pallas kernels, by_parts(): pl.pallas_call(kernel, grid=(rows // count,), out_shape=[pltpu.HBM((rows,...  11.7 us
  transfers between devices with their start and end apart: 58, of which 15 were waited for; matrix products, arithmetic and copies ran while one was open for 4% of the time, Pallas kernels for 51%

profile of v6, /device:TPU:0, one launch (start us, length us, event | category | flops | bytes accessed | tf_op | source)
XLA Modules:
  0.0 245.9 jit_solution(7669920609541153273)
XLA Ops:
  0.7 0.9 convert.7
  1.6 0.9 convert.6
  2.6 3.1 %collective-permute-start = (bf16[24,3072]{1,0:T(8,128)(2,1)S(1)}, bf16[24,3072]{1,0:T(8,128)(2,1)S(1)}, u32[]{:S(2)}, u32[]{:S(2)}) collective-permute-start(bf16[24,3072]{1,0:T(8,128)(2,1)S(1)} %pad_maximum_fusion.10), channel_id=1, source_target_pairs={{0,2},{1,3},{2,0},{3,1},{4,6},{5,7},{6,4},{7,5},{8,10},{9,11},{10,... | collective-permute-start | bytes 442376 | tf_op jit(solution)/shard_map/ppermute | solution.py:34
  5.7 2.6 %collective-permute-start.1 = (bf16[24,3072]{1,0:T(8,128)(2,1)S(1)}, bf16[24,3072]{1,0:T(8,128)(2,1)S(1)}, u32[]{:S(2)}, u32[]{:S(2)}) collective-permute-start(bf16[24,3072]{1,0:T(8,128)(2,1)S(1)} %pad_maximum_fusion.10), channel_id=1, source_target_pairs={{0,4},{1,5},{2,6},{3,7},{4,0},{5,1},{6,2},{7,3},{8,12},{9,13},{10,... | collective-permute-start | bytes 442376 | tf_op jit(solution)/shard_map/ppermute | solution.py:34
  8.3 0.9 convert_element_type.110
  9.2 1.8 collective-permute-start.3
  13.8 1.0 convert_element_type.118
  14.8 6.0 %norm_rows.1 = (f32[896,768]{1,0:T(8,128)}, bf16[896,768]{1,0:T(8,128)(2,1)}) custom-call(f32[512,768]{1,0:T(8,128)} %bitcast.104, f32[384,768]{1,0:T(8,128)} %bitcast.107, f32[1,768]{1,0:T(1,128)S(1)} %reshape.185.refs_0_.gain_ref), custom_call_target="tpu_custom_call" | custom-call | flops 2752512 | bytes 6881280 | tf_op jit(solution)/shard_map/norm_rows/pallas_call | solution.py:966
  21.5 1.8 collective-permute-start.8
  23.3 5.7 %round_rows.1 = (f32[896,768]{1,0:T(8,128)}, bf16[896,768]{1,0:T(8,128)(2,1)}) custom-call(f32[512,768]{1,0:T(8,128)} %bitcast.106, f32[384,768]{1,0:T(8,128)} %bitcast.108), custom_call_target="tpu_custom_call" | custom-call | flops 2752512 | bytes 6881280 | tf_op jit(solution)/shard_map/round_rows/pallas_call | solution.py:966
  29.4 1.6 collective-permute-start.9
  31.1 1.6 collective-permute-start.10
  33.1 0.9 collective-permute-start.4
  34.1 3.2 %collective-permute-start.5 = (bf16[24,4096]{1,0:T(8,128)(2,1)S(1)}, bf16[24,4096]{1,0:T(8,128)(2,1)S(1)}, u32[]{:S(2)}, u32[]{:S(2)}) collective-permute-start(bf16[24,4096]{1,0:T(8,128)(2,1)S(1)} %convert_element_type.118), channel_id=1, source_target_pairs={{0,4},{1,5},{2,6},{3,7},{4,0},{5,1},{6,2},{7,3},{8,12},{9,13},{10,... | collective-permute-start | bytes 589832 | tf_op jit(solution)/shard_map/ppermute | solution.py:34
  37.2 9.7 %collective-permute-done.11 = bf16[2,64,768]{2,1,0:T(8,128)(2,1)S(1)} collective-permute-done((bf16[2,64,768]{2,1,0:T(8,128)(2,1)S(1)}, bf16[2,64,768]{2,1,0:T(8,128)(2,1)S(1)}, u32[]{:S(2)}, u32[]{:S(2)}) %collective-permute-start.11) | collective-permute-done | bytes 196640 | tf_op jit(solution)/shard_map/ppermute | solution.py:34
  46.9 3.5 %collective-permute-start.6 = (bf16[24,4096]{1,0:T(8,128)(2,1)S(1)}, bf16[24,4096]{1,0:T(8,128)(2,1)S(1)}, u32[]{:S(2)}, u32[]{:S(2)}) collective-permute-start(bf16[24,4096]{1,0:T(8,128)(2,1)S(1)} %convert_element_type.118), channel_id=1, source_target_pairs={{0,6},{1,7},{2,4},{3,5},{4,2},{5,3},{6,0},{7,1},{8,14},{9,15},{10,... | collective-permute-start | bytes 589832 | tf_op jit(solution)/shard_map/ppermute | solution.py:34
  51.1 3.4 %collective-permute-done.6 = bf16[24,4096]{1,0:T(8,128)(2,1)S(1)} collective-permute-done((bf16[24,4096]{1,0:T(8,128)(2,1)S(1)}, bf16[24,4096]{1,0:T(8,128)(2,1)S(1)}, u32[]{:S(2)}, u32[]{:S(2)}) %collective-permute-start.6) | collective-permute-done | bytes 196640 | tf_op jit(solution)/shard_map/ppermute | solution.py:34
  54.6 1.6 collective-permute-start.12
  56.8 1.1 collective-permute-start.13
  58.2 0.8 collective-permute-done.17.refs_7_
  59.0 6.5 %project.1 = (bf16[896,2304]{1,0:T(8,128)(2,1)}, bf16[2,2,4,2,24,3072]{5,4,3,2,1,0:T(8,128)(2,1)}) custom-call(s32[4]{0:T(128)S(1)} %pad_add_fusion.place_ref, bf16[2,2,24,3072]{3,2,1,0:T(8,128)(2,1)S(1)} %bitcast.96, bf16[2,2,24,3072]{3,2,1,0:T(8,128)(2,1)S(1)} %collective-permute-done.9.refs_1_, bf16[2,2,24,3072]{3,2,1,0:T(8,128)(2,1)S(1)} %pad_maximum_fusion.3.refs_2_, ...), custom_call_target="tpu_custom_call" | custom-call | flops 3170893824 | bytes 14942208 | tf_op jit(solution)/shard_map/project/pallas_call | solution.py:1011
  65.5 2.3 collective-permute-done.13
  68.1 1.1 collective-permute-start.18
  70.0 3.4 %collective-permute-start.20 = (bf16[2,2,64,768]{3,2,1,0:T(8,128)(2,1)S(1)}, bf16[2,2,64,768]{3,2,1,0:T(8,128)(2,1)S(1)}, u32[]{:S(2)}, u32[]{:S(2)}) collective-permute-start(bf16[2,2,64,768]{3,2,1,0:T(8,128)(2,1)S(1)} %pad_maximum_fusion.4.refs_0_), channel_id=1, source_target_pairs={{0,4},{1,5},{2,6},{3,7},{4,0},{5,1},{6,2},{7,3},{8,12},{9,13},{10,... | collective-permute-start | bytes 1179656 | tf_op jit(solution)/shard_map/ppermute | solution.py:34
  73.9 13.6 %attend.1 = (bf16[896,768]{1,0:T(8,128)(2,1)S(1)}, f32[12,512,512]{2,1,0:T(8,128)}, f32[12,384,128]{2,1,0:T(8,128)}) custom-call(bf16[896,2304]{1,0:T(8,128)(2,1)} %get-tuple-element.222.q_ref.k_ref.v_ref, bf16[896,2304]{1,0:T(8,128)(2,1)} %get-tuple-element.222.q_ref.k_ref.v_ref, bf16[896,2304]{1,0:T(8,128)(2,1)} %get-tuple-element.222.q_ref.k_ref.v_ref, ...), custom_call_target="tpu_custom_call" | custom-call | flops 1912602624 | bytes 18087936 | tf_op jit(solution)/shard_map/attend/pallas_call | solution.py:482
  87.5 2.2 collective-permute-done.20.refs_2_
  90.2 4.5 %middle_forward.1 = (f32[896,768]{1,0:T(8,128)}, bf16[896,768]{1,0:T(8,128)(2,1)S(1)}) custom-call(f32[896,768]{1,0:T(8,128)} %get-tuple-element.200.refs_0_.rows_ref, bf16[896,768]{1,0:T(8,128)(2,1)S(1)} %get-tuple-element.232.refs_1_.mixed_hbm, bf16[768,3072]{1,0:T(8,128)(2,1)} %bitcast.97, f32[1,768]{1,0:T(1,128)S(1)} %reshape.192.refs_3_.gain_ref), custom_call_target="tpu_custom_call" | custom-call | flops 1056964608 | bytes 9437184 | tf_op jit(solution)/shard_map/middle_forward/pallas_call | solution.py:1052
  94.9 2.0 collective-permute-start.22
  97.0 15.4 %gate_forward.1 = (bf16[896,2048]{1,0:T(8,128)(2,1)}, f32[896,2048]{1,0:T(8,128)}, f32[896,2048]{1,0:T(8,128)}, bf16[2,512,768]{2,1,0:T(8,128)(2,1)S(1)}, bf16[2...) custom-call(s32[4]{0:T(128)S(1)} %pad_add_fusion.place_ref, bf16[2,2,24,4096]{3,2,1,0:T(8,128)(2,1)S(1)} %bitcast.93, ...), custom_call_target="tpu_custom_call" | custom-call | flops 8455716864 | bytes 30932992 | tf_op jit(solution)/shard_map/gate_forward/pallas_call | solution.py:752
  113.4 3.1 %collective-permute-done.29.refs_5_ = bf16[2,2,64,768]{3,2,1,0:T(8,128)(2,1)S(1)} collective-permute-done((bf16[2,2,64,768]{3,2,1,0:T(8,128)(2,1)S(1)}, bf16[2,2,64,768]{3,2,1,0:T(8,128)(2,1)S(1)}, u32[]{:S(2)}, u32[]{:S(2)}) %collective-permute-start.29) | collective-permute-done | bytes 393248 | tf_op jit(solution)/shard_map/ppermute | solution.py:34
  117.8 0.8 collective-permute-start.32
  118.6 15.9 %gate_back.1 = (bf16[2,896,2048]{2,1,0:T(8,128)(2,1)}, bf16[2,192,4096]{2,1,0:T(8,128)(2,1)S(1)}, bf16[2,192,4096]{2,1,0:T(8,128)(2,1)S(1)}, bf16[2,2,4,2,64,768]{5,4,3,2,1,0:T(8,128)(2,1)}) custom-call(s32[4]{0:T(128)S(1)} %pad_add_fusion.place_ref, bf16[2,2,64,768]{3,2,1,0:T(8,128)(2,1)S(1)} %pad_maximum_fusion.4.refs_0_, ...), custom_call_target="tpu_custom_call" | custom-call | flops 8455716864 | bytes 34603008 | tf_op jit(solution)/shard_map/gate_back/pallas_call | solution.py:812
  134.5 3.2 %collective-permute-done.32.refs_2_ = bf16[2,4,64,768]{3,2,1,0:T(8,128)(2,1)S(1)} collective-permute-done((bf16[2,4,64,768]{3,2,1,0:T(8,128)(2,1)S(1)}, bf16[2,4,64,768]{3,2,1,0:T(8,128)(2,1)S(1)}, u32[]{:S(2)}, u32[]{:S(2)}) %collective-permute-start.32) | collective-permute-done | bytes 786464 | tf_op jit(solution)/shard_map/ppermute | solution.py:34
  138.4 1.3 collective-permute-start.33
  139.7 14.3 %middle_back.1 = (f32[896,768]{1,0:T(8,128)}, bf16[896,768]{1,0:T(8,128)(2,1)}, bf16[896,768]{1,0:T(8,128)(2,1)}, f32[1,768]{1,0:T(1,128)S(1)}) custom-call(bf16[2,896,2048]{2,1,0:T(8,128)(2,1)} %get-tuple-element.272.gates_hbm, bf16[768,4096]{1,0:T(8,128)(2,1)} %bitcast.111, bf16[768,3072]{1,0:T(8,128)(2,1)} %bitcast.98, ...), custom_call_target="tpu_custom_call" | custom-call | flops 6694109184 | bytes 26017792 | tf_op jit(solution)/shard_map/middle_back/pallas_call | solution.py:917
  154.0 1.0 plane.4
  155.7 0.8 collective-permute-start.39
  156.7 0.8 column.3
  157.9 3.4 %collective-permute-start.36 = (bf16[64,768]{1,0:T(8,128)(2,1)S(1)}, bf16[64,768]{1,0:T(8,128)(2,1)S(1)}, u32[]{:S(2)}, u32[]{:S(2)}) collective-permute-start(bf16[64,768]{1,0:T(8,128)(2,1)S(1)} %get-tuple-element.286), channel_id=1, source_target_pairs={{0,4},{1,5},{2,6},{3,7},{4,0},{5,1},{6,2},{7,3},{8,12},{9,13},{10,... | collective-permute-start | bytes 294920 | tf_op jit(solution)/shard_map/ppermute | solution.py:34
  162.0 15.0 %attend_back.1 = (bf16[3,896,768]{2,1,0:T(8,128)(2,1)S(1)}, f32[6,2,32]{2,1,0:T(2,128)}) custom-call(bf16[896,2304]{1,0:T(8,128)(2,1)} %get-tuple-element.222.q_ref.k_ref.v_ref, bf16[896,2304]{1,0:T(8,128)(2,1)} %get-tuple-element.222.q_ref.k_ref.v_ref, bf16[896,2304]{1,0:T(8,128)(2,1)} %get-tuple-element.222.q_ref.k_ref.v_ref, ...), custom_call_target="tpu_custom_call" | custom-call | flops 3825205248 | bytes 22216704 | tf_op jit(solution)/shard_map/attend_back/pallas_call | solution.py:630
  177.0 0.8 far.4
  177.9 1.3 collective-permute-start.40
  179.2 1.3 collective-permute-start.41
  180.5 9.4 %attention_grads.1 = (bf16[2,192,3072]{2,1,0:T(8,128)(2,1)S(1)}, bf16[2,192,3072]{2,1,0:T(8,128)(2,1)S(1)}, f32[24,128]{1,0:T(8,128)S(1)}) custom-call(s32[4]{0:T(128)S(1)} %pad_add_fusion.place_ref, bf16[896,768]{1,0:T(8,128)(2,1)} %get-tuple-element.220.refs_8_.normed_ref, bf16[3,896,768]{2,1,0:T(8,128)(2,1)S(1)} %get-tuple-element.326.grads_ref, ...), custom_call_target="tpu_custom_call" | custom-call | flops 4227858432 | bytes 16515072 | tf_op jit(solution)/shard_map/attention_grads/pallas_call | solution.py:1152
  190.5 1.2 column.4
  191.7 2.9 %collective-permute-done.43 = f32[24,128]{1,0:T(8,128)S(1)} collective-permute-done((f32[24,128]{1,0:T(8,128)S(1)}, f32[24,128]{1,0:T(8,128)S(1)}, u32[]{:S(2)}, u32[]{:S(2)}) %collective-permute-start.43) | collective-permute-done | bytes 12320 | tf_op jit(solution)/shard_map/ppermute | solution.py:34
  194.6 0.8 plane.5
  195.4 0.8 collective-permute-start.44
  196.2 0.8 collective-permute-start.45
  197.0 2.0 collective-permute-start.47
  199.0 1.8 collective-permute-start.48
  200.9 3.2 %collective-permute-start.49 = (bf16[24,4096]{1,0:T(8,128)(2,1)S(1)}, bf16[24,4096]{1,0:T(8,128)(2,1)S(1)}, u32[]{:S(2)}, u32[]{:S(2)}) collective-permute-start(bf16[24,4096]{1,0:T(8,128)(2,1)S(1)} %get-tuple-element.338), channel_id=1, source_target_pairs={{0,6},{1,7},{2,4},{3,5},{4,2},{5,3},{6,0},{7,1},{8,14},{9,15},{10,... | collective-permute-start | bytes 589832 | tf_op jit(solution)/shard_map/ppermute | solution.py:34
  204.0 8.2 %input_back.1 = (f32[512,768]{1,0:T(8,128)}, f32[384,768]{1,0:T(8,128)}) custom-call(bf16[3,896,768]{2,1,0:T(8,128)(2,1)S(1)} %get-tuple-element.326.grads_ref, bf16[768,3072]{1,0:T(8,128)(2,1)} %bitcast.103, f32[896,768]{1,0:T(8,128)} %get-tuple-element.200.refs_0_.rows_ref, f32[896,768]{1,0:T(8,128)} %get-tuple-element.327.residual_ref, ...), custom_call_target="tpu_custom_call" | custom-call | flops 3170893824 | bytes 15925248 | tf_op jit(solution)/shard_map/input_back/pallas_call | solution.py:1213
  212.3 3.9 %collective-permute-done.48 = bf16[24,4096]{1,0:T(8,128)(2,1)S(1)} collective-permute-done((bf16[24,4096]{1,0:T(8,128)(2,1)S(1)}, bf16[24,4096]{1,0:T(8,128)(2,1)S(1)}, u32[]{:S(2)}, u32[]{:S(2)}) %collective-permute-start.48) | collective-permute-done | bytes 196640 | tf_op jit(solution)/shard_map/ppermute | solution.py:34
  217.0 1.3 collective-permute-start.50
  218.2 1.3 collective-permute-start.51
  219.6 3.8 %collective-permute-start.52 = (f32[24,128]{1,0:T(8,128)S(1)}, f32[24,128]{1,0:T(8,128)S(1)}, u32[]{:S(2)}, u32[]{:S(2)}) collective-permute-start(f32[24,128]{1,0:T(8,128)S(1)} %add.172), channel_id=1, source_target_pairs={{0,4},{1,5},{2,6},{3,7},{4,0},{5,1},{6,2},{7,3},{8,12},{9,13},{10,... | collective-permute-start | bytes 36872 | tf_op jit(solution)/shard_map/ppermute | solution.py:34
  223.4 1.7 collective-permute-done.52
  225.1 1.0 column.5
  226.1 2.4 collective-permute-start.55
  228.5 3.0 %collective-permute-start.54 = (bf16[24,3072]{1,0:T(8,128)(2,1)S(1)}, bf16[24,3072]{1,0:T(8,128)(2,1)S(1)}, u32[]{:S(2)}, u32[]{:S(2)}) collective-permute-start(bf16[24,3072]{1,0:T(8,128)(2,1)S(1)} %get-tuple-element.378), channel_id=1, source_target_pairs={{0,4},{1,5},{2,6},{3,7},{4,0},{5,1},{6,2},{7,3},{8,12},{9,13},{10,... | collective-permute-start | bytes 442376 | tf_op jit(solution)/shard_map/ppermute | solution.py:34
  232.3 7.2 %layer_outputs.1 = (f32[512,768]{1,0:T(8,128)}, f32[384,768]{1,0:T(8,128)}) custom-call(f32[896,768]{1,0:T(8,128)} %get-tuple-element.234.middle_hbm.middle_ref, bf16[896,2048]{1,0:T(8,128)(2,1)} %get-tuple-element.370.act_ref, bf16[2048,768]{1,0:T(8,128)(2,1)} %bitcast.112), custom_call_target="tpu_custom_call" | custom-call | flops 2818572288 | bytes 12320768 | tf_op jit(solution)/shard_map/layer_outputs/pallas_call | solution.py:1251
  239.6 1.1 collective-permute-start.57
  241.8 1.0 reshape.206
  (145 shorter events, 19.8 us)
Async XLA Ops:
  0.6 12.0 %copy-start = (f32[32,12]{0,1:T(8,128)S(1)}, f32[32,12]{0,1:T(8,128)}, u32[]{:S(2)}) copy-start(f32[32,12]{0,1:T(8,128)} %param.25) | copy-start | bytes 4612
  0.7 20.2 %copy-start.6 = (f32[64,768]{1,0:T(8,128)S(1)}, f32[64,768]{1,0:T(8,128)}, u32[]{:S(2)}) copy-start(f32[64,768]{1,0:T(8,128)} %param.22) | copy-start | bytes 589828
  2.6 18.3 %collective-permute-start = (bf16[24,3072]{1,0:T(8,128)(2,1)S(1)}, bf16[24,3072]{1,0:T(8,128)(2,1)S(1)}, u32[]{:S(2)}, u32[]{:S(2)}) collective-permute-start(bf16[24,3072]{1,0:T(8,128)(2,1)S(1)} %pad_maximum_fusion.10), channel_id=1, source_target_pairs={{0,2},{1,3},{2,0},{3,1},{4,6},{5,7},{6,4},{7,5},{8,10},{9,11},{10,... | collective-permute-start | bytes 442376 | tf_op jit(solution)/shard_map/ppermute | solution.py:34
  5.7 15.2 %collective-permute-start.1 = (bf16[24,3072]{1,0:T(8,128)(2,1)S(1)}, bf16[24,3072]{1,0:T(8,128)(2,1)S(1)}, u32[]{:S(2)}, u32[]{:S(2)}) collective-permute-start(bf16[24,3072]{1,0:T(8,128)(2,1)S(1)} %pad_maximum_fusion.10), channel_id=1, source_target_pairs={{0,4},{1,5},{2,6},{3,7},{4,0},{5,1},{6,2},{7,3},{8,12},{9,13},{10,... | collective-permute-start | bytes 442376 | tf_op jit(solution)/shard_map/ppermute | solution.py:34
  8.3 12.7 %collective-permute-start.2 = (bf16[24,3072]{1,0:T(8,128)(2,1)S(1)}, bf16[24,3072]{1,0:T(8,128)(2,1)S(1)}, u32[]{:S(2)}, u32[]{:S(2)}) collective-permute-start(bf16[24,3072]{1,0:T(8,128)(2,1)S(1)} %pad_maximum_fusion.10), channel_id=1, source_target_pairs={{0,6},{1,7},{2,4},{3,5},{4,2},{5,3},{6,0},{7,1},{8,14},{9,15},{10,... | collective-permute-start | bytes 442376 | tf_op jit(solution)/shard_map/ppermute | solution.py:34
  9.2 11.6 %collective-permute-start.3 = (bf16[64,768]{1,0:T(8,128)(2,1)S(1)}, bf16[64,768]{1,0:T(8,128)(2,1)S(1)}, u32[]{:S(2)}, u32[]{:S(2)}) collective-permute-start(bf16[64,768]{1,0:T(8,128)(2,1)S(1)} %convert_element_type.110), channel_id=1, source_target_pairs={{0,1},{1,0},{2,3},{3,2},{4,5},{5,4},{6,7},{7,6},{8,9},{9,8},{10,11... | collective-permute-start | bytes 294920 | tf_op jit(solution)/shard_map/ppermute | solution.py:34
  21.1 7.9 %collective-permute-start.7 = (bf16[2,24,3072]{2,1,0:T(8,128)(2,1)S(1)}, bf16[2,24,3072]{2,1,0:T(8,128)(2,1)S(1)}, u32[]{:S(2)}, u32[]{:S(2)}) collective-permute-start(bf16[2,24,3072]{2,1,0:T(8,128)(2,1)S(1)} %pad_maximum_fusion.7), channel_id=1, source_target_pairs={{0,1},{1,0},{2,3},{3,2},{4,5},{5,4},{6,7},{7,6},{8,9},{9,8},{10,11... | collective-permute-start | bytes 884744 | tf_op jit(solution)/shard_map/ppermute | solution.py:34
  21.5 7.7 %collective-permute-start.8 = (bf16[2,24,3072]{2,1,0:T(8,128)(2,1)S(1)}, bf16[2,24,3072]{2,1,0:T(8,128)(2,1)S(1)}, u32[]{:S(2)}, u32[]{:S(2)}) collective-permute-start(bf16[2,24,3072]{2,1,0:T(8,128)(2,1)S(1)} %pad_maximum_fusion.8), channel_id=1, source_target_pairs={{0,16},{1,17},{2,18},{3,19},{4,20},{5,21},{6,22},{7,23},{8,24},{9,... | collective-permute-start | bytes 884744 | tf_op jit(solution)/shard_map/ppermute | solution.py:34
  29.4 25.1 %collective-permute-start.9 = (bf16[2,2,24,3072]{3,2,1,0:T(8,128)(2,1)S(1)}, bf16[2,2,24,3072]{3,2,1,0:T(8,128)(2,1)S(1)}, u32[]{:S(2)}, u32[]{:S(2)}) collective-permute-start(bf16[2,2,24,3072]{3,2,1,0:T(8,128)(2,1)S(1)} %bitcast.94), channel_id=1, source_target_pairs={{0,16},{1,17},{2,18},{3,19},{4,20},{5,21},{6,22},{7,23},{8,24},{9,... | collective-permute-start | bytes 1769480 | tf_op jit(solution)/shard_map/ppermute | solution.py:34
  31.1 23.4 %collective-permute-start.10 = (bf16[2,2,24,3072]{3,2,1,0:T(8,128)(2,1)S(1)}, bf16[2,2,24,3072]{3,2,1,0:T(8,128)(2,1)S(1)}, u32[]{:S(2)}, u32[]{:S(2)}) collective-permute-start(bf16[2,2,24,3072]{3,2,1,0:T(8,128)(2,1)S(1)} %pad_maximum_fusion.3.refs_2_), channel_id=1, source_target_pairs={{0,1},{1,0},{2,3},{3,2},{4,5},{5,4},{6,7},{7,6},{8,9},{9,8},{10,11... | collective-permute-start | bytes 1769480 | tf_op jit(solution)/shard_map/ppermute | solution.py:34
  32.6 14.3 %collective-permute-start.11 = (bf16[2,64,768]{2,1,0:T(8,128)(2,1)S(1)}, bf16[2,64,768]{2,1,0:T(8,128)(2,1)S(1)}, u32[]{:S(2)}, u32[]{:S(2)}) collective-permute-start(bf16[2,64,768]{2,1,0:T(8,128)(2,1)S(1)} %pad_maximum_fusion.9), channel_id=1, source_target_pairs={{0,16},{1,17},{2,18},{3,19},{4,20},{5,21},{6,22},{7,23},{8,24},{9,... | collective-permute-start | bytes 589832 | tf_op jit(solution)/shard_map/ppermute | solution.py:34
  33.1 25.9 %copy-start.3 = (bf16[896,768]{1,0:T(8,128)(2,1)S(1)}, bf16[896,768]{1,0:T(8,128)(2,1)}, u32[]{:S(2)}) copy-start(bf16[896,768]{1,0:T(8,128)(2,1)} %get-tuple-element.220.refs_8_.normed_ref) | copy-start | bytes 4128772
  33.1 17.4 %collective-permute-start.4 = (bf16[24,4096]{1,0:T(8,128)(2,1)S(1)}, bf16[24,4096]{1,0:T(8,128)(2,1)S(1)}, u32[]{:S(2)}, u32[]{:S(2)}) collective-permute-start(bf16[24,4096]{1,0:T(8,128)(2,1)S(1)} %convert_element_type.118), channel_id=1, source_target_pairs={{0,2},{1,3},{2,0},{3,1},{4,6},{5,7},{6,4},{7,5},{8,10},{9,11},{10,... | collective-permute-start | bytes 589832 | tf_op jit(solution)/shard_map/ppermute | solution.py:34
  34.1 16.6 %collective-permute-start.5 = (bf16[24,4096]{1,0:T(8,128)(2,1)S(1)}, bf16[24,4096]{1,0:T(8,128)(2,1)S(1)}, u32[]{:S(2)}, u32[]{:S(2)}) collective-permute-start(bf16[24,4096]{1,0:T(8,128)(2,1)S(1)} %convert_element_type.118), channel_id=1, source_target_pairs={{0,4},{1,5},{2,6},{3,7},{4,0},{5,1},{6,2},{7,3},{8,12},{9,13},{10,... | collective-permute-start | bytes 589832 | tf_op jit(solution)/shard_map/ppermute | solution.py:34
  46.9 7.6 %collective-permute-start.6 = (bf16[24,4096]{1,0:T(8,128)(2,1)S(1)}, bf16[24,4096]{1,0:T(8,128)(2,1)S(1)}, u32[]{:S(2)}, u32[]{:S(2)}) collective-permute-start(bf16[24,4096]{1,0:T(8,128)(2,1)S(1)} %convert_element_type.118), channel_id=1, source_target_pairs={{0,6},{1,7},{2,4},{3,5},{4,2},{5,3},{6,0},{7,1},{8,14},{9,15},{10,... | collective-permute-start | bytes 589832 | tf_op jit(solution)/shard_map/ppermute | solution.py:34
  50.6 6.2 %collective-permute-start.14 = (bf16[2,2,24,3072]{3,2,1,0:T(8,128)(2,1)S(1)}, bf16[2,2,24,3072]{3,2,1,0:T(8,128)(2,1)S(1)}, u32[]{:S(2)}, u32[]{:S(2)}) collective-permute-start(bf16[2,2,24,3072]{3,2,1,0:T(8,128)(2,1)S(1)} %bitcast.95), channel_id=1, source_target_pairs={{0,8},{1,9},{2,10},{3,11},{4,12},{5,13},{6,14},{7,15},{8,0},{9,1},... | collective-permute-start | bytes 1769480 | tf_op jit(solution)/shard_map/ppermute | solution.py:34
  50.7 7.3 %collective-permute-start.16 = (bf16[2,2,24,3072]{3,2,1,0:T(8,128)(2,1)S(1)}, bf16[2,2,24,3072]{3,2,1,0:T(8,128)(2,1)S(1)}, u32[]{:S(2)}, u32[]{:S(2)}) collective-permute-start(bf16[2,2,24,3072]{3,2,1,0:T(8,128)(2,1)S(1)} %pad_maximum_fusion.3.refs_2_), channel_id=1, source_target_pairs={{0,8},{1,9},{2,10},{3,11},{4,12},{5,13},{6,14},{7,15},{8,0},{9,1},... | collective-permute-start | bytes 1769480 | tf_op jit(solution)/shard_map/ppermute | solution.py:34
  54.6 10.9 %collective-permute-start.12 = (bf16[2,24,4096]{2,1,0:T(8,128)(2,1)S(1)}, bf16[2,24,4096]{2,1,0:T(8,128)(2,1)S(1)}, u32[]{:S(2)}, u32[]{:S(2)}) collective-permute-start(bf16[2,24,4096]{2,1,0:T(8,128)(2,1)S(1)} %pad_maximum_fusion.5), channel_id=1, source_target_pairs={{0,1},{1,0},{2,3},{3,2},{4,5},{5,4},{6,7},{7,6},{8,9},{9,8},{10,11... | collective-permute-start | bytes 1179656 | tf_op jit(solution)/shard_map/ppermute | solution.py:34
  56.2 2.0 collective-permute-start.15
  56.2 2.8 %collective-permute-start.17 = (bf16[2,2,24,3072]{3,2,1,0:T(8,128)(2,1)S(1)}, bf16[2,2,24,3072]{3,2,1,0:T(8,128)(2,1)S(1)}, u32[]{:S(2)}, u32[]{:S(2)}) collective-permute-start(bf16[2,2,24,3072]{3,2,1,0:T(8,128)(2,1)S(1)} %collective-permute-done.10.refs_3_), channel_id=1, source_target_pairs={{0,8},{1,9},{2,10},{3,11},{4,12},{5,13},{6,14},{7,15},{8,0},{9,1},... | collective-permute-start | bytes 1769480 | tf_op jit(solution)/shard_map/ppermute | solution.py:34
  56.8 11.1 %collective-permute-start.13 = (bf16[2,24,4096]{2,1,0:T(8,128)(2,1)S(1)}, bf16[2,24,4096]{2,1,0:T(8,128)(2,1)S(1)}, u32[]{:S(2)}, u32[]{:S(2)}) collective-permute-start(bf16[2,24,4096]{2,1,0:T(8,128)(2,1)S(1)} %pad_maximum_fusion.6), channel_id=1, source_target_pairs={{0,16},{1,17},{2,18},{3,19},{4,20},{5,21},{6,22},{7,23},{8,24},{9,... | collective-permute-start | bytes 1179656 | tf_op jit(solution)/shard_map/ppermute | solution.py:34
  68.1 21.6 %collective-permute-start.18 = (bf16[2,2,24,4096]{3,2,1,0:T(8,128)(2,1)S(1)}, bf16[2,2,24,4096]{3,2,1,0:T(8,128)(2,1)S(1)}, u32[]{:S(2)}, u32[]{:S(2)}) collective-permute-start(bf16[2,2,24,4096]{3,2,1,0:T(8,128)(2,1)S(1)} %bitcast.91), channel_id=1, source_target_pairs={{0,16},{1,17},{2,18},{3,19},{4,20},{5,21},{6,22},{7,23},{8,24},{9,... | collective-permute-start | bytes 2359304 | tf_op jit(solution)/shard_map/ppermute | solution.py:34
  69.4 20.8 %copy-start.7 = (f32[768]{0:T(1024)S(1)}, f32[768]{0:T(1024)}, u32[]{:S(2)}) copy-start(f32[768]{0:T(1024)} %param.24) | copy-start | bytes 9220
  69.4 20.3 %collective-permute-start.19 = (bf16[2,2,24,4096]{3,2,1,0:T(8,128)(2,1)S(1)}, bf16[2,2,24,4096]{3,2,1,0:T(8,128)(2,1)S(1)}, u32[]{:S(2)}, u32[]{:S(2)}) collective-permute-start(bf16[2,2,24,4096]{3,2,1,0:T(8,128)(2,1)S(1)} %pad_maximum_fusion.1.refs_2_), channel_id=1, source_target_pairs={{0,1},{1,0},{2,3},{3,2},{4,5},{5,4},{6,7},{7,6},{8,9},{9,8},{10,11... | collective-permute-start | bytes 2359304 | tf_op jit(solution)/shard_map/ppermute | solution.py:34
  70.0 19.7 %collective-permute-start.20 = (bf16[2,2,64,768]{3,2,1,0:T(8,128)(2,1)S(1)}, bf16[2,2,64,768]{3,2,1,0:T(8,128)(2,1)S(1)}, u32[]{:S(2)}, u32[]{:S(2)}) collective-permute-start(bf16[2,2,64,768]{3,2,1,0:T(8,128)(2,1)S(1)} %pad_maximum_fusion.4.refs_0_), channel_id=1, source_target_pairs={{0,4},{1,5},{2,6},{3,7},{4,0},{5,1},{6,2},{7,3},{8,12},{9,13},{10,... | collective-permute-start | bytes 1179656 | tf_op jit(solution)/shard_map/ppermute | solution.py:34
  73.4 21.3 %collective-permute-start.25 = (bf16[2,2,24,4096]{3,2,1,0:T(8,128)(2,1)S(1)}, bf16[2,2,24,4096]{3,2,1,0:T(8,128)(2,1)S(1)}, u32[]{:S(2)}, u32[]{:S(2)}) collective-permute-start(bf16[2,2,24,4096]{3,2,1,0:T(8,128)(2,1)S(1)} %bitcast.92), channel_id=1, source_target_pairs={{0,8},{1,9},{2,10},{3,11},{4,12},{5,13},{6,14},{7,15},{8,0},{9,1},... | collective-permute-start | bytes 2359304 | tf_op jit(solution)/shard_map/ppermute | solution.py:34
  73.4 21.4 %collective-permute-start.27 = (bf16[2,2,24,4096]{3,2,1,0:T(8,128)(2,1)S(1)}, bf16[2,2,24,4096]{3,2,1,0:T(8,128)(2,1)S(1)}, u32[]{:S(2)}, u32[]{:S(2)}) collective-permute-start(bf16[2,2,24,4096]{3,2,1,0:T(8,128)(2,1)S(1)} %pad_maximum_fusion.1.refs_2_), channel_id=1, source_target_pairs={{0,8},{1,9},{2,10},{3,11},{4,12},{5,13},{6,14},{7,15},{8,0},{9,1},... | collective-permute-start | bytes 2359304 | tf_op jit(solution)/shard_map/ppermute | solution.py:34
  87.5 7.2 %copy-start.2 = (bf16[896,768]{1,0:T(8,128)(2,1)}, bf16[896,768]{1,0:T(8,128)(2,1)S(1)}, u32[]{:S(2)}) copy-start(bf16[896,768]{1,0:T(8,128)(2,1)S(1)} %get-tuple-element.232.refs_1_.mixed_hbm) | copy-start | bytes 4128772
  89.7 7.2 %collective-permute-start.26 = (bf16[2,2,24,4096]{3,2,1,0:T(8,128)(2,1)S(1)}, bf16[2,2,24,4096]{3,2,1,0:T(8,128)(2,1)S(1)}, u32[]{:S(2)}, u32[]{:S(2)}) collective-permute-start(bf16[2,2,24,4096]{3,2,1,0:T(8,128)(2,1)S(1)} %collective-permute-done.18.refs_1_), channel_id=1, source_target_pairs={{0,8},{1,9},{2,10},{3,11},{4,12},{5,13},{6,14},{7,15},{8,0},{9,1},... | collective-permute-start | bytes 2359304 | tf_op jit(solution)/shard_map/ppermute | solution.py:34
  89.7 7.3 %collective-permute-start.28 = (bf16[2,2,24,4096]{3,2,1,0:T(8,128)(2,1)S(1)}, bf16[2,2,24,4096]{3,2,1,0:T(8,128)(2,1)S(1)}, u32[]{:S(2)}, u32[]{:S(2)}) collective-permute-start(bf16[2,2,24,4096]{3,2,1,0:T(8,128)(2,1)S(1)} %collective-permute-done.19.refs_3_), channel_id=1, source_target_pairs={{0,8},{1,9},{2,10},{3,11},{4,12},{5,13},{6,14},{7,15},{8,0},{9,1},... | collective-permute-start | bytes 2359304 | tf_op jit(solution)/shard_map/ppermute | solution.py:34
  90.2 22.2 %collective-permute-start.21 = (bf16[2,2,64,768]{3,2,1,0:T(8,128)(2,1)S(1)}, bf16[2,2,64,768]{3,2,1,0:T(8,128)(2,1)S(1)}, u32[]{:S(2)}, u32[]{:S(2)}) collective-permute-start(bf16[2,2,64,768]{3,2,1,0:T(8,128)(2,1)S(1)} %pad_maximum_fusion.4.refs_0_), channel_id=1, source_target_pairs={{0,2},{1,3},{2,0},{3,1},{4,6},{5,7},{6,4},{7,5},{8,10},{9,11},{10,... | collective-permute-start | bytes 1179656 | tf_op jit(solution)/shard_map/ppermute | solution.py:34
  94.7 17.7 %collective-permute-start.23 = (bf16[2,2,64,768]{3,2,1,0:T(8,128)(2,1)S(1)}, bf16[2,2,64,768]{3,2,1,0:T(8,128)(2,1)S(1)}, u32[]{:S(2)}, u32[]{:S(2)}) collective-permute-start(bf16[2,2,64,768]{3,2,1,0:T(8,128)(2,1)S(1)} %pad_maximum_fusion.4.refs_0_), channel_id=1, source_target_pairs={{0,8},{1,9},{2,10},{3,11},{4,12},{5,13},{6,14},{7,15},{8,0},{9,1},... | collective-permute-start | bytes 1179656 | tf_op jit(solution)/shard_map/ppermute | solution.py:34
  94.9 17.6 %collective-permute-start.22 = (bf16[2,2,64,768]{3,2,1,0:T(8,128)(2,1)S(1)}, bf16[2,2,64,768]{3,2,1,0:T(8,128)(2,1)S(1)}, u32[]{:S(2)}, u32[]{:S(2)}) collective-permute-start(bf16[2,2,64,768]{3,2,1,0:T(8,128)(2,1)S(1)} %collective-permute-done.20.refs_2_), channel_id=1, source_target_pairs={{0,2},{1,3},{2,0},{3,1},{4,6},{5,7},{6,4},{7,5},{8,10},{9,11},{10,... | collective-permute-start | bytes 1179656 | tf_op jit(solution)/shard_map/ppermute | solution.py:34
  96.9 15.6 %collective-permute-start.24 = (bf16[2,2,64,768]{3,2,1,0:T(8,128)(2,1)S(1)}, bf16[2,2,64,768]{3,2,1,0:T(8,128)(2,1)S(1)}, u32[]{:S(2)}, u32[]{:S(2)}) collective-permute-start(bf16[2,2,64,768]{3,2,1,0:T(8,128)(2,1)S(1)} %collective-permute-done.20.refs_2_), channel_id=1, source_target_pairs={{0,8},{1,9},{2,10},{3,11},{4,12},{5,13},{6,14},{7,15},{8,0},{9,1},... | collective-permute-start | bytes 1179656 | tf_op jit(solution)/shard_map/ppermute | solution.py:34
  112.5 4.6 %collective-permute-start.31 = (bf16[2,512,768]{2,1,0:T(8,128)(2,1)S(1)}, bf16[2,512,768]{2,1,0:T(8,128)(2,1)S(1)}, u32[]{:S(2)}, u32[]{:S(2)}) collective-permute-start(bf16[2,512,768]{2,1,0:T(8,128)(2,1)S(1)} %get-tuple-element.256), channel_id=1, source_target_pairs={{0,8},{1,9},{2,10},{3,11},{4,12},{5,13},{6,14},{7,15},{8,0},{9,1},... | collective-permute-start | bytes 4718600 | tf_op jit(solution)/shard_map/ppermute | solution.py:34
  112.9 3.6 %collective-permute-start.29 = (bf16[2,2,64,768]{3,2,1,0:T(8,128)(2,1)S(1)}, bf16[2,2,64,768]{3,2,1,0:T(8,128)(2,1)S(1)}, u32[]{:S(2)}, u32[]{:S(2)}) collective-permute-start(bf16[2,2,64,768]{3,2,1,0:T(8,128)(2,1)S(1)} %collective-permute-done.21.refs_1_), channel_id=1, source_target_pairs={{0,8},{1,9},{2,10},{3,11},{4,12},{5,13},{6,14},{7,15},{8,0},{9,1},... | collective-permute-start | bytes 1179656 | tf_op jit(solution)/shard_map/ppermute | solution.py:34
  113.0 4.0 %collective-permute-start.30 = (bf16[2,2,64,768]{3,2,1,0:T(8,128)(2,1)S(1)}, bf16[2,2,64,768]{3,2,1,0:T(8,128)(2,1)S(1)}, u32[]{:S(2)}, u32[]{:S(2)}) collective-permute-start(bf16[2,2,64,768]{3,2,1,0:T(8,128)(2,1)S(1)} %collective-permute-done.22.refs_3_), channel_id=1, source_target_pairs={{0,8},{1,9},{2,10},{3,11},{4,12},{5,13},{6,14},{7,15},{8,0},{9,1},... | collective-permute-start | bytes 1179656 | tf_op jit(solution)/shard_map/ppermute | solution.py:34
  117.8 19.9 %collective-permute-start.32 = (bf16[2,4,64,768]{3,2,1,0:T(8,128)(2,1)S(1)}, bf16[2,4,64,768]{3,2,1,0:T(8,128)(2,1)S(1)}, u32[]{:S(2)}, u32[]{:S(2)}) collective-permute-start(bf16[2,4,64,768]{3,2,1,0:T(8,128)(2,1)S(1)} %plane.3), channel_id=1, source_target_pairs={{0,1},{1,0},{2,3},{3,2},{4,5},{5,4},{6,7},{7,6},{8,9},{9,8},{10,11... | collective-permute-start | bytes 2359304 | tf_op jit(solution)/shard_map/ppermute | solution.py:34
  137.7 16.3 %collective-permute-start.34 = (bf16[2,192,4096]{2,1,0:T(8,128)(2,1)S(1)}, bf16[2,192,4096]{2,1,0:T(8,128)(2,1)S(1)}, u32[]{:S(2)}, u32[]{:S(2)}) collective-permute-start(bf16[2,192,4096]{2,1,0:T(8,128)(2,1)S(1)} %get-tuple-element.277), channel_id=1, source_target_pairs={{0,8},{1,9},{2,10},{3,11},{4,12},{5,13},{6,14},{7,15},{8,0},{9,1},... | collective-permute-start | bytes 9437192 | tf_op jit(solution)/shard_map/ppermute | solution.py:34
  138.4 15.6 %collective-permute-start.33 = (bf16[4,64,768]{2,1,0:T(8,128)(2,1)S(1)}, bf16[4,64,768]{2,1,0:T(8,128)(2,1)S(1)}, u32[]{:S(2)}, u32[]{:S(2)}) collective-permute-start(bf16[4,64,768]{2,1,0:T(8,128)(2,1)S(1)} %far.3), channel_id=1, source_target_pairs={{0,16},{1,17},{2,18},{3,19},{4,20},{5,21},{6,22},{7,23},{8,24},{9,... | collective-permute-start | bytes 1179656 | tf_op jit(solution)/shard_map/ppermute | solution.py:34
  155.0 22.0 %collective-permute-start.38 = (bf16[2,2,24,4096]{3,2,1,0:T(8,128)(2,1)S(1)}, bf16[2,2,24,4096]{3,2,1,0:T(8,128)(2,1)S(1)}, u32[]{:S(2)}, u32[]{:S(2)}) collective-permute-start(bf16[2,2,24,4096]{3,2,1,0:T(8,128)(2,1)S(1)} %get-tuple-element.290), channel_id=1, source_target_pairs={{0,1},{1,0},{2,3},{3,2},{4,5},{5,4},{6,7},{7,6},{8,9},{9,8},{10,11... | collective-permute-start | bytes 2359304 | tf_op jit(solution)/shard_map/ppermute | solution.py:34
  155.7 21.3 %collective-permute-start.39 = (bf16[2,2,24,4096]{3,2,1,0:T(8,128)(2,1)S(1)}, bf16[2,2,24,4096]{3,2,1,0:T(8,128)(2,1)S(1)}, u32[]{:S(2)}, u32[]{:S(2)}) collective-permute-start(bf16[2,2,24,4096]{3,2,1,0:T(8,128)(2,1)S(1)} %get-tuple-element.291), channel_id=1, source_target_pairs={{0,16},{1,17},{2,18},{3,19},{4,20},{5,21},{6,22},{7,23},{8,24},{9,... | collective-permute-start | bytes 2359304 | tf_op jit(solution)/shard_map/ppermute | solution.py:34
  157.5 19.5 %collective-permute-start.35 = (bf16[64,768]{1,0:T(8,128)(2,1)S(1)}, bf16[64,768]{1,0:T(8,128)(2,1)S(1)}, u32[]{:S(2)}, u32[]{:S(2)}) collective-permute-start(bf16[64,768]{1,0:T(8,128)(2,1)S(1)} %get-tuple-element.285), channel_id=1, source_target_pairs={{0,2},{1,3},{2,0},{3,1},{4,6},{5,7},{6,4},{7,5},{8,10},{9,11},{10,... | collective-permute-start | bytes 294920 | tf_op jit(solution)/shard_map/ppermute | solution.py:34
  157.9 19.0 %collective-permute-start.36 = (bf16[64,768]{1,0:T(8,128)(2,1)S(1)}, bf16[64,768]{1,0:T(8,128)(2,1)S(1)}, u32[]{:S(2)}, u32[]{:S(2)}) collective-permute-start(bf16[64,768]{1,0:T(8,128)(2,1)S(1)} %get-tuple-element.286), channel_id=1, source_target_pairs={{0,4},{1,5},{2,6},{3,7},{4,0},{5,1},{6,2},{7,3},{8,12},{9,13},{10,... | collective-permute-start | bytes 294920 | tf_op jit(solution)/shard_map/ppermute | solution.py:34
  161.3 15.7 %collective-permute-start.37 = (bf16[64,768]{1,0:T(8,128)(2,1)S(1)}, bf16[64,768]{1,0:T(8,128)(2,1)S(1)}, u32[]{:S(2)}, u32[]{:S(2)}) collective-permute-start(bf16[64,768]{1,0:T(8,128)(2,1)S(1)} %get-tuple-element.287), channel_id=1, source_target_pairs={{0,6},{1,7},{2,4},{3,5},{4,2},{5,3},{6,0},{7,1},{8,14},{9,15},{10,... | collective-permute-start | bytes 294920 | tf_op jit(solution)/shard_map/ppermute | solution.py:34
  177.9 12.1 %collective-permute-start.40 = (bf16[2,24,4096]{2,1,0:T(8,128)(2,1)S(1)}, bf16[2,24,4096]{2,1,0:T(8,128)(2,1)S(1)}, u32[]{:S(2)}, u32[]{:S(2)}) collective-permute-start(bf16[2,24,4096]{2,1,0:T(8,128)(2,1)S(1)} %get-tuple-element.300), channel_id=1, source_target_pairs={{0,16},{1,17},{2,18},{3,19},{4,20},{5,21},{6,22},{7,23},{8,24},{9,... | collective-permute-start | bytes 1179656 | tf_op jit(solution)/shard_map/ppermute | solution.py:34
  179.2 10.8 %collective-permute-start.41 = (bf16[2,24,4096]{2,1,0:T(8,128)(2,1)S(1)}, bf16[2,24,4096]{2,1,0:T(8,128)(2,1)S(1)}, u32[]{:S(2)}, u32[]{:S(2)}) collective-permute-start(bf16[2,24,4096]{2,1,0:T(8,128)(2,1)S(1)} %get-tuple-element.301), channel_id=1, source_target_pairs={{0,1},{1,0},{2,3},{3,2},{4,5},{5,4},{6,7},{7,6},{8,9},{9,8},{10,11... | collective-permute-start | bytes 1179656 | tf_op jit(solution)/shard_map/ppermute | solution.py:34
  189.9 4.6 %collective-permute-start.42 = (bf16[2,192,3072]{2,1,0:T(8,128)(2,1)S(1)}, bf16[2,192,3072]{2,1,0:T(8,128)(2,1)S(1)}, u32[]{:S(2)}, u32[]{:S(2)}) collective-permute-start(bf16[2,192,3072]{2,1,0:T(8,128)(2,1)S(1)} %get-tuple-element.309), channel_id=1, source_target_pairs={{0,8},{1,9},{2,10},{3,11},{4,12},{5,13},{6,14},{7,15},{8,0},{9,1},... | collective-permute-start | bytes 7077896 | tf_op jit(solution)/shard_map/ppermute | solution.py:34
  190.0 4.5 %collective-permute-start.43 = (f32[24,128]{1,0:T(8,128)S(1)}, f32[24,128]{1,0:T(8,128)S(1)}, u32[]{:S(2)}, u32[]{:S(2)}) collective-permute-start(f32[24,128]{1,0:T(8,128)S(1)} %get-tuple-element.316), channel_id=1, source_target_pairs={{0,8},{1,9},{2,10},{3,11},{4,12},{5,13},{6,14},{7,15},{8,0},{9,1},... | collective-permute-start | bytes 36872 | tf_op jit(solution)/shard_map/ppermute | solution.py:34
  195.4 20.8 %collective-permute-start.44 = (bf16[2,2,24,3072]{3,2,1,0:T(8,128)(2,1)S(1)}, bf16[2,2,24,3072]{3,2,1,0:T(8,128)(2,1)S(1)}, u32[]{:S(2)}, u32[]{:S(2)}) collective-permute-start(bf16[2,2,24,3072]{3,2,1,0:T(8,128)(2,1)S(1)} %get-tuple-element.324), channel_id=1, source_target_pairs={{0,1},{1,0},{2,3},{3,2},{4,5},{5,4},{6,7},{7,6},{8,9},{9,8},{10,11... | collective-permute-start | bytes 1769480 | tf_op jit(solution)/shard_map/ppermute | solution.py:34
  196.2 20.0 %collective-permute-start.45 = (bf16[2,2,24,3072]{3,2,1,0:T(8,128)(2,1)S(1)}, bf16[2,2,24,3072]{3,2,1,0:T(8,128)(2,1)S(1)}, u32[]{:S(2)}, u32[]{:S(2)}) collective-permute-start(bf16[2,2,24,3072]{3,2,1,0:T(8,128)(2,1)S(1)} %get-tuple-element.325), channel_id=1, source_target_pairs={{0,16},{1,17},{2,18},{3,19},{4,20},{5,21},{6,22},{7,23},{8,24},{9,... | collective-permute-start | bytes 1769480 | tf_op jit(solution)/shard_map/ppermute | solution.py:34
  197.0 3.9 %collective-permute-start.46 = (f32[24,128]{1,0:T(8,128)S(1)}, f32[24,128]{1,0:T(8,128)S(1)}, u32[]{:S(2)}, u32[]{:S(2)}) collective-permute-start(f32[24,128]{1,0:T(8,128)S(1)} %add.171), channel_id=1, source_target_pairs={{0,2},{1,3},{2,0},{3,1},{4,6},{5,7},{6,4},{7,5},{8,10},{9,11},{10,... | collective-permute-start | bytes 36872 | tf_op jit(solution)/shard_map/ppermute | solution.py:34
  197.0 15.3 %collective-permute-start.47 = (bf16[24,4096]{1,0:T(8,128)(2,1)S(1)}, bf16[24,4096]{1,0:T(8,128)(2,1)S(1)}, u32[]{:S(2)}, u32[]{:S(2)}) collective-permute-start(bf16[24,4096]{1,0:T(8,128)(2,1)S(1)} %get-tuple-element.336), channel_id=1, source_target_pairs={{0,2},{1,3},{2,0},{3,1},{4,6},{5,7},{6,4},{7,5},{8,10},{9,11},{10,... | collective-permute-start | bytes 589832 | tf_op jit(solution)/shard_map/ppermute | solution.py:34
  199.0 17.2 %collective-permute-start.48 = (bf16[24,4096]{1,0:T(8,128)(2,1)S(1)}, bf16[24,4096]{1,0:T(8,128)(2,1)S(1)}, u32[]{:S(2)}, u32[]{:S(2)}) collective-permute-start(bf16[24,4096]{1,0:T(8,128)(2,1)S(1)} %get-tuple-element.337), channel_id=1, source_target_pairs={{0,4},{1,5},{2,6},{3,7},{4,0},{5,1},{6,2},{7,3},{8,12},{9,13},{10,... | collective-permute-start | bytes 589832 | tf_op jit(solution)/shard_map/ppermute | solution.py:34
  200.9 15.3 %collective-permute-start.49 = (bf16[24,4096]{1,0:T(8,128)(2,1)S(1)}, bf16[24,4096]{1,0:T(8,128)(2,1)S(1)}, u32[]{:S(2)}, u32[]{:S(2)}) collective-permute-start(bf16[24,4096]{1,0:T(8,128)(2,1)S(1)} %get-tuple-element.338), channel_id=1, source_target_pairs={{0,6},{1,7},{2,4},{3,5},{4,2},{5,3},{6,0},{7,1},{8,14},{9,15},{10,... | collective-permute-start | bytes 589832 | tf_op jit(solution)/shard_map/ppermute | solution.py:34
  217.0 8.1 %collective-permute-start.50 = (bf16[2,24,3072]{2,1,0:T(8,128)(2,1)S(1)}, bf16[2,24,3072]{2,1,0:T(8,128)(2,1)S(1)}, u32[]{:S(2)}, u32[]{:S(2)}) collective-permute-start(bf16[2,24,3072]{2,1,0:T(8,128)(2,1)S(1)} %get-tuple-element.342), channel_id=1, source_target_pairs={{0,16},{1,17},{2,18},{3,19},{4,20},{5,21},{6,22},{7,23},{8,24},{9,... | collective-permute-start | bytes 884744 | tf_op jit(solution)/shard_map/ppermute | solution.py:34
  218.2 6.8 %collective-permute-start.51 = (bf16[2,24,3072]{2,1,0:T(8,128)(2,1)S(1)}, bf16[2,24,3072]{2,1,0:T(8,128)(2,1)S(1)}, u32[]{:S(2)}, u32[]{:S(2)}) collective-permute-start(bf16[2,24,3072]{2,1,0:T(8,128)(2,1)S(1)} %get-tuple-element.343), channel_id=1, source_target_pairs={{0,1},{1,0},{2,3},{3,2},{4,5},{5,4},{6,7},{7,6},{8,9},{9,8},{10,11... | collective-permute-start | bytes 884744 | tf_op jit(solution)/shard_map/ppermute | solution.py:34
  219.6 5.5 %collective-permute-start.52 = (f32[24,128]{1,0:T(8,128)S(1)}, f32[24,128]{1,0:T(8,128)S(1)}, u32[]{:S(2)}, u32[]{:S(2)}) collective-permute-start(f32[24,128]{1,0:T(8,128)S(1)} %add.172), channel_id=1, source_target_pairs={{0,4},{1,5},{2,6},{3,7},{4,0},{5,1},{6,2},{7,3},{8,12},{9,13},{10,... | collective-permute-start | bytes 36872 | tf_op jit(solution)/shard_map/ppermute | solution.py:34
  226.1 18.5 %collective-permute-start.55 = (bf16[24,3072]{1,0:T(8,128)(2,1)S(1)}, bf16[24,3072]{1,0:T(8,128)(2,1)S(1)}, u32[]{:S(2)}, u32[]{:S(2)}) collective-permute-start(bf16[24,3072]{1,0:T(8,128)(2,1)S(1)} %get-tuple-element.379), channel_id=1, source_target_pairs={{0,6},{1,7},{2,4},{3,5},{4,2},{5,3},{6,0},{7,1},{8,14},{9,15},{10,... | collective-permute-start | bytes 442376 | tf_op jit(solution)/shard_map/ppermute | solution.py:34
  228.5 16.0 %collective-permute-start.54 = (bf16[24,3072]{1,0:T(8,128)(2,1)S(1)}, bf16[24,3072]{1,0:T(8,128)(2,1)S(1)}, u32[]{:S(2)}, u32[]{:S(2)}) collective-permute-start(bf16[24,3072]{1,0:T(8,128)(2,1)S(1)} %get-tuple-element.378), channel_id=1, source_target_pairs={{0,4},{1,5},{2,6},{3,7},{4,0},{5,1},{6,2},{7,3},{8,12},{9,13},{10,... | collective-permute-start | bytes 442376 | tf_op jit(solution)/shard_map/ppermute | solution.py:34
  231.5 13.1 %collective-permute-start.53 = (bf16[24,3072]{1,0:T(8,128)(2,1)S(1)}, bf16[24,3072]{1,0:T(8,128)(2,1)S(1)}, u32[]{:S(2)}, u32[]{:S(2)}) collective-permute-start(bf16[24,3072]{1,0:T(8,128)(2,1)S(1)} %get-tuple-element.377), channel_id=1, source_target_pairs={{0,2},{1,3},{2,0},{3,1},{4,6},{5,7},{6,4},{7,5},{8,10},{9,11},{10,... | collective-permute-start | bytes 442376 | tf_op jit(solution)/shard_map/ppermute | solution.py:34
  232.0 7.6 %collective-permute-start.56 = (f32[24,128]{1,0:T(8,128)S(1)}, f32[24,128]{1,0:T(8,128)S(1)}, u32[]{:S(2)}, u32[]{:S(2)}) collective-permute-start(f32[24,128]{1,0:T(8,128)S(1)} %add.173), channel_id=1, source_target_pairs={{0,1},{1,0},{2,3},{3,2},{4,5},{5,4},{6,7},{7,6},{8,9},{9,8},{10,11... | collective-permute-start | bytes 36872 | tf_op jit(solution)/shard_map/ppermute | solution.py:34
  232.3 13.6 %copy-start.1 = (f32[32,12]{0,1:T(8,128)S(1)}, f32[32,12]{0,1:T(8,128)}, u32[]{:S(2)}) copy-start(f32[32,12]{0,1:T(8,128)} %param.25) | copy-start | bytes 4612
  239.6 3.8 %collective-permute-start.57 = (f32[24,128]{1,0:T(8,128)S(1)}, f32[24,128]{1,0:T(8,128)S(1)}, u32[]{:S(2)}, u32[]{:S(2)}) collective-permute-start(f32[24,128]{1,0:T(8,128)S(1)} %add.186), channel_id=1, source_target_pairs={{0,16},{1,17},{2,18},{3,19},{4,20},{5,21},{6,22},{7,23},{8,24},{9,... | collective-permute-start | bytes 36872 | tf_op jit(solution)/shard_map/ppermute | solution.py:34
  (2 other events, 9.6 us)

commit v7 on v6

--- a/solution.py
+++ b/solution.py
@@ -773,7 +773,7 @@
             transcendentals=rows * hidden,
         ),
         name="gate_forward",
-    )(place, *pieces, normed_two, *in_hbm(cot_low))
+    )(place, *pieces, normed_two, cot_low)
     return (*results, full.reshape(width, columns))
 
 

time: 247 us -> 246 us (level)
  transfers between devices with their start and end apart: 58 -> 58, of which waited for: 15 -> 15; matrix products, arithmetic and copies ran while one was open for 4% -> 4% of each run, Pallas kernels for 51% -> 50%
where the time goes in v7:
time: 246 us; the launch traced here: 245 us
  Pallas kernels  129 us (52%)
  starting transfers between devices  67.6 us (27%)
  waiting for transfers between devices  34.8 us (14%)
  other arithmetic  7.98 us (3%)
  local copies, waits for them, and re-layouts  4.5 us (2%)
    ppermute x58, starting transfers between devices, swap(): return lax.ppermute(values, both, flip_pairs(**flips))  67.6 us
    ppermute x58, waiting for transfers between devices, swap(): return lax.ppermute(values, both, flip_pairs(**flips))  34.8 us
    pallas_call x1, Pallas kernels, gate_back(): pl.pallas_call(kernel, grid=(hidden // tile,), out_shape=(pltpu.HBM((2, r...  15.9 us
    pallas_call x1, Pallas kernels, attend_back(): pl.pallas_call(functools.partial(attend_back_kernel, docs, length), grid=...  15 us
    pallas_call x1, Pallas kernels, gate_forward(): pl.pallas_call(kernel, grid=(hidden // tile,), out_shape=(pltpu.HBM((rows...  14.6 us
    pallas_call x1, Pallas kernels, middle_back(): pl.pallas_call(middle_back_kernel, out_shape=(pltpu.HBM((rows, width), jn...  14.3 us
    pallas_call x1, Pallas kernels, attend(): pl.pallas_call(functools.partial(attend_kernel, docs, length, group), gri...  13.6 us
    pallas_call x2, Pallas kernels, by_parts(): pl.pallas_call(kernel, grid=(rows // count,), out_shape=[pltpu.HBM((rows,...  11.7 us
  transfers between devices with their start and end apart: 58, of which 15 were waited for; matrix products, arithmetic and copies ran while one was open for 4% of the time, Pallas kernels for 50%

profile of v7, /device:TPU:0, one launch (start us, length us, event | category | flops | bytes accessed | tf_op | source)
XLA Modules:
  0.0 245.2 jit_solution(16864626624453872829)
XLA Ops:
  0.7 0.9 convert.7
  1.6 0.9 convert.6
  2.6 3.1 %collective-permute-start = (bf16[24,3072]{1,0:T(8,128)(2,1)S(1)}, bf16[24,3072]{1,0:T(8,128)(2,1)S(1)}, u32[]{:S(2)}, u32[]{:S(2)}) collective-permute-start(bf16[24,3072]{1,0:T(8,128)(2,1)S(1)} %pad_maximum_fusion.10), channel_id=1, source_target_pairs={{0,2},{1,3},{2,0},{3,1},{4,6},{5,7},{6,4},{7,5},{8,10},{9,11},{10,... | collective-permute-start | bytes 442376 | tf_op jit(solution)/shard_map/ppermute | solution.py:34
  5.7 2.6 %collective-permute-start.1 = (bf16[24,3072]{1,0:T(8,128)(2,1)S(1)}, bf16[24,3072]{1,0:T(8,128)(2,1)S(1)}, u32[]{:S(2)}, u32[]{:S(2)}) collective-permute-start(bf16[24,3072]{1,0:T(8,128)(2,1)S(1)} %pad_maximum_fusion.10), channel_id=1, source_target_pairs={{0,4},{1,5},{2,6},{3,7},{4,0},{5,1},{6,2},{7,3},{8,12},{9,13},{10,... | collective-permute-start | bytes 442376 | tf_op jit(solution)/shard_map/ppermute | solution.py:34
  8.3 0.9 convert_element_type.110
  9.2 1.8 collective-permute-start.3
  13.8 1.0 convert_element_type.118
  14.8 6.0 %norm_rows.1 = (f32[896,768]{1,0:T(8,128)}, bf16[896,768]{1,0:T(8,128)(2,1)}) custom-call(f32[512,768]{1,0:T(8,128)} %bitcast.104, f32[384,768]{1,0:T(8,128)} %bitcast.107, f32[1,768]{1,0:T(1,128)S(1)} %reshape.185.refs_0_.gain_ref), custom_call_target="tpu_custom_call" | custom-call | flops 2752512 | bytes 6881280 | tf_op jit(solution)/shard_map/norm_rows/pallas_call | solution.py:966
  21.5 1.8 collective-permute-start.8
  23.3 5.7 %round_rows.1 = (f32[896,768]{1,0:T(8,128)}, bf16[896,768]{1,0:T(8,128)(2,1)}) custom-call(f32[512,768]{1,0:T(8,128)} %bitcast.106, f32[384,768]{1,0:T(8,128)} %bitcast.108), custom_call_target="tpu_custom_call" | custom-call | flops 2752512 | bytes 6881280 | tf_op jit(solution)/shard_map/round_rows/pallas_call | solution.py:966
  29.4 1.6 collective-permute-start.9
  31.1 1.6 collective-permute-start.10
  33.1 0.9 collective-permute-start.4
  34.1 3.2 %collective-permute-start.5 = (bf16[24,4096]{1,0:T(8,128)(2,1)S(1)}, bf16[24,4096]{1,0:T(8,128)(2,1)S(1)}, u32[]{:S(2)}, u32[]{:S(2)}) collective-permute-start(bf16[24,4096]{1,0:T(8,128)(2,1)S(1)} %convert_element_type.118), channel_id=1, source_target_pairs={{0,4},{1,5},{2,6},{3,7},{4,0},{5,1},{6,2},{7,3},{8,12},{9,13},{10,... | collective-permute-start | bytes 589832 | tf_op jit(solution)/shard_map/ppermute | solution.py:34
  37.2 9.7 %collective-permute-done.11 = bf16[2,64,768]{2,1,0:T(8,128)(2,1)S(1)} collective-permute-done((bf16[2,64,768]{2,1,0:T(8,128)(2,1)S(1)}, bf16[2,64,768]{2,1,0:T(8,128)(2,1)S(1)}, u32[]{:S(2)}, u32[]{:S(2)}) %collective-permute-start.11) | collective-permute-done | bytes 196640 | tf_op jit(solution)/shard_map/ppermute | solution.py:34
  46.9 3.5 %collective-permute-start.6 = (bf16[24,4096]{1,0:T(8,128)(2,1)S(1)}, bf16[24,4096]{1,0:T(8,128)(2,1)S(1)}, u32[]{:S(2)}, u32[]{:S(2)}) collective-permute-start(bf16[24,4096]{1,0:T(8,128)(2,1)S(1)} %convert_element_type.118), channel_id=1, source_target_pairs={{0,6},{1,7},{2,4},{3,5},{4,2},{5,3},{6,0},{7,1},{8,14},{9,15},{10,... | collective-permute-start | bytes 589832 | tf_op jit(solution)/shard_map/ppermute | solution.py:34
  51.1 3.4 %collective-permute-done.6 = bf16[24,4096]{1,0:T(8,128)(2,1)S(1)} collective-permute-done((bf16[24,4096]{1,0:T(8,128)(2,1)S(1)}, bf16[24,4096]{1,0:T(8,128)(2,1)S(1)}, u32[]{:S(2)}, u32[]{:S(2)}) %collective-permute-start.6) | collective-permute-done | bytes 196640 | tf_op jit(solution)/shard_map/ppermute | solution.py:34
  54.6 1.6 collective-permute-start.12
  56.8 1.1 collective-permute-start.13
  58.2 0.8 collective-permute-done.17.refs_7_
  59.0 6.5 %project.1 = (bf16[896,2304]{1,0:T(8,128)(2,1)}, bf16[2,2,4,2,24,3072]{5,4,3,2,1,0:T(8,128)(2,1)}) custom-call(s32[4]{0:T(128)S(1)} %pad_add_fusion.place_ref, bf16[2,2,24,3072]{3,2,1,0:T(8,128)(2,1)S(1)} %bitcast.96, bf16[2,2,24,3072]{3,2,1,0:T(8,128)(2,1)S(1)} %collective-permute-done.9.refs_1_, bf16[2,2,24,3072]{3,2,1,0:T(8,128)(2,1)S(1)} %pad_maximum_fusion.3.refs_2_, ...), custom_call_target="tpu_custom_call" | custom-call | flops 3170893824 | bytes 14942208 | tf_op jit(solution)/shard_map/project/pallas_call | solution.py:1011
  65.5 2.3 collective-permute-done.13
  68.1 1.1 collective-permute-start.18
  70.0 3.4 %collective-permute-start.20 = (bf16[2,2,64,768]{3,2,1,0:T(8,128)(2,1)S(1)}, bf16[2,2,64,768]{3,2,1,0:T(8,128)(2,1)S(1)}, u32[]{:S(2)}, u32[]{:S(2)}) collective-permute-start(bf16[2,2,64,768]{3,2,1,0:T(8,128)(2,1)S(1)} %pad_maximum_fusion.4.refs_0_), channel_id=1, source_target_pairs={{0,4},{1,5},{2,6},{3,7},{4,0},{5,1},{6,2},{7,3},{8,12},{9,13},{10,... | collective-permute-start | bytes 1179656 | tf_op jit(solution)/shard_map/ppermute | solution.py:34
  73.9 13.6 %attend.1 = (bf16[896,768]{1,0:T(8,128)(2,1)S(1)}, f32[12,512,512]{2,1,0:T(8,128)}, f32[12,384,128]{2,1,0:T(8,128)}) custom-call(bf16[896,2304]{1,0:T(8,128)(2,1)} %get-tuple-element.222.q_ref.k_ref.v_ref, bf16[896,2304]{1,0:T(8,128)(2,1)} %get-tuple-element.222.q_ref.k_ref.v_ref, bf16[896,2304]{1,0:T(8,128)(2,1)} %get-tuple-element.222.q_ref.k_ref.v_ref, ...), custom_call_target="tpu_custom_call" | custom-call | flops 1912602624 | bytes 18087936 | tf_op jit(solution)/shard_map/attend/pallas_call | solution.py:482
  87.5 2.2 collective-permute-done.20.refs_2_
  90.3 4.6 %middle_forward.1 = (f32[896,768]{1,0:T(8,128)}, bf16[896,768]{1,0:T(8,128)(2,1)S(1)}) custom-call(f32[896,768]{1,0:T(8,128)} %get-tuple-element.200.refs_0_.rows_ref, bf16[896,768]{1,0:T(8,128)(2,1)S(1)} %get-tuple-element.232.refs_1_.mixed_hbm, bf16[768,3072]{1,0:T(8,128)(2,1)} %bitcast.97, f32[1,768]{1,0:T(1,128)S(1)} %reshape.192.refs_3_.gain_ref), custom_call_target="tpu_custom_call" | custom-call | flops 1056964608 | bytes 9437184 | tf_op jit(solution)/shard_map/middle_forward/pallas_call | solution.py:1052
  95.0 2.0 collective-permute-start.22
  97.1 14.6 %gate_forward.1 = (bf16[896,2048]{1,0:T(8,128)(2,1)}, f32[896,2048]{1,0:T(8,128)}, f32[896,2048]{1,0:T(8,128)}, bf16[2,512,768]{2,1,0:T(8,128)(2,1)S(1)}, bf16[2...) custom-call(s32[4]{0:T(128)S(1)} %pad_add_fusion.place_ref, bf16[2,2,24,4096]{3,2,1,0:T(8,128)(2,1)S(1)} %bitcast.93, ...), custom_call_target="tpu_custom_call" | custom-call | flops 8455716864 | bytes 30932992 | tf_op jit(solution)/shard_map/gate_forward/pallas_call | solution.py:752
  112.7 3.1 %collective-permute-done.29.refs_5_ = bf16[2,2,64,768]{3,2,1,0:T(8,128)(2,1)S(1)} collective-permute-done((bf16[2,2,64,768]{3,2,1,0:T(8,128)(2,1)S(1)}, bf16[2,2,64,768]{3,2,1,0:T(8,128)(2,1)S(1)}, u32[]{:S(2)}, u32[]{:S(2)}) %collective-permute-start.29) | collective-permute-done | bytes 393248 | tf_op jit(solution)/shard_map/ppermute | solution.py:34
  117.1 0.8 collective-permute-start.32
  117.9 15.9 %gate_back.1 = (bf16[2,896,2048]{2,1,0:T(8,128)(2,1)}, bf16[2,192,4096]{2,1,0:T(8,128)(2,1)S(1)}, bf16[2,192,4096]{2,1,0:T(8,128)(2,1)S(1)}, bf16[2,2,4,2,64,768]{5,4,3,2,1,0:T(8,128)(2,1)}) custom-call(s32[4]{0:T(128)S(1)} %pad_add_fusion.place_ref, bf16[2,2,64,768]{3,2,1,0:T(8,128)(2,1)S(1)} %pad_maximum_fusion.4.refs_0_, ...), custom_call_target="tpu_custom_call" | custom-call | flops 8455716864 | bytes 34603008 | tf_op jit(solution)/shard_map/gate_back/pallas_call | solution.py:812
  133.8 3.1 %collective-permute-done.32.refs_2_ = bf16[2,4,64,768]{3,2,1,0:T(8,128)(2,1)S(1)} collective-permute-done((bf16[2,4,64,768]{3,2,1,0:T(8,128)(2,1)S(1)}, bf16[2,4,64,768]{3,2,1,0:T(8,128)(2,1)S(1)}, u32[]{:S(2)}, u32[]{:S(2)}) %collective-permute-start.32) | collective-permute-done | bytes 786464 | tf_op jit(solution)/shard_map/ppermute | solution.py:34
  137.7 1.3 collective-permute-start.33
  139.0 14.3 %middle_back.1 = (f32[896,768]{1,0:T(8,128)}, bf16[896,768]{1,0:T(8,128)(2,1)}, bf16[896,768]{1,0:T(8,128)(2,1)}, f32[1,768]{1,0:T(1,128)S(1)}) custom-call(bf16[2,896,2048]{2,1,0:T(8,128)(2,1)} %get-tuple-element.272.gates_hbm, bf16[768,4096]{1,0:T(8,128)(2,1)} %bitcast.111, bf16[768,3072]{1,0:T(8,128)(2,1)} %bitcast.98, ...), custom_call_target="tpu_custom_call" | custom-call | flops 6694109184 | bytes 26017792 | tf_op jit(solution)/shard_map/middle_back/pallas_call | solution.py:917
  153.3 1.0 plane.4
  154.3 0.8 collective-permute-start.38
  155.1 0.8 collective-permute-start.39
  156.0 0.8 column.3
  157.3 3.4 %collective-permute-start.36 = (bf16[64,768]{1,0:T(8,128)(2,1)S(1)}, bf16[64,768]{1,0:T(8,128)(2,1)S(1)}, u32[]{:S(2)}, u32[]{:S(2)}) collective-permute-start(bf16[64,768]{1,0:T(8,128)(2,1)S(1)} %get-tuple-element.286), channel_id=1, source_target_pairs={{0,4},{1,5},{2,6},{3,7},{4,0},{5,1},{6,2},{7,3},{8,12},{9,13},{10,... | collective-permute-start | bytes 294920 | tf_op jit(solution)/shard_map/ppermute | solution.py:34
  161.3 15.0 %attend_back.1 = (bf16[3,896,768]{2,1,0:T(8,128)(2,1)S(1)}, f32[6,2,32]{2,1,0:T(2,128)}) custom-call(bf16[896,2304]{1,0:T(8,128)(2,1)} %get-tuple-element.222.q_ref.k_ref.v_ref, bf16[896,2304]{1,0:T(8,128)(2,1)} %get-tuple-element.222.q_ref.k_ref.v_ref, bf16[896,2304]{1,0:T(8,128)(2,1)} %get-tuple-element.222.q_ref.k_ref.v_ref, ...), custom_call_target="tpu_custom_call" | custom-call | flops 3825205248 | bytes 22216704 | tf_op jit(solution)/shard_map/attend_back/pallas_call | solution.py:630
  176.3 0.8 far.4
  177.2 1.3 collective-permute-start.40
  178.5 1.3 collective-permute-start.41
  179.8 9.4 %attention_grads.1 = (bf16[2,192,3072]{2,1,0:T(8,128)(2,1)S(1)}, bf16[2,192,3072]{2,1,0:T(8,128)(2,1)S(1)}, f32[24,128]{1,0:T(8,128)S(1)}) custom-call(s32[4]{0:T(128)S(1)} %pad_add_fusion.place_ref, bf16[896,768]{1,0:T(8,128)(2,1)} %get-tuple-element.220.refs_8_.normed_ref, bf16[3,896,768]{2,1,0:T(8,128)(2,1)S(1)} %get-tuple-element.326.grads_ref, ...), custom_call_target="tpu_custom_call" | custom-call | flops 4227858432 | bytes 16515072 | tf_op jit(solution)/shard_map/attention_grads/pallas_call | solution.py:1152
  189.8 1.2 column.4
  191.0 2.9 %collective-permute-done.43 = f32[24,128]{1,0:T(8,128)S(1)} collective-permute-done((f32[24,128]{1,0:T(8,128)S(1)}, f32[24,128]{1,0:T(8,128)S(1)}, u32[]{:S(2)}, u32[]{:S(2)}) %collective-permute-start.43) | collective-permute-done | bytes 12320 | tf_op jit(solution)/shard_map/ppermute | solution.py:34
  193.9 0.8 plane.5
  195.5 0.8 collective-permute-start.45
  196.3 2.0 collective-permute-start.47
  198.3 1.8 collective-permute-start.48
  200.2 3.2 %collective-permute-start.49 = (bf16[24,4096]{1,0:T(8,128)(2,1)S(1)}, bf16[24,4096]{1,0:T(8,128)(2,1)S(1)}, u32[]{:S(2)}, u32[]{:S(2)}) collective-permute-start(bf16[24,4096]{1,0:T(8,128)(2,1)S(1)} %get-tuple-element.338), channel_id=1, source_target_pairs={{0,6},{1,7},{2,4},{3,5},{4,2},{5,3},{6,0},{7,1},{8,14},{9,15},{10,... | collective-permute-start | bytes 589832 | tf_op jit(solution)/shard_map/ppermute | solution.py:34
  203.4 8.2 %input_back.1 = (f32[512,768]{1,0:T(8,128)}, f32[384,768]{1,0:T(8,128)}) custom-call(bf16[3,896,768]{2,1,0:T(8,128)(2,1)S(1)} %get-tuple-element.326.grads_ref, bf16[768,3072]{1,0:T(8,128)(2,1)} %bitcast.103, f32[896,768]{1,0:T(8,128)} %get-tuple-element.200.refs_0_.rows_ref, f32[896,768]{1,0:T(8,128)} %get-tuple-element.327.residual_ref, ...), custom_call_target="tpu_custom_call" | custom-call | flops 3170893824 | bytes 15925248 | tf_op jit(solution)/shard_map/input_back/pallas_call | solution.py:1213
  211.6 3.9 %collective-permute-done.48 = bf16[24,4096]{1,0:T(8,128)(2,1)S(1)} collective-permute-done((bf16[24,4096]{1,0:T(8,128)(2,1)S(1)}, bf16[24,4096]{1,0:T(8,128)(2,1)S(1)}, u32[]{:S(2)}, u32[]{:S(2)}) %collective-permute-start.48) | collective-permute-done | bytes 196640 | tf_op jit(solution)/shard_map/ppermute | solution.py:34
  216.3 1.3 collective-permute-start.50
  217.6 1.3 collective-permute-start.51
  218.9 3.8 %collective-permute-start.52 = (f32[24,128]{1,0:T(8,128)S(1)}, f32[24,128]{1,0:T(8,128)S(1)}, u32[]{:S(2)}, u32[]{:S(2)}) collective-permute-start(f32[24,128]{1,0:T(8,128)S(1)} %add.172), channel_id=1, source_target_pairs={{0,4},{1,5},{2,6},{3,7},{4,0},{5,1},{6,2},{7,3},{8,12},{9,13},{10,... | collective-permute-start | bytes 36872 | tf_op jit(solution)/shard_map/ppermute | solution.py:34
  222.7 1.7 collective-permute-done.52
  224.4 1.0 column.5
  225.4 2.4 collective-permute-start.55
  227.8 2.9 %collective-permute-start.54 = (bf16[24,3072]{1,0:T(8,128)(2,1)S(1)}, bf16[24,3072]{1,0:T(8,128)(2,1)S(1)}, u32[]{:S(2)}, u32[]{:S(2)}) collective-permute-start(bf16[24,3072]{1,0:T(8,128)(2,1)S(1)} %get-tuple-element.378), channel_id=1, source_target_pairs={{0,4},{1,5},{2,6},{3,7},{4,0},{5,1},{6,2},{7,3},{8,12},{9,13},{10,... | collective-permute-start | bytes 442376 | tf_op jit(solution)/shard_map/ppermute | solution.py:34
  231.6 7.2 %layer_outputs.1 = (f32[512,768]{1,0:T(8,128)}, f32[384,768]{1,0:T(8,128)}) custom-call(f32[896,768]{1,0:T(8,128)} %get-tuple-element.234.middle_hbm.middle_ref, bf16[896,2048]{1,0:T(8,128)(2,1)} %get-tuple-element.370.act_ref, bf16[2048,768]{1,0:T(8,128)(2,1)} %bitcast.112), custom_call_target="tpu_custom_call" | custom-call | flops 2818572288 | bytes 12320768 | tf_op jit(solution)/shard_map/layer_outputs/pallas_call | solution.py:1251
  238.9 1.1 collective-permute-start.57
  241.1 1.0 reshape.206
  (145 shorter events, 19.8 us)
Async XLA Ops:
  0.6 12.0 %copy-start = (f32[32,12]{0,1:T(8,128)S(1)}, f32[32,12]{0,1:T(8,128)}, u32[]{:S(2)}) copy-start(f32[32,12]{0,1:T(8,128)} %param.25) | copy-start | bytes 4612
  0.7 20.2 %copy-start.6 = (f32[64,768]{1,0:T(8,128)S(1)}, f32[64,768]{1,0:T(8,128)}, u32[]{:S(2)}) copy-start(f32[64,768]{1,0:T(8,128)} %param.22) | copy-start | bytes 589828
  2.6 18.3 %collective-permute-start = (bf16[24,3072]{1,0:T(8,128)(2,1)S(1)}, bf16[24,3072]{1,0:T(8,128)(2,1)S(1)}, u32[]{:S(2)}, u32[]{:S(2)}) collective-permute-start(bf16[24,3072]{1,0:T(8,128)(2,1)S(1)} %pad_maximum_fusion.10), channel_id=1, source_target_pairs={{0,2},{1,3},{2,0},{3,1},{4,6},{5,7},{6,4},{7,5},{8,10},{9,11},{10,... | collective-permute-start | bytes 442376 | tf_op jit(solution)/shard_map/ppermute | solution.py:34
  5.7 15.2 %collective-permute-start.1 = (bf16[24,3072]{1,0:T(8,128)(2,1)S(1)}, bf16[24,3072]{1,0:T(8,128)(2,1)S(1)}, u32[]{:S(2)}, u32[]{:S(2)}) collective-permute-start(bf16[24,3072]{1,0:T(8,128)(2,1)S(1)} %pad_maximum_fusion.10), channel_id=1, source_target_pairs={{0,4},{1,5},{2,6},{3,7},{4,0},{5,1},{6,2},{7,3},{8,12},{9,13},{10,... | collective-permute-start | bytes 442376 | tf_op jit(solution)/shard_map/ppermute | solution.py:34
  8.3 12.7 %collective-permute-start.2 = (bf16[24,3072]{1,0:T(8,128)(2,1)S(1)}, bf16[24,3072]{1,0:T(8,128)(2,1)S(1)}, u32[]{:S(2)}, u32[]{:S(2)}) collective-permute-start(bf16[24,3072]{1,0:T(8,128)(2,1)S(1)} %pad_maximum_fusion.10), channel_id=1, source_target_pairs={{0,6},{1,7},{2,4},{3,5},{4,2},{5,3},{6,0},{7,1},{8,14},{9,15},{10,... | collective-permute-start | bytes 442376 | tf_op jit(solution)/shard_map/ppermute | solution.py:34
  9.2 11.6 %collective-permute-start.3 = (bf16[64,768]{1,0:T(8,128)(2,1)S(1)}, bf16[64,768]{1,0:T(8,128)(2,1)S(1)}, u32[]{:S(2)}, u32[]{:S(2)}) collective-permute-start(bf16[64,768]{1,0:T(8,128)(2,1)S(1)} %convert_element_type.110), channel_id=1, source_target_pairs={{0,1},{1,0},{2,3},{3,2},{4,5},{5,4},{6,7},{7,6},{8,9},{9,8},{10,11... | collective-permute-start | bytes 294920 | tf_op jit(solution)/shard_map/ppermute | solution.py:34
  21.1 7.9 %collective-permute-start.7 = (bf16[2,24,3072]{2,1,0:T(8,128)(2,1)S(1)}, bf16[2,24,3072]{2,1,0:T(8,128)(2,1)S(1)}, u32[]{:S(2)}, u32[]{:S(2)}) collective-permute-start(bf16[2,24,3072]{2,1,0:T(8,128)(2,1)S(1)} %pad_maximum_fusion.7), channel_id=1, source_target_pairs={{0,1},{1,0},{2,3},{3,2},{4,5},{5,4},{6,7},{7,6},{8,9},{9,8},{10,11... | collective-permute-start | bytes 884744 | tf_op jit(solution)/shard_map/ppermute | solution.py:34
  21.5 7.7 %collective-permute-start.8 = (bf16[2,24,3072]{2,1,0:T(8,128)(2,1)S(1)}, bf16[2,24,3072]{2,1,0:T(8,128)(2,1)S(1)}, u32[]{:S(2)}, u32[]{:S(2)}) collective-permute-start(bf16[2,24,3072]{2,1,0:T(8,128)(2,1)S(1)} %pad_maximum_fusion.8), channel_id=1, source_target_pairs={{0,16},{1,17},{2,18},{3,19},{4,20},{5,21},{6,22},{7,23},{8,24},{9,... | collective-permute-start | bytes 884744 | tf_op jit(solution)/shard_map/ppermute | solution.py:34
  29.4 25.1 %collective-permute-start.9 = (bf16[2,2,24,3072]{3,2,1,0:T(8,128)(2,1)S(1)}, bf16[2,2,24,3072]{3,2,1,0:T(8,128)(2,1)S(1)}, u32[]{:S(2)}, u32[]{:S(2)}) collective-permute-start(bf16[2,2,24,3072]{3,2,1,0:T(8,128)(2,1)S(1)} %bitcast.94), channel_id=1, source_target_pairs={{0,16},{1,17},{2,18},{3,19},{4,20},{5,21},{6,22},{7,23},{8,24},{9,... | collective-permute-start | bytes 1769480 | tf_op jit(solution)/shard_map/ppermute | solution.py:34
  31.1 23.4 %collective-permute-start.10 = (bf16[2,2,24,3072]{3,2,1,0:T(8,128)(2,1)S(1)}, bf16[2,2,24,3072]{3,2,1,0:T(8,128)(2,1)S(1)}, u32[]{:S(2)}, u32[]{:S(2)}) collective-permute-start(bf16[2,2,24,3072]{3,2,1,0:T(8,128)(2,1)S(1)} %pad_maximum_fusion.3.refs_2_), channel_id=1, source_target_pairs={{0,1},{1,0},{2,3},{3,2},{4,5},{5,4},{6,7},{7,6},{8,9},{9,8},{10,11... | collective-permute-start | bytes 1769480 | tf_op jit(solution)/shard_map/ppermute | solution.py:34
  32.6 14.3 %collective-permute-start.11 = (bf16[2,64,768]{2,1,0:T(8,128)(2,1)S(1)}, bf16[2,64,768]{2,1,0:T(8,128)(2,1)S(1)}, u32[]{:S(2)}, u32[]{:S(2)}) collective-permute-start(bf16[2,64,768]{2,1,0:T(8,128)(2,1)S(1)} %pad_maximum_fusion.9), channel_id=1, source_target_pairs={{0,16},{1,17},{2,18},{3,19},{4,20},{5,21},{6,22},{7,23},{8,24},{9,... | collective-permute-start | bytes 589832 | tf_op jit(solution)/shard_map/ppermute | solution.py:34
  33.1 25.9 %copy-start.3 = (bf16[896,768]{1,0:T(8,128)(2,1)S(1)}, bf16[896,768]{1,0:T(8,128)(2,1)}, u32[]{:S(2)}) copy-start(bf16[896,768]{1,0:T(8,128)(2,1)} %get-tuple-element.220.refs_8_.normed_ref) | copy-start | bytes 4128772
  33.1 17.4 %collective-permute-start.4 = (bf16[24,4096]{1,0:T(8,128)(2,1)S(1)}, bf16[24,4096]{1,0:T(8,128)(2,1)S(1)}, u32[]{:S(2)}, u32[]{:S(2)}) collective-permute-start(bf16[24,4096]{1,0:T(8,128)(2,1)S(1)} %convert_element_type.118), channel_id=1, source_target_pairs={{0,2},{1,3},{2,0},{3,1},{4,6},{5,7},{6,4},{7,5},{8,10},{9,11},{10,... | collective-permute-start | bytes 589832 | tf_op jit(solution)/shard_map/ppermute | solution.py:34
  34.1 16.6 %collective-permute-start.5 = (bf16[24,4096]{1,0:T(8,128)(2,1)S(1)}, bf16[24,4096]{1,0:T(8,128)(2,1)S(1)}, u32[]{:S(2)}, u32[]{:S(2)}) collective-permute-start(bf16[24,4096]{1,0:T(8,128)(2,1)S(1)} %convert_element_type.118), channel_id=1, source_target_pairs={{0,4},{1,5},{2,6},{3,7},{4,0},{5,1},{6,2},{7,3},{8,12},{9,13},{10,... | collective-permute-start | bytes 589832 | tf_op jit(solution)/shard_map/ppermute | solution.py:34
  46.9 7.6 %collective-permute-start.6 = (bf16[24,4096]{1,0:T(8,128)(2,1)S(1)}, bf16[24,4096]{1,0:T(8,128)(2,1)S(1)}, u32[]{:S(2)}, u32[]{:S(2)}) collective-permute-start(bf16[24,4096]{1,0:T(8,128)(2,1)S(1)} %convert_element_type.118), channel_id=1, source_target_pairs={{0,6},{1,7},{2,4},{3,5},{4,2},{5,3},{6,0},{7,1},{8,14},{9,15},{10,... | collective-permute-start | bytes 589832 | tf_op jit(solution)/shard_map/ppermute | solution.py:34
  50.6 6.2 %collective-permute-start.14 = (bf16[2,2,24,3072]{3,2,1,0:T(8,128)(2,1)S(1)}, bf16[2,2,24,3072]{3,2,1,0:T(8,128)(2,1)S(1)}, u32[]{:S(2)}, u32[]{:S(2)}) collective-permute-start(bf16[2,2,24,3072]{3,2,1,0:T(8,128)(2,1)S(1)} %bitcast.95), channel_id=1, source_target_pairs={{0,8},{1,9},{2,10},{3,11},{4,12},{5,13},{6,14},{7,15},{8,0},{9,1},... | collective-permute-start | bytes 1769480 | tf_op jit(solution)/shard_map/ppermute | solution.py:34
  50.7 7.3 %collective-permute-start.16 = (bf16[2,2,24,3072]{3,2,1,0:T(8,128)(2,1)S(1)}, bf16[2,2,24,3072]{3,2,1,0:T(8,128)(2,1)S(1)}, u32[]{:S(2)}, u32[]{:S(2)}) collective-permute-start(bf16[2,2,24,3072]{3,2,1,0:T(8,128)(2,1)S(1)} %pad_maximum_fusion.3.refs_2_), channel_id=1, source_target_pairs={{0,8},{1,9},{2,10},{3,11},{4,12},{5,13},{6,14},{7,15},{8,0},{9,1},... | collective-permute-start | bytes 1769480 | tf_op jit(solution)/shard_map/ppermute | solution.py:34
  54.6 10.9 %collective-permute-start.12 = (bf16[2,24,4096]{2,1,0:T(8,128)(2,1)S(1)}, bf16[2,24,4096]{2,1,0:T(8,128)(2,1)S(1)}, u32[]{:S(2)}, u32[]{:S(2)}) collective-permute-start(bf16[2,24,4096]{2,1,0:T(8,128)(2,1)S(1)} %pad_maximum_fusion.5), channel_id=1, source_target_pairs={{0,1},{1,0},{2,3},{3,2},{4,5},{5,4},{6,7},{7,6},{8,9},{9,8},{10,11... | collective-permute-start | bytes 1179656 | tf_op jit(solution)/shard_map/ppermute | solution.py:34
  56.2 2.0 collective-permute-start.15
  56.2 2.8 %collective-permute-start.17 = (bf16[2,2,24,3072]{3,2,1,0:T(8,128)(2,1)S(1)}, bf16[2,2,24,3072]{3,2,1,0:T(8,128)(2,1)S(1)}, u32[]{:S(2)}, u32[]{:S(2)}) collective-permute-start(bf16[2,2,24,3072]{3,2,1,0:T(8,128)(2,1)S(1)} %collective-permute-done.10.refs_3_), channel_id=1, source_target_pairs={{0,8},{1,9},{2,10},{3,11},{4,12},{5,13},{6,14},{7,15},{8,0},{9,1},... | collective-permute-start | bytes 1769480 | tf_op jit(solution)/shard_map/ppermute | solution.py:34
  56.8 11.1 %collective-permute-start.13 = (bf16[2,24,4096]{2,1,0:T(8,128)(2,1)S(1)}, bf16[2,24,4096]{2,1,0:T(8,128)(2,1)S(1)}, u32[]{:S(2)}, u32[]{:S(2)}) collective-permute-start(bf16[2,24,4096]{2,1,0:T(8,128)(2,1)S(1)} %pad_maximum_fusion.6), channel_id=1, source_target_pairs={{0,16},{1,17},{2,18},{3,19},{4,20},{5,21},{6,22},{7,23},{8,24},{9,... | collective-permute-start | bytes 1179656 | tf_op jit(solution)/shard_map/ppermute | solution.py:34
  68.1 21.6 %collective-permute-start.18 = (bf16[2,2,24,4096]{3,2,1,0:T(8,128)(2,1)S(1)}, bf16[2,2,24,4096]{3,2,1,0:T(8,128)(2,1)S(1)}, u32[]{:S(2)}, u32[]{:S(2)}) collective-permute-start(bf16[2,2,24,4096]{3,2,1,0:T(8,128)(2,1)S(1)} %bitcast.91), channel_id=1, source_target_pairs={{0,16},{1,17},{2,18},{3,19},{4,20},{5,21},{6,22},{7,23},{8,24},{9,... | collective-permute-start | bytes 2359304 | tf_op jit(solution)/shard_map/ppermute | solution.py:34
  69.4 20.8 %copy-start.7 = (f32[768]{0:T(1024)S(1)}, f32[768]{0:T(1024)}, u32[]{:S(2)}) copy-start(f32[768]{0:T(1024)} %param.24) | copy-start | bytes 9220
  69.4 20.3 %collective-permute-start.19 = (bf16[2,2,24,4096]{3,2,1,0:T(8,128)(2,1)S(1)}, bf16[2,2,24,4096]{3,2,1,0:T(8,128)(2,1)S(1)}, u32[]{:S(2)}, u32[]{:S(2)}) collective-permute-start(bf16[2,2,24,4096]{3,2,1,0:T(8,128)(2,1)S(1)} %pad_maximum_fusion.1.refs_2_), channel_id=1, source_target_pairs={{0,1},{1,0},{2,3},{3,2},{4,5},{5,4},{6,7},{7,6},{8,9},{9,8},{10,11... | collective-permute-start | bytes 2359304 | tf_op jit(solution)/shard_map/ppermute | solution.py:34
  70.0 19.7 %collective-permute-start.20 = (bf16[2,2,64,768]{3,2,1,0:T(8,128)(2,1)S(1)}, bf16[2,2,64,768]{3,2,1,0:T(8,128)(2,1)S(1)}, u32[]{:S(2)}, u32[]{:S(2)}) collective-permute-start(bf16[2,2,64,768]{3,2,1,0:T(8,128)(2,1)S(1)} %pad_maximum_fusion.4.refs_0_), channel_id=1, source_target_pairs={{0,4},{1,5},{2,6},{3,7},{4,0},{5,1},{6,2},{7,3},{8,12},{9,13},{10,... | collective-permute-start | bytes 1179656 | tf_op jit(solution)/shard_map/ppermute | solution.py:34
  73.4 21.4 %collective-permute-start.25 = (bf16[2,2,24,4096]{3,2,1,0:T(8,128)(2,1)S(1)}, bf16[2,2,24,4096]{3,2,1,0:T(8,128)(2,1)S(1)}, u32[]{:S(2)}, u32[]{:S(2)}) collective-permute-start(bf16[2,2,24,4096]{3,2,1,0:T(8,128)(2,1)S(1)} %bitcast.92), channel_id=1, source_target_pairs={{0,8},{1,9},{2,10},{3,11},{4,12},{5,13},{6,14},{7,15},{8,0},{9,1},... | collective-permute-start | bytes 2359304 | tf_op jit(solution)/shard_map/ppermute | solution.py:34
  73.4 21.6 %collective-permute-start.27 = (bf16[2,2,24,4096]{3,2,1,0:T(8,128)(2,1)S(1)}, bf16[2,2,24,4096]{3,2,1,0:T(8,128)(2,1)S(1)}, u32[]{:S(2)}, u32[]{:S(2)}) collective-permute-start(bf16[2,2,24,4096]{3,2,1,0:T(8,128)(2,1)S(1)} %pad_maximum_fusion.1.refs_2_), channel_id=1, source_target_pairs={{0,8},{1,9},{2,10},{3,11},{4,12},{5,13},{6,14},{7,15},{8,0},{9,1},... | collective-permute-start | bytes 2359304 | tf_op jit(solution)/shard_map/ppermute | solution.py:34
  87.5 7.3 %copy-start.2 = (bf16[896,768]{1,0:T(8,128)(2,1)}, bf16[896,768]{1,0:T(8,128)(2,1)S(1)}, u32[]{:S(2)}) copy-start(bf16[896,768]{1,0:T(8,128)(2,1)S(1)} %get-tuple-element.232.refs_1_.mixed_hbm) | copy-start | bytes 4128772
  89.7 7.3 %collective-permute-start.26 = (bf16[2,2,24,4096]{3,2,1,0:T(8,128)(2,1)S(1)}, bf16[2,2,24,4096]{3,2,1,0:T(8,128)(2,1)S(1)}, u32[]{:S(2)}, u32[]{:S(2)}) collective-permute-start(bf16[2,2,24,4096]{3,2,1,0:T(8,128)(2,1)S(1)} %collective-permute-done.18.refs_1_), channel_id=1, source_target_pairs={{0,8},{1,9},{2,10},{3,11},{4,12},{5,13},{6,14},{7,15},{8,0},{9,1},... | collective-permute-start | bytes 2359304 | tf_op jit(solution)/shard_map/ppermute | solution.py:34
  89.7 7.4 %collective-permute-start.28 = (bf16[2,2,24,4096]{3,2,1,0:T(8,128)(2,1)S(1)}, bf16[2,2,24,4096]{3,2,1,0:T(8,128)(2,1)S(1)}, u32[]{:S(2)}, u32[]{:S(2)}) collective-permute-start(bf16[2,2,24,4096]{3,2,1,0:T(8,128)(2,1)S(1)} %collective-permute-done.19.refs_3_), channel_id=1, source_target_pairs={{0,8},{1,9},{2,10},{3,11},{4,12},{5,13},{6,14},{7,15},{8,0},{9,1},... | collective-permute-start | bytes 2359304 | tf_op jit(solution)/shard_map/ppermute | solution.py:34
  90.2 21.5 %collective-permute-start.21 = (bf16[2,2,64,768]{3,2,1,0:T(8,128)(2,1)S(1)}, bf16[2,2,64,768]{3,2,1,0:T(8,128)(2,1)S(1)}, u32[]{:S(2)}, u32[]{:S(2)}) collective-permute-start(bf16[2,2,64,768]{3,2,1,0:T(8,128)(2,1)S(1)} %pad_maximum_fusion.4.refs_0_), channel_id=1, source_target_pairs={{0,2},{1,3},{2,0},{3,1},{4,6},{5,7},{6,4},{7,5},{8,10},{9,11},{10,... | collective-permute-start | bytes 1179656 | tf_op jit(solution)/shard_map/ppermute | solution.py:34
  94.8 16.9 %collective-permute-start.23 = (bf16[2,2,64,768]{3,2,1,0:T(8,128)(2,1)S(1)}, bf16[2,2,64,768]{3,2,1,0:T(8,128)(2,1)S(1)}, u32[]{:S(2)}, u32[]{:S(2)}) collective-permute-start(bf16[2,2,64,768]{3,2,1,0:T(8,128)(2,1)S(1)} %pad_maximum_fusion.4.refs_0_), channel_id=1, source_target_pairs={{0,8},{1,9},{2,10},{3,11},{4,12},{5,13},{6,14},{7,15},{8,0},{9,1},... | collective-permute-start | bytes 1179656 | tf_op jit(solution)/shard_map/ppermute | solution.py:34
  95.0 16.8 %collective-permute-start.22 = (bf16[2,2,64,768]{3,2,1,0:T(8,128)(2,1)S(1)}, bf16[2,2,64,768]{3,2,1,0:T(8,128)(2,1)S(1)}, u32[]{:S(2)}, u32[]{:S(2)}) collective-permute-start(bf16[2,2,64,768]{3,2,1,0:T(8,128)(2,1)S(1)} %collective-permute-done.20.refs_2_), channel_id=1, source_target_pairs={{0,2},{1,3},{2,0},{3,1},{4,6},{5,7},{6,4},{7,5},{8,10},{9,11},{10,... | collective-permute-start | bytes 1179656 | tf_op jit(solution)/shard_map/ppermute | solution.py:34
  97.0 14.8 %collective-permute-start.24 = (bf16[2,2,64,768]{3,2,1,0:T(8,128)(2,1)S(1)}, bf16[2,2,64,768]{3,2,1,0:T(8,128)(2,1)S(1)}, u32[]{:S(2)}, u32[]{:S(2)}) collective-permute-start(bf16[2,2,64,768]{3,2,1,0:T(8,128)(2,1)S(1)} %collective-permute-done.20.refs_2_), channel_id=1, source_target_pairs={{0,8},{1,9},{2,10},{3,11},{4,12},{5,13},{6,14},{7,15},{8,0},{9,1},... | collective-permute-start | bytes 1179656 | tf_op jit(solution)/shard_map/ppermute | solution.py:34
  111.8 4.6 %collective-permute-start.31 = (bf16[2,512,768]{2,1,0:T(8,128)(2,1)S(1)}, bf16[2,512,768]{2,1,0:T(8,128)(2,1)S(1)}, u32[]{:S(2)}, u32[]{:S(2)}) collective-permute-start(bf16[2,512,768]{2,1,0:T(8,128)(2,1)S(1)} %get-tuple-element.256), channel_id=1, source_target_pairs={{0,8},{1,9},{2,10},{3,11},{4,12},{5,13},{6,14},{7,15},{8,0},{9,1},... | collective-permute-start | bytes 4718600 | tf_op jit(solution)/shard_map/ppermute | solution.py:34
  112.2 3.6 %collective-permute-start.29 = (bf16[2,2,64,768]{3,2,1,0:T(8,128)(2,1)S(1)}, bf16[2,2,64,768]{3,2,1,0:T(8,128)(2,1)S(1)}, u32[]{:S(2)}, u32[]{:S(2)}) collective-permute-start(bf16[2,2,64,768]{3,2,1,0:T(8,128)(2,1)S(1)} %collective-permute-done.21.refs_1_), channel_id=1, source_target_pairs={{0,8},{1,9},{2,10},{3,11},{4,12},{5,13},{6,14},{7,15},{8,0},{9,1},... | collective-permute-start | bytes 1179656 | tf_op jit(solution)/shard_map/ppermute | solution.py:34
  112.4 4.0 %collective-permute-start.30 = (bf16[2,2,64,768]{3,2,1,0:T(8,128)(2,1)S(1)}, bf16[2,2,64,768]{3,2,1,0:T(8,128)(2,1)S(1)}, u32[]{:S(2)}, u32[]{:S(2)}) collective-permute-start(bf16[2,2,64,768]{3,2,1,0:T(8,128)(2,1)S(1)} %collective-permute-done.22.refs_3_), channel_id=1, source_target_pairs={{0,8},{1,9},{2,10},{3,11},{4,12},{5,13},{6,14},{7,15},{8,0},{9,1},... | collective-permute-start | bytes 1179656 | tf_op jit(solution)/shard_map/ppermute | solution.py:34
  117.1 19.9 %collective-permute-start.32 = (bf16[2,4,64,768]{3,2,1,0:T(8,128)(2,1)S(1)}, bf16[2,4,64,768]{3,2,1,0:T(8,128)(2,1)S(1)}, u32[]{:S(2)}, u32[]{:S(2)}) collective-permute-start(bf16[2,4,64,768]{3,2,1,0:T(8,128)(2,1)S(1)} %plane.3), channel_id=1, source_target_pairs={{0,1},{1,0},{2,3},{3,2},{4,5},{5,4},{6,7},{7,6},{8,9},{9,8},{10,11... | collective-permute-start | bytes 2359304 | tf_op jit(solution)/shard_map/ppermute | solution.py:34
  137.0 16.3 %collective-permute-start.34 = (bf16[2,192,4096]{2,1,0:T(8,128)(2,1)S(1)}, bf16[2,192,4096]{2,1,0:T(8,128)(2,1)S(1)}, u32[]{:S(2)}, u32[]{:S(2)}) collective-permute-start(bf16[2,192,4096]{2,1,0:T(8,128)(2,1)S(1)} %get-tuple-element.277), channel_id=1, source_target_pairs={{0,8},{1,9},{2,10},{3,11},{4,12},{5,13},{6,14},{7,15},{8,0},{9,1},... | collective-permute-start | bytes 9437192 | tf_op jit(solution)/shard_map/ppermute | solution.py:34
  137.7 15.6 %collective-permute-start.33 = (bf16[4,64,768]{2,1,0:T(8,128)(2,1)S(1)}, bf16[4,64,768]{2,1,0:T(8,128)(2,1)S(1)}, u32[]{:S(2)}, u32[]{:S(2)}) collective-permute-start(bf16[4,64,768]{2,1,0:T(8,128)(2,1)S(1)} %far.3), channel_id=1, source_target_pairs={{0,16},{1,17},{2,18},{3,19},{4,20},{5,21},{6,22},{7,23},{8,24},{9,... | collective-permute-start | bytes 1179656 | tf_op jit(solution)/shard_map/ppermute | solution.py:34
  154.3 22.0 %collective-permute-start.38 = (bf16[2,2,24,4096]{3,2,1,0:T(8,128)(2,1)S(1)}, bf16[2,2,24,4096]{3,2,1,0:T(8,128)(2,1)S(1)}, u32[]{:S(2)}, u32[]{:S(2)}) collective-permute-start(bf16[2,2,24,4096]{3,2,1,0:T(8,128)(2,1)S(1)} %get-tuple-element.290), channel_id=1, source_target_pairs={{0,1},{1,0},{2,3},{3,2},{4,5},{5,4},{6,7},{7,6},{8,9},{9,8},{10,11... | collective-permute-start | bytes 2359304 | tf_op jit(solution)/shard_map/ppermute | solution.py:34
  155.1 21.3 %collective-permute-start.39 = (bf16[2,2,24,4096]{3,2,1,0:T(8,128)(2,1)S(1)}, bf16[2,2,24,4096]{3,2,1,0:T(8,128)(2,1)S(1)}, u32[]{:S(2)}, u32[]{:S(2)}) collective-permute-start(bf16[2,2,24,4096]{3,2,1,0:T(8,128)(2,1)S(1)} %get-tuple-element.291), channel_id=1, source_target_pairs={{0,16},{1,17},{2,18},{3,19},{4,20},{5,21},{6,22},{7,23},{8,24},{9,... | collective-permute-start | bytes 2359304 | tf_op jit(solution)/shard_map/ppermute | solution.py:34
  156.8 19.5 %collective-permute-start.35 = (bf16[64,768]{1,0:T(8,128)(2,1)S(1)}, bf16[64,768]{1,0:T(8,128)(2,1)S(1)}, u32[]{:S(2)}, u32[]{:S(2)}) collective-permute-start(bf16[64,768]{1,0:T(8,128)(2,1)S(1)} %get-tuple-element.285), channel_id=1, source_target_pairs={{0,2},{1,3},{2,0},{3,1},{4,6},{5,7},{6,4},{7,5},{8,10},{9,11},{10,... | collective-permute-start | bytes 294920 | tf_op jit(solution)/shard_map/ppermute | solution.py:34
  157.3 19.0 %collective-permute-start.36 = (bf16[64,768]{1,0:T(8,128)(2,1)S(1)}, bf16[64,768]{1,0:T(8,128)(2,1)S(1)}, u32[]{:S(2)}, u32[]{:S(2)}) collective-permute-start(bf16[64,768]{1,0:T(8,128)(2,1)S(1)} %get-tuple-element.286), channel_id=1, source_target_pairs={{0,4},{1,5},{2,6},{3,7},{4,0},{5,1},{6,2},{7,3},{8,12},{9,13},{10,... | collective-permute-start | bytes 294920 | tf_op jit(solution)/shard_map/ppermute | solution.py:34
  160.6 15.7 %collective-permute-start.37 = (bf16[64,768]{1,0:T(8,128)(2,1)S(1)}, bf16[64,768]{1,0:T(8,128)(2,1)S(1)}, u32[]{:S(2)}, u32[]{:S(2)}) collective-permute-start(bf16[64,768]{1,0:T(8,128)(2,1)S(1)} %get-tuple-element.287), channel_id=1, source_target_pairs={{0,6},{1,7},{2,4},{3,5},{4,2},{5,3},{6,0},{7,1},{8,14},{9,15},{10,... | collective-permute-start | bytes 294920 | tf_op jit(solution)/shard_map/ppermute | solution.py:34
  177.2 12.1 %collective-permute-start.40 = (bf16[2,24,4096]{2,1,0:T(8,128)(2,1)S(1)}, bf16[2,24,4096]{2,1,0:T(8,128)(2,1)S(1)}, u32[]{:S(2)}, u32[]{:S(2)}) collective-permute-start(bf16[2,24,4096]{2,1,0:T(8,128)(2,1)S(1)} %get-tuple-element.300), channel_id=1, source_target_pairs={{0,16},{1,17},{2,18},{3,19},{4,20},{5,21},{6,22},{7,23},{8,24},{9,... | collective-permute-start | bytes 1179656 | tf_op jit(solution)/shard_map/ppermute | solution.py:34
  178.5 10.8 %collective-permute-start.41 = (bf16[2,24,4096]{2,1,0:T(8,128)(2,1)S(1)}, bf16[2,24,4096]{2,1,0:T(8,128)(2,1)S(1)}, u32[]{:S(2)}, u32[]{:S(2)}) collective-permute-start(bf16[2,24,4096]{2,1,0:T(8,128)(2,1)S(1)} %get-tuple-element.301), channel_id=1, source_target_pairs={{0,1},{1,0},{2,3},{3,2},{4,5},{5,4},{6,7},{7,6},{8,9},{9,8},{10,11... | collective-permute-start | bytes 1179656 | tf_op jit(solution)/shard_map/ppermute | solution.py:34
  189.3 4.6 %collective-permute-start.42 = (bf16[2,192,3072]{2,1,0:T(8,128)(2,1)S(1)}, bf16[2,192,3072]{2,1,0:T(8,128)(2,1)S(1)}, u32[]{:S(2)}, u32[]{:S(2)}) collective-permute-start(bf16[2,192,3072]{2,1,0:T(8,128)(2,1)S(1)} %get-tuple-element.309), channel_id=1, source_target_pairs={{0,8},{1,9},{2,10},{3,11},{4,12},{5,13},{6,14},{7,15},{8,0},{9,1},... | collective-permute-start | bytes 7077896 | tf_op jit(solution)/shard_map/ppermute | solution.py:34
  189.3 4.5 %collective-permute-start.43 = (f32[24,128]{1,0:T(8,128)S(1)}, f32[24,128]{1,0:T(8,128)S(1)}, u32[]{:S(2)}, u32[]{:S(2)}) collective-permute-start(f32[24,128]{1,0:T(8,128)S(1)} %get-tuple-element.316), channel_id=1, source_target_pairs={{0,8},{1,9},{2,10},{3,11},{4,12},{5,13},{6,14},{7,15},{8,0},{9,1},... | collective-permute-start | bytes 36872 | tf_op jit(solution)/shard_map/ppermute | solution.py:34
  194.7 20.8 %collective-permute-start.44 = (bf16[2,2,24,3072]{3,2,1,0:T(8,128)(2,1)S(1)}, bf16[2,2,24,3072]{3,2,1,0:T(8,128)(2,1)S(1)}, u32[]{:S(2)}, u32[]{:S(2)}) collective-permute-start(bf16[2,2,24,3072]{3,2,1,0:T(8,128)(2,1)S(1)} %get-tuple-element.324), channel_id=1, source_target_pairs={{0,1},{1,0},{2,3},{3,2},{4,5},{5,4},{6,7},{7,6},{8,9},{9,8},{10,11... | collective-permute-start | bytes 1769480 | tf_op jit(solution)/shard_map/ppermute | solution.py:34
  195.5 20.0 %collective-permute-start.45 = (bf16[2,2,24,3072]{3,2,1,0:T(8,128)(2,1)S(1)}, bf16[2,2,24,3072]{3,2,1,0:T(8,128)(2,1)S(1)}, u32[]{:S(2)}, u32[]{:S(2)}) collective-permute-start(bf16[2,2,24,3072]{3,2,1,0:T(8,128)(2,1)S(1)} %get-tuple-element.325), channel_id=1, source_target_pairs={{0,16},{1,17},{2,18},{3,19},{4,20},{5,21},{6,22},{7,23},{8,24},{9,... | collective-permute-start | bytes 1769480 | tf_op jit(solution)/shard_map/ppermute | solution.py:34
  196.3 3.9 %collective-permute-start.46 = (f32[24,128]{1,0:T(8,128)S(1)}, f32[24,128]{1,0:T(8,128)S(1)}, u32[]{:S(2)}, u32[]{:S(2)}) collective-permute-start(f32[24,128]{1,0:T(8,128)S(1)} %add.171), channel_id=1, source_target_pairs={{0,2},{1,3},{2,0},{3,1},{4,6},{5,7},{6,4},{7,5},{8,10},{9,11},{10,... | collective-permute-start | bytes 36872 | tf_op jit(solution)/shard_map/ppermute | solution.py:34
  196.3 15.3 %collective-permute-start.47 = (bf16[24,4096]{1,0:T(8,128)(2,1)S(1)}, bf16[24,4096]{1,0:T(8,128)(2,1)S(1)}, u32[]{:S(2)}, u32[]{:S(2)}) collective-permute-start(bf16[24,4096]{1,0:T(8,128)(2,1)S(1)} %get-tuple-element.336), channel_id=1, source_target_pairs={{0,2},{1,3},{2,0},{3,1},{4,6},{5,7},{6,4},{7,5},{8,10},{9,11},{10,... | collective-permute-start | bytes 589832 | tf_op jit(solution)/shard_map/ppermute | solution.py:34
  198.3 17.2 %collective-permute-start.48 = (bf16[24,4096]{1,0:T(8,128)(2,1)S(1)}, bf16[24,4096]{1,0:T(8,128)(2,1)S(1)}, u32[]{:S(2)}, u32[]{:S(2)}) collective-permute-start(bf16[24,4096]{1,0:T(8,128)(2,1)S(1)} %get-tuple-element.337), channel_id=1, source_target_pairs={{0,4},{1,5},{2,6},{3,7},{4,0},{5,1},{6,2},{7,3},{8,12},{9,13},{10,... | collective-permute-start | bytes 589832 | tf_op jit(solution)/shard_map/ppermute | solution.py:34
  200.2 15.3 %collective-permute-start.49 = (bf16[24,4096]{1,0:T(8,128)(2,1)S(1)}, bf16[24,4096]{1,0:T(8,128)(2,1)S(1)}, u32[]{:S(2)}, u32[]{:S(2)}) collective-permute-start(bf16[24,4096]{1,0:T(8,128)(2,1)S(1)} %get-tuple-element.338), channel_id=1, source_target_pairs={{0,6},{1,7},{2,4},{3,5},{4,2},{5,3},{6,0},{7,1},{8,14},{9,15},{10,... | collective-permute-start | bytes 589832 | tf_op jit(solution)/shard_map/ppermute | solution.py:34
  216.3 8.1 %collective-permute-start.50 = (bf16[2,24,3072]{2,1,0:T(8,128)(2,1)S(1)}, bf16[2,24,3072]{2,1,0:T(8,128)(2,1)S(1)}, u32[]{:S(2)}, u32[]{:S(2)}) collective-permute-start(bf16[2,24,3072]{2,1,0:T(8,128)(2,1)S(1)} %get-tuple-element.342), channel_id=1, source_target_pairs={{0,16},{1,17},{2,18},{3,19},{4,20},{5,21},{6,22},{7,23},{8,24},{9,... | collective-permute-start | bytes 884744 | tf_op jit(solution)/shard_map/ppermute | solution.py:34
  217.6 6.8 %collective-permute-start.51 = (bf16[2,24,3072]{2,1,0:T(8,128)(2,1)S(1)}, bf16[2,24,3072]{2,1,0:T(8,128)(2,1)S(1)}, u32[]{:S(2)}, u32[]{:S(2)}) collective-permute-start(bf16[2,24,3072]{2,1,0:T(8,128)(2,1)S(1)} %get-tuple-element.343), channel_id=1, source_target_pairs={{0,1},{1,0},{2,3},{3,2},{4,5},{5,4},{6,7},{7,6},{8,9},{9,8},{10,11... | collective-permute-start | bytes 884744 | tf_op jit(solution)/shard_map/ppermute | solution.py:34
  218.9 5.5 %collective-permute-start.52 = (f32[24,128]{1,0:T(8,128)S(1)}, f32[24,128]{1,0:T(8,128)S(1)}, u32[]{:S(2)}, u32[]{:S(2)}) collective-permute-start(f32[24,128]{1,0:T(8,128)S(1)} %add.172), channel_id=1, source_target_pairs={{0,4},{1,5},{2,6},{3,7},{4,0},{5,1},{6,2},{7,3},{8,12},{9,13},{10,... | collective-permute-start | bytes 36872 | tf_op jit(solution)/shard_map/ppermute | solution.py:34
  225.4 18.4 %collective-permute-start.55 = (bf16[24,3072]{1,0:T(8,128)(2,1)S(1)}, bf16[24,3072]{1,0:T(8,128)(2,1)S(1)}, u32[]{:S(2)}, u32[]{:S(2)}) collective-permute-start(bf16[24,3072]{1,0:T(8,128)(2,1)S(1)} %get-tuple-element.379), channel_id=1, source_target_pairs={{0,6},{1,7},{2,4},{3,5},{4,2},{5,3},{6,0},{7,1},{8,14},{9,15},{10,... | collective-permute-start | bytes 442376 | tf_op jit(solution)/shard_map/ppermute | solution.py:34
  227.8 16.0 %collective-permute-start.54 = (bf16[24,3072]{1,0:T(8,128)(2,1)S(1)}, bf16[24,3072]{1,0:T(8,128)(2,1)S(1)}, u32[]{:S(2)}, u32[]{:S(2)}) collective-permute-start(bf16[24,3072]{1,0:T(8,128)(2,1)S(1)} %get-tuple-element.378), channel_id=1, source_target_pairs={{0,4},{1,5},{2,6},{3,7},{4,0},{5,1},{6,2},{7,3},{8,12},{9,13},{10,... | collective-permute-start | bytes 442376 | tf_op jit(solution)/shard_map/ppermute | solution.py:34
  230.8 13.1 %collective-permute-start.53 = (bf16[24,3072]{1,0:T(8,128)(2,1)S(1)}, bf16[24,3072]{1,0:T(8,128)(2,1)S(1)}, u32[]{:S(2)}, u32[]{:S(2)}) collective-permute-start(bf16[24,3072]{1,0:T(8,128)(2,1)S(1)} %get-tuple-element.377), channel_id=1, source_target_pairs={{0,2},{1,3},{2,0},{3,1},{4,6},{5,7},{6,4},{7,5},{8,10},{9,11},{10,... | collective-permute-start | bytes 442376 | tf_op jit(solution)/shard_map/ppermute | solution.py:34
  231.3 7.6 %collective-permute-start.56 = (f32[24,128]{1,0:T(8,128)S(1)}, f32[24,128]{1,0:T(8,128)S(1)}, u32[]{:S(2)}, u32[]{:S(2)}) collective-permute-start(f32[24,128]{1,0:T(8,128)S(1)} %add.173), channel_id=1, source_target_pairs={{0,1},{1,0},{2,3},{3,2},{4,5},{5,4},{6,7},{7,6},{8,9},{9,8},{10,11... | collective-permute-start | bytes 36872 | tf_op jit(solution)/shard_map/ppermute | solution.py:34
  231.6 13.6 %copy-start.1 = (f32[32,12]{0,1:T(8,128)S(1)}, f32[32,12]{0,1:T(8,128)}, u32[]{:S(2)}) copy-start(f32[32,12]{0,1:T(8,128)} %param.25) | copy-start | bytes 4612
  238.9 3.8 %collective-permute-start.57 = (f32[24,128]{1,0:T(8,128)S(1)}, f32[24,128]{1,0:T(8,128)S(1)}, u32[]{:S(2)}, u32[]{:S(2)}) collective-permute-start(f32[24,128]{1,0:T(8,128)S(1)} %add.186), channel_id=1, source_target_pairs={{0,16},{1,17},{2,18},{3,19},{4,20},{5,21},{6,22},{7,23},{8,24},{9,... | collective-permute-start | bytes 36872 | tf_op jit(solution)/shard_map/ppermute | solution.py:34
  (2 other events, 10.4 us)
